TPU v7x, 32 devices: a whole 2x2x4 slice. The times are simulated.
32 devices in a mesh: grp: 2 (over y), seq: 4 (over z), tp: 4 (over x, core).
Axes of the slice: x: 2, y: 2, z: 4, core: 2. Of those that a mesh axis runs over, the one named last changes fastest.
Arguments:
- ssm_input: bfloat16 [2048, 8192], P(('grp', 'seq'), 'tp'), parts along dimension 0, may hold values from -6 to 6
- bmat: bfloat16 [2048, 1024], P(('grp', 'seq'), 'tp'), parts along dimension 0, may hold values from -6 to 6
- cmat: bfloat16 [2048, 1024], P(('grp', 'seq'), 'tp'), parts along dimension 0, may hold values from -6 to 6
- dt_raw: bfloat16 [2048, 128], P(('grp', 'seq'), 'tp'), parts along dimension 0
- a_log: float32 [128], P('tp'), may hold values from -0.5 to 0.5
- d_skip: float32 [128], P('tp'), may hold values from 0.5 to 1.5
- prompt_len: int32 [16], P('grp'), parts along dimension 0, may hold values from 1 to 1024, as said below
- owner: int32 [16], P('grp'), parts along dimension 0, may hold values from 0 to 3, as said below
- dec_x: bfloat16 [8, 4, 4, 8192], P(('grp', 'seq'), None, None, 'tp'), parts along dimension 0, may hold values from -6 to 6
- dec_b: bfloat16 [8, 4, 4, 1024], P(('grp', 'seq'), None, None, 'tp'), parts along dimension 0, may hold values from -6 to 6
- dec_c: bfloat16 [8, 4, 4, 1024], P(('grp', 'seq'), None, None, 'tp'), parts along dimension 0, may hold values from -6 to 6
- dec_dt: bfloat16 [8, 4, 4, 128], P(('grp', 'seq'), None, None, 'tp'), parts along dimension 0
Outputs:
- prefill_out: bfloat16 [2048, 8192], P(('grp', 'seq'), 'tp'), parts along dimension 0
- decode_out: bfloat16 [8, 4, 4, 8192], P(('grp', 'seq'), None, None, 'tp'), parts along dimension 0
There are 2 independent parts, one for each index of `grp`. A program takes and returns all parts, laid end to end along the dimension named above; an argument that names none is the same for every part. Nothing has to cross between parts.
Inputs may be any that keep to these rules, and one draw needn't show every extreme that they name: `prompt_len`: no two requests have both the same owner and the same 256-position part of the prompt holding their last prompt position. Each owner decodes at most 4 requests and each part holds the last position of at most 4; some owner and some part reach that in every draw. `owner`: every index of seq owns at least one request.
All inputs are finite; a program needn't handle non-finite values.
Results may differ from a plain program's by a relative error of at most 0.0055.
Values may be sent and summed in bfloat16 or wider, within the bound.
No kernel may reach another device: no remote copies, remote signals or barrier semaphores. Data moves between devices by JAX's collectives and lax.ppermute only.
A program may use at most 128 MiB of HBM per device.

v0:
```python
import math

import jax
import jax.numpy as jnp
from jax import lax
from jax.sharding import PartitionSpec as P

H = 128
P_SIZE = 64
N = 128
G = 8
SPAN = 128
STEPS = 4


def carried_in(value, axis, join, neutral):
    count, mine = (lax.axis_size(axis), lax.axis_index(axis))
    pieces = jax.tree.map(lambda part: lax.all_gather(part, axis), value)
    total = jax.tree.map(
        lambda part, zero: jnp.full_like(part, 0) + jnp.asarray(zero, part.dtype), value, neutral
    )

    def lap(position, total):
        longer = join(total, jax.tree.map(lambda part: part[position], pieces))
        return jax.tree.map(lambda new, old: jnp.where(position < mine, new, old), longer, total)

    return lax.fori_loop(0, count - 1, lap, total)


def blocked(function, arrays, batch_size):
    leading = arrays[0].shape[0]
    split = tuple(
        (item.reshape((leading // batch_size, batch_size) + item.shape[1:]) for item in arrays)
    )
    results = lax.map(lambda items: jax.vmap(function)(*items), split)
    return jax.tree.map(lambda value: value.reshape((leading,) + value.shape[2:]), results)


def shards(
    ssm_input, bmat, cmat, dt_raw, a_log, d_skip, prompt_len, owner, dec_x, dec_b, dec_c, dec_dt
):
    highest = lax.Precision.HIGHEST
    tensor_count = lax.axis_size("tp")
    seq_count = lax.axis_size("seq")
    my_index = lax.axis_index("seq")
    heads_here = H // tensor_count
    groups_here = G // tensor_count
    per_group = H // G
    token_count = ssm_input.shape[0]
    span_count = token_count // SPAN
    step_size = jax.nn.softplus(dt_raw.astype(jnp.float32))
    log_decay = -jnp.exp(a_log)[None, :] * step_size
    cumulative = jnp.cumsum(log_decay.reshape(span_count, SPAN, heads_here), axis=1)
    step_spans = step_size.reshape(span_count, SPAN, heads_here)
    x_spans = ssm_input.reshape(span_count, SPAN, heads_here, P_SIZE)
    b_spans = bmat.reshape(span_count, SPAN, groups_here, N)
    c_spans = cmat.reshape(span_count, SPAN, groups_here, N)
    causal = jnp.arange(SPAN)[:, None] >= jnp.arange(SPAN)[None, :]

    def group_scaled(b_part, factor):
        grouped = factor.reshape(SPAN, groups_here, per_group)[:, :, :, None]
        product = b_part.astype(jnp.float32)[:, :, None, :] * grouped
        return product.astype(jnp.bfloat16).reshape(SPAN, heads_here, N)

    def span_local(x_part, b_part, c_part, cum_part, step_part):
        score_values = jnp.einsum(
            "tgn,sgn->gts", c_part, b_part, preferred_element_type=jnp.float32
        )
        head_scores = jnp.repeat(score_values, per_group, axis=0)
        spread = cum_part.T[:, :, None] - cum_part.T[:, None, :]
        decay = jnp.where(causal[None], jnp.exp(jnp.where(causal[None], spread, 0.0)), 0.0)
        weights = (head_scores * decay * step_part.T[:, None, :]).astype(jnp.bfloat16)
        inner = jnp.einsum("hts,shp->thp", weights, x_part, preferred_element_type=jnp.float32)
        scaled = group_scaled(b_part, jnp.exp(cum_part[-1][None, :] - cum_part) * step_part)
        span_state = jnp.einsum("shp,shn->hpn", x_part, scaled, preferred_element_type=jnp.float32)
        return (inner, span_state)

    inner_all, span_states = blocked(
        span_local, (x_spans, b_spans, c_spans, cumulative, step_spans), math.gcd(4, span_count)
    )
    block_ends = cumulative[:, -1, :]

    def carry_local(state, items):
        ending, span_state = items
        return (jnp.exp(ending)[:, None, None] * state + span_state, state)

    zero_state = jnp.zeros((heads_here, P_SIZE, N), jnp.float32)
    local_total, local_starts = lax.scan(carry_local, zero_state, (block_ends, span_states))

    def combine(earlier, later):
        return (earlier[0] + later[0], jnp.exp(later[0])[:, None, None] * earlier[1] + later[1])

    device_decay = jnp.sum(block_ends, axis=0)
    incoming = carried_in(
        (device_decay, local_total),
        "seq",
        combine,
        (jnp.zeros((heads_here,), jnp.float32), zero_state),
    )[1]
    decay_before = jnp.exp(jnp.cumsum(block_ends, axis=0) - block_ends)
    span_start = decay_before[:, :, None, None] * incoming[None] + local_starts
    carried = jnp.einsum(
        "ctgn,cgjpn->ctgjp",
        c_spans.astype(jnp.float32),
        span_start.reshape(span_count, groups_here, per_group, P_SIZE, N),
        precision=highest,
    )
    outer = jnp.exp(cumulative)[..., None] * carried.reshape(span_count, SPAN, heads_here, P_SIZE)
    prefill = (
        inner_all + outer + d_skip[None, None, :, None] * x_spans.astype(jnp.float32)
    ).astype(jnp.bfloat16)
    prefill = prefill.reshape(token_count, heads_here * P_SIZE)
    last_token = prompt_len - 1
    sources = last_token // token_count
    targets = jnp.arange(seq_count, dtype=jnp.int32)
    mine = (sources == my_index)[None, :] & (owner[None, :] == targets[:, None])
    offsets = jnp.sum(jnp.where(mine, last_token[None, :] - my_index * token_count, 0), axis=1)
    positions = jnp.arange(SPAN)

    def request_state(spot):
        span_index = spot // SPAN
        offset = spot % SPAN
        x_part = lax.dynamic_index_in_dim(x_spans, span_index, 0, keepdims=False)
        b_part = lax.dynamic_index_in_dim(b_spans, span_index, 0, keepdims=False)
        cum_part = lax.dynamic_index_in_dim(cumulative, span_index, 0, keepdims=False)
        step_part = lax.dynamic_index_in_dim(step_spans, span_index, 0, keepdims=False)
        state = lax.dynamic_index_in_dim(span_start, span_index, 0, keepdims=False)
        cum_last = lax.dynamic_index_in_dim(cum_part, offset, 0, keepdims=False)
        upto = positions[:, None] <= offset
        weight = jnp.where(
            upto, jnp.exp(jnp.where(upto, cum_last[None, :] - cum_part, 0.0)) * step_part, 0.0
        )
        scaled = group_scaled(b_part, weight)
        local_sum = jnp.einsum("shp,shn->hpn", x_part, scaled, preferred_element_type=jnp.float32)
        return (jnp.exp(cum_last)[:, None, None] * state + local_sum).astype(jnp.bfloat16)

    states = blocked(request_state, (offsets,), math.gcd(4, seq_count))
    arrived = (
        lax.all_to_all(dec_x[0], "seq", split_axis=0, concat_axis=0, tiled=True),
        lax.all_to_all(dec_b[0], "seq", split_axis=0, concat_axis=0, tiled=True),
        lax.all_to_all(dec_c[0], "seq", split_axis=0, concat_axis=0, tiled=True),
        lax.all_to_all(dec_dt[0], "seq", split_axis=0, concat_axis=0, tiled=True),
    )
    present = jnp.any(mine, axis=1)
    slots = states.shape[0]
    x_values = arrived[0].reshape(slots, STEPS, heads_here, P_SIZE).astype(jnp.float32)
    b_values = arrived[1].reshape(slots, STEPS, groups_here, N)
    c_values = arrived[2].reshape(slots, STEPS, groups_here, N)
    steps_now = jax.nn.softplus(arrived[3].astype(jnp.float32))
    running = jnp.cumsum(-jnp.exp(a_log)[None, None, :] * steps_now, axis=1)
    from_state = jnp.einsum(
        "sgjpn,skgn->skgjp",
        states.reshape(slots, groups_here, per_group, P_SIZE, N),
        c_values,
        preferred_element_type=jnp.float32,
    )
    from_state = from_state.reshape(slots, STEPS, heads_here, P_SIZE)
    pair_scores = jnp.einsum(
        "skgn,slgn->sklg", c_values, b_values, preferred_element_type=jnp.float32
    )
    pair_heads = jnp.repeat(pair_scores, per_group, axis=3)
    lower = jnp.arange(STEPS)[:, None] >= jnp.arange(STEPS)[None, :]
    gaps = running[:, :, None, :] - running[:, None, :, :]
    factors = jnp.where(
        lower[None, :, :, None],
        jnp.exp(jnp.where(lower[None, :, :, None], gaps, 0.0)) * steps_now[:, None, :, :],
        0.0,
    )
    fresh = jnp.einsum("sklh,slhp->skhp", factors * pair_heads, x_values, precision=highest)
    result = (
        jnp.exp(running)[..., None] * from_state + fresh + d_skip[None, None, :, None] * x_values
    )
    result = jnp.where(present[:, None, None, None], result, 0.0)
    local_result = result.astype(jnp.bfloat16).reshape(slots, STEPS, heads_here * P_SIZE)
    decoded = lax.all_to_all(local_result, "seq", split_axis=0, concat_axis=0, tiled=True)
    return (prefill, decoded[None])


def solution(mesh):
    placed = (
        P(("grp", "seq"), "tp"),
        P(("grp", "seq"), "tp"),
        P(("grp", "seq"), "tp"),
        P(("grp", "seq"), "tp"),
        P("tp"),
        P("tp"),
        P("grp"),
        P("grp"),
        P(("grp", "seq"), None, None, "tp"),
        P(("grp", "seq"), None, None, "tp"),
        P(("grp", "seq"), None, None, "tp"),
        P(("grp", "seq"), None, None, "tp"),
    )
    return jax.shard_map(
        shards,
        mesh=mesh,
        in_specs=placed,
        out_specs=(P(("grp", "seq"), "tp"), P(("grp", "seq"), None, None, "tp")),
        check_vma=False,
    )
```

profile of v0, /device:TPU:0, one launch (start us, length us, event | category | flops | bytes accessed | tf_op | source)
XLA Modules:
  0.0 146.8 jit_solution(14673091983803329230)
XLA Ops:
  7.2 0.7 exponential_negate_fusion
  7.9 0.8 compare_select_fusion
  9.5 0.9 squeeze.81
  10.6 0.7 fusion.65
  11.3 0.7 copy.104
  12.0 1.5 %copy.99 = bf16[256,2048]{0,1:T(8,128)(2,1)S(1)} copy(bf16[256,2048]{1,0:T(8,128)(2,1)} %param.16) | data formatting | bytes 2097152 | tf_op args[0]
  13.5 1.3 squeeze.83
  15.3 0.7 copy-done.5
  16.0 2.1 %fusion.16 = f32[2,32,64,128]{3,2,1,0:T(8,128)S(1)} fusion(f32[2,128,32,128]{3,1,2,0:T(8,128)S(1)} %bitcast.129, f32[2,128,32]{1,2,0:T(8,128)S(1)} %copy-done.12, bf16[2,128,32,64]{1,0,3,2:T(2,128)(2,1)S(1)} %copy-done.5), kind=kOutput, calls=%fused_computation.33 | convolution fusion | flops 136314880 | bytes 7372800 | tf_op jit(solution)/shard_map/while/body/eval_jaxpr/vmap(shp,shn->hpn)/dot_general | solution.py:75
  18.1 2.6 %while.8 = (s32[]{:T(128)}, f32[32,64,128]{2,1,0:T(8,128)S(1)}, f32[2,32,64,128]{3,2,1,0:T(8,128)}, f32[2,32]{1,0:T(2,128)S(1)}, f32[2,32,64,128]{3,2,1,0:T(8,128)S(1)}, /*index=5*/s32[]{:T(128)}, s32[]{:T(128)}) while((s32[]{:T(128)}, f32[32,64,128]{2,1,0:T(8,128)S(1)}, f32[2,32,64,128]{3,2,1,0:T(8,128)}, f32[2,32]{1,0:T(2,128)S(1)}, ...), condition=%wide.region_4.5_spmd.clone, body=%wide.region_3.4_spmd.clone.sunk | while | flops 1048579 | bytes 5243372 | solution.py:88
  18.1 1.1 bitcast_dynamic-update-slice_fusion.2
  19.4 1.1 bitcast_dynamic-update-slice_fusion.2
  20.7 1.0 copy-done
  21.8 6.4 %all-to-all-start = ((bf16[4,4,32]{2,1,0:T(4,128)(2,1)}), bf16[4,4,32]{2,1,0:T(4,128)(2,1)S(1)}, u32[]{:S(2)}, u32[]{:S(2)}) async-start(bf16[4,4,32]{2,1,0:T(4,128)(2,1)} %bitcast.14), calls=%async_computation | async-start | bytes 8192 | tf_op jit(solution)/shard_map/all_to_all | solution.py:142
  28.3 1.0 squeeze.80
  29.4 0.7 fusion.59
  30.1 0.7 add_subtract_fusion
  32.1 0.6 gather_fusion.5
  32.8 0.6 subtract_exponential_fusion
  33.4 0.7 multiply_select_fusion
  34.9 0.8 copy-done.6
  35.7 3.3 %fusion.17 = f32[2,128,32,64]{1,3,2,0:T(8,128)} fusion(f32[2,32,128,128]{3,2,1,0:T(8,128)S(1)} %bitcast.135, f32[2,32,128]{2,1,0:T(8,128)S(1)} %copy.98, f32[2,32,128]{2,1,0:T(8,128)S(1)} %copy.95, pred[128,128]{1,0:T(8,128)(4,1)S(1)} %iota_compare_fusion, bf16[2,128,32,64]{1,0,3,2:T(2,128)(2,1)S(1)} %copy-done.6), kind=kOutput, calls=%fused_computation.35 | convolution fusion | flops 140509184 | bytes 7421952 | tf_op jit(solution)/shard_map/while/body/eval_jaxpr/vmap(hts,shp->thp)/dot_general | solution.py:73
  39.0 0.7 fusion.50
  39.7 5.1 %all-to-all-start.2 = ((bf16[4,4,256]{2,1,0:T(4,128)(2,1)}), bf16[4,4,256]{2,1,0:T(4,128)(2,1)S(1)}, u32[]{:S(2)}, u32[]{:S(2)}) async-start(bf16[4,4,256]{2,1,0:T(4,128)(2,1)} %bitcast.26), calls=%async_computation.2 | async-start | bytes 16384 | tf_op jit(solution)/shard_map/all_to_all | solution.py:140
  45.2 0.6 exp.96
  46.1 1.2 dynamic-slice.2
  48.1 0.8 dynamic-update-slice
  48.9 12.6 %all-reduce.2 = f32[128]{0:T(128)S(1)} all-reduce(f32[128]{0:T(128)S(1)} %dynamic-update-slice), channel_id=2, replica_groups=mesh['grp'=2,'seq'=4,'tp'=4] {'seq'}, use_global_device_ids=true, to_apply=%add.2 | all-reduce | flops 128 | bytes 1024
  61.5 0.7 copy.102
  62.2 4.7 %copy.101 = f32[2,128,32,64]{1,0,3,2:T(2,128)} copy(f32[2,128,32,64]{1,3,2,0:T(8,128)} %fusion.17) | data formatting | bytes 4194304 | tf_op jit(solution)/shard_map/while/body/eval_jaxpr/vmap(hts,shp->thp)/transpose | solution.py:73
  66.9 0.7 mul.220
  67.6 2.2 %gather_fusion.2 = bf16[4,128,32,64]{1,3,2,0:T(8,128)(2,1)} fusion(bf16[2,128,32,64]{1,3,2,0:T(8,128)(2,1)S(1)} %copy.100, s32[4]{0:T(128)S(1)} %get-tuple-element.252), kind=kCustom, calls=%fused_computation.2 | custom fusion | bytes 4194368 | tf_op jit(solution)/shard_map/while/body/eval_jaxpr/vmap(jit(dynamic_index_in_dim))/gather | solution.py:123
  69.8 0.6 gather_fusion.3
  70.5 0.6 copy-done.19
  71.0 3.2 %all-to-all-start.1 = ((bf16[4,4,256]{2,1,0:T(4,128)(2,1)}), bf16[4,4,256]{2,1,0:T(4,128)(2,1)S(1)}, u32[]{:S(2)}, u32[]{:S(2)}) async-start(bf16[4,4,256]{2,1,0:T(4,128)(2,1)} %bitcast.20), calls=%async_computation.1 | async-start | bytes 16384 | tf_op jit(solution)/shard_map/all_to_all | solution.py:141
  74.4 0.7 copy.115
  75.1 0.7 copy.117
  75.8 0.7 copy.109
  76.6 4.0 %all-to-all-done.1 = bf16[4,4,256]{2,1,0:T(4,128)(2,1)S(1)} async-done(((bf16[4,4,256]{2,1,0:T(4,128)(2,1)}), bf16[4,4,256]{2,1,0:T(4,128)(2,1)S(1)}, u32[]{:S(2)}, u32[]{:S(2)}) %all-to-all-start.1) | async-done | bytes 8224 | tf_op jit(solution)/shard_map/all_to_all | solution.py:141
  80.6 3.5 %all-to-all-start.3 = ((bf16[4,4,2048]{2,1,0:T(4,128)(2,1)}), bf16[4,4,2048]{2,1,0:T(4,128)(2,1)S(1)}, u32[]{:S(2)}, u32[]{:S(2)}) async-start(bf16[4,4,2048]{2,1,0:T(4,128)(2,1)} %bitcast.30), calls=%async_computation.3 | async-start | bytes 131072 | tf_op jit(solution)/shard_map/all_to_all | solution.py:139
  84.1 0.8 convolution_bitcast_fusion.2
  84.9 0.7 copy.118
  85.6 4.5 %all-to-all-done.3 = bf16[4,4,2048]{2,1,0:T(4,128)(2,1)S(1)} async-done(((bf16[4,4,2048]{2,1,0:T(4,128)(2,1)}), bf16[4,4,2048]{2,1,0:T(4,128)(2,1)S(1)}, u32[]{:S(2)}, u32[]{:S(2)}) %all-to-all-start.3) | async-done | bytes 65568 | tf_op jit(solution)/shard_map/all_to_all | solution.py:139
  90.1 0.8 reshape.322
  90.9 16.5 %all-gather.4.cloned.1.call-done = f32[128,64,128]{2,1,0:T(8,128)} async-done(((f32[32,64,128]{2,1,0:T(8,128)}), f32[128,64,128]{2,1,0:T(8,128)}) %all-gather.4.cloned.1.call-update) | async-done | bytes 4194320 | tf_op jit(solution)/shard_map/all_gather | solution.py:18
  107.4 4.5 %while.18 = (s32[]{:T(128)}, f32[32,64,128]{2,1,0:T(8,128)S(1)}, s32[]{:T(128)}, f32[4,32]{1,0:T(4,128)S(1)}, f32[4,32,64,128]{3,2,1,0:T(8,128)}, /*index=5*/s32[]{:T(128)}, s32[]{:T(128)}) while((s32[]{:T(128)}, f32[32,64,128]{2,1,0:T(8,128)S(1)}, s32[]{:T(128)}, f32[4,32]{1,0:T(4,128)S(1)}, f32[4,32,64,128]{3,2,1,0:T(8,128)}, ...), condition=%wide.region_6.7_spmd.clone, body=%wide.region_5.6_spmd.clone.sunk | while | flops 1048580 | bytes 3146225 | solution.py:27
  107.4 1.5 fusion.72
  108.9 1.5 fusion.72
  110.4 1.5 fusion.72
  111.9 1.8 %multiply_add_fusion = f32[2,32,64,128]{3,2,1,0:T(8,128)S(1)} fusion(f32[2,32,64,128]{3,2,1,0:T(8,128)} %get-tuple-element.180, f32[32,64,128]{2,1,0:T(8,128)S(1)} %get-tuple-element.179, f32[2,32]{1,0:T(2,128)S(1)} %copy-done.21), kind=kLoop, calls=%fused_computation.26 | loop fusion | flops 1048576 | bytes 5243136 | tf_op jit(solution)/shard_map/add | solution.py:101
  113.7 2.8 %gather_fusion.1 = f32[4,32,64,128]{3,2,1,0:T(8,128)} fusion(f32[2,32,64,128]{3,2,1,0:T(8,128)S(1)} %multiply_add_fusion, s32[4]{0:T(128)S(1)} %get-tuple-element.252), kind=kCustom, calls=%fused_computation.1 | custom fusion | bytes 8388672 | tf_op jit(solution)/shard_map/while/body/eval_jaxpr/vmap(jit(dynamic_index_in_dim))/gather | solution.py:127
  116.5 1.1 convolution_bitcast_fusion
  117.6 3.0 %copy.107 = f32[2,128,2,16,64]{1,0,4,3,2:T(2,128)} copy(f32[2,128,2,16,64]{1,4,3,2,0:T(8,128)S(1)} %convolution_bitcast_fusion) | data formatting | bytes 4194304 | tf_op jit(solution)/shard_map/ctgn,cgjpn->ctgjp/transpose | solution.py:102
  120.6 1.0 mul.229
  122.2 1.2 copy-done.2
  123.4 3.3 %add_convert_fusion = bf16[4,32,64,128]{3,2,1,0:T(8,128)(2,1)S(1)} fusion(f32[4,32,64,128]{3,2,1,0:T(8,128)S(1)} %copy-done.2, f32[4,32]{1,0:T(4,128)S(1)} %copy-done.20, bf16[4,128,32,64]{1,3,2,0:T(8,128)(2,1)S(1)} %copy-done.1, f32[4,128,32,128]{3,1,2,0:T(8,128)S(1)} %bitcast.128, f32[4,128,32]{1,2,0:T(8,128)S(1)} %copy-done.10), kind=kOutput, calls=%fused_computation.16 | convolution fusion | flops 275775488 | bytes 16843264 | tf_op jit(solution)/shard_map/while/body/eval_jaxpr/vmap(shp,shn->hpn)/dot_general | solution.py:134
  126.9 1.7 %fusion.45 = f32[4,2,16,64,4]{3,4,2,1,0:T(4,128)S(1)} fusion(bf16[4,2,16,64,128]{4,3,2,1,0:T(8,128)(2,1)S(1)} %bitcast.132, bf16[4,4,256]{2,1,0:T(4,128)(2,1)S(1)} %all-to-all-done.1), kind=kOutput, calls=%fused_computation.75 | convolution fusion | flops 8388608 | bytes 2236416 | tf_op jit(solution)/shard_map/sgjpn,skgn->skgjp/dot_general | solution.py:151
  128.7 0.8 fusion.21
  129.6 0.8 reshape.323
  130.4 3.3 %all-to-all-start.4 = ((bf16[4,4,2048]{2,1,0:T(4,128)(2,1)}), bf16[4,4,2048]{2,1,0:T(4,128)(2,1)S(1)}, u32[]{:S(2)}, u32[]{:S(2)}) async-start(bf16[4,4,2048]{2,1,0:T(4,128)(2,1)} %reshape.323), calls=%async_computation.4 | async-start | bytes 131072 | tf_op jit(solution)/shard_map/all_to_all | solution.py:175
  134.2 1.0 copy-done.8
  135.2 1.6 %fusion.9 = bf16[256,2048]{0,1:T(8,128)(2,1)} fusion(f32[256,8,2,128]{3,2,1,0:T(2,128)S(1)} %bitcast.131, f32[256,8,2,128]{3,2,1,0:T(2,128)S(1)} %bitcast.133, f32[256,8,2,128]{3,2,1,0:T(2,128)S(1)} %bitcast.130, bf16[256,2048]{0,1:T(8,128)(2,1)S(1)} %copy-done.4, f32[2048]{0:T(1024)S(1)} %copy-done.18), kind=kLoop, calls=%fused_computation.25 | loop fusion | flops 3145728 | bytes 8396800 | tf_op jit(solution)/shard_map/convert_element_type | solution.py:111
  136.8 2.3 %copy.122 = bf16[256,2048]{1,0:T(8,128)(2,1)} copy(bf16[256,2048]{0,1:T(8,128)(2,1)} %fusion.9) | data formatting | bytes 2097152
  139.4 0.6 copy.164
  (102 shorter events, 7.0 us)
Async XLA Ops:
  7.2 100.2 %all-gather.4.cloned.1.call-start = ((), (), s32[]{:S(2)}) async-start(), calls=%async_computation.5 | async-start | bytes 5242880 | tf_op jit(solution)/shard_map/all_gather | solution.py:18
  7.9 0.9 copy-start.22
  13.5 1.8 %copy-start.3 = (bf16[256,2048]{0,1:T(8,128)(2,1)}, bf16[256,2048]{0,1:T(8,128)(2,1)S(1)}, u32[]{:S(2)}) copy-start(bf16[256,2048]{0,1:T(8,128)(2,1)S(1)} %copy.99) | copy-start | bytes 3145732
  14.7 1.2 copy-start.5
  14.7 1.2 copy-start.12
  18.1 12.7 %copy-start.26 = (s32[8]{0:T(128)S(1)}, s32[8]{0:T(128)}, u32[]{:S(2)}) copy-start(s32[8]{0:T(128)} %param.23) | copy-start | bytes 100
  20.7 1.0 copy-start
  21.8 17.9 %all-to-all-start = ((bf16[4,4,32]{2,1,0:T(4,128)(2,1)}), bf16[4,4,32]{2,1,0:T(4,128)(2,1)S(1)}, u32[]{:S(2)}, u32[]{:S(2)}) async-start(bf16[4,4,32]{2,1,0:T(4,128)(2,1)} %bitcast.14), calls=%async_computation | async-start | bytes 8192 | tf_op jit(solution)/shard_map/all_to_all | solution.py:142
  34.4 1.3 copy-start.6
  35.7 3.3 %copy-start.27 = (s32[8]{0:T(128)S(1)}, s32[8]{0:T(128)}, u32[]{:S(2)}) copy-start(s32[8]{0:T(128)} %param.23) | copy-start | bytes 100
  39.0 22.5 %copy-start.9 = (f32[2,128,32]{2,1,0:T(8,128)S(1)}, f32[2,128,32]{2,1,0:T(8,128)}, u32[]{:S(2)}) copy-start(f32[2,128,32]{2,1,0:T(8,128)} %get-tuple-element.243) | copy-start | bytes 98308
  39.7 30.8 %all-to-all-start.2 = ((bf16[4,4,256]{2,1,0:T(4,128)(2,1)}), bf16[4,4,256]{2,1,0:T(4,128)(2,1)S(1)}, u32[]{:S(2)}, u32[]{:S(2)}) async-start(bf16[4,4,256]{2,1,0:T(4,128)(2,1)} %bitcast.26), calls=%async_computation.2 | async-start | bytes 16384 | tf_op jit(solution)/shard_map/all_to_all | solution.py:140
  62.2 4.7 %copy-start.24 = (f32[32]{0:T(128)S(1)}, f32[32]{0:T(128)}, u32[]{:S(2)}) copy-start(f32[32]{0:T(128)} %param.21) | copy-start | bytes 388
  67.6 6.7 %copy-start.23 = (f32[32]{0:T(128)S(1)}, f32[32]{0:T(128)}, u32[]{:S(2)}) copy-start(f32[32]{0:T(128)} %copy-done.22) | copy-start | bytes 388
  70.4 0.6 copy-start.19
  71.0 9.5 %all-to-all-start.1 = ((bf16[4,4,256]{2,1,0:T(4,128)(2,1)}), bf16[4,4,256]{2,1,0:T(4,128)(2,1)S(1)}, u32[]{:S(2)}, u32[]{:S(2)}) async-start(bf16[4,4,256]{2,1,0:T(4,128)(2,1)} %bitcast.20), calls=%async_computation.1 | async-start | bytes 16384 | tf_op jit(solution)/shard_map/all_to_all | solution.py:141
  80.6 9.5 %all-to-all-start.3 = ((bf16[4,4,2048]{2,1,0:T(4,128)(2,1)}), bf16[4,4,2048]{2,1,0:T(4,128)(2,1)S(1)}, u32[]{:S(2)}, u32[]{:S(2)}) async-start(bf16[4,4,2048]{2,1,0:T(4,128)(2,1)} %bitcast.30), calls=%async_computation.3 | async-start | bytes 131072 | tf_op jit(solution)/shard_map/all_to_all | solution.py:139
  107.4 4.5 %copy-start.21 = (f32[2,32]{1,0:T(2,128)S(1)}, f32[2,32]{1,0:T(2,128)}, u32[]{:S(2)}) copy-start(f32[2,32]{1,0:T(2,128)} %subtract_exponential_fusion) | copy-start | bytes 772
  120.6 1.6 %copy-start.1 = (bf16[4,128,32,64]{1,3,2,0:T(8,128)(2,1)S(1)}, bf16[4,128,32,64]{1,3,2,0:T(8,128)(2,1)}, u32[]{:S(2)}) copy-start(bf16[4,128,32,64]{1,3,2,0:T(8,128)(2,1)} %gather_fusion.2) | copy-start | bytes 6291460
  120.6 2.8 %copy-start.2 = (f32[4,32,64,128]{3,2,1,0:T(8,128)S(1)}, f32[4,32,64,128]{3,2,1,0:T(8,128)}, u32[]{:S(2)}) copy-start(f32[4,32,64,128]{3,2,1,0:T(8,128)} %gather_fusion.1) | copy-start | bytes 12582916
  120.6 2.8 %copy-start.10 = (f32[4,128,32]{1,2,0:T(8,128)S(1)}, f32[4,128,32]{1,2,0:T(8,128)}, u32[]{:S(2)}) copy-start(f32[4,128,32]{1,2,0:T(8,128)} %multiply_select_fusion) | copy-start | bytes 196612
  120.6 2.8 %copy-start.20 = (f32[4,32]{1,0:T(4,128)S(1)}, f32[4,32]{1,0:T(4,128)}, u32[]{:S(2)}) copy-start(f32[4,32]{1,0:T(4,128)} %exp.96) | copy-start | bytes 1540
  126.8 1.8 %copy-start.14 = (f32[4,4,4,2]{2,1,3,0:T(4,128)S(1)}, f32[4,4,4,2]{2,1,3,0:T(4,128)}, u32[]{:S(2)}) copy-start(f32[4,4,4,2]{2,1,3,0:T(4,128)} %copy.118) | copy-start | bytes 1540
  126.8 1.9 %copy-start.13 = (bf16[4,4,32,64]{3,2,1,0:T(8,128)(2,1)S(1)}, bf16[4,4,32,64]{3,2,1,0:T(8,128)(2,1)}, u32[]{:S(2)}) copy-start(bf16[4,4,32,64]{3,2,1,0:T(8,128)(2,1)} %reshape.322) | copy-start | bytes 196612
  126.8 1.9 %copy-start.15 = (f32[4,4,32]{1,2,0:T(8,128)S(1)}, f32[4,4,32]{1,2,0:T(8,128)}, u32[]{:S(2)}) copy-start(f32[4,4,32]{1,2,0:T(8,128)} %copy.115) | copy-start | bytes 6148
  126.8 1.9 %copy-start.16 = (f32[4,4,32]{1,2,0:T(8,128)S(1)}, f32[4,4,32]{1,2,0:T(8,128)}, u32[]{:S(2)}) copy-start(f32[4,4,32]{1,2,0:T(8,128)} %copy.117) | copy-start | bytes 6148
  126.8 1.9 %copy-start.17 = (f32[4,4,32]{1,2,0:T(8,128)S(1)}, f32[4,4,32]{1,2,0:T(8,128)}, u32[]{:S(2)}) copy-start(f32[4,4,32]{1,2,0:T(8,128)} %copy.109) | copy-start | bytes 6148
  126.8 1.9 %copy-start.25 = (f32[32]{0:T(128)S(1)}, f32[32]{0:T(128)}, u32[]{:S(2)}) copy-start(f32[32]{0:T(128)} %param.21) | copy-start | bytes 388
  126.8 1.8 %copy-start.28 = (pred[4]{0:T(512)(128)(4,1)S(1)}, pred[4]{0:T(512)(128)(4,1)}, u32[]{:S(2)}) copy-start(pred[4]{0:T(512)(128)(4,1)} %fusion.50) | copy-start | bytes 16
  126.9 1.8 %copy-start.29 = (pred[4,4]{1,0:T(4,128)(4,1)S(1)}, pred[4,4]{1,0:T(4,128)(4,1)}, u32[]{:S(2)}) copy-start(pred[4,4]{1,0:T(4,128)(4,1)} %iota_compare_fusion.1) | copy-start | bytes 52
  128.6 5.1 %copy-start.11 = (f32[2,128,32]{1,0,2:T(2,128)S(1)}, f32[2,128,32]{1,0,2:T(2,128)}, u32[]{:S(2)}) copy-start(f32[2,128,32]{1,0,2:T(2,128)} %copy.102) | copy-start | bytes 98308
  128.7 5.5 %copy-start.4 = (bf16[256,2048]{0,1:T(8,128)(2,1)S(1)}, bf16[256,2048]{0,1:T(8,128)(2,1)}, u32[]{:S(2)}) copy-start(bf16[256,2048]{0,1:T(8,128)(2,1)} %copy-done.3) | copy-start | bytes 3145732
  128.7 5.5 %copy-start.7 = (f32[2,128,32,64]{1,0,3,2:T(2,128)S(1)}, f32[2,128,32,64]{1,0,3,2:T(2,128)}, u32[]{:S(2)}) copy-start(f32[2,128,32,64]{1,0,3,2:T(2,128)} %copy.101) | copy-start | bytes 6291460
  128.7 5.5 %copy-start.18 = (f32[2048]{0:T(1024)S(1)}, f32[2048]{0:T(1024)}, u32[]{:S(2)}) copy-start(f32[2048]{0:T(1024)} %mul.220) | copy-start | bytes 24580
  130.4 9.0 %all-to-all-start.4 = ((bf16[4,4,2048]{2,1,0:T(4,128)(2,1)}), bf16[4,4,2048]{2,1,0:T(4,128)(2,1)S(1)}, u32[]{:S(2)}, u32[]{:S(2)}) async-start(bf16[4,4,2048]{2,1,0:T(4,128)(2,1)} %reshape.323), calls=%async_computation.4 | async-start | bytes 131072 | tf_op jit(solution)/shard_map/all_to_all | solution.py:175
  133.6 1.6 %copy-start.8 = (f32[2,128,2,16,64]{1,0,4,3,2:T(2,128)S(1)}, f32[2,128,2,16,64]{1,0,4,3,2:T(2,128)}, u32[]{:S(2)}) copy-start(f32[2,128,2,16,64]{1,0,4,3,2:T(2,128)} %copy.107) | copy-start | bytes 6291460
Sparse Core Ops, SparseCore 0:
  21.9 85.4 all-gather.3
where the time goes:
time: 148 us; the launch traced here: 147 us
  local copies, waits for them, and re-layouts  41.4 us (28%)
  waiting for transfers between devices  25.2 us (17%)
  starting transfers between devices  21.5 us (15%)
  other arithmetic  17.5 us (12%)
  between operations  15.2 us (10%)
  matrix products  13.3 us (9%)
  blocking collectives  12.6 us (9%)
    all_gather x1, waiting for transfers between devices, carried_in(): pieces = jax.tree.map(lambda part: lax.all_gather(part, axis), value)  16.5 us
    unnamed x1, blocking collectives  12.6 us
    unnamed x66, local copies, waits for them, and re-layouts  12.4 us
    all_to_all x1, starting transfers between devices, shards(): lax.all_to_all(dec_dt[0], 'seq', split_axis=0, concat_axis=0, tiled=True)  6.35 us
    all_to_all x1, starting transfers between devices, shards(): lax.all_to_all(dec_b[0], 'seq', split_axis=0, concat_axis=0, tiled=True)  5.07 us
    transpose x1, local copies, waits for them, and re-layouts, span_local(): jnp.einsum('hts,shp->thp', weights, x_part, preferred_element_type=jnp.fl...  4.67 us
    all_to_all x1, waiting for transfers between devices, shards(): lax.all_to_all(dec_x[0], 'seq', split_axis=0, concat_axis=0, tiled=True)  4.48 us
    select_n x3, other arithmetic, lap(): jnp.where(position < mine, new, old)  4.38 us
  transfers between devices with their start and end apart: 6, of which 4 were waited for; matrix products, arithmetic and copies ran while one was open for 22% of the time, Pallas kernels for 0%

commit v1 on v0

v1 whole, which is shorter than its diff:
```python
import functools
import math

import jax
import jax.numpy as jnp
from jax import lax
from jax.experimental import pallas as pl
from jax.experimental.pallas import tpu as pltpu
from jax.sharding import PartitionSpec as P

H = 128
P_SIZE = 64
N = 128
G = 8
SPAN = 128
STEPS = 4
LOG2E = math.log2(math.e)
F32 = jnp.float32
BF16 = jnp.bfloat16
VMEM_LIMIT = 32 * 1024 * 1024


def softplus(value):
    small = jnp.exp(-jnp.abs(value))
    series = small * (1.0 - small * (0.5 - small * (1.0 / 3.0 - small * 0.25)))
    return jnp.maximum(value, 0.0) + jnp.where(small < 0.02, series, jnp.log(1.0 + small))


def dot(left, right, left_dim=1, right_dim=0):
    return lax.dot_general(
        left, right, (((left_dim,), (right_dim,)), ((), ())), preferred_element_type=F32
    )


def split(value, pieces):
    result = []
    for _ in range(pieces):
        piece = value.astype(BF16)
        result.append(piece)
        value = value - piece.astype(F32)
    return result


def exact_dot(ones, value, pieces=3, left_dim=1):
    return sum(dot(ones, piece, left_dim) for piece in split(value, pieces))


def spread_matrix(heads, first, width):
    lane = lax.broadcasted_iota(jnp.int32, (heads, width), 1) + first
    head = lax.broadcasted_iota(jnp.int32, (heads, width), 0)
    return jnp.where(lane // P_SIZE == head, 1.0, 0.0).astype(BF16)


def over_lanes(value, first, width, pieces=2):
    return exact_dot_right(value, spread_matrix(value.shape[1], first, width), pieces)


def exact_dot_right(value, ones, pieces):
    return sum(dot(piece, ones) for piece in split(value, pieces))


def state_kernel(
    x_ref, b_ref, dt_ref, a_ref, d_ref,
    total_ref, sent_ref, decay_ref, skip_ref, cum_ref, far_ref, row_ref,
):
    tokens, heads = dt_ref.shape
    spans = tokens // SPAN
    chunks, _, width = total_ref.shape
    step = softplus(dt_ref[...].astype(F32))
    rate = step * (jnp.exp(a_ref[...]) * -LOG2E)
    t_index = lax.broadcasted_iota(jnp.int32, (SPAN, SPAN), 0)
    s_index = lax.broadcasted_iota(jnp.int32, (SPAN, SPAN), 1)
    lower = jnp.where(t_index >= s_index, 1.0, 0.0).astype(BF16)
    cums, ends = [], []
    for i in range(spans):
        cum = exact_dot(lower, rate[i * SPAN : (i + 1) * SPAN])
        cums.append(cum)
        ends.append(cum[SPAN - 1 : SPAN, :])
    before = jnp.zeros_like(ends[0])
    for i in range(spans):
        cum_ref[i * SPAN : (i + 1) * SPAN, :] = cums[i]
        far_ref[i * SPAN : (i + 1) * SPAN, :] = cums[i] + before
        before = before + ends[i]
    log_step = jnp.log2(step)
    rows = log_step - jnp.concatenate(cums, axis=0)
    row_ref[...] = rows.T
    after = jnp.zeros_like(ends[0])
    weights = [None] * spans
    for i in reversed(range(spans)):
        after = after + ends[i]
        weights[i] = jnp.exp2(after - cums[i]) * step[i * SPAN : (i + 1) * SPAN]
    weight = jnp.concatenate(weights, axis=0)
    per_group = H // G
    for k in range(chunks):
        first = k * width
        g = first // (per_group * P_SIZE)
        lanes = slice(first, first + width)
        scaled = (x_ref[:, lanes].astype(F32) * over_lanes(weight, first, width)).astype(BF16)
        total = dot(b_ref[:, g * N : (g + 1) * N], scaled, 0, 0)
        total_ref[k] = total
        sent_ref[k] = total.astype(BF16)
        decay_ref[k] = over_lanes(jnp.exp2(after), first, width, 3)
        skip_ref[:, lanes] = over_lanes(d_ref[...], first, width, 3)


def inner_kernel(
    x_ref, b_ref, c_ref, cum_ref, far_ref, row_ref, skip_ref, spot_ref, ask_ref,
    inner_ref, local_ref, gain_ref,
):
    tokens, heads = cum_ref.shape
    spans = tokens // SPAN
    asks = ask_ref.shape[0]
    per_group = H // G
    groups = heads // per_group
    t_index = lax.broadcasted_iota(jnp.int32, (SPAN, SPAN), 0)
    s_index = lax.broadcasted_iota(jnp.int32, (SPAN, SPAN), 1)
    causal = t_index >= s_index
    spot = spot_ref[...]
    position = lax.broadcasted_iota(jnp.int32, (asks, tokens), 1)
    picked = jnp.where(position == spot, 1.0, 0.0).astype(BF16)
    cum = cum_ref[...]
    rows = row_ref[...]
    near_ask = exact_dot(picked, cum)
    far_ask = exact_dot(picked, far_ref[...])
    gain_ref[...] = far_ask
    upto = position <= spot
    ends = [cum[(i + 1) * SPAN - 1 : (i + 1) * SPAN, :] for i in range(spans)]
    ask_columns = []
    for j in range(spans):
        start = sum(ends[:j], jnp.zeros_like(ends[0]))
        later = far_ask - start
        ask_columns.append(jnp.where(spot < (j + 1) * SPAN, near_ask, later))
    row_ends = [rows[:, 0:1] * 0.0]
    lane = lax.broadcasted_iota(jnp.int32, (1, 2 * P_SIZE), 1)
    first_half = lane < P_SIZE
    for g in range(groups):
        b_part = b_ref[:, g * N : (g + 1) * N]
        c_part = c_ref[:, g * N : (g + 1) * N]
        scores = dot(c_part, b_part, 1, 1)
        ask_scores = dot(ask_ref[:, g * N : (g + 1) * N], b_part, 1, 1)
        for pair in range(per_group // 2):
            h0 = g * per_group + 2 * pair
            lanes = slice(h0 * P_SIZE, (h0 + 2) * P_SIZE)
            x_part = x_ref[:, lanes]
            zero = jnp.zeros_like(x_part)
            halves = (jnp.where(first_half, x_part, zero), jnp.where(first_half, zero, x_part))
            weights = [[None, None] for _ in range(spans)]
            for e in range(2):
                h = h0 + e
                row = rows[h : h + 1, :]
                for i in range(spans):
                    column = jnp.broadcast_to(
                        cum[i * SPAN : (i + 1) * SPAN, h : h + 1], (SPAN, SPAN)
                    )
                    parts = []
                    for j in range(i + 1):
                        shift = row[:, j * SPAN : (j + 1) * SPAN]
                        for m in range(j, i):
                            shift = shift + ends[m][:, h : h + 1]
                        score = scores[i * SPAN : (i + 1) * SPAN, j * SPAN : (j + 1) * SPAN]
                        part = score * jnp.exp2(column + shift)
                        if i == j:
                            part = jnp.where(causal, part, 0.0)
                        parts.append(part.astype(BF16))
                    if i == spans - 1:
                        asked = []
                        for j in range(spans):
                            span = slice(j * SPAN, (j + 1) * SPAN)
                            part = ask_scores[:, span] * jnp.exp2(
                                ask_columns[j][:, h : h + 1] + row[:, span]
                            )
                            asked.append(jnp.where(upto[:, span], part, 0.0).astype(BF16))
                        parts = [
                            jnp.concatenate([part, ask], axis=0) for part, ask in zip(parts, asked)
                        ]
                    weights[i][e] = jnp.concatenate(parts, axis=1) if i else parts[0]
            skip = skip_ref[:, lanes]
            for i in range(spans):
                reach = (i + 1) * SPAN
                left = jnp.concatenate(weights[i], axis=1)
                right = jnp.concatenate([half[:reach] for half in halves], axis=0)
                result = dot(left, right)
                mine = slice(i * SPAN, (i + 1) * SPAN)
                inner_ref[mine, lanes] = result[:SPAN] + skip * x_part[mine].astype(F32)
                if i == spans - 1:
                    local_ref[:, lanes] = result[SPAN:]


def outer_kernel(c_ref, ask_ref, far_ref, gain_ref, inner_ref, local_ref, *rest):
    carry_refs, (out_ref, read_ref) = rest[:-2], rest[-2:]
    chunks = len(carry_refs)
    tokens, heads = far_ref.shape
    width = out_ref.shape[1] // chunks
    per_group = H // G
    gain = jnp.exp2(far_ref[...])
    ask_gain = jnp.exp2(gain_ref[...])
    for k in range(chunks):
        first = k * width
        g = first // (per_group * P_SIZE)
        lanes = slice(first, first + width)
        state = carry_refs[k][...]
        carried = dot(c_ref[:, g * N : (g + 1) * N], state)
        out = inner_ref[:, lanes] + over_lanes(gain, first, width) * carried
        out_ref[:, lanes] = out.astype(BF16)
        ask_carried = dot(ask_ref[:, g * N : (g + 1) * N], state)
        read_ref[:, lanes] = local_ref[:, lanes] + over_lanes(ask_gain, first, width) * ask_carried


def fresh_kernel(x_ref, b_ref, c_ref, dt_ref, a_ref, d_ref, fresh_ref, keep_ref):
    rows, heads = dt_ref.shape
    per_group = H // G
    groups = heads // per_group
    width = x_ref.shape[1]
    turn = lax.broadcasted_iota(jnp.int32, (rows, 1), 0) % STEPS
    step = softplus(dt_ref[...].astype(F32))
    rate = step * (jnp.exp(a_ref[...]) * -LOG2E)

    def earlier(value, gap):
        if not gap:
            return value
        moved = jnp.concatenate([jnp.zeros_like(value[:gap]), value[:-gap]], axis=0)
        return jnp.where(turn >= gap, moved, 0.0)

    running = sum(earlier(rate, gap) for gap in range(STEPS))
    keep_ref[...] = over_lanes(jnp.exp2(running), 0, width)
    x_values = x_ref[...].astype(F32)
    b_values = b_ref[...].astype(F32)
    c_values = c_ref[...].astype(F32)
    head = lax.broadcasted_iota(jnp.int32, (rows, heads), 1)
    fresh = over_lanes(d_ref[...], 0, width, 3) * x_values
    since = jnp.zeros_like(rate)
    for gap in range(STEPS):
        if gap:
            since = since + earlier(rate, gap - 1)
        products = c_values * earlier(b_values, gap)
        pair = jnp.zeros((rows, heads), F32)
        for g in range(groups):
            score = jnp.sum(products[:, g * N : (g + 1) * N], axis=1, keepdims=True)
            pair = jnp.where(head // per_group == g, score, pair)
        factor = jnp.where(turn >= gap, jnp.exp2(since) * earlier(step, gap) * pair, 0.0)
        fresh = fresh + over_lanes(factor, 0, width) * earlier(x_values, gap)
    fresh_ref[...] = fresh


def call(kernel, out_shape, flops, moved):
    return pl.pallas_call(
        kernel,
        out_shape=out_shape,
        compiler_params=pltpu.CompilerParams(vmem_limit_bytes=VMEM_LIMIT),
        cost_estimate=pl.CostEstimate(flops=flops, bytes_accessed=moved, transcendentals=0),
    )


def shards(
    ssm_input, bmat, cmat, dt_raw, a_log, d_skip, prompt_len, owner, dec_x, dec_b, dec_c, dec_dt
):
    seq_count = lax.axis_size("seq")
    my_index = lax.axis_index("seq")
    token_count, heads = dt_raw.shape
    groups = heads // (H // G)
    lanes = heads * P_SIZE
    rows = seq_count * STEPS
    chunks = 2 * groups if seq_count <= 4 else groups
    width = lanes // chunks
    shape = jax.ShapeDtypeStruct
    a_row = a_log.reshape(1, heads)
    d_row = d_skip.reshape(1, heads)

    total, sent, decay, skip, cum, far, row = call(
        state_kernel,
        (
            shape((chunks, N, width), F32),
            shape((chunks, N, width), BF16),
            shape((chunks, 1, width), F32),
            shape((1, lanes), F32),
            shape((token_count, heads), F32),
            shape((token_count, heads), F32),
            shape((heads, token_count), F32),
        ),
        2 * token_count * N * lanes,
        4 * token_count * lanes,
    )(ssm_input, bmat, dt_raw, a_row, d_row)

    carry = [None] * chunks
    moving = [sent[k] for k in range(chunks)]
    for hop in range(1, seq_count):
        for k in range(chunks):
            got = lax.ppermute(moving[k], "seq", [(hop - 1, hop)])
            carry[k] = got if hop == 1 else carry[k] + got
            if hop < seq_count - 1:
                moving[k] = (got.astype(F32) * decay[k] + total[k]).astype(BF16)

    asked = lax.all_to_all(dec_c[0], "seq", split_axis=0, concat_axis=0, tiled=True)
    ask = asked.reshape(rows, groups * N)
    last_token = prompt_len - 1
    sources = last_token // token_count
    indices = jnp.arange(seq_count, dtype=jnp.int32)
    mine = (sources == my_index)[None, :] & (owner[None, :] == indices[:, None])
    offsets = jnp.sum(jnp.where(mine, last_token[None, :] - my_index * token_count, 0), axis=1)
    spot = jnp.repeat(offsets, STEPS).reshape(rows, 1).astype(jnp.int32)

    inner, local, gain = call(
        inner_kernel,
        (
            shape((token_count, lanes), F32),
            shape((rows, lanes), F32),
            shape((rows, heads), F32),
        ),
        4 * token_count * token_count * lanes,
        16 * token_count * lanes,
    )(ssm_input, bmat, cmat, cum, far, row, skip, spot, ask)

    fresh, keep = call(
        fresh_kernel,
        (shape((rows, lanes), F32), shape((rows, lanes), F32)),
        64 * rows * lanes,
        16 * rows * lanes,
    )(
        dec_x.reshape(rows, lanes),
        dec_b.reshape(rows, groups * N),
        dec_c.reshape(rows, groups * N),
        dec_dt.reshape(rows, heads),
        a_row,
        d_row,
    )

    prefill, reading = call(
        outer_kernel,
        (shape((token_count, lanes), BF16), shape((rows, lanes), F32)),
        2 * token_count * N * lanes,
        8 * token_count * lanes,
    )(cmat, ask, far, gain, inner, local, *carry)

    back = lax.all_to_all(
        reading.reshape(seq_count, STEPS, lanes), "seq", split_axis=0, concat_axis=0, tiled=True
    )
    held = jnp.any((owner == my_index)[None, :] & (sources[None, :] == indices[:, None]), axis=1)
    decoded = back * keep.reshape(seq_count, STEPS, lanes) + fresh.reshape(seq_count, STEPS, lanes)
    decoded = jnp.where(held[:, None, None], decoded, 0.0).astype(BF16)
    return (prefill, decoded[None])


def solution(mesh):
    placed = (
        P(("grp", "seq"), "tp"),
        P(("grp", "seq"), "tp"),
        P(("grp", "seq"), "tp"),
        P(("grp", "seq"), "tp"),
        P("tp"),
        P("tp"),
        P("grp"),
        P("grp"),
        P(("grp", "seq"), None, None, "tp"),
        P(("grp", "seq"), None, None, "tp"),
        P(("grp", "seq"), None, None, "tp"),
        P(("grp", "seq"), None, None, "tp"),
    )
    return jax.shard_map(
        shards,
        mesh=mesh,
        in_specs=placed,
        out_specs=(P(("grp", "seq"), "tp"), P(("grp", "seq"), None, None, "tp")),
        check_vma=False,
    )
```

time: 148 us -> 66 us (0.45)
  local copies, waits for them, and re-layouts: 41.4 us -> 6.04 us
  starting transfers between devices: 21.5 us -> 41.2 us
  waiting for transfers between devices: 25.2 us -> 8.5 us
  other arithmetic: 17.5 us -> 2.18 us
  between operations: 15.2 us -> 1.07 us
  matrix products: 13.3 us -> 0 us
  blocking collectives: 12.6 us -> 0 us
  Pallas kernels: 0 us -> 6.46 us
    all_gather x1 -> x0, waiting for transfers between devices: 16.5 us -> none  [carried_in(): pieces = jax.tree.map(lambda part: lax.all_gather(part, axis), value)]
    ppermute x0 -> x12, starting transfers between devices: none -> 14.3 us  [shards(): got = lax.ppermute(moving[k], 'seq', [(hop - 1, hop)])]
    dot_general x8 -> x0, matrix products: 13.3 us -> none  [the longest x1 3.34 us: request_state(): jnp.einsum('shp,shn->hpn', x_part, scaled, preferred_element_type=jnp.flo...]
    unnamed x1 -> x0, blocking collectives: 12.6 us -> none
    transpose x5 -> x0, local copies, waits for them, and re-layouts: 8.56 us -> none  [the longest x1 4.67 us: span_local(): jnp.einsum('hts,shp->thp', weights, x_part, preferred_element_type=jnp.fl...]
    unnamed x66 -> x37, local copies, waits for them, and re-layouts: 12.4 us -> 4.34 us
    gather x7 -> x0, local copies, waits for them, and re-layouts: 7.42 us -> none  [the longest x1 2.78 us: request_state(): state = lax.dynamic_index_in_dim(span_start, span_index, 0, keepdims=False)]
    pallas_call x0 -> x4, Pallas kernels: none -> 6.46 us  [the longest x1 2.13 us: shards(): call(outer_kernel, (shape((token_count, lanes), BF16), shape((rows, lanes...]
  transfers between devices with their start and end apart: 6 -> 14, of which waited for: 4 -> 3; matrix products, arithmetic and copies ran while one was open for 22% -> 4% of each run, Pallas kernels for 0% -> 4%
where the time goes in v1:
time: 66 us; the launch traced here: 65.4 us
  starting transfers between devices  41.2 us (62%)
  waiting for transfers between devices  8.5 us (13%)
  Pallas kernels  6.46 us (10%)
  local copies, waits for them, and re-layouts  6.04 us (9%)
  other arithmetic  2.18 us (3%)
  between operations  1.07 us (2%)
    all_to_all x1, starting transfers between devices, shards(): lax.all_to_all(reading.reshape(seq_count, STEPS, lanes), 'seq', split_axi...  23.6 us
    ppermute x12, starting transfers between devices, shards(): got = lax.ppermute(moving[k], 'seq', [(hop - 1, hop)])  14.3 us
    all_to_all x1, waiting for transfers between devices, shards(): lax.all_to_all(reading.reshape(seq_count, STEPS, lanes), 'seq', split_axi...  4.5 us
    unnamed x37, local copies, waits for them, and re-layouts  4.34 us
    ppermute x12, waiting for transfers between devices, shards(): got = lax.ppermute(moving[k], 'seq', [(hop - 1, hop)])  3.99 us
    all_to_all x1, starting transfers between devices, shards(): lax.all_to_all(dec_c[0], 'seq', split_axis=0, concat_axis=0, tiled=True)  3.26 us
    pallas_call x1, Pallas kernels, shards(): call(outer_kernel, (shape((token_count, lanes), BF16), shape((rows, lanes...  2.13 us
    pallas_call x1, Pallas kernels, shards(): call(inner_kernel, (shape((token_count, lanes), F32), shape((rows, lanes)...  2.12 us
  transfers between devices with their start and end apart: 14, of which 3 were waited for; matrix products, arithmetic and copies ran while one was open for 4% of the time, Pallas kernels for 4%

profile of v1, /device:TPU:0, one launch (start us, length us, event | category | flops | bytes accessed | tf_op | source)
XLA Modules:
  0.0 65.4 jit_solution(1066717891723561661)
XLA Ops:
  0.6 0.0 copy-start.16
  0.6 0.8 %copy.16.dt_ref = bf16[256,32]{1,0:T(8,128)(2,1)S(1)} copy(bf16[256,32]{0,1:T(8,128)(2,1)} %param.15) | data formatting | bytes 32768 | tf_op args[3]
  1.5 0.0 copy-start
  1.5 1.2 %copy-done = bf16[256,2048]{1,0:T(8,128)(2,1)S(1)} copy-done((bf16[256,2048]{1,0:T(8,128)(2,1)S(1)}, bf16[256,2048]{1,0:T(8,128)(2,1)}, u32[]{:S(2)}) %copy-start) | copy-done | bytes 1048600
  2.7 0.9 %copy-done.3 = bf16[256,256]{1,0:T(8,128)(2,1)S(1)} copy-done((bf16[256,256]{1,0:T(8,128)(2,1)S(1)}, bf16[256,256]{1,0:T(8,128)(2,1)}, u32[]{:S(2)}) %copy-start.3) | copy-done | bytes 131096
  3.6 0.7 copy-done.6
  4.3 0.7 copy-done.8
  4.9 1.8 %shard_map.131 = (f32[4,128,512]{2,1,0:T(8,128)S(1)}, bf16[4,128,512]{2,1,0:T(8,128)(2,1)S(1)}, f32[4,1,512]{2,1,0:T(1,128)S(1)}, f32[1,2048]{1,0:T(1,128)S(1)},...) custom-call(bf16[256,2048]{1,0:T(8,128)(2,1)S(1)} %copy-done, ...), custom_call_target="tpu_custom_call" | custom-call | flops 134217728 | bytes 2097152 | tf_op jit(solution)/shard_map/pallas_call | solution.py:269
  6.8 4.9 %collective-permute-start = (bf16[128,512]{1,0:T(8,128)(2,1)S(1)}, bf16[128,512]{1,0:T(8,128)(2,1)S(1)}, u32[]{:S(2)}, u32[]{:S(2)}) collective-permute-start(bf16[128,512]{1,0:T(8,128)(2,1)S(1)} %get-tuple-element.43), channel_id=1, source_target_pairs={{0,4},{1,5},{2,6},{3,7},{16,20},{17,21},{18,22},{19,23}} | collective-permute-start | bytes 393224 | tf_op jit(solution)/shard_map/ppermute | solution.py:288
  11.7 1.3 %collective-permute-start.3 = (bf16[128,512]{1,0:T(8,128)(2,1)S(1)}, bf16[128,512]{1,0:T(8,128)(2,1)S(1)}, u32[]{:S(2)}, u32[]{:S(2)}) collective-permute-start(bf16[128,512]{1,0:T(8,128)(2,1)S(1)} %get-tuple-element.42), channel_id=1, source_target_pairs={{0,4},{1,5},{2,6},{3,7},{16,20},{17,21},{18,22},{19,23}} | collective-permute-start | bytes 393224 | tf_op jit(solution)/shard_map/ppermute | solution.py:288
  13.0 1.3 %collective-permute-start.6 = (bf16[128,512]{1,0:T(8,128)(2,1)S(1)}, bf16[128,512]{1,0:T(8,128)(2,1)S(1)}, u32[]{:S(2)}, u32[]{:S(2)}) collective-permute-start(bf16[128,512]{1,0:T(8,128)(2,1)S(1)} %get-tuple-element.41), channel_id=1, source_target_pairs={{0,4},{1,5},{2,6},{3,7},{16,20},{17,21},{18,22},{19,23}} | collective-permute-start | bytes 393224 | tf_op jit(solution)/shard_map/ppermute | solution.py:288
  14.3 1.3 %collective-permute-start.9 = (bf16[128,512]{1,0:T(8,128)(2,1)S(1)}, bf16[128,512]{1,0:T(8,128)(2,1)S(1)}, u32[]{:S(2)}, u32[]{:S(2)}) collective-permute-start(bf16[128,512]{1,0:T(8,128)(2,1)S(1)} %get-tuple-element.40), channel_id=1, source_target_pairs={{0,4},{1,5},{2,6},{3,7},{16,20},{17,21},{18,22},{19,23}} | collective-permute-start | bytes 393224 | tf_op jit(solution)/shard_map/ppermute | solution.py:288
  15.6 3.3 %all-to-all-start = ((bf16[4,4,256]{2,1,0:T(4,128)(2,1)}), bf16[4,4,256]{2,1,0:T(4,128)(2,1)S(1)}, u32[]{:S(2)}, u32[]{:S(2)}) async-start(bf16[4,4,256]{2,1,0:T(4,128)(2,1)} %bitcast), calls=%async_computation | async-start | bytes 16384 | tf_op jit(solution)/shard_map/all_to_all | solution.py:293
  18.9 0.0 copy-done.16
  18.9 0.0 collective-permute-done
  18.9 0.0 collective-permute-done.3
  19.0 2.2 %collective-permute-done.6 = bf16[128,512]{1,0:T(8,128)(2,1)S(1)} collective-permute-done((bf16[128,512]{1,0:T(8,128)(2,1)S(1)}, bf16[128,512]{1,0:T(8,128)(2,1)S(1)}, u32[]{:S(2)}, u32[]{:S(2)}) %collective-permute-start.6) | collective-permute-done | bytes 131104 | tf_op jit(solution)/shard_map/ppermute | solution.py:288
  21.2 1.7 %collective-permute-done.9 = bf16[128,512]{1,0:T(8,128)(2,1)S(1)} collective-permute-done((bf16[128,512]{1,0:T(8,128)(2,1)S(1)}, bf16[128,512]{1,0:T(8,128)(2,1)S(1)}, u32[]{:S(2)}, u32[]{:S(2)}) %collective-permute-start.9) | collective-permute-done | bytes 131104 | tf_op jit(solution)/shard_map/ppermute | solution.py:288
  22.9 0.2 fusion
  23.1 0.8 %collective-permute-start.1 = (bf16[128,512]{1,0:T(8,128)(2,1)S(1)}, bf16[128,512]{1,0:T(8,128)(2,1)S(1)}, u32[]{:S(2)}, u32[]{:S(2)}) collective-permute-start(bf16[128,512]{1,0:T(8,128)(2,1)S(1)} %get-tuple-element.39), channel_id=1, source_target_pairs={{4,8},{5,9},{6,10},{7,11},{20,24},{21,25},{22,26},{23,27}} | collective-permute-start | bytes 393224 | tf_op jit(solution)/shard_map/ppermute | solution.py:288
  23.9 0.7 %collective-permute-start.10 = (bf16[128,512]{1,0:T(8,128)(2,1)S(1)}, bf16[128,512]{1,0:T(8,128)(2,1)S(1)}, u32[]{:S(2)}, u32[]{:S(2)}) collective-permute-start(bf16[128,512]{1,0:T(8,128)(2,1)S(1)} %get-tuple-element.36), channel_id=1, source_target_pairs={{4,8},{5,9},{6,10},{7,11},{20,24},{21,25},{22,26},{23,27}} | collective-permute-start | bytes 393224 | tf_op jit(solution)/shard_map/ppermute | solution.py:288
  24.6 0.7 %collective-permute-start.4 = (bf16[128,512]{1,0:T(8,128)(2,1)S(1)}, bf16[128,512]{1,0:T(8,128)(2,1)S(1)}, u32[]{:S(2)}, u32[]{:S(2)}) collective-permute-start(bf16[128,512]{1,0:T(8,128)(2,1)S(1)} %get-tuple-element.38), channel_id=1, source_target_pairs={{4,8},{5,9},{6,10},{7,11},{20,24},{21,25},{22,26},{23,27}} | collective-permute-start | bytes 393224 | tf_op jit(solution)/shard_map/ppermute | solution.py:288
  25.3 0.7 %collective-permute-start.7 = (bf16[128,512]{1,0:T(8,128)(2,1)S(1)}, bf16[128,512]{1,0:T(8,128)(2,1)S(1)}, u32[]{:S(2)}, u32[]{:S(2)}) collective-permute-start(bf16[128,512]{1,0:T(8,128)(2,1)S(1)} %get-tuple-element.37), channel_id=1, source_target_pairs={{4,8},{5,9},{6,10},{7,11},{20,24},{21,25},{22,26},{23,27}} | collective-permute-start | bytes 393224 | tf_op jit(solution)/shard_map/ppermute | solution.py:288
  26.0 0.0 collective-permute-done.1
  26.0 0.0 collective-permute-done.10
  26.0 0.0 copy-start.10
  26.0 0.0 collective-permute-done.4
  26.0 0.0 collective-permute-done.7
  26.0 0.0 copy-start.12
  26.0 0.9 %fusion.1 = (bf16[128,512]{1,0:T(8,128)(2,1)}, bf16[128,512]{1,0:T(8,128)(2,1)}, bf16[128,512]{1,0:T(8,128)(2,1)}, bf16[128,512]{1,0:T(8,128)(2,1)}) fusion(bf16[128,512]{1,0:T(8,128)(2,1)S(1)} %collective-permute-done.10, f32[4,128,512]{2,1,0:T(8,128)S(1)} %get-tuple-element.25, f32[512]{0:T(512)S(1)} %bitcast.52, f32[512]{0:T(512)S(1)} %bitcast.58, ...), kind=kLoop, calls=%fused_computation.3 | loop fusion | flops 1048576 | bytes 2105344 | tf_op jit(solution)/shard_map/convert_element_type | solution.py:291
  26.9 0.7 %collective-permute-start.11 = (bf16[128,512]{1,0:T(8,128)(2,1)}, bf16[128,512]{1,0:T(8,128)(2,1)S(1)}, u32[]{:S(2)}, u32[]{:S(2)}) collective-permute-start(bf16[128,512]{1,0:T(8,128)(2,1)} %get-tuple-element.32), channel_id=1, source_target_pairs={{8,12},{9,13},{10,14},{11,15},{24,28},{25,29},{26,30},{27,31}} | collective-permute-start | bytes 393224 | tf_op jit(solution)/shard_map/ppermute | solution.py:288
  27.6 0.0 copy-done.17
  27.6 0.1 select_reduce_fusion
  27.7 0.0 copy-done.10
  27.7 0.0 copy-done.12
  27.7 0.1 broadcast_in_dim.40
  27.8 0.1 reshape_reshape.4.spot_ref
  27.9 0.0 all-to-all-done
  27.9 0.0 copy-done.1
  27.9 0.0 copy-done.2
  27.9 2.1 %shard_map.132 = (f32[256,2048]{1,0:T(8,128)S(1)}, f32[16,2048]{1,0:T(8,128)S(1)}, f32[16,32]{1,0:T(8,128)S(1)}) custom-call(bf16[256,2048]{1,0:T(8,128)(2,1)S(1)} %copy-done.1, bf16[256,256]{1,0:T(8,128)(2,1)S(1)} %copy-done.4, bf16[256,256]{1,0:T(8,128)(2,1)S(1)} %copy-done.2, f32[256,32]{1,0:T(8,128)S(1)} %get-tuple-element.17.cum_ref, ...), custom_call_target="tpu_custom_call" | custom-call | flops 536870912 | bytes 8388608 | tf_op jit(solution)/shard_map/pallas_call | solution.py:302
  30.1 0.7 %collective-permute-start.8 = (bf16[128,512]{1,0:T(8,128)(2,1)}, bf16[128,512]{1,0:T(8,128)(2,1)S(1)}, u32[]{:S(2)}, u32[]{:S(2)}) collective-permute-start(bf16[128,512]{1,0:T(8,128)(2,1)} %get-tuple-element.35), channel_id=1, source_target_pairs={{8,12},{9,13},{10,14},{11,15},{24,28},{25,29},{26,30},{27,31}} | collective-permute-start | bytes 393224 | tf_op jit(solution)/shard_map/ppermute | solution.py:288
  30.7 0.7 %collective-permute-start.5 = (bf16[128,512]{1,0:T(8,128)(2,1)}, bf16[128,512]{1,0:T(8,128)(2,1)S(1)}, u32[]{:S(2)}, u32[]{:S(2)}) collective-permute-start(bf16[128,512]{1,0:T(8,128)(2,1)} %get-tuple-element.34), channel_id=1, source_target_pairs={{8,12},{9,13},{10,14},{11,15},{24,28},{25,29},{26,30},{27,31}} | collective-permute-start | bytes 393224 | tf_op jit(solution)/shard_map/ppermute | solution.py:288
  31.4 0.7 %collective-permute-start.2 = (bf16[128,512]{1,0:T(8,128)(2,1)}, bf16[128,512]{1,0:T(8,128)(2,1)S(1)}, u32[]{:S(2)}, u32[]{:S(2)}) collective-permute-start(bf16[128,512]{1,0:T(8,128)(2,1)} %get-tuple-element.33), channel_id=1, source_target_pairs={{8,12},{9,13},{10,14},{11,15},{24,28},{25,29},{26,30},{27,31}} | collective-permute-start | bytes 393224 | tf_op jit(solution)/shard_map/ppermute | solution.py:288
  32.1 0.0 collective-permute-done.11
  32.1 0.0 collective-permute-done.8
  32.2 0.0 collective-permute-done.5
  32.2 0.0 copy-start.14
  32.3 0.0 copy-start.15
  32.3 0.0 copy-start.5
  32.3 0.0 copy-start.7
  32.3 0.0 copy-start.9
  32.3 0.0 collective-permute-done.2
  32.3 2.1 %shard_map.133 = (bf16[256,2048]{1,0:T(8,128)(2,1)}, f32[16,2048]{1,0:T(8,128)S(1)}) custom-call(bf16[256,256]{1,0:T(8,128)(2,1)S(1)} %copy-done.2, bf16[16,256]{1,0:T(8,128)(2,1)S(1)} %reshape.45.ask_ref, f32[256,32]{1,0:T(8,128)S(1)} %get-tuple-element.16.far_ref, f32[16,32]{1,0:T(8,128)S(1)} %get-tuple-element.20.gain_ref, ...), custom_call_target="tpu_custom_call" | custom-call | flops 134217728 | bytes 4194304 | tf_op jit(solution)/shard_map/pallas_call | solution.py:327
  34.5 0.7 %reshape.48 = f32[4,4,2048]{2,1,0:T(4,128)} reshape(f32[16,2048]{1,0:T(8,128)S(1)} %get-tuple-element.27) | data formatting | bytes 262144 | tf_op jit(solution)/shard_map/reshape | solution.py:335
  35.2 23.6 %all-to-all-start.1 = ((f32[4,4,2048]{2,1,0:T(4,128)}), f32[4,4,2048]{2,1,0:T(4,128)S(1)}, u32[]{:S(2)}, u32[]{:S(2)}) async-start(f32[4,4,2048]{2,1,0:T(4,128)} %reshape.48), calls=%async_computation.1 | async-start | bytes 262144 | tf_op jit(solution)/shard_map/all_to_all | solution.py:334
  58.8 0.7 %reshape.51.c_ref = bf16[16,256]{1,0:T(8,128)(2,1)S(1)} reshape(bf16[1,4,4,256]{3,2,1,0:T(4,128)(2,1)} %param.22) | data formatting | bytes 16384 | tf_op jit(solution)/shard_map/reshape | solution.py:321
  59.5 0.0 copy-done.5
  59.5 0.0 copy-done.7
  59.6 0.0 copy-done.9
  59.6 0.4 shard_map.134
  60.1 0.1 fusion.11
  60.2 4.5 %all-to-all-done.1 = f32[4,4,2048]{2,1,0:T(4,128)S(1)} async-done(((f32[4,4,2048]{2,1,0:T(4,128)}), f32[4,4,2048]{2,1,0:T(4,128)S(1)}, u32[]{:S(2)}, u32[]{:S(2)}) %all-to-all-start.1) | async-done | bytes 131104 | tf_op jit(solution)/shard_map/all_to_all | solution.py:334
  64.7 0.7 %fusion.8 = bf16[1,4,4,2048]{3,2,1,0:T(4,128)(2,1)} fusion(f32[4,4,2048]{2,1,0:T(4,128)S(1)} %reshape.54, f32[4,4,2048]{2,1,0:T(4,128)S(1)} %all-to-all-done.1, f32[4,4,2048]{2,1,0:T(4,128)S(1)} %reshape.53, pred[4]{0:T(512)(128)(4,1)S(1)} %fusion.11), kind=kLoop, calls=%fused_computation.25 | loop fusion | flops 131072 | bytes 458756 | tf_op jit(solution)/shard_map/broadcast_in_dim | solution.py:340
  (28 shorter events, 0.3 us)
Async XLA Ops:
  0.6 18.3 %copy-start.16 = (s32[8]{0:T(128)S(1)}, s32[8]{0:T(128)}, u32[]{:S(2)}) copy-start(s32[8]{0:T(128)} %param.18) | copy-start | bytes 100
  1.5 1.2 %copy-start = (bf16[256,2048]{1,0:T(8,128)(2,1)S(1)}, bf16[256,2048]{1,0:T(8,128)(2,1)}, u32[]{:S(2)}) copy-start(bf16[256,2048]{1,0:T(8,128)(2,1)} %x_ref.3) | copy-start | bytes 3145732
  2.7 0.9 %copy-start.3 = (bf16[256,256]{1,0:T(8,128)(2,1)S(1)}, bf16[256,256]{1,0:T(8,128)(2,1)}, u32[]{:S(2)}) copy-start(bf16[256,256]{1,0:T(8,128)(2,1)} %b_ref.3) | copy-start | bytes 393220
  3.6 0.7 %copy-start.6 = (f32[32]{0:T(128)S(1)}, f32[32]{0:T(128)}, u32[]{:S(2)}) copy-start(f32[32]{0:T(128)} %param.16) | copy-start | bytes 388
  4.3 0.7 %copy-start.8 = (f32[32]{0:T(128)S(1)}, f32[32]{0:T(128)}, u32[]{:S(2)}) copy-start(f32[32]{0:T(128)} %param.17) | copy-start | bytes 388
  6.8 12.2 %collective-permute-start = (bf16[128,512]{1,0:T(8,128)(2,1)S(1)}, bf16[128,512]{1,0:T(8,128)(2,1)S(1)}, u32[]{:S(2)}, u32[]{:S(2)}) collective-permute-start(bf16[128,512]{1,0:T(8,128)(2,1)S(1)} %get-tuple-element.43), channel_id=1, source_target_pairs={{0,4},{1,5},{2,6},{3,7},{16,20},{17,21},{18,22},{19,23}} | collective-permute-start | bytes 393224 | tf_op jit(solution)/shard_map/ppermute | solution.py:288
  11.7 7.2 %collective-permute-start.3 = (bf16[128,512]{1,0:T(8,128)(2,1)S(1)}, bf16[128,512]{1,0:T(8,128)(2,1)S(1)}, u32[]{:S(2)}, u32[]{:S(2)}) collective-permute-start(bf16[128,512]{1,0:T(8,128)(2,1)S(1)} %get-tuple-element.42), channel_id=1, source_target_pairs={{0,4},{1,5},{2,6},{3,7},{16,20},{17,21},{18,22},{19,23}} | collective-permute-start | bytes 393224 | tf_op jit(solution)/shard_map/ppermute | solution.py:288
  13.0 8.2 %collective-permute-start.6 = (bf16[128,512]{1,0:T(8,128)(2,1)S(1)}, bf16[128,512]{1,0:T(8,128)(2,1)S(1)}, u32[]{:S(2)}, u32[]{:S(2)}) collective-permute-start(bf16[128,512]{1,0:T(8,128)(2,1)S(1)} %get-tuple-element.41), channel_id=1, source_target_pairs={{0,4},{1,5},{2,6},{3,7},{16,20},{17,21},{18,22},{19,23}} | collective-permute-start | bytes 393224 | tf_op jit(solution)/shard_map/ppermute | solution.py:288
  14.3 8.6 %collective-permute-start.9 = (bf16[128,512]{1,0:T(8,128)(2,1)S(1)}, bf16[128,512]{1,0:T(8,128)(2,1)S(1)}, u32[]{:S(2)}, u32[]{:S(2)}) collective-permute-start(bf16[128,512]{1,0:T(8,128)(2,1)S(1)} %get-tuple-element.40), channel_id=1, source_target_pairs={{0,4},{1,5},{2,6},{3,7},{16,20},{17,21},{18,22},{19,23}} | collective-permute-start | bytes 393224 | tf_op jit(solution)/shard_map/ppermute | solution.py:288
  15.6 12.3 %all-to-all-start = ((bf16[4,4,256]{2,1,0:T(4,128)(2,1)}), bf16[4,4,256]{2,1,0:T(4,128)(2,1)S(1)}, u32[]{:S(2)}, u32[]{:S(2)}) async-start(bf16[4,4,256]{2,1,0:T(4,128)(2,1)} %bitcast), calls=%async_computation | async-start | bytes 16384 | tf_op jit(solution)/shard_map/all_to_all | solution.py:293
  22.9 4.7 %copy-start.17 = (s32[8]{0:T(128)S(1)}, s32[8]{0:T(128)}, u32[]{:S(2)}) copy-start(s32[8]{0:T(128)} %param.19) | copy-start | bytes 100
  22.9 5.0 %copy-start.1 = (bf16[256,2048]{1,0:T(8,128)(2,1)S(1)}, bf16[256,2048]{1,0:T(8,128)(2,1)}, u32[]{:S(2)}) copy-start(bf16[256,2048]{1,0:T(8,128)(2,1)} %x_ref.3) | copy-start | bytes 3145732
  22.9 5.0 %copy-start.2 = (bf16[256,256]{1,0:T(8,128)(2,1)S(1)}, bf16[256,256]{1,0:T(8,128)(2,1)}, u32[]{:S(2)}) copy-start(bf16[256,256]{1,0:T(8,128)(2,1)} %c_ref.3) | copy-start | bytes 393220
  22.9 5.0 %copy-start.4 = (bf16[256,256]{1,0:T(8,128)(2,1)S(1)}, bf16[256,256]{1,0:T(8,128)(2,1)}, u32[]{:S(2)}) copy-start(bf16[256,256]{1,0:T(8,128)(2,1)} %b_ref.3) | copy-start | bytes 393220
  23.1 2.9 %collective-permute-start.1 = (bf16[128,512]{1,0:T(8,128)(2,1)S(1)}, bf16[128,512]{1,0:T(8,128)(2,1)S(1)}, u32[]{:S(2)}, u32[]{:S(2)}) collective-permute-start(bf16[128,512]{1,0:T(8,128)(2,1)S(1)} %get-tuple-element.39), channel_id=1, source_target_pairs={{4,8},{5,9},{6,10},{7,11},{20,24},{21,25},{22,26},{23,27}} | collective-permute-start | bytes 393224 | tf_op jit(solution)/shard_map/ppermute | solution.py:288
  23.9 2.1 %collective-permute-start.10 = (bf16[128,512]{1,0:T(8,128)(2,1)S(1)}, bf16[128,512]{1,0:T(8,128)(2,1)S(1)}, u32[]{:S(2)}, u32[]{:S(2)}) collective-permute-start(bf16[128,512]{1,0:T(8,128)(2,1)S(1)} %get-tuple-element.36), channel_id=1, source_target_pairs={{4,8},{5,9},{6,10},{7,11},{20,24},{21,25},{22,26},{23,27}} | collective-permute-start | bytes 393224 | tf_op jit(solution)/shard_map/ppermute | solution.py:288
  24.6 1.4 %collective-permute-start.4 = (bf16[128,512]{1,0:T(8,128)(2,1)S(1)}, bf16[128,512]{1,0:T(8,128)(2,1)S(1)}, u32[]{:S(2)}, u32[]{:S(2)}) collective-permute-start(bf16[128,512]{1,0:T(8,128)(2,1)S(1)} %get-tuple-element.38), channel_id=1, source_target_pairs={{4,8},{5,9},{6,10},{7,11},{20,24},{21,25},{22,26},{23,27}} | collective-permute-start | bytes 393224 | tf_op jit(solution)/shard_map/ppermute | solution.py:288
  25.3 0.7 %collective-permute-start.7 = (bf16[128,512]{1,0:T(8,128)(2,1)S(1)}, bf16[128,512]{1,0:T(8,128)(2,1)S(1)}, u32[]{:S(2)}, u32[]{:S(2)}) collective-permute-start(bf16[128,512]{1,0:T(8,128)(2,1)S(1)} %get-tuple-element.37), channel_id=1, source_target_pairs={{4,8},{5,9},{6,10},{7,11},{20,24},{21,25},{22,26},{23,27}} | collective-permute-start | bytes 393224 | tf_op jit(solution)/shard_map/ppermute | solution.py:288
  26.0 1.7 %copy-start.10 = (bf16[128,512]{1,0:T(8,128)(2,1)}, bf16[128,512]{1,0:T(8,128)(2,1)S(1)}, u32[]{:S(2)}) copy-start(bf16[128,512]{1,0:T(8,128)(2,1)S(1)} %collective-permute-done.10) | copy-start | bytes 393220
  26.0 1.7 %copy-start.12 = (bf16[128,512]{1,0:T(8,128)(2,1)}, bf16[128,512]{1,0:T(8,128)(2,1)S(1)}, u32[]{:S(2)}) copy-start(bf16[128,512]{1,0:T(8,128)(2,1)S(1)} %collective-permute-done.7) | copy-start | bytes 393220
  26.9 5.2 %collective-permute-start.11 = (bf16[128,512]{1,0:T(8,128)(2,1)}, bf16[128,512]{1,0:T(8,128)(2,1)S(1)}, u32[]{:S(2)}, u32[]{:S(2)}) collective-permute-start(bf16[128,512]{1,0:T(8,128)(2,1)} %get-tuple-element.32), channel_id=1, source_target_pairs={{8,12},{9,13},{10,14},{11,15},{24,28},{25,29},{26,30},{27,31}} | collective-permute-start | bytes 393224 | tf_op jit(solution)/shard_map/ppermute | solution.py:288
  27.8 4.3 %copy-start.11 = (bf16[128,512]{1,0:T(8,128)(2,1)S(1)}, bf16[128,512]{1,0:T(8,128)(2,1)}, u32[]{:S(2)}) copy-start(bf16[128,512]{1,0:T(8,128)(2,1)} %copy-done.10) | copy-start | bytes 393220
  27.8 4.3 %copy-start.13 = (bf16[128,512]{1,0:T(8,128)(2,1)S(1)}, bf16[128,512]{1,0:T(8,128)(2,1)}, u32[]{:S(2)}) copy-start(bf16[128,512]{1,0:T(8,128)(2,1)} %copy-done.12) | copy-start | bytes 393220
  30.1 2.1 %collective-permute-start.8 = (bf16[128,512]{1,0:T(8,128)(2,1)}, bf16[128,512]{1,0:T(8,128)(2,1)S(1)}, u32[]{:S(2)}, u32[]{:S(2)}) collective-permute-start(bf16[128,512]{1,0:T(8,128)(2,1)} %get-tuple-element.35), channel_id=1, source_target_pairs={{8,12},{9,13},{10,14},{11,15},{24,28},{25,29},{26,30},{27,31}} | collective-permute-start | bytes 393224 | tf_op jit(solution)/shard_map/ppermute | solution.py:288
  30.7 1.5 %collective-permute-start.5 = (bf16[128,512]{1,0:T(8,128)(2,1)}, bf16[128,512]{1,0:T(8,128)(2,1)S(1)}, u32[]{:S(2)}, u32[]{:S(2)}) collective-permute-start(bf16[128,512]{1,0:T(8,128)(2,1)} %get-tuple-element.34), channel_id=1, source_target_pairs={{8,12},{9,13},{10,14},{11,15},{24,28},{25,29},{26,30},{27,31}} | collective-permute-start | bytes 393224 | tf_op jit(solution)/shard_map/ppermute | solution.py:288
  31.4 0.9 %collective-permute-start.2 = (bf16[128,512]{1,0:T(8,128)(2,1)}, bf16[128,512]{1,0:T(8,128)(2,1)S(1)}, u32[]{:S(2)}, u32[]{:S(2)}) collective-permute-start(bf16[128,512]{1,0:T(8,128)(2,1)} %get-tuple-element.33), channel_id=1, source_target_pairs={{8,12},{9,13},{10,14},{11,15},{24,28},{25,29},{26,30},{27,31}} | collective-permute-start | bytes 393224 | tf_op jit(solution)/shard_map/ppermute | solution.py:288
  32.2 27.3 %copy-start.14 = (bf16[1,4,4,2048]{3,2,1,0:T(4,128)(2,1)S(1)}, bf16[1,4,4,2048]{3,2,1,0:T(4,128)(2,1)}, u32[]{:S(2)}) copy-start(bf16[1,4,4,2048]{3,2,1,0:T(4,128)(2,1)} %param.20) | copy-start | bytes 196612
  32.3 27.3 %copy-start.15 = (bf16[1,4,4,256]{3,2,1,0:T(4,128)(2,1)S(1)}, bf16[1,4,4,256]{3,2,1,0:T(4,128)(2,1)}, u32[]{:S(2)}) copy-start(bf16[1,4,4,256]{3,2,1,0:T(4,128)(2,1)} %param.21) | copy-start | bytes 24580
  32.3 27.3 %copy-start.5 = (bf16[1,4,4,32]{3,2,1,0:T(4,128)(2,1)S(1)}, bf16[1,4,4,32]{3,2,1,0:T(4,128)(2,1)}, u32[]{:S(2)}) copy-start(bf16[1,4,4,32]{3,2,1,0:T(4,128)(2,1)} %param.23) | copy-start | bytes 3076
  32.3 27.3 %copy-start.7 = (f32[32]{0:T(128)S(1)}, f32[32]{0:T(128)}, u32[]{:S(2)}) copy-start(f32[32]{0:T(128)} %param.16) | copy-start | bytes 388
  32.3 27.3 %copy-start.9 = (f32[32]{0:T(128)S(1)}, f32[32]{0:T(128)}, u32[]{:S(2)}) copy-start(f32[32]{0:T(128)} %param.17) | copy-start | bytes 388
  35.2 29.5 %all-to-all-start.1 = ((f32[4,4,2048]{2,1,0:T(4,128)}), f32[4,4,2048]{2,1,0:T(4,128)S(1)}, u32[]{:S(2)}, u32[]{:S(2)}) async-start(f32[4,4,2048]{2,1,0:T(4,128)} %reshape.48), calls=%async_computation.1 | async-start | bytes 262144 | tf_op jit(solution)/shard_map/all_to_all | solution.py:334

commit v2 on v1

v2 whole, which is shorter than its diff:
```python
import functools
import math

import jax
import jax.numpy as jnp
from jax import lax
from jax.experimental import pallas as pl
from jax.experimental.pallas import tpu as pltpu
from jax.sharding import PartitionSpec as P

H = 128
P_SIZE = 64
N = 128
G = 8
SPAN = 128
STEPS = 4
LOG2E = math.log2(math.e)
F32 = jnp.float32
BF16 = jnp.bfloat16
CHUNKS = 8
LAG = 2
VMEM_LIMIT = 32 * 1024 * 1024


def softplus(value):
    small = jnp.exp(-jnp.abs(value))
    series = small * (1.0 - small * (0.5 - small * (1.0 / 3.0 - small * 0.25)))
    return jnp.maximum(value, 0.0) + jnp.where(small < 0.02, series, jnp.log(1.0 + small))


def dot(left, right, left_dim=1, right_dim=0):
    return lax.dot_general(
        left, right, (((left_dim,), (right_dim,)), ((), ())), preferred_element_type=F32
    )


def split(value, pieces):
    result = []
    for _ in range(pieces):
        piece = value.astype(BF16)
        result.append(piece)
        value = value - piece.astype(F32)
    return result


def exact_dot(ones, value, pieces=3, left_dim=1):
    return sum(dot(ones, piece, left_dim) for piece in split(value, pieces))


def spread_matrix(heads, first, width):
    lane = lax.broadcasted_iota(jnp.int32, (heads, width), 1) + first
    head = lax.broadcasted_iota(jnp.int32, (heads, width), 0)
    return jnp.where(lane // P_SIZE == head, 1.0, 0.0).astype(BF16)


def over_lanes(value, first, width, pieces=2):
    return exact_dot_right(value, spread_matrix(value.shape[1], first, width), pieces)


def exact_dot_right(value, ones, pieces):
    return sum(dot(piece, ones) for piece in split(value, pieces))


def shape(dims, dtype=F32):
    return jax.ShapeDtypeStruct(dims, dtype)


def call(kernel, out_shape, flops, moved, **options):
    return pl.pallas_call(
        kernel,
        out_shape=out_shape,
        compiler_params=pltpu.CompilerParams(vmem_limit_bytes=VMEM_LIMIT),
        cost_estimate=pl.CostEstimate(flops=flops, bytes_accessed=moved, transcendentals=0),
        **options,
    )


def triangle(keep):
    row = lax.broadcasted_iota(jnp.int32, (SPAN, SPAN), 0)
    column = lax.broadcasted_iota(jnp.int32, (SPAN, SPAN), 1)
    return jnp.where(keep(row, column), 1.0, 0.0).astype(BF16)


def state_kernel(
    x_hbm, b_hbm, dt_hbm, a_hbm, c_hbm, *rest,
):
    moving_refs = rest[:LAG]
    total_ref, decay_ref, cum_ref, row_ref = rest[LAG : LAG + 4]
    x_ref, b_ref, dt_ref, a_ref, sems = rest[LAG + 4 :]
    heads, tokens = dt_ref.shape
    spans = tokens // SPAN
    chunks, _, width = total_ref.shape
    per_group = H // G
    first_copies = [
        pltpu.make_async_copy(dt_hbm, dt_ref, sems.at[0]),
        pltpu.make_async_copy(a_hbm, a_ref, sems.at[1]),
        pltpu.make_async_copy(b_hbm, b_ref, sems.at[2]),
        pltpu.make_async_copy(c_hbm, moving_refs[0].at[N:, : c_hbm.shape[1]], sems.at[3]),
    ]
    x_copies = []
    for k in range(chunks):
        lanes = slice(k * width, (k + 1) * width)
        x_copies.append(
            pltpu.make_async_copy(x_hbm.at[:, lanes], x_ref.at[:, lanes], sems.at[4 + k])
        )
    for copy in first_copies[:3] + x_copies + first_copies[3:]:
        copy.start()
    upper = triangle(lambda s, t: s <= t)
    eye = lax.broadcasted_iota(jnp.int32, (heads, heads), 0) == lax.broadcasted_iota(
        jnp.int32, (heads, heads), 1
    )
    first_copies[0].wait()
    first_copies[1].wait()
    a_column = jnp.sum(jnp.where(eye, a_ref[...], 0.0), axis=1, keepdims=True)
    step = softplus(dt_ref[...].astype(F32))
    rate = step * (jnp.exp(a_column) * -LOG2E)
    cums = [exact_dot_right(rate[:, i * SPAN : (i + 1) * SPAN], upper, 3) for i in range(spans)]
    ends = [cum[:, SPAN - 1 : SPAN] for cum in cums]
    after = jnp.zeros_like(ends[0])
    weights = [None] * spans
    for i in reversed(range(spans)):
        after = after + ends[i]
        weights[i] = jnp.exp2(after - cums[i]) * step[:, i * SPAN : (i + 1) * SPAN]
    weight = jnp.concatenate(weights, axis=1).T
    whole = jnp.sum(jnp.where(eye, jnp.exp2(after), 0.0), axis=0, keepdims=True)
    first_copies[2].wait()
    turned = [
        b_ref[:, g * N : (g + 1) * N].astype(F32).T.astype(BF16)
        for g in range(heads // per_group)
    ]
    for k in range(chunks):
        first = k * width
        lanes = slice(first, first + width)
        x_copies[k].wait()
        scaled = (x_ref[:, lanes].astype(F32) * over_lanes(weight, first, width)).astype(BF16)
        total = dot(turned[first // (per_group * P_SIZE)], scaled)
        total_ref[k] = total
        if k < LAG:
            moving_refs[k][:N] = total.astype(BF16)
        decay_ref[k] = over_lanes(whole, first, width, 3)
    cum = jnp.concatenate(cums, axis=1)
    cum_ref[...] = cum
    row_ref[...] = jnp.log2(step) - cum
    first_copies[3].wait()


def pass_kernel(step, total_ref, decay_ref, got_ref, *rest):
    (moving_ref, carry_ref) = rest[-2:]
    chunks = total_ref.shape[0]
    me = lax.axis_index("seq")
    wanted = step - LAG * me
    k = jnp.clip(wanted, 0, chunks - 1)
    slot = jnp.where((me > 0) & (wanted == k), k, chunks)
    if len(rest) == 2:
        carry_ref[...] = jnp.zeros_like(carry_ref)
    got = jnp.where(me > 0, got_ref[:N].astype(F32), 0.0)
    moving_ref[:N] = (total_ref[k] + decay_ref[k] * got).astype(BF16)
    carry_ref[slot] = got_ref[:N]
    if moving_ref.shape[0] > N:
        moving_ref[N:] = got_ref[N:]


def inner_kernel(
    g, x_ref, b_ref, c_ref, cum_ref, row_ref, d_ref, spot_ref, own_ref, *rest
):
    ask_refs = rest[:-4]
    inner_ref, local_ref, gain_ref, asked_ref = rest[-4:]
    heads, tokens = cum_ref.shape
    spans = tokens // SPAN
    asks = own_ref.shape[0]
    per_group = H // G
    me = lax.axis_index("seq")
    names = slice(g * N, (g + 1) * N)
    blocks = [own_ref[:, names]] + [ref[N:, names] for ref in ask_refs]
    row_index = lax.broadcasted_iota(jnp.int32, (asks, asks * len(blocks)), 0)
    block_index = lax.broadcasted_iota(jnp.int32, (asks, asks * len(blocks)), 1)
    wanted = (row_index // STEPS) * asks + me * STEPS + row_index % STEPS
    chosen = jnp.where(block_index == wanted, 1.0, 0.0).astype(BF16)
    asked = dot(chosen, jnp.concatenate(blocks, axis=0)).astype(BF16)
    asked_ref[...] = asked
    t_index = lax.broadcasted_iota(jnp.int32, (SPAN, SPAN), 0)
    s_index = lax.broadcasted_iota(jnp.int32, (SPAN, SPAN), 1)
    causal = t_index >= s_index
    spot = spot_ref[...]
    position = lax.broadcasted_iota(jnp.int32, (asks, tokens), 1)
    picked = jnp.where(position == spot, 1.0, 0.0).astype(BF16)
    rows = row_ref[...]
    cum = cum_ref[...].T
    ends = [cum[(i + 1) * SPAN - 1 : (i + 1) * SPAN, :] for i in range(spans)]
    near_ask = exact_dot(picked, cum)
    upto = position <= spot
    starts = [jnp.zeros_like(ends[0])]
    for i in range(spans):
        starts.append(starts[i] + ends[i])
    ask_start = starts[0]
    for i in range(1, spans):
        ask_start = jnp.where(spot >= i * SPAN, starts[i], ask_start)
    gain_ref[...] = near_ask + ask_start
    ask_columns = []
    for j in range(spans):
        column = near_ask
        for i in range(j + 1, spans):
            between = sum(ends[j + 1 : i], ends[j])
            column = jnp.where(spot // SPAN == i, near_ask + between, column)
        ask_columns.append(column)
    first_half = lax.broadcasted_iota(jnp.int32, (1, 2 * P_SIZE), 1) < P_SIZE
    b_part = b_ref[:, names]
    scores = dot(c_ref[:, names], b_part, 1, 1)
    ask_scores = dot(asked, b_part, 1, 1)
    for pair in range(per_group // 2):
        h0 = g * per_group + 2 * pair
        lanes = slice(h0 * P_SIZE, (h0 + 2) * P_SIZE)
        here = slice(2 * pair * P_SIZE, (2 * pair + 2) * P_SIZE)
        x_part = x_ref[:, lanes]
        zero = jnp.zeros_like(x_part)
        halves = (jnp.where(first_half, x_part, zero), jnp.where(first_half, zero, x_part))
        weights = [[None, None] for _ in range(spans)]
        for e in range(2):
            h = h0 + e
            row = rows[h : h + 1, :]
            for i in range(spans):
                column = jnp.broadcast_to(cum[i * SPAN : (i + 1) * SPAN, h : h + 1], (SPAN, SPAN))
                parts = []
                for j in range(i + 1):
                    shift = row[:, j * SPAN : (j + 1) * SPAN]
                    for m in range(j, i):
                        shift = shift + ends[m][:, h : h + 1]
                    score = scores[i * SPAN : (i + 1) * SPAN, j * SPAN : (j + 1) * SPAN]
                    part = score * jnp.exp2(column + shift)
                    if i == j:
                        part = jnp.where(causal, part, 0.0)
                    parts.append(part.astype(BF16))
                if i == spans - 1:
                    for j in range(spans):
                        span = slice(j * SPAN, (j + 1) * SPAN)
                        part = ask_scores[:, span] * jnp.exp2(
                            ask_columns[j][:, h : h + 1] + row[:, span]
                        )
                        part = jnp.where(upto[:, span], part, 0.0).astype(BF16)
                        parts[j] = jnp.concatenate([parts[j], part], axis=0)
                weights[i][e] = jnp.concatenate(parts, axis=1) if i else parts[0]
        skip = jnp.where(first_half, d_ref[:, h0 : h0 + 1], d_ref[:, h0 + 1 : h0 + 2])
        for i in range(spans):
            reach = (i + 1) * SPAN
            left = jnp.concatenate(weights[i], axis=1)
            right = jnp.concatenate([half[:reach] for half in halves], axis=0)
            result = dot(left, right)
            mine = slice(i * SPAN, (i + 1) * SPAN)
            inner_ref[mine, here] = result[:SPAN] + skip * x_part[mine].astype(F32)
            if i == spans - 1:
                local_ref[:, here] = result[SPAN:]


def read_kernel(groups, gain_ref, carry_in_ref, *rest):
    asked_refs, local_refs = rest[:groups], rest[groups : 2 * groups]
    got_refs = rest[2 * groups : 2 * groups + LAG]
    carry_ref, read_refs = rest[2 * groups + LAG], rest[2 * groups + LAG + 1 :]
    chunks, _, width = carry_ref.shape
    chunks = chunks - 1
    count = len(read_refs)
    me = lax.axis_index("seq")
    for i, got_ref in enumerate(got_refs):
        wanted = chunks + LAG * (count - 1) - LAG + i - LAG * me
        k = jnp.clip(wanted, 0, chunks - 1)
        carry_ref[jnp.where((me > 0) & (wanted == k), k, chunks)] = got_ref[:N]
    gain = jnp.exp2(gain_ref[...])
    per_group = H // G
    for k in range(chunks):
        first = k * width
        g = first // (per_group * P_SIZE)
        here = slice(first - g * per_group * P_SIZE, first - g * per_group * P_SIZE + width)
        carried = dot(asked_refs[g][...], carry_ref[k])
        reading = local_refs[g][:, here] + over_lanes(gain, first, width) * carried
        for r in range(count):
            read_refs[r][:, first : first + width] = reading[r * STEPS : (r + 1) * STEPS]


def outer_kernel(groups, c_ref, cum_ref, carry_ref, *rest):
    inner_refs, out_hbm, out_ref, sems = rest[:groups], rest[-3], rest[-2], rest[-1]
    heads, tokens = cum_ref.shape
    spans = tokens // SPAN
    chunks, _, width = carry_ref.shape
    chunks = chunks - 1
    per_group = H // G
    start = jnp.zeros((heads, 1), F32)
    gains = []
    for i in range(spans):
        cum = cum_ref[:, i * SPAN : (i + 1) * SPAN]
        gains.append(jnp.exp2(cum + start))
        start = start + cum[:, SPAN - 1 : SPAN]
    gain = jnp.concatenate(gains, axis=1).T
    copies = []
    for k in range(chunks):
        first = k * width
        g = first // (per_group * P_SIZE)
        lanes = slice(first, first + width)
        here = slice(first - g * per_group * P_SIZE, first - g * per_group * P_SIZE + width)
        carried = dot(c_ref[:, g * N : (g + 1) * N], carry_ref[k])
        out = inner_refs[g][:, here] + over_lanes(gain, first, width) * carried
        out_ref[:, lanes] = out.astype(BF16)
        copies.append(
            pltpu.make_async_copy(out_ref.at[:, lanes], out_hbm.at[:, lanes], sems.at[k])
        )
        copies[k].start()
    for copy in copies:
        copy.wait()


def fresh_kernel(x_ref, b_ref, c_ref, dt_ref, a_ref, d_ref, keep_ref, fresh_ref):
    rows, heads = dt_ref.shape
    per_group = H // G
    groups = heads // per_group
    width = x_ref.shape[1]
    turn = lax.broadcasted_iota(jnp.int32, (rows, 1), 0) % STEPS
    step = softplus(dt_ref[...].astype(F32))
    rate = step * (jnp.exp(a_ref[...]) * -LOG2E)

    def earlier(value, gap):
        if not gap:
            return value
        moved = jnp.concatenate([jnp.zeros_like(value[:gap]), value[:-gap]], axis=0)
        return jnp.where(turn >= gap, moved, 0.0)

    running = sum(earlier(rate, gap) for gap in range(STEPS))
    keep = over_lanes(jnp.exp2(running), 0, width)
    x_values = x_ref[...].astype(F32)
    b_values = b_ref[...].astype(F32)
    c_values = c_ref[...].astype(F32)
    head = lax.broadcasted_iota(jnp.int32, (rows, heads), 1)
    fresh = over_lanes(d_ref[...], 0, width, 3) * x_values
    since = jnp.zeros_like(rate)
    for gap in range(STEPS):
        if gap:
            since = since + earlier(rate, gap - 1)
        products = c_values * earlier(b_values, gap)
        pair = jnp.zeros((rows, heads), F32)
        for g in range(groups):
            score = jnp.sum(products[:, g * N : (g + 1) * N], axis=1, keepdims=True)
            pair = jnp.where(head // per_group == g, score, pair)
        factor = jnp.where(turn >= gap, jnp.exp2(since) * earlier(step, gap) * pair, 0.0)
        fresh = fresh + over_lanes(factor, 0, width) * earlier(x_values, gap)
    for i in range(rows // STEPS):
        keep_ref[i] = keep[i * STEPS : (i + 1) * STEPS]
        fresh_ref[i] = fresh[i * STEPS : (i + 1) * STEPS]


def finish_kernel(held_ref, keep_ref, fresh_ref, *rest):
    back_refs, out_ref = rest[:-1], rest[-1]
    count = len(back_refs)
    me = lax.axis_index("seq")
    for r in range(count):
        source = lax.rem(me + r, count)
        value = back_refs[r][...] * keep_ref[source] + fresh_ref[source]
        out_ref[source] = jnp.where(held_ref[source] > 0, value, 0.0).astype(BF16)


def shards(
    ssm_input, bmat, cmat, dt_raw, a_log, d_skip, prompt_len, owner, dec_x, dec_b, dec_c, dec_dt
):
    count = lax.axis_size("seq")
    me = lax.axis_index("seq")
    tokens, heads = dt_raw.shape
    groups = heads // (H // G)
    names = groups * N
    lanes = heads * P_SIZE
    group_lanes = lanes // groups
    rows = count * STEPS
    width = lanes // CHUNKS
    a_row = a_log.reshape(1, heads)
    d_row = d_skip.reshape(1, heads)
    own = dec_c.reshape(rows, names)
    anywhere = pl.BlockSpec(memory_space=pl.ANY)
    steps = CHUNKS + LAG * (count - 2)

    def carries_asks(s):
        return s % LAG == 0 and s // LAG < count - 1

    def sent_shape(s):
        return shape((N + rows * carries_asks(s), width), BF16)

    *moving, total, decay, cum, row = call(
        state_kernel,
        tuple(sent_shape(s) for s in range(LAG))
        + (
            shape((CHUNKS, N, width)),
            shape((CHUNKS, 1, width)),
            shape((heads, tokens)),
            shape((heads, tokens)),
        ),
        2 * tokens * N * lanes,
        4 * tokens * lanes,
        in_specs=[anywhere] * 5,
        scratch_shapes=[
            pltpu.VMEM((tokens, lanes), BF16),
            pltpu.VMEM((tokens, names), BF16),
            pltpu.VMEM((heads, tokens), BF16),
            pltpu.VMEM((1, heads), F32),
            pltpu.SemaphoreType.DMA((4 + CHUNKS,)),
        ],
    )(ssm_input, bmat, dt_raw.T, a_row, own)

    ring = [(d, (d + 1) % count) for d in range(count)]
    got = []
    carry = None
    for s in range(steps):
        if s >= LAG:
            before = () if carry is None else (carry,)
            sent, carry = call(
                functools.partial(pass_kernel, s),
                (sent_shape(s), shape((CHUNKS + 1, N, width), BF16)),
                2 * N * width,
                8 * N * width,
                input_output_aliases={3: 1} if before else {},
            )(total, decay, got[s - LAG], *before)
            moving.append(sent)
        got.append(lax.ppermute(moving[s], "seq", ring))

    last_token = prompt_len - 1
    sources = last_token // tokens
    indices = jnp.arange(count, dtype=jnp.int32)
    owners = (me - indices) % count
    mine = (sources == me)[None, :] & (owner[None, :] == owners[:, None])
    offsets = jnp.sum(jnp.where(mine, last_token[None, :] - me * tokens, 0), axis=1)
    spot = jnp.repeat(offsets, STEPS).reshape(rows, 1).astype(jnp.int32)
    held = jnp.any((owner == me)[None, :] & (sources[None, :] == indices[:, None]), axis=1)

    ask_blocks = [got[s] for s in range(steps) if carries_asks(s)]
    inner, local, asked = [], [], []
    for g in range(groups):
        inner_g, local_g, gain, asked_g = call(
            functools.partial(inner_kernel, g),
            (
                shape((tokens, group_lanes)),
                shape((rows, group_lanes)),
                shape((rows, heads)),
                shape((rows, N), BF16),
            ),
            4 * tokens * tokens * group_lanes,
            16 * tokens * group_lanes,
        )(ssm_input, bmat, cmat, cum, row, d_row, spot, own, *ask_blocks)
        inner.append(inner_g)
        local.append(local_g)
        asked.append(asked_g)

    keep, fresh = call(
        fresh_kernel,
        (shape((count, STEPS, lanes)), shape((count, STEPS, lanes))),
        64 * rows * lanes,
        16 * rows * lanes,
    )(
        dec_x.reshape(rows, lanes),
        dec_b.reshape(rows, names),
        own,
        dec_dt.reshape(rows, heads),
        a_row,
        d_row,
    )

    carry, *reading = call(
        functools.partial(read_kernel, groups),
        (shape(carry.shape, BF16),) + (shape((STEPS, lanes)),) * count,
        2 * rows * N * lanes,
        4 * N * lanes,
        input_output_aliases={1: 0},
    )(gain, carry, *asked, *local, *got[steps - LAG :])
    back = [reading[0]]
    for r in range(1, count):
        there = [(d, (d - r) % count) for d in range(count)]
        back.append(lax.ppermute(reading[r], "seq", there))

    prefill = call(
        functools.partial(outer_kernel, groups),
        shape((tokens, lanes), BF16),
        2 * tokens * N * lanes,
        8 * tokens * lanes,
        out_specs=anywhere,
        scratch_shapes=[
            pltpu.VMEM((tokens, lanes), BF16),
            pltpu.SemaphoreType.DMA((CHUNKS,)),
        ],
    )(cmat, cum, carry, *inner)

    decoded = call(
        finish_kernel,
        shape((count, STEPS, lanes), BF16),
        4 * rows * lanes,
        16 * rows * lanes,
        in_specs=[pl.BlockSpec(memory_space=pltpu.SMEM)]
        + [pl.BlockSpec(memory_space=pltpu.VMEM)] * (2 + count),
    )(held.astype(jnp.int32), keep, fresh, *back)
    return (prefill, decoded[None])


def solution(mesh):
    placed = (
        P(("grp", "seq"), "tp"),
        P(("grp", "seq"), "tp"),
        P(("grp", "seq"), "tp"),
        P(("grp", "seq"), "tp"),
        P("tp"),
        P("tp"),
        P("grp"),
        P("grp"),
        P(("grp", "seq"), None, None, "tp"),
        P(("grp", "seq"), None, None, "tp"),
        P(("grp", "seq"), None, None, "tp"),
        P(("grp", "seq"), None, None, "tp"),
    )
    return jax.shard_map(
        shards,
        mesh=mesh,
        in_specs=placed,
        out_specs=(P(("grp", "seq"), "tp"), P(("grp", "seq"), None, None, "tp")),
        check_vma=False,
    )
```

time: 66 us -> 60.3 us (0.914)
  starting transfers between devices: 41.2 us -> 9.72 us
  waiting for transfers between devices: 8.5 us -> 31.3 us
  Pallas kernels: 6.46 us -> 11 us
  other arithmetic: 2.18 us -> 0.34 us
  local copies, waits for them, and re-layouts: 6.04 us -> 6.79 us
    ppermute x12 -> x15, waiting for transfers between devices: 3.99 us -> 31.3 us  [the longest x12 30.9 us: shards(): got.append(lax.ppermute(moving[s], 'seq', ring))]
    all_to_all x2 -> x0, starting transfers between devices: 26.9 us -> none  [the longest x1 23.6 us: shards(): lax.all_to_all(reading.reshape(seq_count, STEPS, lanes), 'seq', split_axi...]
    ppermute x12 -> x15, starting transfers between devices: 14.3 us -> 9.72 us  [the longest x12 5.95 us: shards(): got.append(lax.ppermute(moving[s], 'seq', ring))]
    all_to_all x2 -> x0, waiting for transfers between devices: 4.5 us -> none  [the longest x1 4.5 us: shards(): lax.all_to_all(reading.reshape(seq_count, STEPS, lanes), 'seq', split_axi...]
    pallas_call x4 -> x17, Pallas kernels: 6.46 us -> 11 us  [the longest x1 4.47 us: shards(): call(state_kernel, tuple((sent_shape(s) for s in range(LAG))) + (shape((C...]
    convert_element_type x2 -> x1, other arithmetic: 1.09 us -> 0.01 us  [shards(): held.astype(jnp.int32)]
    reshape x1, local copies, waits for them, and re-layouts: 0.02 us -> 0.86 us  [shards(): dec_x.reshape(rows, lanes)]
    reshape x6 -> x2, local copies, waits for them, and re-layouts: 1.49 us -> 0.72 us  [the longest x1 0.71 us: shards(): own = dec_c.reshape(rows, names)]
  transfers between devices with their start and end apart: 14 -> 15, of which waited for: 3 -> 13; matrix products, arithmetic and copies ran while one was open for 4% -> 2% of each run, Pallas kernels for 4% -> 8%
where the time goes in v2:
time: 60.3 us; the launch traced here: 60 us
  waiting for transfers between devices  31.3 us (52%)
  Pallas kernels  11 us (18%)
  starting transfers between devices  9.72 us (16%)
  local copies, waits for them, and re-layouts  6.79 us (11%)
  between operations  0.88 us (1%)
    ppermute x12, waiting for transfers between devices, shards(): got.append(lax.ppermute(moving[s], 'seq', ring))  30.9 us
    ppermute x12, starting transfers between devices, shards(): got.append(lax.ppermute(moving[s], 'seq', ring))  5.95 us
    unnamed x28, local copies, waits for them, and re-layouts  5.06 us
    pallas_call x1, Pallas kernels, shards(): call(state_kernel, tuple((sent_shape(s) for s in range(LAG))) + (shape((C...  4.47 us
    ppermute x3, starting transfers between devices, shards(): back.append(lax.ppermute(reading[r], 'seq', there))  3.77 us
    pallas_call x2, Pallas kernels, shards(): call(functools.partial(inner_kernel, g), (shape((tokens, group_lanes)), s...  2.41 us
    pallas_call x1, Pallas kernels, shards(): call(functools.partial(outer_kernel, groups), shape((tokens, lanes), BF16...  1.89 us
    pallas_call x1, Pallas kernels, shards(): call(finish_kernel, shape((count, STEPS, lanes), BF16), 4 * rows * lanes,...  1.22 us
  transfers between devices with their start and end apart: 15, of which 13 were waited for; matrix products, arithmetic and copies ran while one was open for 2% of the time, Pallas kernels for 8%

profile of v2, /device:TPU:0, one launch (start us, length us, event | category | flops | bytes accessed | tf_op | source)
XLA Modules:
  0.0 60.0 jit_solution(12331415392615491210)
XLA Ops:
  0.6 0.0 copy-start.7
  0.6 0.7 %reshape.44.c_hbm.own_ref.c_ref = bf16[16,256]{1,0:T(8,128)(2,1)S(1)} reshape(bf16[1,4,4,256]{3,2,1,0:T(4,128)(2,1)} %param.22) | data formatting | bytes 16384 | tf_op jit(solution)/shard_map/reshape | solution.py:371
  1.4 0.0 copy-start.10
  1.4 0.0 copy-done.7
  1.4 0.7 %copy-done.10 = f32[32]{0:T(128)S(1)} copy-done((f32[32]{0:T(128)S(1)}, f32[32]{0:T(128)}, u32[]{:S(2)}) %copy-start.10) | copy-done | bytes 152
  2.0 1.2 %copy-done = bf16[256,2048]{1,0:T(8,128)(2,1)S(1)} copy-done((bf16[256,2048]{1,0:T(8,128)(2,1)S(1)}, bf16[256,2048]{1,0:T(8,128)(2,1)}, u32[]{:S(2)}) %copy-start) | copy-done | bytes 1048600
  3.2 0.9 %copy-done.2 = bf16[256,256]{1,0:T(8,128)(2,1)S(1)} copy-done((bf16[256,256]{1,0:T(8,128)(2,1)S(1)}, bf16[256,256]{1,0:T(8,128)(2,1)}, u32[]{:S(2)}) %copy-start.2) | copy-done | bytes 131096
  4.1 4.5 %shard_map.131 = (bf16[144,256]{1,0:T(8,128)(2,1)S(1)}, bf16[128,256]{1,0:T(8,128)(2,1)S(1)}, f32[8,128,256]{2,1,0:T(8,128)S(1)}, f32[8,1,256]{2,1,0:T(1,128)S(1...) custom-call(bf16[256,2048]{1,0:T(8,128)(2,1)S(1)} %copy-done, bf16[256,256]{1,0:T(8,128)(2,1)S(1)} %copy-done.2, ...), custom_call_target="tpu_custom_call" | custom-call | flops 134217728 | bytes 2097152 | tf_op jit(solution)/shard_map/pallas_call | solution.py:381
  8.6 3.1 %collective-permute-start = (bf16[144,256]{1,0:T(8,128)(2,1)S(1)}, bf16[144,256]{1,0:T(8,128)(2,1)S(1)}, u32[]{:S(2)}, u32[]{:S(2)}) collective-permute-start(bf16[144,256]{1,0:T(8,128)(2,1)S(1)} %get-tuple-element.44), channel_id=1, source_target_pairs={{0,4},{4,8},{8,12},{12,0},{1,5},{5,9},{9,13},{13,1},{2,6},{6,10},{... | collective-permute-start | bytes 221192 | tf_op jit(solution)/shard_map/ppermute | solution.py:416
  11.7 1.6 %collective-permute-start.2 = (bf16[128,256]{1,0:T(8,128)(2,1)S(1)}, bf16[128,256]{1,0:T(8,128)(2,1)S(1)}, u32[]{:S(2)}, u32[]{:S(2)}) collective-permute-start(bf16[128,256]{1,0:T(8,128)(2,1)S(1)} %get-tuple-element.48), channel_id=1, source_target_pairs={{0,4},{4,8},{8,12},{12,0},{1,5},{5,9},{9,13},{13,1},{2,6},{6,10},{... | collective-permute-start | bytes 196616 | tf_op jit(solution)/shard_map/ppermute | solution.py:416
  13.3 3.3 %collective-permute-done.got_ref.rest_0_ = bf16[144,256]{1,0:T(8,128)(2,1)S(1)} collective-permute-done((bf16[144,256]{1,0:T(8,128)(2,1)S(1)}, bf16[144,256]{1,0:T(8,128)(2,1)S(1)}, u32[]{:S(2)}, u32[]{:S(2)}) %collective-permute-start) | collective-permute-done | bytes 73760 | tf_op jit(solution)/shard_map/ppermute | solution.py:416
  16.5 0.1 shard_map.132
  16.6 0.2 collective-permute-start.1
  16.8 1.0 %collective-permute-done.2.got_ref = bf16[128,256]{1,0:T(8,128)(2,1)S(1)} collective-permute-done((bf16[128,256]{1,0:T(8,128)(2,1)S(1)}, bf16[128,256]{1,0:T(8,128)(2,1)S(1)}, u32[]{:S(2)}, u32[]{:S(2)}) %collective-permute-start.2) | collective-permute-done | bytes 65568 | tf_op jit(solution)/shard_map/ppermute | solution.py:416
  17.8 0.7 %collective-permute-start.4 = (bf16[128,256]{1,0:T(8,128)(2,1)S(1)}, bf16[128,256]{1,0:T(8,128)(2,1)S(1)}, u32[]{:S(2)}, u32[]{:S(2)}) collective-permute-start(bf16[128,256]{1,0:T(8,128)(2,1)S(1)} %get-tuple-element.53), channel_id=1, source_target_pairs={{0,4},{4,8},{8,12},{12,0},{1,5},{5,9},{9,13},{13,1},{2,6},{6,10},{... | collective-permute-start | bytes 196616 | tf_op jit(solution)/shard_map/ppermute | solution.py:416
  18.4 4.4 %collective-permute-done.1.got_ref.rest_1_ = bf16[144,256]{1,0:T(8,128)(2,1)S(1)} collective-permute-done((bf16[144,256]{1,0:T(8,128)(2,1)S(1)}, bf16[144,256]{1,0:T(8,128)(2,1)S(1)}, u32[]{:S(2)}, u32[]{:S(2)}) %collective-permute-start.1) | collective-permute-done | bytes 73760 | tf_op jit(solution)/shard_map/ppermute | solution.py:416
  22.8 0.1 collective-permute-start.3
  22.9 1.0 %collective-permute-done.4.got_ref = bf16[128,256]{1,0:T(8,128)(2,1)S(1)} collective-permute-done((bf16[128,256]{1,0:T(8,128)(2,1)S(1)}, bf16[128,256]{1,0:T(8,128)(2,1)S(1)}, u32[]{:S(2)}, u32[]{:S(2)}) %collective-permute-start.4) | collective-permute-done | bytes 65568 | tf_op jit(solution)/shard_map/ppermute | solution.py:416
  23.9 0.0 copy-start.12
  23.9 0.0 copy-start.13
  23.9 0.1 collective-permute-start.5
  24.0 0.6 copy-done.12
  24.6 0.0 copy-done.13
  24.6 4.4 %collective-permute-done.3.rest_2_.got_ref = bf16[144,256]{1,0:T(8,128)(2,1)S(1)} collective-permute-done((bf16[144,256]{1,0:T(8,128)(2,1)S(1)}, bf16[144,256]{1,0:T(8,128)(2,1)S(1)}, u32[]{:S(2)}, u32[]{:S(2)}) %collective-permute-start.3) | collective-permute-done | bytes 73760 | tf_op jit(solution)/shard_map/ppermute | solution.py:416
  29.1 0.1 collective-permute-start.7
  29.1 1.3 %collective-permute-done.5.got_ref = bf16[128,256]{1,0:T(8,128)(2,1)S(1)} collective-permute-done((bf16[128,256]{1,0:T(8,128)(2,1)S(1)}, bf16[128,256]{1,0:T(8,128)(2,1)S(1)}, u32[]{:S(2)}, u32[]{:S(2)}) %collective-permute-start.5) | collective-permute-done | bytes 65568 | tf_op jit(solution)/shard_map/ppermute | solution.py:416
  30.5 0.1 collective-permute-start.6
  30.6 4.8 %collective-permute-done.7.got_ref = bf16[128,256]{1,0:T(8,128)(2,1)S(1)} collective-permute-done((bf16[128,256]{1,0:T(8,128)(2,1)S(1)}, bf16[128,256]{1,0:T(8,128)(2,1)S(1)}, u32[]{:S(2)}, u32[]{:S(2)}) %collective-permute-start.7) | collective-permute-done | bytes 65568 | tf_op jit(solution)/shard_map/ppermute | solution.py:416
  35.4 0.1 collective-permute-start.9
  35.5 1.6 %collective-permute-done.6.got_ref = bf16[128,256]{1,0:T(8,128)(2,1)S(1)} collective-permute-done((bf16[128,256]{1,0:T(8,128)(2,1)S(1)}, bf16[128,256]{1,0:T(8,128)(2,1)S(1)}, u32[]{:S(2)}, u32[]{:S(2)}) %collective-permute-start.6) | collective-permute-done | bytes 65568 | tf_op jit(solution)/shard_map/ppermute | solution.py:416
  37.1 0.1 collective-permute-start.8
  37.1 4.4 %collective-permute-done.9.got_ref = bf16[128,256]{1,0:T(8,128)(2,1)S(1)} collective-permute-done((bf16[128,256]{1,0:T(8,128)(2,1)S(1)}, bf16[128,256]{1,0:T(8,128)(2,1)S(1)}, u32[]{:S(2)}, u32[]{:S(2)}) %collective-permute-start.9) | collective-permute-done | bytes 65568 | tf_op jit(solution)/shard_map/ppermute | solution.py:416
  41.5 0.0 copy-start.1
  41.6 2.2 %collective-permute-done.8.got_ref = bf16[128,256]{1,0:T(8,128)(2,1)S(1)} collective-permute-done((bf16[128,256]{1,0:T(8,128)(2,1)S(1)}, bf16[128,256]{1,0:T(8,128)(2,1)S(1)}, u32[]{:S(2)}, u32[]{:S(2)}) %collective-permute-start.8) | collective-permute-done | bytes 65568 | tf_op jit(solution)/shard_map/ppermute | solution.py:416
  43.8 0.1 collective-permute-start.11
  43.8 0.1 collective-permute-start.10
  43.9 0.2 select_reduce_fusion
  44.1 0.1 broadcast_in_dim.27
  44.2 0.1 reshape_reshape.4.spot_ref
  44.3 0.0 copy-done.1
  44.3 0.4 copy-done.3
  44.6 0.1 copy-done.4
  44.7 0.2 copy-done.8
  44.9 1.2 %shard_map.143 = (f32[256,1024]{1,0:T(8,128)S(1)}, f32[16,1024]{1,0:T(8,128)S(1)}, f32[16,32]{1,0:T(8,128)}, bf16[16,128]{1,0:T(8,128)(2,1)S(1)}) custom-call(bf16[256,2048]{1,0:T(8,128)(2,1)S(1)} %copy-done.1, bf16[256,256]{1,0:T(8,128)(2,1)S(1)} %copy-done.3, bf16[256,256]{1,0:T(8,128)(2,1)S(1)} %copy-done.4, f32[32,256]{1,0:T(8,128)S(1)} %get-tuple-element.42.cum_ref, ...), custom_call_target="tpu_custom_call" | custom-call | flops 268435456 | bytes 4194304 | tf_op jit(solution)/shard_map/pallas_call | solution.py:430
  46.2 0.0 copy-start.9
  46.2 1.2 %shard_map.135 = (f32[256,1024]{1,0:T(8,128)S(1)}, f32[16,1024]{1,0:T(8,128)S(1)}, f32[16,32]{1,0:T(8,128)S(1)}, bf16[16,128]{1,0:T(8,128)(2,1)S(1)}) custom-call(bf16[256,2048]{1,0:T(8,128)(2,1)S(1)} %copy-done.1, bf16[256,256]{1,0:T(8,128)(2,1)S(1)} %copy-done.3, bf16[256,256]{1,0:T(8,128)(2,1)S(1)} %copy-done.4, f32[32,256]{1,0:T(8,128)S(1)} %get-tuple-element.42.cum_ref, ...), custom_call_target="tpu_custom_call" | custom-call | flops 268435456 | bytes 4194304 | tf_op jit(solution)/shard_map/pallas_call | solution.py:430
  47.4 1.0 %copy-done.5 = f32[256,1024]{1,0:T(8,128)} copy-done((f32[256,1024]{1,0:T(8,128)}, f32[256,1024]{1,0:T(8,128)S(1)}, u32[]{:S(2)}) %copy-start.5) | copy-done | bytes 1048600
  48.4 1.5 %collective-permute-done.11.rest_5_ = bf16[128,256]{1,0:T(8,128)(2,1)S(1)} collective-permute-done((bf16[128,256]{1,0:T(8,128)(2,1)S(1)}, bf16[128,256]{1,0:T(8,128)(2,1)S(1)}, u32[]{:S(2)}, u32[]{:S(2)}) %collective-permute-start.11) | collective-permute-done | bytes 65568 | tf_op jit(solution)/shard_map/ppermute | solution.py:416
  49.9 1.1 %collective-permute-done.10.rest_4_ = bf16[128,256]{1,0:T(8,128)(2,1)S(1)} collective-permute-done((bf16[128,256]{1,0:T(8,128)(2,1)S(1)}, bf16[128,256]{1,0:T(8,128)(2,1)S(1)}, u32[]{:S(2)}, u32[]{:S(2)}) %collective-permute-start.10) | collective-permute-done | bytes 65568 | tf_op jit(solution)/shard_map/ppermute | solution.py:416
  51.0 0.3 shard_map.144
  51.2 1.2 %collective-permute-start.12 = (f32[4,2048]{1,0:T(4,128)S(1)}, f32[4,2048]{1,0:T(4,128)S(1)}, u32[]{:S(2)}, u32[]{:S(2)}) collective-permute-start(f32[4,2048]{1,0:T(4,128)S(1)} %get-tuple-element.79), channel_id=1, source_target_pairs={{0,12},{4,0},{8,4},{12,8},{1,13},{5,1},{9,5},{13,9},{2,14},{6,2},{... | collective-permute-start | bytes 98312 | tf_op jit(solution)/shard_map/ppermute | solution.py:469
  52.5 0.6 collective-permute-start.13
  53.0 1.9 %collective-permute-start.14 = (f32[4,2048]{1,0:T(4,128)S(1)}, f32[4,2048]{1,0:T(4,128)S(1)}, u32[]{:S(2)}, u32[]{:S(2)}) collective-permute-start(f32[4,2048]{1,0:T(4,128)S(1)} %get-tuple-element.81), channel_id=1, source_target_pairs={{0,4},{4,8},{8,12},{12,0},{1,5},{5,9},{9,13},{13,1},{2,6},{6,10},{... | collective-permute-start | bytes 98312 | tf_op jit(solution)/shard_map/ppermute | solution.py:469
  55.0 0.1 fusion.1
  55.1 0.9 %reshape.46.x_ref = bf16[16,2048]{1,0:T(8,128)(2,1)S(1)} reshape(bf16[1,4,4,2048]{3,2,1,0:T(4,128)(2,1)} %param.20) | data formatting | bytes 131072 | tf_op jit(solution)/shard_map/reshape | solution.py:451
  56.0 0.0 copy-done.11
  56.0 0.0 copy-done.9
  56.0 0.4 shard_map.146
  56.4 0.0 copy-done.6
  56.4 1.9 %shard_map.145 = bf16[256,2048]{1,0:T(8,128)(2,1)} custom-call(bf16[256,256]{1,0:T(8,128)(2,1)S(1)} %copy-done.4, f32[32,256]{1,0:T(8,128)S(1)} %get-tuple-element.42.cum_ref, bf16[9,128,256]{2,1,0:T(8,128)(2,1)S(1)} %get-tuple-element.73.carry_ref, f32[256,1024]{1,0:T(8,128)S(1)} %get-tuple-element.74.rest_0_, f32[256,1024]{1,0:T(8,128)S(1)} %copy-done.6), custom_call_target="tpu_custom_call" | custom-call | flops 134217728 | bytes 4194304 | tf_op jit(solution)/shard_map/pallas_call | solution.py:471
  58.3 0.0 collective-permute-done.12.rest_1_
  58.4 0.0 collective-permute-done.13.rest_2_
  58.4 0.4 collective-permute-done.14.rest_3_
  58.8 1.2 %shard_map.147 = bf16[4,4,2048]{2,1,0:T(4,128)(2,1)} custom-call(s32[4]{0:T(128)S(1)} %convert_element_type.3.held_ref, f32[4,4,2048]{2,1,0:T(4,128)S(1)} %get-tuple-element.76.keep_ref, f32[4,4,2048]{2,1,0:T(4,128)S(1)} %get-tuple-element.77.fresh_ref, f32[4,2048]{1,0:T(4,128)S(1)} %get-tuple-element.78.rest_0_, ...), custom_call_target="tpu_custom_call" | custom-call | flops 131072 | bytes 524288 | tf_op jit(solution)/shard_map/pallas_call | solution.py:483
  (22 shorter events, 0.3 us)
Async XLA Ops:
  0.6 0.7 %copy-start.7 = (bf16[256,32]{0,1:T(8,128)(2,1)S(1)}, bf16[256,32]{0,1:T(8,128)(2,1)}, u32[]{:S(2)}) copy-start(bf16[256,32]{0,1:T(8,128)(2,1)} %param.15) | copy-start | bytes 49156
  1.4 0.7 %copy-start.10 = (f32[32]{0:T(128)S(1)}, f32[32]{0:T(128)}, u32[]{:S(2)}) copy-start(f32[32]{0:T(128)} %param.16) | copy-start | bytes 388
  2.0 1.2 %copy-start = (bf16[256,2048]{1,0:T(8,128)(2,1)S(1)}, bf16[256,2048]{1,0:T(8,128)(2,1)}, u32[]{:S(2)}) copy-start(bf16[256,2048]{1,0:T(8,128)(2,1)} %x_ref.3) | copy-start | bytes 3145732
  3.2 0.9 %copy-start.2 = (bf16[256,256]{1,0:T(8,128)(2,1)S(1)}, bf16[256,256]{1,0:T(8,128)(2,1)}, u32[]{:S(2)}) copy-start(bf16[256,256]{1,0:T(8,128)(2,1)} %b_ref.3) | copy-start | bytes 393220
  8.6 7.9 %collective-permute-start = (bf16[144,256]{1,0:T(8,128)(2,1)S(1)}, bf16[144,256]{1,0:T(8,128)(2,1)S(1)}, u32[]{:S(2)}, u32[]{:S(2)}) collective-permute-start(bf16[144,256]{1,0:T(8,128)(2,1)S(1)} %get-tuple-element.44), channel_id=1, source_target_pairs={{0,4},{4,8},{8,12},{12,0},{1,5},{5,9},{9,13},{13,1},{2,6},{6,10},{... | collective-permute-start | bytes 221192 | tf_op jit(solution)/shard_map/ppermute | solution.py:416
  11.7 6.1 %collective-permute-start.2 = (bf16[128,256]{1,0:T(8,128)(2,1)S(1)}, bf16[128,256]{1,0:T(8,128)(2,1)S(1)}, u32[]{:S(2)}, u32[]{:S(2)}) collective-permute-start(bf16[128,256]{1,0:T(8,128)(2,1)S(1)} %get-tuple-element.48), channel_id=1, source_target_pairs={{0,4},{4,8},{8,12},{12,0},{1,5},{5,9},{9,13},{13,1},{2,6},{6,10},{... | collective-permute-start | bytes 196616 | tf_op jit(solution)/shard_map/ppermute | solution.py:416
  16.6 6.2 %collective-permute-start.1 = (bf16[144,256]{1,0:T(8,128)(2,1)S(1)}, bf16[144,256]{1,0:T(8,128)(2,1)S(1)}, u32[]{:S(2)}, u32[]{:S(2)}) collective-permute-start(bf16[144,256]{1,0:T(8,128)(2,1)S(1)} %get-tuple-element.47), channel_id=1, source_target_pairs={{0,4},{4,8},{8,12},{12,0},{1,5},{5,9},{9,13},{13,1},{2,6},{6,10},{... | collective-permute-start | bytes 221192 | tf_op jit(solution)/shard_map/ppermute | solution.py:416
  17.8 6.1 %collective-permute-start.4 = (bf16[128,256]{1,0:T(8,128)(2,1)S(1)}, bf16[128,256]{1,0:T(8,128)(2,1)S(1)}, u32[]{:S(2)}, u32[]{:S(2)}) collective-permute-start(bf16[128,256]{1,0:T(8,128)(2,1)S(1)} %get-tuple-element.53), channel_id=1, source_target_pairs={{0,4},{4,8},{8,12},{12,0},{1,5},{5,9},{9,13},{13,1},{2,6},{6,10},{... | collective-permute-start | bytes 196616 | tf_op jit(solution)/shard_map/ppermute | solution.py:416
  22.8 6.2 %collective-permute-start.3 = (bf16[144,256]{1,0:T(8,128)(2,1)S(1)}, bf16[144,256]{1,0:T(8,128)(2,1)S(1)}, u32[]{:S(2)}, u32[]{:S(2)}) collective-permute-start(bf16[144,256]{1,0:T(8,128)(2,1)S(1)} %get-tuple-element.51), channel_id=1, source_target_pairs={{0,4},{4,8},{8,12},{12,0},{1,5},{5,9},{9,13},{13,1},{2,6},{6,10},{... | collective-permute-start | bytes 221192 | tf_op jit(solution)/shard_map/ppermute | solution.py:416
  23.9 0.7 %copy-start.12 = (s32[8]{0:T(128)S(1)}, s32[8]{0:T(128)}, u32[]{:S(2)}) copy-start(s32[8]{0:T(128)} %param.19) | copy-start | bytes 100
  23.9 0.7 %copy-start.13 = (s32[8]{0:T(128)S(1)}, s32[8]{0:T(128)}, u32[]{:S(2)}) copy-start(s32[8]{0:T(128)} %param.18) | copy-start | bytes 100
  23.9 6.5 %collective-permute-start.5 = (bf16[128,256]{1,0:T(8,128)(2,1)S(1)}, bf16[128,256]{1,0:T(8,128)(2,1)S(1)}, u32[]{:S(2)}, u32[]{:S(2)}) collective-permute-start(bf16[128,256]{1,0:T(8,128)(2,1)S(1)} %get-tuple-element.55), channel_id=1, source_target_pairs={{0,4},{4,8},{8,12},{12,0},{1,5},{5,9},{9,13},{13,1},{2,6},{6,10},{... | collective-permute-start | bytes 196616 | tf_op jit(solution)/shard_map/ppermute | solution.py:416
  29.1 6.3 %collective-permute-start.7 = (bf16[128,256]{1,0:T(8,128)(2,1)S(1)}, bf16[128,256]{1,0:T(8,128)(2,1)S(1)}, u32[]{:S(2)}, u32[]{:S(2)}) collective-permute-start(bf16[128,256]{1,0:T(8,128)(2,1)S(1)} %get-tuple-element.59), channel_id=1, source_target_pairs={{0,4},{4,8},{8,12},{12,0},{1,5},{5,9},{9,13},{13,1},{2,6},{6,10},{... | collective-permute-start | bytes 196616 | tf_op jit(solution)/shard_map/ppermute | solution.py:416
  30.5 6.6 %collective-permute-start.6 = (bf16[128,256]{1,0:T(8,128)(2,1)S(1)}, bf16[128,256]{1,0:T(8,128)(2,1)S(1)}, u32[]{:S(2)}, u32[]{:S(2)}) collective-permute-start(bf16[128,256]{1,0:T(8,128)(2,1)S(1)} %get-tuple-element.58), channel_id=1, source_target_pairs={{0,4},{4,8},{8,12},{12,0},{1,5},{5,9},{9,13},{13,1},{2,6},{6,10},{... | collective-permute-start | bytes 196616 | tf_op jit(solution)/shard_map/ppermute | solution.py:416
  35.4 6.1 %collective-permute-start.9 = (bf16[128,256]{1,0:T(8,128)(2,1)S(1)}, bf16[128,256]{1,0:T(8,128)(2,1)S(1)}, u32[]{:S(2)}, u32[]{:S(2)}) collective-permute-start(bf16[128,256]{1,0:T(8,128)(2,1)S(1)} %get-tuple-element.63), channel_id=1, source_target_pairs={{0,4},{4,8},{8,12},{12,0},{1,5},{5,9},{9,13},{13,1},{2,6},{6,10},{... | collective-permute-start | bytes 196616 | tf_op jit(solution)/shard_map/ppermute | solution.py:416
  37.1 6.7 %collective-permute-start.8 = (bf16[128,256]{1,0:T(8,128)(2,1)S(1)}, bf16[128,256]{1,0:T(8,128)(2,1)S(1)}, u32[]{:S(2)}, u32[]{:S(2)}) collective-permute-start(bf16[128,256]{1,0:T(8,128)(2,1)S(1)} %get-tuple-element.62), channel_id=1, source_target_pairs={{0,4},{4,8},{8,12},{12,0},{1,5},{5,9},{9,13},{13,1},{2,6},{6,10},{... | collective-permute-start | bytes 196616 | tf_op jit(solution)/shard_map/ppermute | solution.py:416
  41.5 2.7 %copy-start.1 = (bf16[256,2048]{1,0:T(8,128)(2,1)S(1)}, bf16[256,2048]{1,0:T(8,128)(2,1)}, u32[]{:S(2)}) copy-start(bf16[256,2048]{1,0:T(8,128)(2,1)} %x_ref.3) | copy-start | bytes 3145732
  43.7 0.9 %copy-start.3 = (bf16[256,256]{1,0:T(8,128)(2,1)S(1)}, bf16[256,256]{1,0:T(8,128)(2,1)}, u32[]{:S(2)}) copy-start(bf16[256,256]{1,0:T(8,128)(2,1)} %b_ref.3) | copy-start | bytes 393220
  43.7 1.0 %copy-start.4 = (bf16[256,256]{1,0:T(8,128)(2,1)S(1)}, bf16[256,256]{1,0:T(8,128)(2,1)}, u32[]{:S(2)}) copy-start(bf16[256,256]{1,0:T(8,128)(2,1)} %c_ref.5) | copy-start | bytes 393220
  43.8 6.1 %collective-permute-start.11 = (bf16[128,256]{1,0:T(8,128)(2,1)S(1)}, bf16[128,256]{1,0:T(8,128)(2,1)S(1)}, u32[]{:S(2)}, u32[]{:S(2)}) collective-permute-start(bf16[128,256]{1,0:T(8,128)(2,1)S(1)} %get-tuple-element.72), channel_id=1, source_target_pairs={{0,4},{4,8},{8,12},{12,0},{1,5},{5,9},{9,13},{13,1},{2,6},{6,10},{... | collective-permute-start | bytes 196616 | tf_op jit(solution)/shard_map/ppermute | solution.py:416
  43.8 7.1 %collective-permute-start.10 = (bf16[128,256]{1,0:T(8,128)(2,1)S(1)}, bf16[128,256]{1,0:T(8,128)(2,1)S(1)}, u32[]{:S(2)}, u32[]{:S(2)}) collective-permute-start(bf16[128,256]{1,0:T(8,128)(2,1)S(1)} %get-tuple-element.71), channel_id=1, source_target_pairs={{0,4},{4,8},{8,12},{12,0},{1,5},{5,9},{9,13},{13,1},{2,6},{6,10},{... | collective-permute-start | bytes 196616 | tf_op jit(solution)/shard_map/ppermute | solution.py:416
  44.3 0.7 %copy-start.8 = (f32[32]{0:T(128)S(1)}, f32[32]{0:T(128)}, u32[]{:S(2)}) copy-start(f32[32]{0:T(128)} %param.17) | copy-start | bytes 388
  46.2 9.8 %copy-start.11 = (bf16[1,4,4,256]{3,2,1,0:T(4,128)(2,1)S(1)}, bf16[1,4,4,256]{3,2,1,0:T(4,128)(2,1)}, u32[]{:S(2)}) copy-start(bf16[1,4,4,256]{3,2,1,0:T(4,128)(2,1)} %param.21) | copy-start | bytes 24580
  46.2 9.8 %copy-start.9 = (bf16[1,4,4,32]{3,2,1,0:T(4,128)(2,1)S(1)}, bf16[1,4,4,32]{3,2,1,0:T(4,128)(2,1)}, u32[]{:S(2)}) copy-start(bf16[1,4,4,32]{3,2,1,0:T(4,128)(2,1)} %param.23) | copy-start | bytes 3076
  47.4 1.0 %copy-start.5 = (f32[256,1024]{1,0:T(8,128)}, f32[256,1024]{1,0:T(8,128)S(1)}, u32[]{:S(2)}) copy-start(f32[256,1024]{1,0:T(8,128)S(1)} %get-tuple-element.75.rest_1_) | copy-start | bytes 3145732
  49.9 6.5 %copy-start.6 = (f32[256,1024]{1,0:T(8,128)S(1)}, f32[256,1024]{1,0:T(8,128)}, u32[]{:S(2)}) copy-start(f32[256,1024]{1,0:T(8,128)} %copy-done.5) | copy-start | bytes 3145732
  51.2 7.1 %collective-permute-start.12 = (f32[4,2048]{1,0:T(4,128)S(1)}, f32[4,2048]{1,0:T(4,128)S(1)}, u32[]{:S(2)}, u32[]{:S(2)}) collective-permute-start(f32[4,2048]{1,0:T(4,128)S(1)} %get-tuple-element.79), channel_id=1, source_target_pairs={{0,12},{4,0},{8,4},{12,8},{1,13},{5,1},{9,5},{13,9},{2,14},{6,2},{... | collective-permute-start | bytes 98312 | tf_op jit(solution)/shard_map/ppermute | solution.py:469
  52.5 5.9 %collective-permute-start.13 = (f32[4,2048]{1,0:T(4,128)S(1)}, f32[4,2048]{1,0:T(4,128)S(1)}, u32[]{:S(2)}, u32[]{:S(2)}) collective-permute-start(f32[4,2048]{1,0:T(4,128)S(1)} %get-tuple-element.80), channel_id=1, source_target_pairs={{0,8},{4,12},{8,0},{12,4},{1,9},{5,13},{9,1},{13,5},{2,10},{6,14},... | collective-permute-start | bytes 98312 | tf_op jit(solution)/shard_map/ppermute | solution.py:469
  53.0 5.7 %collective-permute-start.14 = (f32[4,2048]{1,0:T(4,128)S(1)}, f32[4,2048]{1,0:T(4,128)S(1)}, u32[]{:S(2)}, u32[]{:S(2)}) collective-permute-start(f32[4,2048]{1,0:T(4,128)S(1)} %get-tuple-element.81), channel_id=1, source_target_pairs={{0,4},{4,8},{8,12},{12,0},{1,5},{5,9},{9,13},{13,1},{2,6},{6,10},{... | collective-permute-start | bytes 98312 | tf_op jit(solution)/shard_map/ppermute | solution.py:469

commit v3 on v2

v3 whole, which is shorter than its diff:
```python
import functools
import math

import jax
import jax.numpy as jnp
from jax import lax
from jax.experimental import pallas as pl
from jax.experimental.pallas import tpu as pltpu
from jax.sharding import PartitionSpec as P

H = 128
P_SIZE = 64
N = 128
G = 8
SPAN = 128
STEPS = 4
LOG2E = math.log2(math.e)
F32 = jnp.float32
BF16 = jnp.bfloat16
CHUNKS = 4
VMEM_LIMIT = 32 * 1024 * 1024


def softplus(value):
    small = jnp.exp(-jnp.abs(value))
    series = small * (1.0 - small * (0.5 - small * (1.0 / 3.0 - small * 0.25)))
    return jnp.maximum(value, 0.0) + jnp.where(small < 0.02, series, jnp.log(1.0 + small))


def dot(left, right, left_dim=1, right_dim=0):
    return lax.dot_general(
        left, right, (((left_dim,), (right_dim,)), ((), ())), preferred_element_type=F32
    )


def split(value, pieces):
    result = []
    for _ in range(pieces):
        piece = value.astype(BF16)
        result.append(piece)
        value = value - piece.astype(F32)
    return result


def exact_dot(ones, value, pieces=3, left_dim=1):
    return sum(dot(ones, piece, left_dim) for piece in split(value, pieces))


def spread_matrix(heads, first, width):
    lane = lax.broadcasted_iota(jnp.int32, (heads, width), 1) + first
    head = lax.broadcasted_iota(jnp.int32, (heads, width), 0)
    return jnp.where(lane // P_SIZE == head, 1.0, 0.0).astype(BF16)


def over_lanes(value, first, width, pieces=2):
    return exact_dot_right(value, spread_matrix(value.shape[1], first, width), pieces)


def exact_dot_right(value, ones, pieces):
    return sum(dot(piece, ones) for piece in split(value, pieces))


def shape(dims, dtype=F32):
    return jax.ShapeDtypeStruct(dims, dtype)


def call(kernel, out_shape, flops, moved, **options):
    return pl.pallas_call(
        kernel,
        out_shape=out_shape,
        compiler_params=pltpu.CompilerParams(vmem_limit_bytes=VMEM_LIMIT),
        cost_estimate=pl.CostEstimate(flops=flops, bytes_accessed=moved, transcendentals=0),
        **options,
    )


def triangle(keep):
    row = lax.broadcasted_iota(jnp.int32, (SPAN, SPAN), 0)
    column = lax.broadcasted_iota(jnp.int32, (SPAN, SPAN), 1)
    return jnp.where(keep(row, column), 1.0, 0.0).astype(BF16)


def state_kernel(
    x_hbm, b_hbm, dt_hbm, a_hbm, total_ref, sent_ref, decay_ref, cum_ref, row_ref,
    x_ref, b_ref, dt_ref, a_ref, sems,
):
    heads, tokens = dt_ref.shape
    spans = tokens // SPAN
    chunks, _, width = total_ref.shape
    per_group = H // G
    groups = heads // per_group
    group_lanes = per_group * P_SIZE
    copies = [
        pltpu.make_async_copy(dt_hbm, dt_ref, sems.at[0]),
        pltpu.make_async_copy(a_hbm, a_ref, sems.at[1]),
        pltpu.make_async_copy(b_hbm, b_ref, sems.at[2]),
    ]
    for g in range(groups):
        lanes = slice(g * group_lanes, (g + 1) * group_lanes)
        copies.append(
            pltpu.make_async_copy(x_hbm.at[:, lanes], x_ref.at[:, lanes], sems.at[3 + g])
        )
    for copy in copies:
        copy.start()
    upper = triangle(lambda s, t: s <= t)
    eye = lax.broadcasted_iota(jnp.int32, (heads, heads), 0) == lax.broadcasted_iota(
        jnp.int32, (heads, heads), 1
    )
    copies[0].wait()
    copies[1].wait()
    a_column = jnp.sum(jnp.where(eye, a_ref[...], 0.0), axis=1, keepdims=True)
    step = softplus(dt_ref[...].astype(F32))
    rate = step * (jnp.exp(a_column) * -LOG2E)
    cums = [exact_dot_right(rate[:, i * SPAN : (i + 1) * SPAN], upper, 3) for i in range(spans)]
    ends = [cum[:, SPAN - 1 : SPAN] for cum in cums]
    after = jnp.zeros_like(ends[0])
    weights = [None] * spans
    for i in reversed(range(spans)):
        after = after + ends[i]
        weights[i] = jnp.exp2(after - cums[i]) * step[:, i * SPAN : (i + 1) * SPAN]
    weight = jnp.concatenate(weights, axis=1).T
    whole = jnp.sum(jnp.where(eye, jnp.exp2(after), 0.0), axis=0, keepdims=True)
    cum = jnp.concatenate(cums, axis=1)
    cum_ref[...] = cum
    row_ref[...] = jnp.log2(step) - cum
    copies[2].wait()
    for g in range(groups):
        turned = b_ref[:, g * N : (g + 1) * N].astype(F32).T.astype(BF16)
        copies[3 + g].wait()
        for k in range(chunks):
            first = k * width
            if first // group_lanes != g:
                continue
            lanes = slice(first, first + width)
            scaled = (x_ref[:, lanes].astype(F32) * over_lanes(weight, first, width)).astype(BF16)
            total = dot(turned, scaled)
            total_ref[k] = total
            sent_ref[k] = total.astype(BF16)
            decay_ref[k] = over_lanes(whole, first, width, 3)


def pass_kernel(hop, k, got_ref, total_ref, decay_ref, *rest):
    moving_ref, carry_ref = rest[-2:]
    first = hop == 1 and k == 0
    if first:
        carry_ref[...] = jnp.zeros_like(carry_ref)
    got = got_ref[...]
    moving_ref[...] = (total_ref[...] + decay_ref[...] * got.astype(F32)).astype(BF16)

    @pl.when(lax.axis_index("seq") == hop)
    def _():
        carry_ref[k] = got


def pair_halves(x_part):
    first_half = lax.broadcasted_iota(jnp.int32, (1, 2 * P_SIZE), 1) < P_SIZE
    zero = jnp.zeros_like(x_part)
    return jnp.where(first_half, x_part, zero), jnp.where(first_half, zero, x_part)


def span_starts(cum, spans):
    ends = [cum[(i + 1) * SPAN - 1 : (i + 1) * SPAN, :] for i in range(spans)]
    starts = [jnp.zeros_like(ends[0])]
    for i in range(spans):
        starts.append(starts[i] + ends[i])
    return ends, starts


def inner_kernel(g, x_ref, b_ref, c_ref, cum_ref, row_ref, d_ref, *rest):
    inner_ref = rest[-1]
    heads, tokens = cum_ref.shape
    spans = tokens // SPAN
    per_group = H // G
    names = slice(g * N, (g + 1) * N)
    t_index = lax.broadcasted_iota(jnp.int32, (SPAN, SPAN), 0)
    s_index = lax.broadcasted_iota(jnp.int32, (SPAN, SPAN), 1)
    causal = t_index >= s_index
    rows = row_ref[...]
    cum = cum_ref[...].T
    ends, _ = span_starts(cum, spans)
    first_half = lax.broadcasted_iota(jnp.int32, (1, 2 * P_SIZE), 1) < P_SIZE
    scores = dot(c_ref[:, names], b_ref[:, names], 1, 1)
    for pair in range(per_group // 2):
        h0 = g * per_group + 2 * pair
        lanes = slice(h0 * P_SIZE, (h0 + 2) * P_SIZE)
        here = slice(2 * pair * P_SIZE, (2 * pair + 2) * P_SIZE)
        x_part = x_ref[:, lanes]
        halves = pair_halves(x_part)
        weights = [[None, None] for _ in range(spans)]
        for e in range(2):
            h = h0 + e
            row = rows[h : h + 1, :]
            for i in range(spans):
                column = jnp.broadcast_to(cum[i * SPAN : (i + 1) * SPAN, h : h + 1], (SPAN, SPAN))
                parts = []
                for j in range(i + 1):
                    shift = row[:, j * SPAN : (j + 1) * SPAN]
                    for m in range(j, i):
                        shift = shift + ends[m][:, h : h + 1]
                    score = scores[i * SPAN : (i + 1) * SPAN, j * SPAN : (j + 1) * SPAN]
                    part = score * jnp.exp2(column + shift)
                    if i == j:
                        part = jnp.where(causal, part, 0.0)
                    parts.append(part.astype(BF16))
                weights[i][e] = jnp.concatenate(parts, axis=1) if i else parts[0]
        skip = jnp.where(first_half, d_ref[:, h0 : h0 + 1], d_ref[:, h0 + 1 : h0 + 2])
        for i in range(spans):
            reach = (i + 1) * SPAN
            left = jnp.concatenate(weights[i], axis=1)
            right = jnp.concatenate([half[:reach] for half in halves], axis=0)
            mine = slice(i * SPAN, (i + 1) * SPAN)
            inner_ref[mine, here] = dot(left, right) + skip * x_part[mine].astype(F32)


def ask_kernel(count, x_ref, b_ref, cum_ref, row_ref, spot_ref, *rest):
    ask_refs = rest[:count]
    local_ref, gain_ref, asked_ref = rest[-3:]
    heads, tokens = cum_ref.shape
    spans = tokens // SPAN
    asks = local_ref.shape[0]
    per_group = H // G
    groups = heads // per_group
    me = lax.axis_index("seq")
    asked = jnp.concatenate([ref[me].astype(F32) for ref in ask_refs], axis=0).astype(BF16)
    asked_ref[...] = asked
    spot = spot_ref[...]
    position = lax.broadcasted_iota(jnp.int32, (asks, tokens), 1)
    picked = jnp.where(position == spot, 1.0, 0.0).astype(BF16)
    upto = position <= spot
    rows = row_ref[...]
    cum = cum_ref[...].T
    ends, starts = span_starts(cum, spans)
    near_ask = exact_dot(picked, cum)
    ask_start = starts[0]
    for i in range(1, spans):
        ask_start = jnp.where(spot >= i * SPAN, starts[i], ask_start)
    gain_ref[...] = near_ask + ask_start
    columns = []
    for j in range(spans):
        column = near_ask
        for i in range(j + 1, spans):
            column = jnp.where(spot // SPAN == i, near_ask + sum(ends[j + 1 : i], ends[j]), column)
        columns.append(column)
    for g in range(groups):
        names = slice(g * N, (g + 1) * N)
        scores = jnp.where(upto, dot(asked[:, names], b_ref[:, names], 1, 1), 0.0)
        for pair in range(per_group // 2):
            h0 = g * per_group + 2 * pair
            lanes = slice(h0 * P_SIZE, (h0 + 2) * P_SIZE)
            parts = []
            for h in (h0, h0 + 1):
                for j in range(spans):
                    span = slice(j * SPAN, (j + 1) * SPAN)
                    part = scores[:, span] * jnp.exp2(columns[j][:, h : h + 1] + rows[h : h + 1, span])
                    parts.append(jnp.where(upto[:, span], part, 0.0).astype(BF16))
            right = jnp.concatenate(pair_halves(x_ref[:, lanes]), axis=0)
            local_ref[:, lanes] = dot(jnp.concatenate(parts, axis=1), right)


def read_kernel(chunks, gain_ref, asked_ref, local_ref, carry_ref, *rest):
    got_refs, read_refs = rest[: len(chunks)], rest[len(chunks) :]
    width = got_refs[0].shape[1]
    count = len(read_refs)
    last = lax.axis_index("seq") == count - 1
    gain = jnp.exp2(gain_ref[...])
    for i, k in enumerate(chunks):
        first = k * width
        g = first // (H // G * P_SIZE)
        state = jnp.where(last, got_refs[i][...], carry_ref[k])
        carried = dot(asked_ref[:, g * N : (g + 1) * N], state)
        reading = local_ref[:, first : first + width] + over_lanes(gain, first, width) * carried
        here = slice(i * width, (i + 1) * width)
        for r in range(count):
            read_refs[r][:, here] = reading[r * STEPS : (r + 1) * STEPS]


def outer_kernel(chunks, count, c_ref, cum_ref, carry_ref, *rest):
    got_refs = rest[: len(chunks)]
    inner_refs = rest[len(chunks) : -3]
    out_hbm, out_ref, sems = rest[-3:]
    heads, tokens = cum_ref.shape
    spans = tokens // SPAN
    width = got_refs[0].shape[1]
    group_lanes = H // G * P_SIZE
    last = lax.axis_index("seq") == count - 1
    start = jnp.zeros((heads, 1), F32)
    gains = []
    for i in range(spans):
        cum = cum_ref[:, i * SPAN : (i + 1) * SPAN]
        gains.append(jnp.exp2(cum + start))
        start = start + cum[:, SPAN - 1 : SPAN]
    gain = jnp.concatenate(gains, axis=1).T
    copies = []
    for i, k in enumerate(chunks):
        first = k * width
        g = first // group_lanes
        state = jnp.where(last, got_refs[i][...], carry_ref[k])
        carried = dot(c_ref[:, g * N : (g + 1) * N], state)
        inner = inner_refs[g][:, first - g * group_lanes : first - g * group_lanes + width]
        out_ref[i] = (inner + over_lanes(gain, first, width) * carried).astype(BF16)
        copies.append(
            pltpu.make_async_copy(out_ref.at[i], out_hbm.at[:, first : first + width], sems.at[i])
        )
        copies[i].start()
    for copy in copies:
        copy.wait()


def fresh_kernel(x_ref, b_ref, c_ref, dt_ref, a_ref, d_ref, *rest):
    keep_ref, fresh_ref = rest[-2:]
    count, _, heads = dt_ref.shape
    rows = count * STEPS
    per_group = H // G
    groups = heads // per_group
    width = x_ref.shape[2]

    def flat(ref):
        return jnp.concatenate([ref[i].astype(F32) for i in range(count)], axis=0)

    turn = lax.broadcasted_iota(jnp.int32, (rows, 1), 0) % STEPS
    step = softplus(flat(dt_ref))
    rate = step * (jnp.exp(a_ref[...]) * -LOG2E)

    def earlier(value, gap):
        if not gap:
            return value
        moved = jnp.concatenate([jnp.zeros_like(value[:gap]), value[:-gap]], axis=0)
        return jnp.where(turn >= gap, moved, 0.0)

    running = sum(earlier(rate, gap) for gap in range(STEPS))
    keep = over_lanes(jnp.exp2(running), 0, width)
    x_values = flat(x_ref)
    b_values = flat(b_ref)
    c_values = flat(c_ref)
    head = lax.broadcasted_iota(jnp.int32, (rows, heads), 1)
    fresh = over_lanes(d_ref[...], 0, width, 3) * x_values
    since = jnp.zeros_like(rate)
    for gap in range(STEPS):
        if gap:
            since = since + earlier(rate, gap - 1)
        products = c_values * earlier(b_values, gap)
        pair = jnp.zeros((rows, heads), F32)
        for g in range(groups):
            score = jnp.sum(products[:, g * N : (g + 1) * N], axis=1, keepdims=True)
            pair = jnp.where(head // per_group == g, score, pair)
        factor = jnp.where(turn >= gap, jnp.exp2(since) * earlier(step, gap) * pair, 0.0)
        fresh = fresh + over_lanes(factor, 0, width) * earlier(x_values, gap)
    for i in range(rows // STEPS):
        keep_ref[i] = keep[i * STEPS : (i + 1) * STEPS]
        fresh_ref[i] = fresh[i * STEPS : (i + 1) * STEPS]


def finish_kernel(held_ref, keep_ref, fresh_ref, *rest):
    back_refs, out_ref = rest[:-1], rest[-1]
    count = len(back_refs)
    me = lax.axis_index("seq")
    for r in range(count):
        source = lax.rem(me + r, count)
        value = back_refs[r][...] * keep_ref[source] + fresh_ref[source]
        out_ref[source] = jnp.where(held_ref[source] > 0, value, 0.0).astype(BF16)


def shards(
    ssm_input, bmat, cmat, dt_raw, a_log, d_skip, prompt_len, owner, dec_x, dec_b, dec_c, dec_dt
):
    count = lax.axis_size("seq")
    me = lax.axis_index("seq")
    tokens, heads = dt_raw.shape
    groups = heads // (H // G)
    names = groups * N
    lanes = heads * P_SIZE
    group_lanes = lanes // groups
    rows = count * STEPS
    chunks = CHUNKS if count <= 4 else groups
    width = lanes // chunks
    a_row = a_log.reshape(1, heads)
    d_row = d_skip.reshape(1, heads)
    anywhere = pl.BlockSpec(memory_space=pl.ANY)
    in_hbm = pl.BlockSpec(memory_space=pltpu.HBM)
    in_vmem = pl.BlockSpec(memory_space=pltpu.VMEM)

    total, sent, decay, cum, row = call(
        state_kernel,
        (
            shape((chunks, N, width)),
            shape((chunks, N, width), BF16),
            shape((chunks, 1, width)),
            shape((heads, tokens)),
            shape((heads, tokens)),
        ),
        2 * tokens * N * lanes,
        4 * tokens * lanes,
        in_specs=[in_hbm] * 4,
        scratch_shapes=[
            pltpu.VMEM((tokens, lanes), BF16),
            pltpu.VMEM((tokens, names), BF16),
            pltpu.VMEM((heads, tokens), BF16),
            pltpu.VMEM((1, heads), F32),
            pltpu.SemaphoreType.DMA((3 + groups,)),
        ],
    )(ssm_input, bmat, dt_raw.T, a_row)

    def swap(value, hop):
        pairs = {hop - 1: hop, hop: hop - 1}
        return lax.ppermute(value, "seq", [(d, pairs.get(d, d)) for d in range(count)])

    def shift(value, by):
        return lax.ppermute(value, "seq", [(d, (d + by) % count) for d in range(count)])

    got = {(1, k): swap(sent[k], 1) for k in range(chunks)}
    asks = [dec_c[0]] + [shift(dec_c[0], r) for r in range(1, count)]

    last_token = prompt_len - 1
    sources = last_token // tokens
    indices = jnp.arange(count, dtype=jnp.int32)
    owners = (me - indices) % count
    mine = (sources == me)[None, :] & (owner[None, :] == owners[:, None])
    offsets = jnp.sum(jnp.where(mine, last_token[None, :] - me * tokens, 0), axis=1)
    spot = jnp.repeat(offsets, STEPS).reshape(rows, 1).astype(jnp.int32)
    held = jnp.any((owner == me)[None, :] & (sources[None, :] == indices[:, None]), axis=1)

    def inner_part(g, *after):
        return call(
            functools.partial(inner_kernel, g),
            shape((tokens, group_lanes)),
            2 * tokens * tokens * group_lanes,
            16 * tokens * group_lanes,
            in_specs=[in_vmem] * 6 + [anywhere] * len(after),
        )(ssm_input, bmat, cmat, cum, row, d_row, *after)

    def ask_part(*after):
        return call(
            functools.partial(ask_kernel, count),
            (shape((rows, lanes)), shape((rows, heads)), shape((rows, names), BF16)),
            2 * rows * tokens * lanes,
            4 * tokens * lanes,
            in_specs=[in_vmem] * (5 + count) + [anywhere] * len(after),
        )(ssm_input, bmat, cum, row, spot, *asks, *after)

    def fresh_part(*after):
        return call(
            fresh_kernel,
            (shape((count, STEPS, lanes)), shape((count, STEPS, lanes))),
            64 * rows * lanes,
            16 * rows * lanes,
            in_specs=[in_vmem] * 6 + [anywhere] * len(after),
        )(dec_x[0], dec_b[0], dec_c[0], dec_dt[0], a_row, d_row, *after)

    order = sorted(
        (k + hop, hop, k) for hop in range(1, count - 1) for k in range(chunks)
    )
    work = [functools.partial(inner_part, g) for g in range(groups)] + [ask_part, fresh_part]
    results = [work[0]()]
    carry = None
    tie = None
    for place, (_, hop, k) in enumerate(order):
        if 0 < place < len(work):
            results.append(work[place](tie))
        after = jax.tree.leaves(results[place])[:1] if place < len(results) else []
        held_before = [] if carry is None else [carry]
        moving, carry = call(
            functools.partial(pass_kernel, hop, k),
            (shape((N, width), BF16), shape((chunks, N, width), BF16)),
            2 * N * width,
            8 * N * width,
            in_specs=[in_vmem] * (3 + len(held_before)) + [anywhere] * len(after),
            input_output_aliases={3: 1} if held_before else {},
        )(got[hop, k], total[k], decay[k], *held_before, *after)
        got[hop + 1, k] = swap(moving, hop + 1)
        tie = moving
    *inner, (local, gain, asked), (keep, fresh) = results
    arrived = [got[count - 1, k] for k in range(chunks)]

    all_chunks = tuple(range(chunks))
    reading = call(
        functools.partial(read_kernel, all_chunks),
        (shape((STEPS, lanes)),) * count,
        2 * rows * N * lanes,
        4 * N * lanes,
    )(gain, asked, local, carry, *arrived)
    back = [reading[0]] + [None] * (count - 1)
    for r in reversed(range(1, count)):
        back[r] = shift(reading[r], -r)

    prefill = call(
        functools.partial(outer_kernel, all_chunks, count),
        shape((tokens, lanes), BF16),
        2 * tokens * N * lanes,
        8 * tokens * lanes,
        out_specs=in_hbm,
        scratch_shapes=[
            pltpu.VMEM((chunks, tokens, width), BF16),
            pltpu.SemaphoreType.DMA((chunks,)),
        ],
    )(cmat, cum, carry, *arrived, *inner)

    decoded = call(
        finish_kernel,
        shape((count, STEPS, lanes), BF16),
        4 * rows * lanes,
        16 * rows * lanes,
        in_specs=[pl.BlockSpec(memory_space=pltpu.SMEM)] + [in_vmem] * (2 + count),
    )(held.astype(jnp.int32), keep, fresh, *back)
    return (prefill, decoded[None])


def solution(mesh):
    placed = (
        P(("grp", "seq"), "tp"),
        P(("grp", "seq"), "tp"),
        P(("grp", "seq"), "tp"),
        P(("grp", "seq"), "tp"),
        P("tp"),
        P("tp"),
        P("grp"),
        P("grp"),
        P(("grp", "seq"), None, None, "tp"),
        P(("grp", "seq"), None, None, "tp"),
        P(("grp", "seq"), None, None, "tp"),
        P(("grp", "seq"), None, None, "tp"),
    )
    return jax.shard_map(
        shards,
        mesh=mesh,
        in_specs=placed,
        out_specs=(P(("grp", "seq"), "tp"), P(("grp", "seq"), None, None, "tp")),
        check_vma=False,
    )
```

time: 60.3 us -> 86.4 us (1.43)
  starting transfers between devices: 9.72 us -> 48.7 us
  waiting for transfers between devices: 31.3 us -> 3.62 us
  local copies, waits for them, and re-layouts: 6.79 us -> 15 us
  Pallas kernels: 11 us -> 15.9 us
    ppermute x15 -> x18, starting transfers between devices: 9.72 us -> 48.7 us  [the longest x6 28.6 us: shift(): lax.ppermute(value, 'seq', [(d, (d + by) % count) for d in range(count)])]
    ppermute x15 -> x18, waiting for transfers between devices: 31.3 us -> 3.62 us  [the longest x6 3.58 us: shift(): lax.ppermute(value, 'seq', [(d, (d + by) % count) for d in range(count)])]
    unnamed x28 -> x82, local copies, waits for them, and re-layouts: 5.06 us -> 11.4 us
    pallas_call x16 -> x15, Pallas kernels: 9.74 us -> 14.7 us  [the longest x8 6.16 us: shards(): call(functools.partial(pass_kernel, hop, k), (shape((N, width), BF16), sh...]
    squeeze x0 -> x3, local copies, waits for them, and re-layouts: none -> 2.21 us  [the longest x1 0.83 us: shards(): got = {(1, k): swap(sent[k], 1) for k in range(chunks)}]
    reshape x3 -> x0, local copies, waits for them, and re-layouts: 1.58 us -> none  [the longest x1 0.86 us: shards(): dec_x.reshape(rows, lanes)]
  transfers between devices with their start and end apart: 15 -> 18, of which waited for: 13 -> 3; matrix products, arithmetic and copies ran while one was open for 2% -> 5% of each run, Pallas kernels for 8% -> 17%
where the time goes in v3:
time: 86.4 us; the launch traced here: 85.3 us
  starting transfers between devices  48.7 us (56%)
  Pallas kernels  15.9 us (18%)
  local copies, waits for them, and re-layouts  15 us (17%)
  waiting for transfers between devices  3.62 us (4%)
  between operations  1.18 us (1%)
  other arithmetic  0.9 us (1%)
    ppermute x6, starting transfers between devices, shift(): lax.ppermute(value, 'seq', [(d, (d + by) % count) for d in range(count)])  28.6 us
    ppermute x12, starting transfers between devices, swap(): lax.ppermute(value, 'seq', [(d, pairs.get(d, d)) for d in range(count)])  20.1 us
    unnamed x82, local copies, waits for them, and re-layouts  11.4 us
    pallas_call x8, Pallas kernels, shards(): call(functools.partial(pass_kernel, hop, k), (shape((N, width), BF16), sh...  6.16 us
    ppermute x6, waiting for transfers between devices, shift(): lax.ppermute(value, 'seq', [(d, (d + by) % count) for d in range(count)])  3.58 us
    pallas_call x1, Pallas kernels, shards(): call(state_kernel, (shape((chunks, N, width)), shape((chunks, N, width),...  2.44 us
    pallas_call x2, Pallas kernels, inner_part(): call(functools.partial(inner_kernel, g), shape((tokens, group_lanes)), 2...  2.03 us
    pallas_call x1, Pallas kernels, shards(): call(functools.partial(outer_kernel, all_chunks, count), shape((tokens, l...  1.76 us
  transfers between devices with their start and end apart: 18, of which 3 were waited for; matrix products, arithmetic and copies ran while one was open for 5% of the time, Pallas kernels for 17%

profile of v3, /device:TPU:0, one launch (start us, length us, event | category | flops | bytes accessed | tf_op | source)
XLA Modules:
  0.0 85.3 jit_solution(15017018508642813883)
XLA Ops:
  0.6 5.1 %collective-permute-start.8 = (bf16[4,4,256]{2,1,0:T(4,128)(2,1)}, bf16[4,4,256]{2,1,0:T(4,128)(2,1)}, u32[]{:S(2)}, u32[]{:S(2)}) collective-permute-start(bf16[4,4,256]{2,1,0:T(4,128)(2,1)} %bitcast.33), channel_id=1, source_target_pairs={{0,12},{4,0},{8,4},{12,8},{1,13},{5,1},{9,5},{13,9},{2,14},{6,2},{... | collective-permute-start | bytes 24584 | tf_op jit(solution)/shard_map/ppermute | solution.py:408
  5.7 0.7 copy-done.34
  6.4 1.2 %copy-done = bf16[256,2048]{1,0:T(8,128)(2,1)S(1)} copy-done((bf16[256,2048]{1,0:T(8,128)(2,1)S(1)}, bf16[256,2048]{1,0:T(8,128)(2,1)}, u32[]{:S(2)}) %copy-start) | copy-done | bytes 1048600
  7.6 0.9 %copy-done.6 = bf16[256,256]{1,0:T(8,128)(2,1)S(1)} copy-done((bf16[256,256]{1,0:T(8,128)(2,1)S(1)}, bf16[256,256]{1,0:T(8,128)(2,1)}, u32[]{:S(2)}) %copy-start.6) | copy-done | bytes 131096
  8.5 0.7 copy-done.29
  9.2 2.4 %shard_map.131 = (f32[4,128,512]{2,1,0:T(8,128)S(1)}, bf16[4,128,512]{2,1,0:T(8,128)(2,1)S(1)}, f32[4,1,512]{2,1,0:T(1,128)S(1)}, f32[32,256]{1,0:T(8,128)S(1)}, f32[32,256]{1,0:T(8,128)S(1)}) custom-call(bf16[256,2048]{1,0:T(8,128)(2,1)S(1)} %copy-done, bf16[256,256]{1,0:T(8,128)(2,1)S(1)} %copy-done.6, bf16[32,256]{1,0:T(8,128)(2,1)S(1)} %bitcast.38, ...), custom_call_target="tpu_custom_call" | custom-call | flops 134217728 | bytes 2097152 | tf_op jit(solution)/shard_map/pallas_call | solution.py:382
  11.7 0.8 slice_bitcast_fusion.4
  12.5 2.9 %collective-permute-start.4 = (bf16[128,512]{1,0:T(8,128)(2,1)}, bf16[128,512]{1,0:T(8,128)(2,1)}, u32[]{:S(2)}, u32[]{:S(2)}) collective-permute-start(bf16[128,512]{1,0:T(8,128)(2,1)} %get-tuple-element.68), channel_id=1, source_target_pairs={{0,4},{4,0},{8,8},{12,12},{1,5},{5,1},{9,9},{13,13},{2,6},{6,2},{1... | collective-permute-start | bytes 393224 | tf_op jit(solution)/shard_map/ppermute | solution.py:405
  15.5 2.9 %collective-permute-start.2 = (bf16[128,512]{1,0:T(8,128)(2,1)}, bf16[128,512]{1,0:T(8,128)(2,1)S(1)}, u32[]{:S(2)}, u32[]{:S(2)}) collective-permute-start(bf16[128,512]{1,0:T(8,128)(2,1)} %get-tuple-element.69), channel_id=1, source_target_pairs={{0,4},{4,0},{8,8},{12,12},{1,5},{5,1},{9,9},{13,13},{2,6},{6,2},{1... | collective-permute-start | bytes 393224 | tf_op jit(solution)/shard_map/ppermute | solution.py:405
  18.4 2.9 %collective-permute-start.1 = (bf16[128,512]{1,0:T(8,128)(2,1)}, bf16[128,512]{1,0:T(8,128)(2,1)}, u32[]{:S(2)}, u32[]{:S(2)}) collective-permute-start(bf16[128,512]{1,0:T(8,128)(2,1)} %get-tuple-element.70), channel_id=1, source_target_pairs={{0,4},{4,0},{8,8},{12,12},{1,5},{5,1},{9,9},{13,13},{2,6},{6,2},{1... | collective-permute-start | bytes 393224 | tf_op jit(solution)/shard_map/ppermute | solution.py:405
  21.3 0.6 slice_bitcast_fusion.8
  21.9 0.0 copy-start.8
  21.9 0.8 slice_bitcast_fusion
  22.7 0.7 copy-done.36
  23.4 0.0 copy-done.38
  23.4 0.6 broadcast_compare_fusion.1
  24.0 0.6 copy-done.31
  24.7 1.0 %shard_map.132.rest_0_.rest_4_ = f32[256,1024]{1,0:T(8,128)S(1)} custom-call(bf16[256,2048]{1,0:T(8,128)(2,1)S(1)} %copy-done.1, bf16[256,256]{1,0:T(8,128)(2,1)S(1)} %copy-done.7, bf16[256,256]{1,0:T(8,128)(2,1)S(1)} %copy-done.8, f32[32,256]{1,0:T(8,128)S(1)} %get-tuple-element.32.cum_ref, f32[32,256]{1,0:T(8,128)S(1)} %copy-done.16, f32[1,32]{1,0:T(1,128)S(1)} %bitcast.40), custom_call_target="tpu_custom_call" | custom-call | flops 134217728 | bytes 4194304 | tf_op jit(solution)/shard_map/pallas_call | solution.py:423
  25.7 0.0 copy-start.19
  25.7 0.6 copy-done.19
  26.3 2.9 %collective-permute-start = (bf16[128,512]{1,0:T(8,128)(2,1)}, bf16[128,512]{1,0:T(8,128)(2,1)}, u32[]{:S(2)}, u32[]{:S(2)}) collective-permute-start(bf16[128,512]{1,0:T(8,128)(2,1)} %get-tuple-element.71), channel_id=1, source_target_pairs={{0,4},{4,0},{8,8},{12,12},{1,5},{5,1},{9,9},{13,13},{2,6},{6,2},{1... | collective-permute-start | bytes 393224 | tf_op jit(solution)/shard_map/ppermute | solution.py:405
  29.3 0.0 copy-start.20
  29.3 0.9 %copy-done.20 = bf16[128,512]{1,0:T(8,128)(2,1)S(1)} copy-done((bf16[128,512]{1,0:T(8,128)(2,1)S(1)}, bf16[128,512]{1,0:T(8,128)(2,1)}, u32[]{:S(2)}) %copy-start.20) | copy-done | bytes 131096
  30.2 0.7 shard_map.133
  30.9 0.2 copy-done.9
  31.1 1.0 %shard_map.134.rest_1_.rest_5_ = f32[256,1024]{1,0:T(8,128)S(1)} custom-call(bf16[256,2048]{1,0:T(8,128)(2,1)S(1)} %copy-done.1, bf16[256,256]{1,0:T(8,128)(2,1)S(1)} %copy-done.7, bf16[256,256]{1,0:T(8,128)(2,1)S(1)} %copy-done.9, f32[32,256]{1,0:T(8,128)S(1)} %copy-done.12, f32[32,256]{1,0:T(8,128)S(1)} %copy-done.17, f32[1,32]{1,0:T(1,128)S(1)} %bitcast.41, ...), custom_call_target="tpu_custom_call" | custom-call | flops 134217728 | bytes 4194304 | tf_op jit(solution)/shard_map/pallas_call | solution.py:423
  32.1 2.2 %collective-permute-start.5 = (bf16[128,512]{1,0:T(8,128)(2,1)}, bf16[128,512]{1,0:T(8,128)(2,1)}, u32[]{:S(2)}, u32[]{:S(2)}) collective-permute-start(bf16[128,512]{1,0:T(8,128)(2,1)} %get-tuple-element.38.rest_0_), channel_id=1, source_target_pairs={{0,0},{4,8},{8,4},{12,12},{1,1},{5,9},{9,5},{13,13},{2,2},{6,10},{... | collective-permute-start | bytes 393224 | tf_op jit(solution)/shard_map/ppermute | solution.py:405
  34.3 1.6 %shard_map.135 = (bf16[128,512]{1,0:T(8,128)(2,1)}, bf16[4,128,512]{2,1,0:T(8,128)(2,1)S(1)}) custom-call(bf16[128,512]{1,0:T(8,128)(2,1)} %collective-permute-done.1.got_ref, f32[128,512]{1,0:T(8,128)S(1)} %get-tuple-element.66.total_ref, f32[1,512]{1,0:T(1,128)S(1)} %get-tuple-element.74.decay_ref, ...), custom_call_target="tpu_custom_call", output_to_operand_aliasing={{1}: (3, {})} | custom-call | flops 131072 | bytes 524288 | tf_op jit(solution)/shard_map/pallas_call | solution.py:461
  35.9 2.2 %collective-permute-start.3 = (bf16[128,512]{1,0:T(8,128)(2,1)}, bf16[128,512]{1,0:T(8,128)(2,1)}, u32[]{:S(2)}, u32[]{:S(2)}) collective-permute-start(bf16[128,512]{1,0:T(8,128)(2,1)} %get-tuple-element.39.rest_4_), channel_id=1, source_target_pairs={{0,0},{4,8},{8,4},{12,12},{1,1},{5,9},{9,5},{13,13},{2,2},{6,10},{... | collective-permute-start | bytes 393224 | tf_op jit(solution)/shard_map/ppermute | solution.py:405
  38.1 2.6 %collective-permute-start.6 = (bf16[4,4,256]{2,1,0:T(4,128)(2,1)S(1)}, bf16[4,4,256]{2,1,0:T(4,128)(2,1)}, u32[]{:S(2)}, u32[]{:S(2)}) collective-permute-start(bf16[4,4,256]{2,1,0:T(4,128)(2,1)S(1)} %bitcast.35), channel_id=1, source_target_pairs={{0,4},{4,8},{8,12},{12,0},{1,5},{5,9},{9,13},{13,1},{2,6},{6,10},{... | collective-permute-start | bytes 24584 | tf_op jit(solution)/shard_map/ppermute | solution.py:408
  40.7 0.2 select_reduce_fusion
  40.9 0.7 broadcast_in_dim.27
  41.6 0.8 reshape_reshape.4.spot_ref
  42.3 1.4 %collective-permute-done.6.rest_1_ = bf16[4,4,256]{2,1,0:T(4,128)(2,1)} collective-permute-done((bf16[4,4,256]{2,1,0:T(4,128)(2,1)S(1)}, bf16[4,4,256]{2,1,0:T(4,128)(2,1)}, u32[]{:S(2)}, u32[]{:S(2)}) %collective-permute-start.6) | collective-permute-done | bytes 8224 | tf_op jit(solution)/shard_map/ppermute | solution.py:408
  43.7 0.8 copy-done.13
  44.5 0.8 copy-done.18
  45.2 1.6 %shard_map.136 = (f32[16,2048]{1,0:T(8,128)S(1)}, f32[16,32]{1,0:T(8,128)S(1)}, bf16[16,256]{1,0:T(8,128)(2,1)S(1)}) custom-call(bf16[256,2048]{1,0:T(8,128)(2,1)S(1)} %copy-done.1, bf16[256,256]{1,0:T(8,128)(2,1)S(1)} %copy-done.7, f32[32,256]{1,0:T(8,128)S(1)} %copy-done.13, f32[32,256]{1,0:T(8,128)S(1)} %copy-done.18, ...), custom_call_target="tpu_custom_call" | custom-call | flops 16777216 | bytes 2097152 | tf_op jit(solution)/shard_map/pallas_call | solution.py:432
  46.8 0.0 collective-permute-done.5.got_ref
  46.9 0.6 copy-done.28
  47.5 1.0 %shard_map.137 = (bf16[128,512]{1,0:T(8,128)(2,1)S(1)}, bf16[4,128,512]{2,1,0:T(8,128)(2,1)S(1)}) custom-call(bf16[128,512]{1,0:T(8,128)(2,1)} %collective-permute-done.5.got_ref, f32[128,512]{1,0:T(8,128)S(1)} %copy-done.5, f32[1,512]{1,0:T(1,128)S(1)} %copy-done.28, ...), custom_call_target="tpu_custom_call", output_to_operand_aliasing={{1}: (3, {})} | custom-call | flops 131072 | bytes 524288 | tf_op jit(solution)/shard_map/pallas_call | solution.py:461
  48.5 0.0 copy-start.35
  48.6 0.6 copy-done.33
  49.2 0.4 shard_map.138
  49.6 0.7 copy-done.24
  50.3 0.9 %shard_map.139 = (bf16[128,512]{1,0:T(8,128)(2,1)S(1)}, bf16[4,128,512]{2,1,0:T(8,128)(2,1)S(1)}) custom-call(bf16[128,512]{1,0:T(8,128)(2,1)} %collective-permute-done.4.got_ref, f32[128,512]{1,0:T(8,128)S(1)} %get-tuple-element.64.total_ref, f32[1,512]{1,0:T(1,128)S(1)} %copy-done.24, ...), custom_call_target="tpu_custom_call", output_to_operand_aliasing={{1}: (3, {})} | custom-call | flops 131072 | bytes 524288 | tf_op jit(solution)/shard_map/pallas_call | solution.py:461
  51.3 0.7 collective-permute-start.10
  51.9 0.9 %shard_map.140 = (bf16[128,512]{1,0:T(8,128)(2,1)S(1)}, bf16[4,128,512]{2,1,0:T(8,128)(2,1)S(1)}) custom-call(bf16[128,512]{1,0:T(8,128)(2,1)} %collective-permute-done.3.got_ref, f32[128,512]{1,0:T(8,128)S(1)} %get-tuple-element.66.total_ref, f32[1,512]{1,0:T(1,128)S(1)} %copy-done.26, ...), custom_call_target="tpu_custom_call", output_to_operand_aliasing={{1}: (3, {})} | custom-call | flops 131072 | bytes 524288 | tf_op jit(solution)/shard_map/pallas_call | solution.py:461
  52.9 0.6 copy-done.23
  53.5 0.9 %shard_map.141 = (bf16[128,512]{1,0:T(8,128)(2,1)S(1)}, bf16[4,128,512]{2,1,0:T(8,128)(2,1)S(1)}) custom-call(bf16[128,512]{1,0:T(8,128)(2,1)} %collective-permute-done.got_ref, f32[128,512]{1,0:T(8,128)S(1)} %get-tuple-element.67.total_ref, f32[1,512]{1,0:T(1,128)S(1)} %copy-done.23, ...), custom_call_target="tpu_custom_call", output_to_operand_aliasing={{1}: (3, {})} | custom-call | flops 131072 | bytes 524288 | tf_op jit(solution)/shard_map/pallas_call | solution.py:461
  54.5 0.7 collective-permute-start.9
  55.2 0.7 collective-permute-start.11
  55.8 0.7 collective-permute-start.12
  56.6 0.8 collective-permute-start.14
  57.4 0.7 collective-permute-start.13
  58.2 0.2 shard_map.145
  58.4 19.9 %collective-permute-start.15 = (f32[4,2048]{1,0:T(4,128)S(1)}, f32[4,2048]{1,0:T(4,128)S(1)}, u32[]{:S(2)}, u32[]{:S(2)}) collective-permute-start(f32[4,2048]{1,0:T(4,128)S(1)} %get-tuple-element.59), channel_id=1, source_target_pairs={{0,12},{4,0},{8,4},{12,8},{1,13},{5,1},{9,5},{13,9},{2,14},{6,2},{... | collective-permute-start | bytes 98312 | tf_op jit(solution)/shard_map/ppermute | solution.py:408
  78.4 0.9 %collective-permute-start.17 = (f32[4,2048]{1,0:T(4,128)S(1)}, f32[4,2048]{1,0:T(4,128)S(1)}, u32[]{:S(2)}, u32[]{:S(2)}) collective-permute-start(f32[4,2048]{1,0:T(4,128)S(1)} %get-tuple-element.61), channel_id=1, source_target_pairs={{0,4},{4,8},{8,12},{12,0},{1,5},{5,9},{9,13},{13,1},{2,6},{6,10},{... | collective-permute-start | bytes 98312 | tf_op jit(solution)/shard_map/ppermute | solution.py:408
  79.3 0.6 copy-done.39
  79.9 0.1 copy-done.40
  80.0 0.1 fusion.1
  80.1 1.8 %shard_map.144 = bf16[256,2048]{1,0:T(8,128)(2,1)} custom-call(bf16[256,256]{1,0:T(8,128)(2,1)S(1)} %copy-done.10, f32[32,256]{1,0:T(8,128)S(1)} %copy-done.14, bf16[4,128,512]{2,1,0:T(8,128)(2,1)S(1)} %get-tuple-element.51.carry_ref, bf16[128,512]{1,0:T(8,128)(2,1)S(1)} %collective-permute-done.11.rest_0_, ...), custom_call_target="tpu_custom_call" | custom-call | flops 134217728 | bytes 4194304 | tf_op jit(solution)/shard_map/pallas_call | solution.py:485
  81.9 1.3 %collective-permute-done.16.rest_2_ = f32[4,2048]{1,0:T(4,128)S(1)} collective-permute-done((f32[4,2048]{1,0:T(4,128)S(1)}, f32[4,2048]{1,0:T(4,128)S(1)}, u32[]{:S(2)}, u32[]{:S(2)}) %collective-permute-start.16) | collective-permute-done | bytes 32800 | tf_op jit(solution)/shard_map/ppermute | solution.py:408
  83.2 0.9 %collective-permute-done.17.rest_3_ = f32[4,2048]{1,0:T(4,128)S(1)} collective-permute-done((f32[4,2048]{1,0:T(4,128)S(1)}, f32[4,2048]{1,0:T(4,128)S(1)}, u32[]{:S(2)}, u32[]{:S(2)}) %collective-permute-start.17) | collective-permute-done | bytes 32800 | tf_op jit(solution)/shard_map/ppermute | solution.py:408
  84.1 1.2 %shard_map.146 = bf16[4,4,2048]{2,1,0:T(4,128)(2,1)} custom-call(s32[4]{0:T(128)S(1)} %convert_element_type.3.held_ref, f32[4,4,2048]{2,1,0:T(4,128)S(1)} %get-tuple-element.44.rest_1_.keep_ref, f32[4,4,2048]{2,1,0:T(4,128)S(1)} %get-tuple-element.55.fresh_ref, f32[4,2048]{1,0:T(4,128)S(1)} %get-tuple-element.58.rest_0_, ...), custom_call_target="tpu_custom_call" | custom-call | flops 131072 | bytes 524288 | tf_op jit(solution)/shard_map/pallas_call | solution.py:497
  (81 shorter events, 0.3 us)
Async XLA Ops:
  0.6 35.3 %collective-permute-start.8 = (bf16[4,4,256]{2,1,0:T(4,128)(2,1)}, bf16[4,4,256]{2,1,0:T(4,128)(2,1)}, u32[]{:S(2)}, u32[]{:S(2)}) collective-permute-start(bf16[4,4,256]{2,1,0:T(4,128)(2,1)} %bitcast.33), channel_id=1, source_target_pairs={{0,12},{4,0},{8,4},{12,8},{1,13},{5,1},{9,5},{13,9},{2,14},{6,2},{... | collective-permute-start | bytes 24584 | tf_op jit(solution)/shard_map/ppermute | solution.py:408
  5.7 32.4 %collective-permute-start.7 = (bf16[4,4,256]{2,1,0:T(4,128)(2,1)}, bf16[4,4,256]{2,1,0:T(4,128)(2,1)}, u32[]{:S(2)}, u32[]{:S(2)}) collective-permute-start(bf16[4,4,256]{2,1,0:T(4,128)(2,1)} %bitcast.34), channel_id=1, source_target_pairs={{0,8},{4,12},{8,0},{12,4},{1,9},{5,13},{9,1},{13,5},{2,10},{6,14},... | collective-permute-start | bytes 24584 | tf_op jit(solution)/shard_map/ppermute | solution.py:408
  5.7 0.7 copy-start.34
  6.4 1.2 %copy-start = (bf16[256,2048]{1,0:T(8,128)(2,1)S(1)}, bf16[256,2048]{1,0:T(8,128)(2,1)}, u32[]{:S(2)}) copy-start(bf16[256,2048]{1,0:T(8,128)(2,1)} %x_ref.5) | copy-start | bytes 3145732
  7.6 0.9 %copy-start.6 = (bf16[256,256]{1,0:T(8,128)(2,1)S(1)}, bf16[256,256]{1,0:T(8,128)(2,1)}, u32[]{:S(2)}) copy-start(bf16[256,256]{1,0:T(8,128)(2,1)} %b_ref.5) | copy-start | bytes 393220
  8.5 0.7 copy-start.29
  11.7 0.9 %copy-start.15 = (f32[32,256]{1,0:T(8,128)}, f32[32,256]{1,0:T(8,128)S(1)}, u32[]{:S(2)}) copy-start(f32[32,256]{1,0:T(8,128)S(1)} %get-tuple-element.36.row_ref) | copy-start | bytes 98308
  11.7 12.3 %copy-start.11 = (f32[32,256]{1,0:T(8,128)}, f32[32,256]{1,0:T(8,128)S(1)}, u32[]{:S(2)}) copy-start(f32[32,256]{1,0:T(8,128)S(1)} %get-tuple-element.32.cum_ref) | copy-start | bytes 98308
  12.5 37.1 %collective-permute-start.4 = (bf16[128,512]{1,0:T(8,128)(2,1)}, bf16[128,512]{1,0:T(8,128)(2,1)}, u32[]{:S(2)}, u32[]{:S(2)}) collective-permute-start(bf16[128,512]{1,0:T(8,128)(2,1)} %get-tuple-element.68), channel_id=1, source_target_pairs={{0,4},{4,0},{8,8},{12,12},{1,5},{5,1},{9,9},{13,13},{2,6},{6,2},{1... | collective-permute-start | bytes 393224 | tf_op jit(solution)/shard_map/ppermute | solution.py:405
  15.5 10.2 %collective-permute-start.2 = (bf16[128,512]{1,0:T(8,128)(2,1)}, bf16[128,512]{1,0:T(8,128)(2,1)S(1)}, u32[]{:S(2)}, u32[]{:S(2)}) collective-permute-start(bf16[128,512]{1,0:T(8,128)(2,1)} %get-tuple-element.69), channel_id=1, source_target_pairs={{0,4},{4,0},{8,8},{12,12},{1,5},{5,1},{9,9},{13,13},{2,6},{6,2},{1... | collective-permute-start | bytes 393224 | tf_op jit(solution)/shard_map/ppermute | solution.py:405
  18.4 13.7 %collective-permute-start.1 = (bf16[128,512]{1,0:T(8,128)(2,1)}, bf16[128,512]{1,0:T(8,128)(2,1)}, u32[]{:S(2)}, u32[]{:S(2)}) collective-permute-start(bf16[128,512]{1,0:T(8,128)(2,1)} %get-tuple-element.70), channel_id=1, source_target_pairs={{0,4},{4,0},{8,8},{12,12},{1,5},{5,1},{9,9},{13,13},{2,6},{6,2},{1... | collective-permute-start | bytes 393224 | tf_op jit(solution)/shard_map/ppermute | solution.py:405
  21.9 7.4 %copy-start.27 = (f32[1,512]{1,0:T(1,128)}, f32[1,512]{1,0:T(1,128)S(1)}, u32[]{:S(2)}) copy-start(f32[1,512]{1,0:T(1,128)S(1)} %get-tuple-element.73.decay_ref) | copy-start | bytes 6148
  21.9 12.4 %copy-start.25 = (f32[1,512]{1,0:T(1,128)}, f32[1,512]{1,0:T(1,128)S(1)}, u32[]{:S(2)}) copy-start(f32[1,512]{1,0:T(1,128)S(1)} %get-tuple-element.74.decay_ref) | copy-start | bytes 6148
  21.9 2.1 %copy-start.1 = (bf16[256,2048]{1,0:T(8,128)(2,1)S(1)}, bf16[256,2048]{1,0:T(8,128)(2,1)}, u32[]{:S(2)}) copy-start(bf16[256,2048]{1,0:T(8,128)(2,1)} %x_ref.5) | copy-start | bytes 3145732
  21.9 2.1 %copy-start.7 = (bf16[256,256]{1,0:T(8,128)(2,1)S(1)}, bf16[256,256]{1,0:T(8,128)(2,1)}, u32[]{:S(2)}) copy-start(bf16[256,256]{1,0:T(8,128)(2,1)} %b_ref.5) | copy-start | bytes 393220
  21.9 2.1 %copy-start.8 = (bf16[256,256]{1,0:T(8,128)(2,1)S(1)}, bf16[256,256]{1,0:T(8,128)(2,1)}, u32[]{:S(2)}) copy-start(bf16[256,256]{1,0:T(8,128)(2,1)} %c_ref.5) | copy-start | bytes 393220
  21.9 2.1 %copy-start.16 = (f32[32,256]{1,0:T(8,128)S(1)}, f32[32,256]{1,0:T(8,128)}, u32[]{:S(2)}) copy-start(f32[32,256]{1,0:T(8,128)} %copy-done.15) | copy-start | bytes 98308
  22.7 0.7 copy-start.36
  22.7 0.7 copy-start.38
  24.0 0.7 copy-start.31
  24.6 4.6 %copy-start.4 = (f32[128,512]{1,0:T(8,128)S(1)}, f32[128,512]{1,0:T(8,128)}, u32[]{:S(2)}) copy-start(f32[128,512]{1,0:T(8,128)} %get-tuple-element.65.total_ref) | copy-start | bytes 786436
  25.7 0.7 copy-start.19
  26.3 26.6 %collective-permute-start = (bf16[128,512]{1,0:T(8,128)(2,1)}, bf16[128,512]{1,0:T(8,128)(2,1)}, u32[]{:S(2)}, u32[]{:S(2)}) collective-permute-start(bf16[128,512]{1,0:T(8,128)(2,1)} %get-tuple-element.71), channel_id=1, source_target_pairs={{0,4},{4,0},{8,8},{12,12},{1,5},{5,1},{9,9},{13,13},{2,6},{6,2},{1... | collective-permute-start | bytes 393224 | tf_op jit(solution)/shard_map/ppermute | solution.py:405
  29.3 0.9 %copy-start.20 = (bf16[128,512]{1,0:T(8,128)(2,1)S(1)}, bf16[128,512]{1,0:T(8,128)(2,1)}, u32[]{:S(2)}) copy-start(bf16[128,512]{1,0:T(8,128)(2,1)} %copy-done.19) | copy-start | bytes 393220
  30.2 0.9 %copy-start.9 = (bf16[256,256]{1,0:T(8,128)(2,1)S(1)}, bf16[256,256]{1,0:T(8,128)(2,1)}, u32[]{:S(2)}) copy-start(bf16[256,256]{1,0:T(8,128)(2,1)} %c_ref.5) | copy-start | bytes 393220
  30.2 0.9 %copy-start.12 = (f32[32,256]{1,0:T(8,128)S(1)}, f32[32,256]{1,0:T(8,128)}, u32[]{:S(2)}) copy-start(f32[32,256]{1,0:T(8,128)} %copy-done.11) | copy-start | bytes 98308
  30.2 0.9 %copy-start.17 = (f32[32,256]{1,0:T(8,128)S(1)}, f32[32,256]{1,0:T(8,128)}, u32[]{:S(2)}) copy-start(f32[32,256]{1,0:T(8,128)} %copy-done.15) | copy-start | bytes 98308
  32.1 3.8 %copy-start.2 = (f32[256,1024]{1,0:T(8,128)}, f32[256,1024]{1,0:T(8,128)S(1)}, u32[]{:S(2)}) copy-start(f32[256,1024]{1,0:T(8,128)S(1)} %shard_map.134.rest_1_.rest_5_) | copy-start | bytes 3145732
  32.1 14.7 %collective-permute-start.5 = (bf16[128,512]{1,0:T(8,128)(2,1)}, bf16[128,512]{1,0:T(8,128)(2,1)}, u32[]{:S(2)}, u32[]{:S(2)}) collective-permute-start(bf16[128,512]{1,0:T(8,128)(2,1)} %get-tuple-element.38.rest_0_), channel_id=1, source_target_pairs={{0,0},{4,8},{8,4},{12,12},{1,1},{5,9},{9,5},{13,13},{2,2},{6,10},{... | collective-permute-start | bytes 393224 | tf_op jit(solution)/shard_map/ppermute | solution.py:405
  34.3 3.8 %copy-start.22 = (bf16[1,4,4,256]{3,2,1,0:T(4,128)(2,1)S(1)}, bf16[1,4,4,256]{3,2,1,0:T(4,128)(2,1)}, u32[]{:S(2)}) copy-start(bf16[1,4,4,256]{3,2,1,0:T(4,128)(2,1)} %param.22) | copy-start | bytes 24580
  35.9 16.0 %collective-permute-start.3 = (bf16[128,512]{1,0:T(8,128)(2,1)}, bf16[128,512]{1,0:T(8,128)(2,1)}, u32[]{:S(2)}, u32[]{:S(2)}) collective-permute-start(bf16[128,512]{1,0:T(8,128)(2,1)} %get-tuple-element.39.rest_4_), channel_id=1, source_target_pairs={{0,0},{4,8},{8,4},{12,12},{1,1},{5,9},{9,5},{13,13},{2,2},{6,10},{... | collective-permute-start | bytes 393224 | tf_op jit(solution)/shard_map/ppermute | solution.py:405
  38.1 2.6 %copy-start.37 = (s32[8]{0:T(128)S(1)}, s32[8]{0:T(128)}, u32[]{:S(2)}) copy-start(s32[8]{0:T(128)} %param.19) | copy-start | bytes 100
  38.1 5.6 %collective-permute-start.6 = (bf16[4,4,256]{2,1,0:T(4,128)(2,1)S(1)}, bf16[4,4,256]{2,1,0:T(4,128)(2,1)}, u32[]{:S(2)}, u32[]{:S(2)}) collective-permute-start(bf16[4,4,256]{2,1,0:T(4,128)(2,1)S(1)} %bitcast.35), channel_id=1, source_target_pairs={{0,4},{4,8},{8,12},{12,0},{1,5},{5,9},{9,13},{13,1},{2,6},{6,10},{... | collective-permute-start | bytes 24584 | tf_op jit(solution)/shard_map/ppermute | solution.py:408
  42.3 4.5 %copy-start.5 = (f32[128,512]{1,0:T(8,128)S(1)}, f32[128,512]{1,0:T(8,128)}, u32[]{:S(2)}) copy-start(f32[128,512]{1,0:T(8,128)} %get-tuple-element.65.total_ref) | copy-start | bytes 786436
  43.7 0.8 copy-start.13
  44.5 0.8 copy-start.18
  46.8 0.7 copy-start.28
  47.5 1.0 %copy-start.21 = (bf16[1,4,4,2048]{3,2,1,0:T(4,128)(2,1)S(1)}, bf16[1,4,4,2048]{3,2,1,0:T(4,128)(2,1)}, u32[]{:S(2)}) copy-start(bf16[1,4,4,2048]{3,2,1,0:T(4,128)(2,1)} %param.20) | copy-start | bytes 196612
  47.5 1.0 %copy-start.30 = (bf16[1,4,4,256]{3,2,1,0:T(4,128)(2,1)S(1)}, bf16[1,4,4,256]{3,2,1,0:T(4,128)(2,1)}, u32[]{:S(2)}) copy-start(bf16[1,4,4,256]{3,2,1,0:T(4,128)(2,1)} %param.21) | copy-start | bytes 24580
  48.5 0.7 copy-start.33
  48.5 0.7 copy-start.32
  48.5 0.7 copy-start.35
  49.6 0.7 copy-start.24
  51.2 0.7 copy-start.26
  51.3 5.3 %collective-permute-start.10 = (bf16[128,512]{1,0:T(8,128)(2,1)S(1)}, bf16[128,512]{1,0:T(8,128)(2,1)S(1)}, u32[]{:S(2)}, u32[]{:S(2)}) collective-permute-start(bf16[128,512]{1,0:T(8,128)(2,1)S(1)} %get-tuple-element.48), channel_id=1, source_target_pairs={{0,0},{4,8},{8,4},{12,12},{1,1},{5,9},{9,5},{13,13},{2,2},{6,10},{... | collective-permute-start | bytes 393224 | tf_op jit(solution)/shard_map/ppermute | solution.py:405
  52.9 0.6 copy-start.23
  54.5 2.1 %collective-permute-start.9 = (bf16[128,512]{1,0:T(8,128)(2,1)S(1)}, bf16[128,512]{1,0:T(8,128)(2,1)S(1)}, u32[]{:S(2)}, u32[]{:S(2)}) collective-permute-start(bf16[128,512]{1,0:T(8,128)(2,1)S(1)} %get-tuple-element.47), channel_id=1, source_target_pairs={{0,0},{4,8},{8,4},{12,12},{1,1},{5,9},{9,5},{13,13},{2,2},{6,10},{... | collective-permute-start | bytes 393224 | tf_op jit(solution)/shard_map/ppermute | solution.py:405
  55.2 3.0 %collective-permute-start.11 = (bf16[128,512]{1,0:T(8,128)(2,1)S(1)}, bf16[128,512]{1,0:T(8,128)(2,1)S(1)}, u32[]{:S(2)}, u32[]{:S(2)}) collective-permute-start(bf16[128,512]{1,0:T(8,128)(2,1)S(1)} %get-tuple-element.43.rest_0_), channel_id=1, source_target_pairs={{0,0},{4,4},{8,12},{12,8},{1,1},{5,5},{9,13},{13,9},{2,2},{6,6},{1... | collective-permute-start | bytes 393224 | tf_op jit(solution)/shard_map/ppermute | solution.py:405
  55.8 2.3 %collective-permute-start.12 = (bf16[128,512]{1,0:T(8,128)(2,1)S(1)}, bf16[128,512]{1,0:T(8,128)(2,1)S(1)}, u32[]{:S(2)}, u32[]{:S(2)}) collective-permute-start(bf16[128,512]{1,0:T(8,128)(2,1)S(1)} %get-tuple-element.52), channel_id=1, source_target_pairs={{0,0},{4,4},{8,12},{12,8},{1,1},{5,5},{9,13},{13,9},{2,2},{6,6},{1... | collective-permute-start | bytes 393224 | tf_op jit(solution)/shard_map/ppermute | solution.py:405
  56.6 23.5 %copy-start.3 = (f32[256,1024]{1,0:T(8,128)S(1)}, f32[256,1024]{1,0:T(8,128)}, u32[]{:S(2)}) copy-start(f32[256,1024]{1,0:T(8,128)} %copy-done.2) | copy-start | bytes 3145732
  56.6 1.5 %collective-permute-start.14 = (bf16[128,512]{1,0:T(8,128)(2,1)S(1)}, bf16[128,512]{1,0:T(8,128)(2,1)S(1)}, u32[]{:S(2)}, u32[]{:S(2)}) collective-permute-start(bf16[128,512]{1,0:T(8,128)(2,1)S(1)} %get-tuple-element.54), channel_id=1, source_target_pairs={{0,0},{4,4},{8,12},{12,8},{1,1},{5,5},{9,13},{13,9},{2,2},{6,6},{1... | collective-permute-start | bytes 393224 | tf_op jit(solution)/shard_map/ppermute | solution.py:405
  57.4 0.7 collective-permute-start.13
  58.2 21.9 %copy-start.10 = (bf16[256,256]{1,0:T(8,128)(2,1)S(1)}, bf16[256,256]{1,0:T(8,128)(2,1)}, u32[]{:S(2)}) copy-start(bf16[256,256]{1,0:T(8,128)(2,1)} %c_ref.5) | copy-start | bytes 393220
  58.2 21.9 %copy-start.14 = (f32[32,256]{1,0:T(8,128)S(1)}, f32[32,256]{1,0:T(8,128)}, u32[]{:S(2)}) copy-start(f32[32,256]{1,0:T(8,128)} %copy-done.11) | copy-start | bytes 98308
  58.4 23.4 %collective-permute-start.15 = (f32[4,2048]{1,0:T(4,128)S(1)}, f32[4,2048]{1,0:T(4,128)S(1)}, u32[]{:S(2)}, u32[]{:S(2)}) collective-permute-start(f32[4,2048]{1,0:T(4,128)S(1)} %get-tuple-element.59), channel_id=1, source_target_pairs={{0,12},{4,0},{8,4},{12,8},{1,13},{5,1},{9,5},{13,9},{2,14},{6,2},{... | collective-permute-start | bytes 98312 | tf_op jit(solution)/shard_map/ppermute | solution.py:408
  78.4 4.8 %collective-permute-start.16 = (f32[4,2048]{1,0:T(4,128)S(1)}, f32[4,2048]{1,0:T(4,128)S(1)}, u32[]{:S(2)}, u32[]{:S(2)}) collective-permute-start(f32[4,2048]{1,0:T(4,128)S(1)} %get-tuple-element.60), channel_id=1, source_target_pairs={{0,8},{4,12},{8,0},{12,4},{1,9},{5,13},{9,1},{13,5},{2,10},{6,14},... | collective-permute-start | bytes 98312 | tf_op jit(solution)/shard_map/ppermute | solution.py:408
  78.4 5.7 %collective-permute-start.17 = (f32[4,2048]{1,0:T(4,128)S(1)}, f32[4,2048]{1,0:T(4,128)S(1)}, u32[]{:S(2)}, u32[]{:S(2)}) collective-permute-start(f32[4,2048]{1,0:T(4,128)S(1)} %get-tuple-element.61), channel_id=1, source_target_pairs={{0,4},{4,8},{8,12},{12,0},{1,5},{5,9},{9,13},{13,1},{2,6},{6,10},{... | collective-permute-start | bytes 98312 | tf_op jit(solution)/shard_map/ppermute | solution.py:408
  79.3 0.6 copy-start.39
  79.3 0.7 copy-start.40

commit v4 on v3

--- a/solution.py
+++ b/solution.py
@@ -61,7 +61,11 @@
 
 
 def shape(dims, dtype=F32):
-    return jax.ShapeDtypeStruct(dims, dtype)
+    return pltpu.VMEM(dims, dtype)
+
+
+def pinned(value, space=pltpu.VMEM):
+    return pltpu.with_memory_space_constraint(value, space)
 
 
 def call(kernel, out_shape, flops, moved, **options):
@@ -81,9 +85,10 @@
 
 
 def state_kernel(
-    x_hbm, b_hbm, dt_hbm, a_hbm, total_ref, sent_ref, decay_ref, cum_ref, row_ref,
-    x_ref, b_ref, dt_ref, a_ref, sems,
+    x_hbm, b_hbm, dt_hbm, a_hbm, asked_hbm, total_ref, decay_ref, cum_ref, row_ref,
+    x_ref, b_ref, asked_ref, *rest,
 ):
+    sent_refs, (dt_ref, a_ref, sems) = rest[:-3], rest[-3:]
     heads, tokens = dt_ref.shape
     spans = tokens // SPAN
     chunks, _, width = total_ref.shape
@@ -100,6 +105,7 @@
         copies.append(
             pltpu.make_async_copy(x_hbm.at[:, lanes], x_ref.at[:, lanes], sems.at[3 + g])
         )
+    copies.append(pltpu.make_async_copy(asked_hbm, asked_ref, sems.at[3 + groups]))
     for copy in copies:
         copy.start()
     upper = triangle(lambda s, t: s <= t)
@@ -135,8 +141,9 @@
             scaled = (x_ref[:, lanes].astype(F32) * over_lanes(weight, first, width)).astype(BF16)
             total = dot(turned, scaled)
             total_ref[k] = total
-            sent_ref[k] = total.astype(BF16)
+            sent_refs[k][...] = total.astype(BF16)
             decay_ref[k] = over_lanes(whole, first, width, 3)
+    copies[-1].wait()
 
 
 def pass_kernel(hop, k, got_ref, total_ref, decay_ref, *rest):
@@ -145,7 +152,7 @@
     if first:
         carry_ref[...] = jnp.zeros_like(carry_ref)
     got = got_ref[...]
-    moving_ref[...] = (total_ref[...] + decay_ref[...] * got.astype(F32)).astype(BF16)
+    moving_ref[...] = (total_ref[k] + decay_ref[k] * got.astype(F32)).astype(BF16)
 
     @pl.when(lax.axis_index("seq") == hop)
     def _():
@@ -168,6 +175,9 @@
 
 def inner_kernel(g, x_ref, b_ref, c_ref, cum_ref, row_ref, d_ref, *rest):
     inner_ref = rest[-1]
+    if g == 0:
+        asked_ref, handed_ref, inner_ref = rest
+        handed_ref[...] = asked_ref[...]
     heads, tokens = cum_ref.shape
     spans = tokens // SPAN
     per_group = H // G
@@ -212,7 +222,7 @@
             inner_ref[mine, here] = dot(left, right) + skip * x_part[mine].astype(F32)
 
 
-def ask_kernel(count, x_ref, b_ref, cum_ref, row_ref, spot_ref, *rest):
+def ask_kernel(count, x_ref, b_ref, cum_ref, row_ref, len_ref, owner_ref, *rest):
     ask_refs = rest[:count]
     local_ref, gain_ref, asked_ref = rest[-3:]
     heads, tokens = cum_ref.shape
@@ -223,7 +233,10 @@
     me = lax.axis_index("seq")
     asked = jnp.concatenate([ref[me].astype(F32) for ref in ask_refs], axis=0).astype(BF16)
     asked_ref[...] = asked
-    spot = spot_ref[...]
+    block = lax.broadcasted_iota(jnp.int32, (asks, 1), 0) // STEPS
+    spot = len_ref[...] - 1 - me * tokens
+    mine = (owner_ref[...] == lax.rem(me + count - block, count)) & (spot >= 0) & (spot < tokens)
+    spot = jnp.sum(jnp.where(mine, spot, 0).astype(F32), axis=1, keepdims=True).astype(jnp.int32)
     position = lax.broadcasted_iota(jnp.int32, (asks, tokens), 1)
     picked = jnp.where(position == spot, 1.0, 0.0).astype(BF16)
     upto = position <= spot
@@ -257,26 +270,26 @@
             local_ref[:, lanes] = dot(jnp.concatenate(parts, axis=1), right)
 
 
-def read_kernel(chunks, gain_ref, asked_ref, local_ref, carry_ref, *rest):
-    got_refs, read_refs = rest[: len(chunks)], rest[len(chunks) :]
+def read_kernel(chunks, filed, gain_ref, asked_ref, local_ref, carry_ref, *rest):
+    got_refs, rest = rest[: len(chunks)], rest[len(chunks) :]
+    read_refs = rest[len(rest) // 2 :] if filed else rest
     width = got_refs[0].shape[1]
     count = len(read_refs)
     last = lax.axis_index("seq") == count - 1
     gain = jnp.exp2(gain_ref[...])
-    for i, k in enumerate(chunks):
+    for got_ref, k in zip(got_refs, chunks):
         first = k * width
         g = first // (H // G * P_SIZE)
-        state = jnp.where(last, got_refs[i][...], carry_ref[k])
+        state = jnp.where(last, got_ref[...], carry_ref[k])
         carried = dot(asked_ref[:, g * N : (g + 1) * N], state)
         reading = local_ref[:, first : first + width] + over_lanes(gain, first, width) * carried
-        here = slice(i * width, (i + 1) * width)
         for r in range(count):
-            read_refs[r][:, here] = reading[r * STEPS : (r + 1) * STEPS]
+            read_refs[r][:, first : first + width] = reading[r * STEPS : (r + 1) * STEPS]
 
 
 def outer_kernel(chunks, count, c_ref, cum_ref, carry_ref, *rest):
     got_refs = rest[: len(chunks)]
-    inner_refs = rest[len(chunks) : -3]
+    inner_refs = rest[len(chunks) :]
     out_hbm, out_ref, sems = rest[-3:]
     heads, tokens = cum_ref.shape
     spans = tokens // SPAN
@@ -306,10 +319,15 @@
         copy.wait()
 
 
-def fresh_kernel(x_ref, b_ref, c_ref, dt_ref, a_ref, d_ref, *rest):
-    keep_ref, fresh_ref = rest[-2:]
+def fresh_kernel(tokens, x_ref, b_ref, c_ref, dt_ref, a_ref, d_ref, len_ref, owner_ref, *rest):
+    keep_ref, fresh_ref, held_ref = rest[-3:]
     count, _, heads = dt_ref.shape
     rows = count * STEPS
+    place = lax.broadcasted_iota(jnp.int32, (rows, 1), 0) // STEPS * tokens
+    spot = len_ref[...] - 1 - place
+    mine = (owner_ref[...] == lax.axis_index("seq")) & (spot >= 0) & (spot < tokens)
+    held = jnp.sum(jnp.where(mine, 1.0, 0.0), axis=1, keepdims=True)
+    held = jnp.broadcast_to(held, (rows, held_ref.shape[2]))
     per_group = H // G
     groups = heads // per_group
     width = x_ref.shape[2]
@@ -348,23 +366,25 @@
     for i in range(rows // STEPS):
         keep_ref[i] = keep[i * STEPS : (i + 1) * STEPS]
         fresh_ref[i] = fresh[i * STEPS : (i + 1) * STEPS]
-
-
-def finish_kernel(held_ref, keep_ref, fresh_ref, *rest):
+        held_ref[i] = held[i * STEPS : (i + 1) * STEPS]
+
+
+def finish_kernel(keep_ref, fresh_ref, held_ref, *rest):
     back_refs, out_ref = rest[:-1], rest[-1]
     count = len(back_refs)
     me = lax.axis_index("seq")
     for r in range(count):
         source = lax.rem(me + r, count)
         value = back_refs[r][...] * keep_ref[source] + fresh_ref[source]
-        out_ref[source] = jnp.where(held_ref[source] > 0, value, 0.0).astype(BF16)
+        held = held_ref[source][:, :1] > 0.0
+        out_ref[source] = jnp.where(held, value, 0.0).astype(BF16)
 
 
 def shards(
     ssm_input, bmat, cmat, dt_raw, a_log, d_skip, prompt_len, owner, dec_x, dec_b, dec_c, dec_dt
 ):
     count = lax.axis_size("seq")
-    me = lax.axis_index("seq")
+    tensor = lax.axis_size("tp")
     tokens, heads = dt_raw.shape
     groups = heads // (H // G)
     names = groups * N
@@ -375,58 +395,70 @@
     width = lanes // chunks
     a_row = a_log.reshape(1, heads)
     d_row = d_skip.reshape(1, heads)
+    len_row = prompt_len.reshape(1, -1)
+    owner_row = owner.reshape(1, -1)
     anywhere = pl.BlockSpec(memory_space=pl.ANY)
     in_hbm = pl.BlockSpec(memory_space=pltpu.HBM)
     in_vmem = pl.BlockSpec(memory_space=pltpu.VMEM)
-
-    total, sent, decay, cum, row = call(
+    sent_shape = shape((N, width), BF16)
+    asked_shape = shape((count, STEPS, names), BF16)
+
+    total, decay, cum, row, x_here, b_here, asked_here, *sent = call(
         state_kernel,
         (
             shape((chunks, N, width)),
-            shape((chunks, N, width), BF16),
             shape((chunks, 1, width)),
             shape((heads, tokens)),
             shape((heads, tokens)),
-        ),
+            shape((tokens, lanes), BF16),
+            shape((tokens, names), BF16),
+            asked_shape,
+        )
+        + (sent_shape,) * chunks,
         2 * tokens * N * lanes,
         4 * tokens * lanes,
-        in_specs=[in_hbm] * 4,
+        in_specs=[in_hbm] * 5,
         scratch_shapes=[
-            pltpu.VMEM((tokens, lanes), BF16),
-            pltpu.VMEM((tokens, names), BF16),
             pltpu.VMEM((heads, tokens), BF16),
             pltpu.VMEM((1, heads), F32),
-            pltpu.SemaphoreType.DMA((3 + groups,)),
+            pltpu.SemaphoreType.DMA((4 + groups,)),
         ],
-    )(ssm_input, bmat, dt_raw.T, a_row)
-
-    def swap(value, hop):
-        pairs = {hop - 1: hop, hop: hop - 1}
-        return lax.ppermute(value, "seq", [(d, pairs.get(d, d)) for d in range(count)])
+    )(
+        pinned(ssm_input, pltpu.HBM),
+        pinned(bmat, pltpu.HBM),
+        pinned(dt_raw.T, pltpu.HBM),
+        pinned(a_row, pltpu.HBM),
+        pinned(dec_c[0], pltpu.HBM),
+    )
+
+    def forward(value, hop):
+        pairs = []
+        for d in range(count):
+            other = d + 1 if (d - hop) % 2 else d - 1
+            for t in range(tensor):
+                alone = not 0 <= other < count
+                there = d * tensor + (t ^ 1) if alone else other * tensor + t
+                pairs.append((d * tensor + t, there))
+        return lax.ppermute(value, ("seq", "tp"), pairs)
 
     def shift(value, by):
         return lax.ppermute(value, "seq", [(d, (d + by) % count) for d in range(count)])
 
-    got = {(1, k): swap(sent[k], 1) for k in range(chunks)}
-    asks = [dec_c[0]] + [shift(dec_c[0], r) for r in range(1, count)]
-
-    last_token = prompt_len - 1
-    sources = last_token // tokens
-    indices = jnp.arange(count, dtype=jnp.int32)
-    owners = (me - indices) % count
-    mine = (sources == me)[None, :] & (owner[None, :] == owners[:, None])
-    offsets = jnp.sum(jnp.where(mine, last_token[None, :] - me * tokens, 0), axis=1)
-    spot = jnp.repeat(offsets, STEPS).reshape(rows, 1).astype(jnp.int32)
-    held = jnp.any((owner == me)[None, :] & (sources[None, :] == indices[:, None]), axis=1)
-
-    def inner_part(g, *after):
+    got = {(1, k): forward(sent[k], 1) for k in range(chunks)}
+
+    def inner_part(g):
+        more = (asked_here,) if g == 0 else ()
+        inner_shape = shape((tokens, group_lanes))
         return call(
             functools.partial(inner_kernel, g),
-            shape((tokens, group_lanes)),
+            (asked_shape, inner_shape) if g == 0 else inner_shape,
             2 * tokens * tokens * group_lanes,
             16 * tokens * group_lanes,
-            in_specs=[in_vmem] * 6 + [anywhere] * len(after),
-        )(ssm_input, bmat, cmat, cum, row, d_row, *after)
+        )(x_here, b_here, cmat, cum, row, d_row, *more)
+
+    handed, first_inner = inner_part(0)
+    inner = [first_inner] + [inner_part(g) for g in range(1, groups)]
+    asks = [handed] + [shift(handed, r) for r in range(1, count)]
 
     def ask_part(*after):
         return call(
@@ -434,73 +466,80 @@
             (shape((rows, lanes)), shape((rows, heads)), shape((rows, names), BF16)),
             2 * rows * tokens * lanes,
             4 * tokens * lanes,
-            in_specs=[in_vmem] * (5 + count) + [anywhere] * len(after),
-        )(ssm_input, bmat, cum, row, spot, *asks, *after)
+            in_specs=[in_vmem] * (6 + count) + [anywhere] * len(after),
+        )(x_here, b_here, cum, row, len_row, owner_row, *asks, *after)
 
     def fresh_part(*after):
         return call(
-            fresh_kernel,
-            (shape((count, STEPS, lanes)), shape((count, STEPS, lanes))),
+            functools.partial(fresh_kernel, tokens),
+            (shape((count, STEPS, lanes)),) * 2 + (shape((count, STEPS, 128)),),
             64 * rows * lanes,
             16 * rows * lanes,
-            in_specs=[in_vmem] * 6 + [anywhere] * len(after),
-        )(dec_x[0], dec_b[0], dec_c[0], dec_dt[0], a_row, d_row, *after)
-
-    order = sorted(
-        (k + hop, hop, k) for hop in range(1, count - 1) for k in range(chunks)
-    )
-    work = [functools.partial(inner_part, g) for g in range(groups)] + [ask_part, fresh_part]
-    results = [work[0]()]
-    carry = None
-    tie = None
+            in_specs=[in_vmem] * 8 + [anywhere] * len(after),
+        )(dec_x[0], dec_b[0], asked_here, dec_dt[0], a_row, d_row, len_row, owner_row, *after)
+
+    order = sorted((k + hop, hop, k) for hop in range(1, count - 1) for k in range(chunks))
+    work = {1: ask_part, 2: fresh_part}
+    results = {}
+    after = inner
+    carry = tie = None
     for place, (_, hop, k) in enumerate(order):
-        if 0 < place < len(work):
-            results.append(work[place](tie))
-        after = jax.tree.leaves(results[place])[:1] if place < len(results) else []
+        if place in work:
+            results[place] = work[place](tie)
+            after = results[place][:1]
         held_before = [] if carry is None else [carry]
         moving, carry = call(
             functools.partial(pass_kernel, hop, k),
-            (shape((N, width), BF16), shape((chunks, N, width), BF16)),
+            (sent_shape, shape((chunks, N, width), BF16)),
             2 * N * width,
             8 * N * width,
             in_specs=[in_vmem] * (3 + len(held_before)) + [anywhere] * len(after),
             input_output_aliases={3: 1} if held_before else {},
-        )(got[hop, k], total[k], decay[k], *held_before, *after)
-        got[hop + 1, k] = swap(moving, hop + 1)
-        tie = moving
-    *inner, (local, gain, asked), (keep, fresh) = results
-    arrived = [got[count - 1, k] for k in range(chunks)]
-
-    all_chunks = tuple(range(chunks))
-    reading = call(
-        functools.partial(read_kernel, all_chunks),
-        (shape((STEPS, lanes)),) * count,
-        2 * rows * N * lanes,
-        4 * N * lanes,
-    )(gain, asked, local, carry, *arrived)
+        )(got[hop, k], total, decay, *held_before, *after)
+        got[hop + 1, k] = forward(moving, hop + 1)
+        tie, after = moving, []
+    local, gain, asked = results[1]
+    keep, fresh, held = results[2]
+
+    def read_part(part, before):
+        return call(
+            functools.partial(read_kernel, part, bool(before)),
+            (shape((STEPS, lanes)),) * count,
+            2 * rows * N * lanes,
+            4 * N * lanes,
+            input_output_aliases={4 + len(part) + r: r for r in range(len(before))},
+        )(gain, asked, local, carry, *[got[count - 1, k] for k in part], *before)
+
+    def outer_part(part, before):
+        return call(
+            functools.partial(outer_kernel, part, count),
+            pltpu.HBM((tokens, lanes), BF16),
+            2 * tokens * N * lanes,
+            8 * tokens * lanes,
+            in_specs=[in_vmem] * (3 + len(part) + groups) + [in_hbm] * len(before),
+            out_specs=in_hbm,
+            scratch_shapes=[
+                pltpu.VMEM((len(part), tokens, width), BF16),
+                pltpu.SemaphoreType.DMA((len(part),)),
+            ],
+            input_output_aliases={3 + len(part) + groups: 0} if before else {},
+        )(cmat, cum, carry, *[got[count - 1, k] for k in part], *inner, *before)
+
+    early, late = tuple(range(chunks - 1)), (chunks - 1,)
+    prefill = outer_part(early, [])
+    reading = read_part(early, [])
+    reading = read_part(late, reading)
     back = [reading[0]] + [None] * (count - 1)
     for r in reversed(range(1, count)):
         back[r] = shift(reading[r], -r)
-
-    prefill = call(
-        functools.partial(outer_kernel, all_chunks, count),
-        shape((tokens, lanes), BF16),
-        2 * tokens * N * lanes,
-        8 * tokens * lanes,
-        out_specs=in_hbm,
-        scratch_shapes=[
-            pltpu.VMEM((chunks, tokens, width), BF16),
-            pltpu.SemaphoreType.DMA((chunks,)),
-        ],
-    )(cmat, cum, carry, *arrived, *inner)
+    prefill = outer_part(late, [prefill])
 
     decoded = call(
         finish_kernel,
-        shape((count, STEPS, lanes), BF16),
+        jax.ShapeDtypeStruct((count, STEPS, lanes), BF16),
         4 * rows * lanes,
         16 * rows * lanes,
-        in_specs=[pl.BlockSpec(memory_space=pltpu.SMEM)] + [in_vmem] * (2 + count),
-    )(held.astype(jnp.int32), keep, fresh, *back)
+    )(keep, fresh, held, *back)
     return (prefill, decoded[None])
 
 

time: 86.4 us -> 48.8 us (0.56); the launches traced: 85.3 us -> 48.6 us
  starting transfers between devices: 48.7 us -> 20.4 us
  local copies, waits for them, and re-layouts: 15 us -> 1.99 us
  waiting for transfers between devices: 3.62 us -> 14.9 us
  Pallas kernels: 15.9 us -> 10.5 us
  other arithmetic: 0.9 us -> 0 us
    ppermute x6, starting transfers between devices: 28.6 us -> 7.1 us  [shift(): lax.ppermute(value, 'seq', [(d, (d + by) % count) for d in range(count)])]
    ppermute x12, waiting for transfers between devices: 0.04 us -> 11.4 us  [forward(): return lax.ppermute(value, ('seq', 'tp'), pairs)]
    unnamed x82 -> x16, local copies, waits for them, and re-layouts: 11.4 us -> 1.99 us
    ppermute x12, starting transfers between devices: 20.1 us -> 13.3 us  [forward(): return lax.ppermute(value, ('seq', 'tp'), pairs)]
    pallas_call x15 -> x17, Pallas kernels: 14.3 us -> 9.59 us  [the longest x1 2.91 us: shards(): call(state_kernel, (shape((chunks, N, width)), shape((chunks, 1, width)),...]
    squeeze x3 -> x0, local copies, waits for them, and re-layouts: 2.21 us -> none  [the longest x1 0.83 us: shards(): got = {(1, k): swap(sent[k], 1) for k in range(chunks)}]
  transfers between devices with their start and end apart: 18 -> 18, of which waited for: 3 -> 8; matrix products, arithmetic and copies ran while one was open for 5% -> 0% of each run, Pallas kernels for 17% -> 14%
where the time goes in v4:
time: 48.8 us; the launch traced here: 48.6 us
  starting transfers between devices  20.4 us (42%)
  waiting for transfers between devices  14.9 us (31%)
  Pallas kernels  10.5 us (22%)
  local copies, waits for them, and re-layouts  1.99 us (4%)
  between operations  0.86 us (2%)
    ppermute x12, starting transfers between devices, forward(): return lax.ppermute(value, ('seq', 'tp'), pairs)  13.3 us
    ppermute x12, waiting for transfers between devices, forward(): return lax.ppermute(value, ('seq', 'tp'), pairs)  11.4 us
    ppermute x6, starting transfers between devices, shift(): lax.ppermute(value, 'seq', [(d, (d + by) % count) for d in range(count)])  7.1 us
    ppermute x6, waiting for transfers between devices, shift(): lax.ppermute(value, 'seq', [(d, (d + by) % count) for d in range(count)])  3.52 us
    pallas_call x1, Pallas kernels, shards(): call(state_kernel, (shape((chunks, N, width)), shape((chunks, 1, width)),...  2.91 us
    pallas_call x2, Pallas kernels, outer_part(): call(functools.partial(outer_kernel, part, count), pltpu.HBM((tokens, lan...  2.71 us
    pallas_call x2, Pallas kernels, inner_part(): call(functools.partial(inner_kernel, g), (asked_shape, inner_shape) if g...  2.15 us
    unnamed x16, local copies, waits for them, and re-layouts  1.99 us
  transfers between devices with their start and end apart: 18, of which 8 were waited for; matrix products, arithmetic and copies ran while one was open for 0% of the time, Pallas kernels for 14%

profile of v4, /device:TPU:0, one launch (start us, length us, event | category | flops | bytes accessed | tf_op | source)
XLA Modules:
  0.0 48.6 jit_solution(13247850610069508031)
XLA Ops:
  0.6 0.0 copy-start
  0.6 2.9 %shard_map.131 = (f32[4,128,512]{2,1,0:T(8,128)S(1)}, f32[4,1,512]{2,1,0:T(1,128)S(1)}, f32[32,256]{1,0:T(8,128)S(1)}, f32[32,256]{1,0:T(8,128)S(1)}, bf16[256,2...) custom-call(bf16[256,2048]{1,0:T(8,128)(2,1)} %x_hbm.1, ...), custom_call_target="tpu_custom_call" | custom-call | flops 134217728 | bytes 2097152 | tf_op jit(solution)/shard_map/pallas_call | solution.py:406
  3.6 3.1 %collective-permute-start.2 = (bf16[128,512]{1,0:T(8,128)(2,1)S(1)}, bf16[128,512]{1,0:T(8,128)(2,1)S(1)}, u32[]{:S(2)}, u32[]{:S(2)}) collective-permute-start(bf16[128,512]{1,0:T(8,128)(2,1)S(1)} %get-tuple-element.50), channel_id=1, source_target_pairs={{0,4},{1,5},{2,6},{3,7},{4,0},{5,1},{6,2},{7,3},{8,12},{9,13},{10,... | collective-permute-start | bytes 393224 | tf_op jit(solution)/shard_map/ppermute | solution.py:442
  6.7 0.1 collective-permute-start.1
  6.7 0.0 copy-start.3
  6.7 0.0 copy-done
  6.7 0.7 %copy-done.3 = f32[32]{0:T(128)S(1)} copy-done((f32[32]{0:T(128)S(1)}, f32[32]{0:T(128)}, u32[]{:S(2)}) %copy-start.3) | copy-done | bytes 152
  7.4 1.1 %shard_map.132 = (bf16[4,4,256]{2,1,0:T(4,128)(2,1)S(1)}, f32[256,1024]{1,0:T(8,128)S(1)}) custom-call(bf16[256,2048]{1,0:T(8,128)(2,1)S(1)} %get-tuple-element.51.x_ref, bf16[256,256]{1,0:T(8,128)(2,1)S(1)} %get-tuple-element.52.b_ref, bf16[256,256]{1,0:T(8,128)(2,1)S(1)} %copy-done, f32[32,256]{1,0:T(8,128)S(1)} %get-tuple-element.45.cum_ref, ...), custom_call_target="tpu_custom_call" | custom-call | flops 134217728 | bytes 4194304 | tf_op jit(solution)/shard_map/pallas_call | solution.py:452
  8.5 4.0 %collective-permute-start.5 = (bf16[4,4,256]{2,1,0:T(4,128)(2,1)S(1)}, bf16[4,4,256]{2,1,0:T(4,128)(2,1)S(1)}, u32[]{:S(2)}, u32[]{:S(2)}) collective-permute-start(bf16[4,4,256]{2,1,0:T(4,128)(2,1)S(1)} %get-tuple-element.57.rest_0_), channel_id=1, source_target_pairs={{0,12},{4,0},{8,4},{12,8},{1,13},{5,1},{9,5},{13,9},{2,14},{6,2},{... | collective-permute-start | bytes 24584 | tf_op jit(solution)/shard_map/ppermute | solution.py:445
  12.5 0.0 collective-permute-start.4
  12.5 1.0 %collective-permute-start.3 = (bf16[4,4,256]{2,1,0:T(4,128)(2,1)S(1)}, bf16[4,4,256]{2,1,0:T(4,128)(2,1)S(1)}, u32[]{:S(2)}, u32[]{:S(2)}) collective-permute-start(bf16[4,4,256]{2,1,0:T(4,128)(2,1)S(1)} %get-tuple-element.57.rest_0_), channel_id=1, source_target_pairs={{0,4},{4,8},{8,12},{12,0},{1,5},{5,9},{9,13},{13,1},{2,6},{6,10},{... | collective-permute-start | bytes 24584 | tf_op jit(solution)/shard_map/ppermute | solution.py:445
  13.5 1.1 %shard_map.133.rest_1_.rest_4_.rest_2_ = f32[256,1024]{1,0:T(8,128)S(1)} custom-call(bf16[256,2048]{1,0:T(8,128)(2,1)S(1)} %get-tuple-element.51.x_ref, bf16[256,256]{1,0:T(8,128)(2,1)S(1)} %get-tuple-element.52.b_ref, bf16[256,256]{1,0:T(8,128)(2,1)S(1)} %copy-done, f32[32,256]{1,0:T(8,128)S(1)} %get-tuple-element.45.cum_ref, ...), custom_call_target="tpu_custom_call" | custom-call | flops 134217728 | bytes 4194304 | tf_op jit(solution)/shard_map/pallas_call | solution.py:452
  14.6 0.0 collective-permute-done.2.got_ref
  14.6 2.5 %collective-permute-start.7 = (bf16[128,512]{1,0:T(8,128)(2,1)S(1)}, bf16[128,512]{1,0:T(8,128)(2,1)S(1)}, u32[]{:S(2)}, u32[]{:S(2)}) collective-permute-start(bf16[128,512]{1,0:T(8,128)(2,1)S(1)} %get-tuple-element.61), channel_id=1, source_target_pairs={{0,4},{1,5},{2,6},{3,7},{4,0},{5,1},{6,2},{7,3},{8,12},{9,13},{10,... | collective-permute-start | bytes 393224 | tf_op jit(solution)/shard_map/ppermute | solution.py:442
  17.1 0.1 shard_map.134
  17.2 0.0 collective-permute-done.5.rest_3_
  17.2 0.1 collective-permute-start.8
  17.3 0.0 collective-permute-done.4.rest_2_
  17.3 0.8 %collective-permute-done.3.rest_1_ = bf16[4,4,256]{2,1,0:T(4,128)(2,1)S(1)} collective-permute-done((bf16[4,4,256]{2,1,0:T(4,128)(2,1)S(1)}, bf16[4,4,256]{2,1,0:T(4,128)(2,1)S(1)}, u32[]{:S(2)}, u32[]{:S(2)}) %collective-permute-start.3) | collective-permute-done | bytes 8224 | tf_op jit(solution)/shard_map/ppermute | solution.py:445
  18.0 0.0 copy-start.6
  18.1 0.0 copy-start.7
  18.1 0.7 %copy-done.6 = s32[8]{0:T(128)S(1)} copy-done((s32[8]{0:T(128)S(1)}, s32[8]{0:T(128)}, u32[]{:S(2)}) %copy-start.6) | copy-done | bytes 56
  18.7 0.0 copy-done.7
  18.7 0.9 %shard_map.135 = (f32[16,2048]{1,0:T(8,128)S(1)}, f32[16,32]{1,0:T(8,128)S(1)}, bf16[16,256]{1,0:T(8,128)(2,1)S(1)}) custom-call(bf16[256,2048]{1,0:T(8,128)(2,1)S(1)} %get-tuple-element.51.x_ref, bf16[256,256]{1,0:T(8,128)(2,1)S(1)} %get-tuple-element.52.b_ref, f32[32,256]{1,0:T(8,128)S(1)} %get-tuple-element.45.cum_ref, ...), custom_call_target="tpu_custom_call" | custom-call | flops 16777216 | bytes 2097152 | tf_op jit(solution)/shard_map/pallas_call | solution.py:464
  19.6 0.0 collective-permute-done.1.got_ref
  19.6 0.0 copy-start.1
  19.7 0.0 copy-start.4
  19.7 0.0 copy-start.2
  19.7 0.1 collective-permute-start.6
  19.8 1.6 %collective-permute-start = (bf16[128,512]{1,0:T(8,128)(2,1)S(1)}, bf16[128,512]{1,0:T(8,128)(2,1)S(1)}, u32[]{:S(2)}, u32[]{:S(2)}) collective-permute-start(bf16[128,512]{1,0:T(8,128)(2,1)S(1)} %get-tuple-element.46), channel_id=1, source_target_pairs={{0,4},{1,5},{2,6},{3,7},{4,0},{5,1},{6,2},{7,3},{8,12},{9,13},{10,... | collective-permute-start | bytes 393224 | tf_op jit(solution)/shard_map/ppermute | solution.py:442
  21.4 0.0 copy-start.5
  21.4 0.0 copy-done.1
  21.4 0.0 copy-done.4
  21.4 0.0 copy-done.2
  21.4 0.6 %copy-done.5 = f32[32]{0:T(128)S(1)} copy-done((f32[32]{0:T(128)S(1)}, f32[32]{0:T(128)}, u32[]{:S(2)}) %copy-start.5) | copy-done | bytes 152
  22.0 0.4 shard_map.137
  22.5 0.0 collective-permute-done.8.got_ref
  22.5 0.0 collective-permute-done.7.got_ref
  22.6 0.1 collective-permute-start.10
  22.6 0.0 collective-permute-done.6.got_ref
  22.7 3.0 %collective-permute-done.got_ref = bf16[128,512]{1,0:T(8,128)(2,1)S(1)} collective-permute-done((bf16[128,512]{1,0:T(8,128)(2,1)S(1)}, bf16[128,512]{1,0:T(8,128)(2,1)S(1)}, u32[]{:S(2)}, u32[]{:S(2)}) %collective-permute-start) | collective-permute-done | bytes 131104 | tf_op jit(solution)/shard_map/ppermute | solution.py:442
  25.8 0.1 collective-permute-start.9
  25.8 1.7 %collective-permute-start.13 = (bf16[128,512]{1,0:T(8,128)(2,1)S(1)}, bf16[128,512]{1,0:T(8,128)(2,1)S(1)}, u32[]{:S(2)}, u32[]{:S(2)}) collective-permute-start(bf16[128,512]{1,0:T(8,128)(2,1)S(1)} %get-tuple-element.74), channel_id=1, source_target_pairs={{0,4},{1,5},{2,6},{3,7},{4,0},{5,1},{6,2},{7,3},{8,12},{9,13},{10,... | collective-permute-start | bytes 393224 | tf_op jit(solution)/shard_map/ppermute | solution.py:442
  27.6 0.3 collective-permute-start.12
  27.9 0.0 collective-permute-done.10.got_ref
  28.0 1.9 %collective-permute-start.14 = (bf16[128,512]{1,0:T(8,128)(2,1)S(1)}, bf16[128,512]{1,0:T(8,128)(2,1)S(1)}, u32[]{:S(2)}, u32[]{:S(2)}) collective-permute-start(bf16[128,512]{1,0:T(8,128)(2,1)S(1)} %get-tuple-element.75), channel_id=1, source_target_pairs={{0,4},{1,5},{2,6},{3,7},{4,0},{5,1},{6,2},{7,3},{8,12},{9,13},{10,... | collective-permute-start | bytes 393224 | tf_op jit(solution)/shard_map/ppermute | solution.py:442
  29.9 0.0 collective-permute-done.9.got_ref
  30.0 1.7 %collective-permute-start.11 = (bf16[128,512]{1,0:T(8,128)(2,1)S(1)}, bf16[128,512]{1,0:T(8,128)(2,1)S(1)}, u32[]{:S(2)}, u32[]{:S(2)}) collective-permute-start(bf16[128,512]{1,0:T(8,128)(2,1)S(1)} %get-tuple-element.72), channel_id=1, source_target_pairs={{0,4},{1,5},{2,6},{3,7},{4,0},{5,1},{6,2},{7,3},{8,12},{9,13},{10,... | collective-permute-start | bytes 393224 | tf_op jit(solution)/shard_map/ppermute | solution.py:442
  31.6 0.6 %collective-permute-done.13.rest_1_ = bf16[128,512]{1,0:T(8,128)(2,1)S(1)} collective-permute-done((bf16[128,512]{1,0:T(8,128)(2,1)S(1)}, bf16[128,512]{1,0:T(8,128)(2,1)S(1)}, u32[]{:S(2)}, u32[]{:S(2)}) %collective-permute-start.13) | collective-permute-done | bytes 131104 | tf_op jit(solution)/shard_map/ppermute | solution.py:442
  32.2 2.8 %collective-permute-done.12.rest_0_ = bf16[128,512]{1,0:T(8,128)(2,1)S(1)} collective-permute-done((bf16[128,512]{1,0:T(8,128)(2,1)S(1)}, bf16[128,512]{1,0:T(8,128)(2,1)S(1)}, u32[]{:S(2)}, u32[]{:S(2)}) %collective-permute-start.12) | collective-permute-done | bytes 131104 | tf_op jit(solution)/shard_map/ppermute | solution.py:442
  35.0 2.8 %collective-permute-done.14.rest_2_ = bf16[128,512]{1,0:T(8,128)(2,1)S(1)} collective-permute-done((bf16[128,512]{1,0:T(8,128)(2,1)S(1)}, bf16[128,512]{1,0:T(8,128)(2,1)S(1)}, u32[]{:S(2)}, u32[]{:S(2)}) %collective-permute-start.14) | collective-permute-done | bytes 131104 | tf_op jit(solution)/shard_map/ppermute | solution.py:442
  37.8 0.2 shard_map.146
  38.0 2.1 %collective-permute-done.11.rest_0_ = bf16[128,512]{1,0:T(8,128)(2,1)S(1)} collective-permute-done((bf16[128,512]{1,0:T(8,128)(2,1)S(1)}, bf16[128,512]{1,0:T(8,128)(2,1)S(1)}, u32[]{:S(2)}, u32[]{:S(2)}) %collective-permute-start.11) | collective-permute-done | bytes 131104 | tf_op jit(solution)/shard_map/ppermute | solution.py:442
  40.2 0.1 shard_map.147
  40.3 0.7 %collective-permute-start.15 = (f32[4,2048]{1,0:T(4,128)S(1)}, f32[4,2048]{1,0:T(4,128)S(1)}, u32[]{:S(2)}, u32[]{:S(2)}) collective-permute-start(f32[4,2048]{1,0:T(4,128)S(1)} %get-tuple-element.85), channel_id=1, source_target_pairs={{0,12},{4,0},{8,4},{12,8},{1,13},{5,1},{9,5},{13,9},{2,14},{6,2},{... | collective-permute-start | bytes 98312 | tf_op jit(solution)/shard_map/ppermute | solution.py:445
  41.0 1.2 %collective-permute-start.16 = (f32[4,2048]{1,0:T(4,128)S(1)}, f32[4,2048]{1,0:T(4,128)S(1)}, u32[]{:S(2)}, u32[]{:S(2)}) collective-permute-start(f32[4,2048]{1,0:T(4,128)S(1)} %get-tuple-element.86), channel_id=1, source_target_pairs={{0,8},{4,12},{8,0},{12,4},{1,9},{5,13},{9,1},{13,5},{2,10},{6,14},... | collective-permute-start | bytes 98312 | tf_op jit(solution)/shard_map/ppermute | solution.py:445
  42.2 0.2 collective-permute-start.17
  42.4 1.6 %shard_map.144.rest_3_ = bf16[256,2048]{1,0:T(8,128)(2,1)} custom-call(bf16[256,256]{1,0:T(8,128)(2,1)S(1)} %copy-done, f32[32,256]{1,0:T(8,128)S(1)} %get-tuple-element.45.cum_ref, bf16[4,128,512]{2,1,0:T(8,128)(2,1)S(1)} %get-tuple-element.71.carry_ref, bf16[128,512]{1,0:T(8,128)(2,1)S(1)} %collective-permute-done.12.rest_0_, ...), custom_call_target="tpu_custom_call" | custom-call | flops 134217728 | bytes 4194304 | tf_op jit(solution)/shard_map/pallas_call | solution.py:514
  44.0 1.1 %shard_map.145 = bf16[256,2048]{1,0:T(8,128)(2,1)} custom-call(bf16[256,256]{1,0:T(8,128)(2,1)S(1)} %copy-done, f32[32,256]{1,0:T(8,128)S(1)} %get-tuple-element.45.cum_ref, bf16[4,128,512]{2,1,0:T(8,128)(2,1)S(1)} %get-tuple-element.71.carry_ref, bf16[128,512]{1,0:T(8,128)(2,1)S(1)} %collective-permute-done.11.rest_0_, ...), custom_call_target="tpu_custom_call", output_to_operand_aliasing={{}: (6, {})} | custom-call | flops 134217728 | bytes 4194304 | tf_op jit(solution)/shard_map/pallas_call | solution.py:514
  45.1 0.0 collective-permute-done.15.rest_1_
  45.1 0.7 %collective-permute-done.16.rest_2_ = f32[4,2048]{1,0:T(4,128)S(1)} collective-permute-done((f32[4,2048]{1,0:T(4,128)S(1)}, f32[4,2048]{1,0:T(4,128)S(1)}, u32[]{:S(2)}, u32[]{:S(2)}) %collective-permute-start.16) | collective-permute-done | bytes 32800 | tf_op jit(solution)/shard_map/ppermute | solution.py:445
  45.8 2.1 %collective-permute-done.17.rest_3_ = f32[4,2048]{1,0:T(4,128)S(1)} collective-permute-done((f32[4,2048]{1,0:T(4,128)S(1)}, f32[4,2048]{1,0:T(4,128)S(1)}, u32[]{:S(2)}, u32[]{:S(2)}) %collective-permute-start.17) | collective-permute-done | bytes 32800 | tf_op jit(solution)/shard_map/ppermute | solution.py:445
  47.9 0.7 %shard_map.148 = bf16[4,4,2048]{2,1,0:T(4,128)(2,1)} custom-call(f32[4,4,2048]{2,1,0:T(4,128)S(1)} %get-tuple-element.63.rest_1_.keep_ref, f32[4,4,2048]{2,1,0:T(4,128)S(1)} %get-tuple-element.76.fresh_ref, f32[4,4,128]{2,1,0:T(4,128)S(1)} %get-tuple-element.77.held_ref, f32[4,2048]{1,0:T(4,128)S(1)} %get-tuple-element.84.rest_0_, ...), custom_call_target="tpu_custom_call" | custom-call | flops 131072 | bytes 524288 | tf_op jit(solution)/shard_map/pallas_call | solution.py:537
  (7 shorter events, 0.3 us)
Async XLA Ops:
  0.6 6.1 %copy-start = (bf16[256,256]{1,0:T(8,128)(2,1)S(1)}, bf16[256,256]{1,0:T(8,128)(2,1)}, u32[]{:S(2)}) copy-start(bf16[256,256]{1,0:T(8,128)(2,1)} %c_ref.7) | copy-start | bytes 393220
  3.6 11.0 %collective-permute-start.2 = (bf16[128,512]{1,0:T(8,128)(2,1)S(1)}, bf16[128,512]{1,0:T(8,128)(2,1)S(1)}, u32[]{:S(2)}, u32[]{:S(2)}) collective-permute-start(bf16[128,512]{1,0:T(8,128)(2,1)S(1)} %get-tuple-element.50), channel_id=1, source_target_pairs={{0,4},{1,5},{2,6},{3,7},{4,0},{5,1},{6,2},{7,3},{8,12},{9,13},{10,... | collective-permute-start | bytes 393224 | tf_op jit(solution)/shard_map/ppermute | solution.py:442
  6.7 13.0 %collective-permute-start.1 = (bf16[128,512]{1,0:T(8,128)(2,1)S(1)}, bf16[128,512]{1,0:T(8,128)(2,1)S(1)}, u32[]{:S(2)}, u32[]{:S(2)}) collective-permute-start(bf16[128,512]{1,0:T(8,128)(2,1)S(1)} %get-tuple-element.49), channel_id=1, source_target_pairs={{0,4},{1,5},{2,6},{3,7},{4,0},{5,1},{6,2},{7,3},{8,12},{9,13},{10,... | collective-permute-start | bytes 393224 | tf_op jit(solution)/shard_map/ppermute | solution.py:442
  6.7 0.7 %copy-start.3 = (f32[32]{0:T(128)S(1)}, f32[32]{0:T(128)}, u32[]{:S(2)}) copy-start(f32[32]{0:T(128)} %param.17) | copy-start | bytes 388
  8.5 8.7 %collective-permute-start.5 = (bf16[4,4,256]{2,1,0:T(4,128)(2,1)S(1)}, bf16[4,4,256]{2,1,0:T(4,128)(2,1)S(1)}, u32[]{:S(2)}, u32[]{:S(2)}) collective-permute-start(bf16[4,4,256]{2,1,0:T(4,128)(2,1)S(1)} %get-tuple-element.57.rest_0_), channel_id=1, source_target_pairs={{0,12},{4,0},{8,4},{12,8},{1,13},{5,1},{9,5},{13,9},{2,14},{6,2},{... | collective-permute-start | bytes 24584 | tf_op jit(solution)/shard_map/ppermute | solution.py:445
  12.5 4.8 %collective-permute-start.4 = (bf16[4,4,256]{2,1,0:T(4,128)(2,1)S(1)}, bf16[4,4,256]{2,1,0:T(4,128)(2,1)S(1)}, u32[]{:S(2)}, u32[]{:S(2)}) collective-permute-start(bf16[4,4,256]{2,1,0:T(4,128)(2,1)S(1)} %get-tuple-element.57.rest_0_), channel_id=1, source_target_pairs={{0,8},{4,12},{8,0},{12,4},{1,9},{5,13},{9,1},{13,5},{2,10},{6,14},... | collective-permute-start | bytes 24584 | tf_op jit(solution)/shard_map/ppermute | solution.py:445
  12.5 5.6 %collective-permute-start.3 = (bf16[4,4,256]{2,1,0:T(4,128)(2,1)S(1)}, bf16[4,4,256]{2,1,0:T(4,128)(2,1)S(1)}, u32[]{:S(2)}, u32[]{:S(2)}) collective-permute-start(bf16[4,4,256]{2,1,0:T(4,128)(2,1)S(1)} %get-tuple-element.57.rest_0_), channel_id=1, source_target_pairs={{0,4},{4,8},{8,12},{12,0},{1,5},{5,9},{9,13},{13,1},{2,6},{6,10},{... | collective-permute-start | bytes 24584 | tf_op jit(solution)/shard_map/ppermute | solution.py:445
  14.6 7.9 %collective-permute-start.7 = (bf16[128,512]{1,0:T(8,128)(2,1)S(1)}, bf16[128,512]{1,0:T(8,128)(2,1)S(1)}, u32[]{:S(2)}, u32[]{:S(2)}) collective-permute-start(bf16[128,512]{1,0:T(8,128)(2,1)S(1)} %get-tuple-element.61), channel_id=1, source_target_pairs={{0,4},{1,5},{2,6},{3,7},{4,0},{5,1},{6,2},{7,3},{8,12},{9,13},{10,... | collective-permute-start | bytes 393224 | tf_op jit(solution)/shard_map/ppermute | solution.py:442
  17.2 5.3 %collective-permute-start.8 = (bf16[128,512]{1,0:T(8,128)(2,1)S(1)}, bf16[128,512]{1,0:T(8,128)(2,1)S(1)}, u32[]{:S(2)}, u32[]{:S(2)}) collective-permute-start(bf16[128,512]{1,0:T(8,128)(2,1)S(1)} %get-tuple-element.58.rest_4_), channel_id=1, source_target_pairs={{0,1},{1,0},{2,3},{3,2},{4,8},{5,9},{6,10},{7,11},{8,4},{9,5},{10,... | collective-permute-start | bytes 393224 | tf_op jit(solution)/shard_map/ppermute | solution.py:442
  18.0 0.7 %copy-start.6 = (s32[8]{0:T(128)S(1)}, s32[8]{0:T(128)}, u32[]{:S(2)}) copy-start(s32[8]{0:T(128)} %param.18) | copy-start | bytes 100
  18.1 0.7 %copy-start.7 = (s32[8]{0:T(128)S(1)}, s32[8]{0:T(128)}, u32[]{:S(2)}) copy-start(s32[8]{0:T(128)} %param.19) | copy-start | bytes 100
  19.6 1.7 %copy-start.1 = (bf16[1,4,4,2048]{3,2,1,0:T(4,128)(2,1)S(1)}, bf16[1,4,4,2048]{3,2,1,0:T(4,128)(2,1)}, u32[]{:S(2)}) copy-start(bf16[1,4,4,2048]{3,2,1,0:T(4,128)(2,1)} %param.20) | copy-start | bytes 196612
  19.7 1.7 %copy-start.4 = (bf16[1,4,4,32]{3,2,1,0:T(4,128)(2,1)S(1)}, bf16[1,4,4,32]{3,2,1,0:T(4,128)(2,1)}, u32[]{:S(2)}) copy-start(bf16[1,4,4,32]{3,2,1,0:T(4,128)(2,1)} %param.23) | copy-start | bytes 3076
  19.7 1.7 %copy-start.2 = (bf16[1,4,4,256]{3,2,1,0:T(4,128)(2,1)S(1)}, bf16[1,4,4,256]{3,2,1,0:T(4,128)(2,1)}, u32[]{:S(2)}) copy-start(bf16[1,4,4,256]{3,2,1,0:T(4,128)(2,1)} %param.21) | copy-start | bytes 24580
  19.7 2.9 %collective-permute-start.6 = (bf16[128,512]{1,0:T(8,128)(2,1)S(1)}, bf16[128,512]{1,0:T(8,128)(2,1)S(1)}, u32[]{:S(2)}, u32[]{:S(2)}) collective-permute-start(bf16[128,512]{1,0:T(8,128)(2,1)S(1)} %get-tuple-element.60.rest_0_), channel_id=1, source_target_pairs={{0,1},{1,0},{2,3},{3,2},{4,8},{5,9},{6,10},{7,11},{8,4},{9,5},{10,... | collective-permute-start | bytes 393224 | tf_op jit(solution)/shard_map/ppermute | solution.py:442
  19.8 5.9 %collective-permute-start = (bf16[128,512]{1,0:T(8,128)(2,1)S(1)}, bf16[128,512]{1,0:T(8,128)(2,1)S(1)}, u32[]{:S(2)}, u32[]{:S(2)}) collective-permute-start(bf16[128,512]{1,0:T(8,128)(2,1)S(1)} %get-tuple-element.46), channel_id=1, source_target_pairs={{0,4},{1,5},{2,6},{3,7},{4,0},{5,1},{6,2},{7,3},{8,12},{9,13},{10,... | collective-permute-start | bytes 393224 | tf_op jit(solution)/shard_map/ppermute | solution.py:442
  21.4 0.7 %copy-start.5 = (f32[32]{0:T(128)S(1)}, f32[32]{0:T(128)}, u32[]{:S(2)}) copy-start(f32[32]{0:T(128)} %param.16) | copy-start | bytes 388
  22.6 5.4 %collective-permute-start.10 = (bf16[128,512]{1,0:T(8,128)(2,1)S(1)}, bf16[128,512]{1,0:T(8,128)(2,1)S(1)}, u32[]{:S(2)}, u32[]{:S(2)}) collective-permute-start(bf16[128,512]{1,0:T(8,128)(2,1)S(1)} %get-tuple-element.68), channel_id=1, source_target_pairs={{0,1},{1,0},{2,3},{3,2},{4,8},{5,9},{6,10},{7,11},{8,4},{9,5},{10,... | collective-permute-start | bytes 393224 | tf_op jit(solution)/shard_map/ppermute | solution.py:442
  25.8 4.2 %collective-permute-start.9 = (bf16[128,512]{1,0:T(8,128)(2,1)S(1)}, bf16[128,512]{1,0:T(8,128)(2,1)S(1)}, u32[]{:S(2)}, u32[]{:S(2)}) collective-permute-start(bf16[128,512]{1,0:T(8,128)(2,1)S(1)} %get-tuple-element.67), channel_id=1, source_target_pairs={{0,1},{1,0},{2,3},{3,2},{4,8},{5,9},{6,10},{7,11},{8,4},{9,5},{10,... | collective-permute-start | bytes 393224 | tf_op jit(solution)/shard_map/ppermute | solution.py:442
  25.8 6.4 %collective-permute-start.13 = (bf16[128,512]{1,0:T(8,128)(2,1)S(1)}, bf16[128,512]{1,0:T(8,128)(2,1)S(1)}, u32[]{:S(2)}, u32[]{:S(2)}) collective-permute-start(bf16[128,512]{1,0:T(8,128)(2,1)S(1)} %get-tuple-element.74), channel_id=1, source_target_pairs={{0,4},{1,5},{2,6},{3,7},{4,0},{5,1},{6,2},{7,3},{8,12},{9,13},{10,... | collective-permute-start | bytes 393224 | tf_op jit(solution)/shard_map/ppermute | solution.py:442
  27.6 7.4 %collective-permute-start.12 = (bf16[128,512]{1,0:T(8,128)(2,1)S(1)}, bf16[128,512]{1,0:T(8,128)(2,1)S(1)}, u32[]{:S(2)}, u32[]{:S(2)}) collective-permute-start(bf16[128,512]{1,0:T(8,128)(2,1)S(1)} %get-tuple-element.73), channel_id=1, source_target_pairs={{0,4},{1,5},{2,6},{3,7},{4,0},{5,1},{6,2},{7,3},{8,12},{9,13},{10,... | collective-permute-start | bytes 393224 | tf_op jit(solution)/shard_map/ppermute | solution.py:442
  28.0 9.8 %collective-permute-start.14 = (bf16[128,512]{1,0:T(8,128)(2,1)S(1)}, bf16[128,512]{1,0:T(8,128)(2,1)S(1)}, u32[]{:S(2)}, u32[]{:S(2)}) collective-permute-start(bf16[128,512]{1,0:T(8,128)(2,1)S(1)} %get-tuple-element.75), channel_id=1, source_target_pairs={{0,4},{1,5},{2,6},{3,7},{4,0},{5,1},{6,2},{7,3},{8,12},{9,13},{10,... | collective-permute-start | bytes 393224 | tf_op jit(solution)/shard_map/ppermute | solution.py:442
  30.0 10.2 %collective-permute-start.11 = (bf16[128,512]{1,0:T(8,128)(2,1)S(1)}, bf16[128,512]{1,0:T(8,128)(2,1)S(1)}, u32[]{:S(2)}, u32[]{:S(2)}) collective-permute-start(bf16[128,512]{1,0:T(8,128)(2,1)S(1)} %get-tuple-element.72), channel_id=1, source_target_pairs={{0,4},{1,5},{2,6},{3,7},{4,0},{5,1},{6,2},{7,3},{8,12},{9,13},{10,... | collective-permute-start | bytes 393224 | tf_op jit(solution)/shard_map/ppermute | solution.py:442
  40.3 4.8 %collective-permute-start.15 = (f32[4,2048]{1,0:T(4,128)S(1)}, f32[4,2048]{1,0:T(4,128)S(1)}, u32[]{:S(2)}, u32[]{:S(2)}) collective-permute-start(f32[4,2048]{1,0:T(4,128)S(1)} %get-tuple-element.85), channel_id=1, source_target_pairs={{0,12},{4,0},{8,4},{12,8},{1,13},{5,1},{9,5},{13,9},{2,14},{6,2},{... | collective-permute-start | bytes 98312 | tf_op jit(solution)/shard_map/ppermute | solution.py:445
  41.0 4.8 %collective-permute-start.16 = (f32[4,2048]{1,0:T(4,128)S(1)}, f32[4,2048]{1,0:T(4,128)S(1)}, u32[]{:S(2)}, u32[]{:S(2)}) collective-permute-start(f32[4,2048]{1,0:T(4,128)S(1)} %get-tuple-element.86), channel_id=1, source_target_pairs={{0,8},{4,12},{8,0},{12,4},{1,9},{5,13},{9,1},{13,5},{2,10},{6,14},... | collective-permute-start | bytes 98312 | tf_op jit(solution)/shard_map/ppermute | solution.py:445
  42.2 5.7 %collective-permute-start.17 = (f32[4,2048]{1,0:T(4,128)S(1)}, f32[4,2048]{1,0:T(4,128)S(1)}, u32[]{:S(2)}, u32[]{:S(2)}) collective-permute-start(f32[4,2048]{1,0:T(4,128)S(1)} %get-tuple-element.87), channel_id=1, source_target_pairs={{0,4},{4,8},{8,12},{12,0},{1,5},{5,9},{9,13},{13,1},{2,6},{6,10},{... | collective-permute-start | bytes 98312 | tf_op jit(solution)/shard_map/ppermute | solution.py:445

commit v5 on v4

--- a/solution.py
+++ b/solution.py
@@ -84,35 +84,35 @@
     return jnp.where(keep(row, column), 1.0, 0.0).astype(BF16)
 
 
-def state_kernel(
-    x_hbm, b_hbm, dt_hbm, a_hbm, asked_hbm, total_ref, decay_ref, cum_ref, row_ref,
-    x_ref, b_ref, asked_ref, *rest,
-):
-    sent_refs, (dt_ref, a_ref, sems) = rest[:-3], rest[-3:]
+def state_kernel(kept, chunks, ride, *refs):
+    hbm, refs = refs[: kept + 1], refs[kept + 1 :]
+    here, refs = refs[:kept], refs[kept:]
+    total_ref, decay_ref, cum_ref, row_ref = refs[:4]
+    sent_refs, (dt_ref, sems) = refs[4 : 4 + chunks], refs[4 + chunks :]
+    x_ref, b_ref, a_ref, asked_ref = here[:4]
     heads, tokens = dt_ref.shape
     spans = tokens // SPAN
-    chunks, _, width = total_ref.shape
+    width = total_ref.shape[2]
     per_group = H // G
     groups = heads // per_group
     group_lanes = per_group * P_SIZE
+    dt_copy = pltpu.make_async_copy(hbm[kept], dt_ref, sems.at[0])
     copies = [
-        pltpu.make_async_copy(dt_hbm, dt_ref, sems.at[0]),
-        pltpu.make_async_copy(a_hbm, a_ref, sems.at[1]),
-        pltpu.make_async_copy(b_hbm, b_ref, sems.at[2]),
+        pltpu.make_async_copy(hbm[i], here[i], sems.at[i]) for i in range(1, kept)
     ]
+    x_copies = []
     for g in range(groups):
         lanes = slice(g * group_lanes, (g + 1) * group_lanes)
-        copies.append(
-            pltpu.make_async_copy(x_hbm.at[:, lanes], x_ref.at[:, lanes], sems.at[3 + g])
+        x_copies.append(
+            pltpu.make_async_copy(hbm[0].at[:, lanes], x_ref.at[:, lanes], sems.at[kept + g])
         )
-    copies.append(pltpu.make_async_copy(asked_hbm, asked_ref, sems.at[3 + groups]))
-    for copy in copies:
+    for copy in [dt_copy, copies[1], copies[0], *x_copies, *copies[2:]]:
         copy.start()
     upper = triangle(lambda s, t: s <= t)
     eye = lax.broadcasted_iota(jnp.int32, (heads, heads), 0) == lax.broadcasted_iota(
         jnp.int32, (heads, heads), 1
     )
-    copies[0].wait()
+    dt_copy.wait()
     copies[1].wait()
     a_column = jnp.sum(jnp.where(eye, a_ref[...], 0.0), axis=1, keepdims=True)
     step = softplus(dt_ref[...].astype(F32))
@@ -129,10 +129,10 @@
     cum = jnp.concatenate(cums, axis=1)
     cum_ref[...] = cum
     row_ref[...] = jnp.log2(step) - cum
-    copies[2].wait()
+    copies[0].wait()
     for g in range(groups):
         turned = b_ref[:, g * N : (g + 1) * N].astype(F32).T.astype(BF16)
-        copies[3 + g].wait()
+        x_copies[g].wait()
         for k in range(chunks):
             first = k * width
             if first // group_lanes != g:
@@ -141,22 +141,40 @@
             scaled = (x_ref[:, lanes].astype(F32) * over_lanes(weight, first, width)).astype(BF16)
             total = dot(turned, scaled)
             total_ref[k] = total
-            sent_refs[k][...] = total.astype(BF16)
+            sent_refs[k][:N] = total.astype(BF16)
             decay_ref[k] = over_lanes(whole, first, width, 3)
-    copies[-1].wait()
-
-
-def pass_kernel(hop, k, got_ref, total_ref, decay_ref, *rest):
+    for copy in copies[2:]:
+        copy.wait()
+    if ride:
+        own = flat(asked_ref).astype(BF16)
+        sent_refs[0][N:] = jnp.concatenate([own, own], axis=1)
+
+
+def flat(ref):
+    return jnp.concatenate([ref[i].astype(F32) for i in range(ref.shape[0])], axis=0)
+
+
+def pass_kernel(hop, k, ride, got_ref, total_ref, decay_ref, *rest):
     moving_ref, carry_ref = rest[-2:]
-    first = hop == 1 and k == 0
-    if first:
+    me = lax.axis_index("seq")
+    if hop == 1 and k == 0:
         carry_ref[...] = jnp.zeros_like(carry_ref)
-    got = got_ref[...]
-    moving_ref[...] = (total_ref[k] + decay_ref[k] * got.astype(F32)).astype(BF16)
-
-    @pl.when(lax.axis_index("seq") == hop)
+    got = got_ref[:N]
+    moving_ref[:N] = (total_ref[k] + decay_ref[k] * got.astype(F32)).astype(BF16)
+
+    @pl.when(me == hop)
     def _():
         carry_ref[k] = got
+
+    if ride and k == 0:
+        tail = got_ref[N:]
+        if hop == 1:
+            own = rest[0][N:]
+            names = tail.shape[1] // 2
+            lane = lax.broadcasted_iota(jnp.int32, tail.shape, 1)
+            mine = (lane // names) == lax.rem(me, 2)
+            tail = jnp.where(mine, own.astype(F32), tail.astype(F32)).astype(BF16)
+        moving_ref[N:] = tail
 
 
 def pair_halves(x_part):
@@ -175,7 +193,7 @@
 
 def inner_kernel(g, x_ref, b_ref, c_ref, cum_ref, row_ref, d_ref, *rest):
     inner_ref = rest[-1]
-    if g == 0:
+    if len(rest) > 1:
         asked_ref, handed_ref, inner_ref = rest
         handed_ref[...] = asked_ref[...]
     heads, tokens = cum_ref.shape
@@ -222,17 +240,35 @@
             inner_ref[mine, here] = dot(left, right) + skip * x_part[mine].astype(F32)
 
 
-def ask_kernel(count, x_ref, b_ref, cum_ref, row_ref, len_ref, owner_ref, *rest):
-    ask_refs = rest[:count]
-    local_ref, gain_ref, asked_ref = rest[-3:]
+def ask_kernel(count, ride, x_ref, b_ref, cum_ref, row_ref, len_ref, owner_ref, *rest):
+    local_ref, gain_ref, next_ref = rest[-3:]
     heads, tokens = cum_ref.shape
     spans = tokens // SPAN
     asks = local_ref.shape[0]
     per_group = H // G
     groups = heads // per_group
     me = lax.axis_index("seq")
-    asked = jnp.concatenate([ref[me].astype(F32) for ref in ask_refs], axis=0).astype(BF16)
-    asked_ref[...] = asked
+    if ride:
+        near, middle, far = [ref[N:].astype(F32) for ref in rest[:3]]
+        far = jnp.where((me == 1) | (me == 2), middle, far)
+        halves = (jnp.where(me < 2, near, far), jnp.where(me < 2, far, near))
+        names = near.shape[1] // 2
+        blocks = [half[:, i * names : (i + 1) * names] for half in halves for i in range(2)]
+    else:
+        blocks = [flat(ref) for ref in rest[:count]]
+    blocks = jnp.concatenate(blocks, axis=0).astype(BF16)
+    row = lax.broadcasted_iota(jnp.int32, (asks, asks * count), 0)
+    column = lax.broadcasted_iota(jnp.int32, (asks, asks * count), 1)
+    place = row // STEPS
+    if ride:
+        place = lax.rem(me + count - place, count)
+
+    def of_source(source):
+        wanted = place * asks + source * STEPS + row % STEPS
+        return dot(jnp.where(column == wanted, 1.0, 0.0).astype(BF16), blocks).astype(BF16)
+
+    asked = of_source(me)
+    next_ref[...] = of_source(lax.rem(me + 1, count))
     block = lax.broadcasted_iota(jnp.int32, (asks, 1), 0) // STEPS
     spot = len_ref[...] - 1 - me * tokens
     mine = (owner_ref[...] == lax.rem(me + count - block, count)) & (spot >= 0) & (spot < tokens)
@@ -247,7 +283,8 @@
     ask_start = starts[0]
     for i in range(1, spans):
         ask_start = jnp.where(spot >= i * SPAN, starts[i], ask_start)
-    gain_ref[...] = near_ask + ask_start
+    gain = near_ask + ask_start
+    gain_ref[...] = jnp.concatenate([gain] * (gain_ref.shape[1] // heads), axis=1)
     columns = []
     for j in range(spans):
         column = near_ask
@@ -270,27 +307,31 @@
             local_ref[:, lanes] = dot(jnp.concatenate(parts, axis=1), right)
 
 
-def read_kernel(chunks, filed, gain_ref, asked_ref, local_ref, carry_ref, *rest):
-    got_refs, rest = rest[: len(chunks)], rest[len(chunks) :]
-    read_refs = rest[len(rest) // 2 :] if filed else rest
-    width = got_refs[0].shape[1]
-    count = len(read_refs)
-    last = lax.axis_index("seq") == count - 1
-    gain = jnp.exp2(gain_ref[...])
-    for got_ref, k in zip(got_refs, chunks):
+def message_kernel(count, chunks, local_ref, gain_ref, next_ref, *rest):
+    moving_refs, message_refs = rest[:-count], rest[-count:]
+    me = lax.axis_index("seq")
+    lanes = local_ref.shape[1]
+    width = lanes // chunks
+    for k in range(chunks):
         first = k * width
         g = first // (H // G * P_SIZE)
-        state = jnp.where(last, got_ref[...], carry_ref[k])
-        carried = dot(asked_ref[:, g * N : (g + 1) * N], state)
-        reading = local_ref[:, first : first + width] + over_lanes(gain, first, width) * carried
+        state = moving_refs[k][:N].astype(F32)
+        for hop in range(1, count - 1):
+            state = jnp.where(me == hop, moving_refs[hop * chunks + k][:N].astype(F32), state)
+        reading = dot(next_ref[:, g * N : (g + 1) * N], state.astype(BF16))
         for r in range(count):
-            read_refs[r][:, first : first + width] = reading[r * STEPS : (r + 1) * STEPS]
+            message_refs[r][:, first : first + width] = reading[r * STEPS : (r + 1) * STEPS]
+    for r in range(count):
+        mine = slice(r * STEPS, (r + 1) * STEPS)
+        message_refs[r][:, lanes : 2 * lanes] = local_ref[mine]
+        message_refs[r][:, 2 * lanes :] = gain_ref[mine]
 
 
 def outer_kernel(chunks, count, c_ref, cum_ref, carry_ref, *rest):
     got_refs = rest[: len(chunks)]
     inner_refs = rest[len(chunks) :]
-    out_hbm, out_ref, sems = rest[-3:]
+    out_hbm, token_ref, out_ref, sems = rest[-4:]
+    token_ref[...] = jnp.zeros_like(token_ref)
     heads, tokens = cum_ref.shape
     spans = tokens // SPAN
     width = got_refs[0].shape[1]
@@ -307,7 +348,7 @@
     for i, k in enumerate(chunks):
         first = k * width
         g = first // group_lanes
-        state = jnp.where(last, got_refs[i][...], carry_ref[k])
+        state = jnp.where(last, got_refs[i][:N], carry_ref[k])
         carried = dot(c_ref[:, g * N : (g + 1) * N], state)
         inner = inner_refs[g][:, first - g * group_lanes : first - g * group_lanes + width]
         out_ref[i] = (inner + over_lanes(gain, first, width) * carried).astype(BF16)
@@ -331,10 +372,6 @@
     per_group = H // G
     groups = heads // per_group
     width = x_ref.shape[2]
-
-    def flat(ref):
-        return jnp.concatenate([ref[i].astype(F32) for i in range(count)], axis=0)
-
     turn = lax.broadcasted_iota(jnp.int32, (rows, 1), 0) % STEPS
     step = softplus(flat(dt_ref))
     rate = step * (jnp.exp(a_ref[...]) * -LOG2E)
@@ -370,12 +407,17 @@
 
 
 def finish_kernel(keep_ref, fresh_ref, held_ref, *rest):
-    back_refs, out_ref = rest[:-1], rest[-1]
+    back_refs, out_ref = rest[:-2], rest[-1]
     count = len(back_refs)
+    lanes = keep_ref.shape[2]
     me = lax.axis_index("seq")
+    gain = jnp.concatenate([ref[:, 2 * lanes :] for ref in back_refs], axis=0)
+    gain = over_lanes(jnp.exp2(gain[:, : lanes // P_SIZE]), 0, lanes)
     for r in range(count):
         source = lax.rem(me + r, count)
-        value = back_refs[r][...] * keep_ref[source] + fresh_ref[source]
+        carried = gain[r * STEPS : (r + 1) * STEPS] * back_refs[r - 1][:, :lanes]
+        reading = back_refs[r][:, lanes : 2 * lanes] + jnp.where(source > 0, carried, 0.0)
+        value = reading * keep_ref[source] + fresh_ref[source]
         held = held_ref[source][:, :1] > 0.0
         out_ref[source] = jnp.where(held, value, 0.0).astype(BF16)
 
@@ -393,43 +435,47 @@
     rows = count * STEPS
     chunks = CHUNKS if count <= 4 else groups
     width = lanes // chunks
-    a_row = a_log.reshape(1, heads)
-    d_row = d_skip.reshape(1, heads)
-    len_row = prompt_len.reshape(1, -1)
-    owner_row = owner.reshape(1, -1)
     anywhere = pl.BlockSpec(memory_space=pl.ANY)
     in_hbm = pl.BlockSpec(memory_space=pltpu.HBM)
     in_vmem = pl.BlockSpec(memory_space=pltpu.VMEM)
-    sent_shape = shape((N, width), BF16)
-    asked_shape = shape((count, STEPS, names), BF16)
-
-    total, decay, cum, row, x_here, b_here, asked_here, *sent = call(
-        state_kernel,
-        (
+    ride = count == 4 and width == 2 * names
+
+    def sent_shape(k):
+        return shape((N + rows * (ride and k == 0), width), BF16)
+
+    inputs = [
+        ssm_input,
+        bmat,
+        a_log.reshape(1, heads),
+        dec_c[0],
+        cmat,
+        d_skip.reshape(1, heads),
+        prompt_len.reshape(1, -1),
+        owner.reshape(1, -1),
+        dec_x[0],
+        dec_b[0],
+        dec_dt[0],
+    ]
+    results = call(
+        functools.partial(state_kernel, len(inputs), chunks, ride),
+        tuple(shape(value.shape, value.dtype) for value in inputs)
+        + (
             shape((chunks, N, width)),
             shape((chunks, 1, width)),
             shape((heads, tokens)),
             shape((heads, tokens)),
-            shape((tokens, lanes), BF16),
-            shape((tokens, names), BF16),
-            asked_shape,
         )
-        + (sent_shape,) * chunks,
+        + tuple(sent_shape(k) for k in range(chunks)),
         2 * tokens * N * lanes,
         4 * tokens * lanes,
-        in_specs=[in_hbm] * 5,
+        in_specs=[in_hbm] * (len(inputs) + 1),
         scratch_shapes=[
             pltpu.VMEM((heads, tokens), BF16),
-            pltpu.VMEM((1, heads), F32),
-            pltpu.SemaphoreType.DMA((4 + groups,)),
+            pltpu.SemaphoreType.DMA((len(inputs) + groups,)),
         ],
-    )(
-        pinned(ssm_input, pltpu.HBM),
-        pinned(bmat, pltpu.HBM),
-        pinned(dt_raw.T, pltpu.HBM),
-        pinned(a_row, pltpu.HBM),
-        pinned(dec_c[0], pltpu.HBM),
-    )
+    )(*[pinned(value, pltpu.HBM) for value in inputs + [dt_raw.T]])
+    x, b, a_row, asked_here, c, d_row, len_row, owner_row, x_dec, b_dec, dt_dec = results[:11]
+    total, decay, cum, row, *sent = results[11:]
 
     def forward(value, hop):
         pairs = []
@@ -445,29 +491,32 @@
         return lax.ppermute(value, "seq", [(d, (d + by) % count) for d in range(count)])
 
     got = {(1, k): forward(sent[k], 1) for k in range(chunks)}
+    moving = {(1, k): sent[k] for k in range(chunks)}
 
     def inner_part(g):
-        more = (asked_here,) if g == 0 else ()
+        more = (asked_here,) if g == 0 and not ride else ()
         inner_shape = shape((tokens, group_lanes))
         return call(
             functools.partial(inner_kernel, g),
-            (asked_shape, inner_shape) if g == 0 else inner_shape,
+            (shape(asked_here.shape, BF16), inner_shape) if more else inner_shape,
             2 * tokens * tokens * group_lanes,
             16 * tokens * group_lanes,
-        )(x_here, b_here, cmat, cum, row, d_row, *more)
-
-    handed, first_inner = inner_part(0)
-    inner = [first_inner] + [inner_part(g) for g in range(1, groups)]
-    asks = [handed] + [shift(handed, r) for r in range(1, count)]
+        )(x, b, c, cum, row, d_row, *more)
+
+    inner = [inner_part(g) for g in range(groups)]
+    if not ride:
+        handed, inner[0] = inner[0]
+        asks = [handed] + [shift(handed, r) for r in range(1, count)]
 
     def ask_part(*after):
+        blocks = (moving[2, 0], got[2, 0], got[3, 0]) if ride else asks
         return call(
-            functools.partial(ask_kernel, count),
-            (shape((rows, lanes)), shape((rows, heads)), shape((rows, names), BF16)),
+            functools.partial(ask_kernel, count, ride),
+            (shape((rows, lanes)), shape((rows, 128)), shape((rows, names), BF16)),
             2 * rows * tokens * lanes,
             4 * tokens * lanes,
-            in_specs=[in_vmem] * (6 + count) + [anywhere] * len(after),
-        )(x_here, b_here, cum, row, len_row, owner_row, *asks, *after)
+            in_specs=[in_vmem] * (6 + len(blocks)) + [anywhere] * len(after),
+        )(x, b, cum, row, len_row, owner_row, *blocks, *after)
 
     def fresh_part(*after):
         return call(
@@ -476,70 +525,68 @@
             64 * rows * lanes,
             16 * rows * lanes,
             in_specs=[in_vmem] * 8 + [anywhere] * len(after),
-        )(dec_x[0], dec_b[0], asked_here, dec_dt[0], a_row, d_row, len_row, owner_row, *after)
-
-    order = sorted((k + hop, hop, k) for hop in range(1, count - 1) for k in range(chunks))
-    work = {1: ask_part, 2: fresh_part}
-    results = {}
-    after = inner
-    carry = tie = None
-    for place, (_, hop, k) in enumerate(order):
-        if place in work:
-            results[place] = work[place](tie)
-            after = results[place][:1]
-        held_before = [] if carry is None else [carry]
-        moving, carry = call(
-            functools.partial(pass_kernel, hop, k),
-            (sent_shape, shape((chunks, N, width), BF16)),
-            2 * N * width,
-            8 * N * width,
-            in_specs=[in_vmem] * (3 + len(held_before)) + [anywhere] * len(after),
-            input_output_aliases={3: 1} if held_before else {},
-        )(got[hop, k], total, decay, *held_before, *after)
-        got[hop + 1, k] = forward(moving, hop + 1)
-        tie, after = moving, []
-    local, gain, asked = results[1]
-    keep, fresh, held = results[2]
-
-    def read_part(part, before):
-        return call(
-            functools.partial(read_kernel, part, bool(before)),
-            (shape((STEPS, lanes)),) * count,
-            2 * rows * N * lanes,
-            4 * N * lanes,
-            input_output_aliases={4 + len(part) + r: r for r in range(len(before))},
-        )(gain, asked, local, carry, *[got[count - 1, k] for k in part], *before)
-
-    def outer_part(part, before):
+        )(x_dec, b_dec, asked_here, dt_dec, a_row, d_row, len_row, owner_row, *after)
+
+    def outer_part(part, carry, before):
         return call(
             functools.partial(outer_kernel, part, count),
-            pltpu.HBM((tokens, lanes), BF16),
+            (pltpu.HBM((tokens, lanes), BF16), shape((8, 128))),
             2 * tokens * N * lanes,
             8 * tokens * lanes,
             in_specs=[in_vmem] * (3 + len(part) + groups) + [in_hbm] * len(before),
-            out_specs=in_hbm,
+            out_specs=(in_hbm, in_vmem),
             scratch_shapes=[
                 pltpu.VMEM((len(part), tokens, width), BF16),
                 pltpu.SemaphoreType.DMA((len(part),)),
             ],
             input_output_aliases={3 + len(part) + groups: 0} if before else {},
-        )(cmat, cum, carry, *[got[count - 1, k] for k in part], *inner, *before)
-
-    early, late = tuple(range(chunks - 1)), (chunks - 1,)
-    prefill = outer_part(early, [])
-    reading = read_part(early, [])
-    reading = read_part(late, reading)
-    back = [reading[0]] + [None] * (count - 1)
+        )(c, cum, carry, *[got[count - 1, k] for k in part], *inner, *before)
+
+    order = sorted((k + hop, hop, k) for hop in range(1, count - 1) for k in range(chunks))
+    early, late = tuple(range(chunks // 2)), tuple(range(chunks // 2, chunks))
+    after = inner
+    carry = tie = None
+    for _, hop, k in order:
+        if (hop, k) == (1, 1):
+            keep, fresh, held = fresh_part(tie)
+            after = [keep]
+        if (hop, k) == (count - 2, chunks - 2):
+            local, gain, asked_next = ask_part(tie)
+            after = [gain]
+        if (hop, k) == (count - 2, chunks - 1):
+            prefill, token = outer_part(early, carry, [])
+            after = [token]
+        tail = [sent[0]] if ride and (hop, k) == (1, 0) else []
+        filed = [] if carry is None else [carry]
+        moving[hop + 1, k], carry = call(
+            functools.partial(pass_kernel, hop, k, ride),
+            (sent_shape(k), shape((chunks, N, width), BF16)),
+            2 * N * width,
+            8 * N * width,
+            in_specs=[in_vmem] * (3 + len(filed) + len(tail)) + [anywhere] * len(after),
+            input_output_aliases={3: 1} if filed else {},
+        )(got[hop, k], total, decay, *filed, *tail, *after)
+        got[hop + 1, k] = forward(moving[hop + 1, k], hop + 1)
+        tie, after = moving[hop + 1, k], []
+
+    message = call(
+        functools.partial(message_kernel, count, chunks),
+        (shape((STEPS, 2 * lanes + 128)),) * count,
+        2 * rows * N * lanes,
+        4 * N * lanes,
+    )(local, gain, asked_next, *[moving[hop, k] for hop in range(1, count) for k in range(chunks)])
+    back = [message[0]] + [None] * (count - 1)
     for r in reversed(range(1, count)):
-        back[r] = shift(reading[r], -r)
-    prefill = outer_part(late, [prefill])
+        back[r] = shift(message[r], -r)
+    prefill, token = outer_part(late, carry, [prefill])
 
     decoded = call(
         finish_kernel,
         jax.ShapeDtypeStruct((count, STEPS, lanes), BF16),
         4 * rows * lanes,
         16 * rows * lanes,
-    )(keep, fresh, held, *back)
+        in_specs=[in_vmem] * (3 + count) + [anywhere],
+    )(keep, fresh, held, *back, token)
     return (prefill, decoded[None])
 
 

time: 48.8 us -> 43.4 us (0.89)
  local copies, waits for them, and re-layouts: 1.99 us -> 0 us
  waiting for transfers between devices: 14.9 us -> 13 us
  starting transfers between devices: 20.4 us -> 18.6 us
    ppermute x6 -> x3, starting transfers between devices: 7.1 us -> 3.55 us  [shift(): lax.ppermute(value, 'seq', [(d, (d + by) % count) for d in range(count)])]
    unnamed x16 -> x0, local copies, waits for them, and re-layouts: 1.99 us -> none
    ppermute x12, starting transfers between devices: 13.3 us -> 15 us  [forward(): return lax.ppermute(value, ('seq', 'tp'), pairs)]
    ppermute x6 -> x3, waiting for transfers between devices: 3.52 us -> 2.5 us  [shift(): lax.ppermute(value, 'seq', [(d, (d + by) % count) for d in range(count)])]
    ppermute x12, waiting for transfers between devices: 11.4 us -> 10.5 us  [forward(): return lax.ppermute(value, ('seq', 'tp'), pairs)]
    pallas_call x16 -> x15, Pallas kernels: 9.36 us -> 9.48 us  [the longest x1 2.99 us: shards(): call(functools.partial(state_kernel, len(inputs), chunks, ride), tuple((s...]
  transfers between devices with their start and end apart: 18 -> 15, of which waited for: 8 -> 8; matrix products, arithmetic and copies ran while one was open for 0% -> 0% of each run, Pallas kernels for 14% -> 16%
where the time goes in v5:
time: 43.4 us; the launch traced here: 43.1 us
  starting transfers between devices  18.6 us (43%)
  waiting for transfers between devices  13 us (30%)
  Pallas kernels  10.8 us (25%)
  between operations  0.79 us (2%)
    ppermute x12, starting transfers between devices, forward(): return lax.ppermute(value, ('seq', 'tp'), pairs)  15 us
    ppermute x12, waiting for transfers between devices, forward(): return lax.ppermute(value, ('seq', 'tp'), pairs)  10.5 us
    ppermute x3, starting transfers between devices, shift(): lax.ppermute(value, 'seq', [(d, (d + by) % count) for d in range(count)])  3.55 us
    pallas_call x1, Pallas kernels, shards(): call(functools.partial(state_kernel, len(inputs), chunks, ride), tuple((s...  2.99 us
    pallas_call x2, Pallas kernels, outer_part(): call(functools.partial(outer_kernel, part, count), (pltpu.HBM((tokens, la...  2.71 us
    ppermute x3, waiting for transfers between devices, shift(): lax.ppermute(value, 'seq', [(d, (d + by) % count) for d in range(count)])  2.5 us
    pallas_call x2, Pallas kernels, inner_part(): call(functools.partial(inner_kernel, g), (shape(asked_here.shape, BF16),...  2.17 us
    pallas_call x1, Pallas kernels, ask_part(): call(functools.partial(ask_kernel, count, ride), (shape((rows, lanes)), s...  0.93 us
  transfers between devices with their start and end apart: 15, of which 8 were waited for; matrix products, arithmetic and copies ran while one was open for 0% of the time, Pallas kernels for 16%

profile of v5, /device:TPU:0, one launch (start us, length us, event | category | flops | bytes accessed | tf_op | source)
XLA Modules:
  0.0 43.1 jit_solution(9309447938678274371)
XLA Ops:
  0.6 3.0 %shard_map.131 = (bf16[256,2048]{1,0:T(8,128)(2,1)S(1)}, bf16[256,256]{1,0:T(8,128)(2,1)S(1)}, f32[1,32]{1,0:T(1,128)S(1)}, bf16[4,4,256]{2,1,0:T(4,128)(2,1)S(1...) custom-call(bf16[256,2048]{1,0:T(8,128)(2,1)} %refs_0_.1, ...), custom_call_target="tpu_custom_call" | custom-call | flops 134217728 | bytes 2097152 | tf_op jit(solution)/shard_map/pallas_call | solution.py:459
  3.6 3.1 %collective-permute-start.2 = (bf16[144,512]{1,0:T(8,128)(2,1)S(1)}, bf16[144,512]{1,0:T(8,128)(2,1)S(1)}, u32[]{:S(2)}, u32[]{:S(2)}) collective-permute-start(bf16[144,512]{1,0:T(8,128)(2,1)S(1)} %get-tuple-element.57.rest_0_), channel_id=1, source_target_pairs={{0,4},{1,5},{2,6},{3,7},{4,0},{5,1},{6,2},{7,3},{8,12},{9,13},{10,... | collective-permute-start | bytes 442376 | tf_op jit(solution)/shard_map/ppermute | solution.py:488
  6.7 0.1 collective-permute-start.1
  6.8 1.1 %shard_map.133.rest_2_.rest_3_ = f32[256,1024]{1,0:T(8,128)S(1)} custom-call(bf16[256,2048]{1,0:T(8,128)(2,1)S(1)} %get-tuple-element.58.x_ref, bf16[256,256]{1,0:T(8,128)(2,1)S(1)} %get-tuple-element.59.b_ref, bf16[256,256]{1,0:T(8,128)(2,1)S(1)} %get-tuple-element.51.c_ref, f32[32,256]{1,0:T(8,128)S(1)} %get-tuple-element.52.cum_ref, ...), custom_call_target="tpu_custom_call" | custom-call | flops 134217728 | bytes 4194304 | tf_op jit(solution)/shard_map/pallas_call | solution.py:499
  7.9 1.1 %shard_map.132.rest_1_.rest_2_ = f32[256,1024]{1,0:T(8,128)S(1)} custom-call(bf16[256,2048]{1,0:T(8,128)(2,1)S(1)} %get-tuple-element.58.x_ref, bf16[256,256]{1,0:T(8,128)(2,1)S(1)} %get-tuple-element.59.b_ref, bf16[256,256]{1,0:T(8,128)(2,1)S(1)} %get-tuple-element.51.c_ref, f32[32,256]{1,0:T(8,128)S(1)} %get-tuple-element.52.cum_ref, ...), custom_call_target="tpu_custom_call" | custom-call | flops 134217728 | bytes 4194304 | tf_op jit(solution)/shard_map/pallas_call | solution.py:499
  9.0 2.4 %collective-permute-done.2.got_ref = bf16[144,512]{1,0:T(8,128)(2,1)S(1)} collective-permute-done((bf16[144,512]{1,0:T(8,128)(2,1)S(1)}, bf16[144,512]{1,0:T(8,128)(2,1)S(1)}, u32[]{:S(2)}, u32[]{:S(2)}) %collective-permute-start.2) | collective-permute-done | bytes 147488 | tf_op jit(solution)/shard_map/ppermute | solution.py:488
  11.4 0.1 shard_map.134
  11.5 0.1 collective-permute-start.5
  11.5 3.6 %collective-permute-start.4 = (bf16[128,512]{1,0:T(8,128)(2,1)S(1)}, bf16[128,512]{1,0:T(8,128)(2,1)S(1)}, u32[]{:S(2)}, u32[]{:S(2)}) collective-permute-start(bf16[128,512]{1,0:T(8,128)(2,1)S(1)} %get-tuple-element.73.rest_2_), channel_id=1, source_target_pairs={{0,4},{1,5},{2,6},{3,7},{4,0},{5,1},{6,2},{7,3},{8,12},{9,13},{10,... | collective-permute-start | bytes 393224 | tf_op jit(solution)/shard_map/ppermute | solution.py:488
  15.2 0.4 shard_map.135
  15.6 0.0 collective-permute-done.1.got_ref
  15.6 0.1 collective-permute-start.3
  15.7 1.7 %collective-permute-start = (bf16[128,512]{1,0:T(8,128)(2,1)S(1)}, bf16[128,512]{1,0:T(8,128)(2,1)S(1)}, u32[]{:S(2)}, u32[]{:S(2)}) collective-permute-start(bf16[128,512]{1,0:T(8,128)(2,1)S(1)} %get-tuple-element.53.rest_3_), channel_id=1, source_target_pairs={{0,4},{1,5},{2,6},{3,7},{4,0},{5,1},{6,2},{7,3},{8,12},{9,13},{10,... | collective-permute-start | bytes 393224 | tf_op jit(solution)/shard_map/ppermute | solution.py:488
  17.4 0.0 collective-permute-done.5.got_ref.rest_1_
  17.4 1.7 %collective-permute-start.8 = (bf16[144,512]{1,0:T(8,128)(2,1)S(1)}, bf16[144,512]{1,0:T(8,128)(2,1)S(1)}, u32[]{:S(2)}, u32[]{:S(2)}) collective-permute-start(bf16[144,512]{1,0:T(8,128)(2,1)S(1)} %get-tuple-element.81.rest_8_), channel_id=1, source_target_pairs={{0,4},{1,5},{2,6},{3,7},{4,0},{5,1},{6,2},{7,3},{8,12},{9,13},{10,... | collective-permute-start | bytes 442376 | tf_op jit(solution)/shard_map/ppermute | solution.py:488
  19.1 0.0 collective-permute-done.4.got_ref
  19.2 0.1 collective-permute-start.7
  19.3 0.0 collective-permute-done.3.got_ref
  19.3 2.5 %collective-permute-start.9 = (bf16[128,512]{1,0:T(8,128)(2,1)S(1)}, bf16[128,512]{1,0:T(8,128)(2,1)S(1)}, u32[]{:S(2)}, u32[]{:S(2)}) collective-permute-start(bf16[128,512]{1,0:T(8,128)(2,1)S(1)} %get-tuple-element.84.rest_9_), channel_id=1, source_target_pairs={{0,4},{1,5},{2,6},{3,7},{4,0},{5,1},{6,2},{7,3},{8,12},{9,13},{10,... | collective-permute-start | bytes 393224 | tf_op jit(solution)/shard_map/ppermute | solution.py:488
  21.8 0.3 collective-permute-done.got_ref
  22.1 0.1 collective-permute-start.6
  22.2 3.0 %collective-permute-done.8.rest_2_.rest_0_ = bf16[144,512]{1,0:T(8,128)(2,1)S(1)} collective-permute-done((bf16[144,512]{1,0:T(8,128)(2,1)S(1)}, bf16[144,512]{1,0:T(8,128)(2,1)S(1)}, u32[]{:S(2)}, u32[]{:S(2)}) %collective-permute-start.8) | collective-permute-done | bytes 147488 | tf_op jit(solution)/shard_map/ppermute | solution.py:488
  25.2 0.9 %shard_map.141 = (f32[16,2048]{1,0:T(8,128)S(1)}, f32[16,128]{1,0:T(8,128)S(1)}, bf16[16,256]{1,0:T(8,128)(2,1)S(1)}) custom-call(bf16[256,2048]{1,0:T(8,128)(2,1)S(1)} %get-tuple-element.58.x_ref, bf16[256,256]{1,0:T(8,128)(2,1)S(1)} %get-tuple-element.59.b_ref, f32[32,256]{1,0:T(8,128)S(1)} %get-tuple-element.52.cum_ref, ...), custom_call_target="tpu_custom_call" | custom-call | flops 16777216 | bytes 2097152 | tf_op jit(solution)/shard_map/pallas_call | solution.py:513
  26.2 0.0 collective-permute-done.7.got_ref
  26.2 1.4 %collective-permute-done.9.rest_1_ = bf16[128,512]{1,0:T(8,128)(2,1)S(1)} collective-permute-done((bf16[128,512]{1,0:T(8,128)(2,1)S(1)}, bf16[128,512]{1,0:T(8,128)(2,1)S(1)}, u32[]{:S(2)}, u32[]{:S(2)}) %collective-permute-start.9) | collective-permute-done | bytes 131104 | tf_op jit(solution)/shard_map/ppermute | solution.py:488
  27.6 1.4 %shard_map.143 = (bf16[256,2048]{1,0:T(8,128)(2,1)}, f32[8,128]{1,0:T(8,128)S(1)}) custom-call(bf16[256,256]{1,0:T(8,128)(2,1)S(1)} %get-tuple-element.51.c_ref, f32[32,256]{1,0:T(8,128)S(1)} %get-tuple-element.52.cum_ref, bf16[4,128,512]{2,1,0:T(8,128)(2,1)S(1)} %get-tuple-element.83.carry_ref.rest_0_, ...), custom_call_target="tpu_custom_call" | custom-call | flops 134217728 | bytes 4194304 | tf_op jit(solution)/shard_map/pallas_call | solution.py:531
  29.0 0.0 collective-permute-done.6.got_ref
  29.0 1.4 %collective-permute-start.11 = (bf16[128,512]{1,0:T(8,128)(2,1)S(1)}, bf16[128,512]{1,0:T(8,128)(2,1)S(1)}, u32[]{:S(2)}, u32[]{:S(2)}) collective-permute-start(bf16[128,512]{1,0:T(8,128)(2,1)S(1)} %get-tuple-element.88.rest_11_), channel_id=1, source_target_pairs={{0,4},{1,5},{2,6},{3,7},{4,0},{5,1},{6,2},{7,3},{8,12},{9,13},{10,... | collective-permute-start | bytes 393224 | tf_op jit(solution)/shard_map/ppermute | solution.py:488
  30.4 0.7 %collective-permute-start.10 = (bf16[128,512]{1,0:T(8,128)(2,1)S(1)}, bf16[128,512]{1,0:T(8,128)(2,1)S(1)}, u32[]{:S(2)}, u32[]{:S(2)}) collective-permute-start(bf16[128,512]{1,0:T(8,128)(2,1)S(1)} %get-tuple-element.87.rest_10_), channel_id=1, source_target_pairs={{0,4},{1,5},{2,6},{3,7},{4,0},{5,1},{6,2},{7,3},{8,12},{9,13},{10,... | collective-permute-start | bytes 393224 | tf_op jit(solution)/shard_map/ppermute | solution.py:488
  31.1 0.3 shard_map.146
  31.4 2.7 %collective-permute-start.12 = (f32[4,4224]{1,0:T(4,128)S(1)}, f32[4,4224]{1,0:T(4,128)S(1)}, u32[]{:S(2)}, u32[]{:S(2)}) collective-permute-start(f32[4,4224]{1,0:T(4,128)S(1)} %get-tuple-element.96), channel_id=1, source_target_pairs={{0,12},{4,0},{8,4},{12,8},{1,13},{5,1},{9,5},{13,9},{2,14},{6,2},{... | collective-permute-start | bytes 202760 | tf_op jit(solution)/shard_map/ppermute | solution.py:491
  34.2 0.1 collective-permute-start.13
  34.2 0.8 %collective-permute-start.14 = (f32[4,4224]{1,0:T(4,128)S(1)}, f32[4,4224]{1,0:T(4,128)S(1)}, u32[]{:S(2)}, u32[]{:S(2)}) collective-permute-start(f32[4,4224]{1,0:T(4,128)S(1)} %get-tuple-element.98), channel_id=1, source_target_pairs={{0,4},{4,8},{8,12},{12,0},{1,5},{5,9},{9,13},{13,1},{2,6},{6,10},{... | collective-permute-start | bytes 202760 | tf_op jit(solution)/shard_map/ppermute | solution.py:491
  35.0 0.5 %collective-permute-done.11.rest_1_ = bf16[128,512]{1,0:T(8,128)(2,1)S(1)} collective-permute-done((bf16[128,512]{1,0:T(8,128)(2,1)S(1)}, bf16[128,512]{1,0:T(8,128)(2,1)S(1)}, u32[]{:S(2)}, u32[]{:S(2)}) %collective-permute-start.11) | collective-permute-done | bytes 131104 | tf_op jit(solution)/shard_map/ppermute | solution.py:488
  35.5 2.9 %collective-permute-done.10.rest_0_ = bf16[128,512]{1,0:T(8,128)(2,1)S(1)} collective-permute-done((bf16[128,512]{1,0:T(8,128)(2,1)S(1)}, bf16[128,512]{1,0:T(8,128)(2,1)S(1)}, u32[]{:S(2)}, u32[]{:S(2)}) %collective-permute-start.10) | collective-permute-done | bytes 131104 | tf_op jit(solution)/shard_map/ppermute | solution.py:488
  38.4 1.4 %shard_map.145 = (bf16[256,2048]{1,0:T(8,128)(2,1)}, f32[8,128]{1,0:T(8,128)S(1)}) custom-call(bf16[256,256]{1,0:T(8,128)(2,1)S(1)} %get-tuple-element.51.c_ref, f32[32,256]{1,0:T(8,128)S(1)} %get-tuple-element.52.cum_ref, bf16[4,128,512]{2,1,0:T(8,128)(2,1)S(1)} %get-tuple-element.86.carry_ref, ...), custom_call_target="tpu_custom_call", output_to_operand_aliasing={{0}: (7, {})} | custom-call | flops 134217728 | bytes 4194304 | tf_op jit(solution)/shard_map/pallas_call | solution.py:531
  39.8 0.0 collective-permute-done.12.rest_1_
  39.8 0.4 collective-permute-done.13.rest_2_
  40.1 2.1 %collective-permute-done.14.rest_3_ = f32[4,4224]{1,0:T(4,128)S(1)} collective-permute-done((f32[4,4224]{1,0:T(4,128)S(1)}, f32[4,4224]{1,0:T(4,128)S(1)}, u32[]{:S(2)}, u32[]{:S(2)}) %collective-permute-start.14) | collective-permute-done | bytes 67616 | tf_op jit(solution)/shard_map/ppermute | solution.py:491
  42.3 0.9 %shard_map.147 = bf16[4,4,2048]{2,1,0:T(4,128)(2,1)} custom-call(f32[4,4,2048]{2,1,0:T(4,128)S(1)} %get-tuple-element.71.rest_1_.keep_ref, f32[4,4,2048]{2,1,0:T(4,128)S(1)} %get-tuple-element.91.fresh_ref, f32[4,4,128]{2,1,0:T(4,128)S(1)} %get-tuple-element.92.held_ref, f32[4,4224]{1,0:T(4,128)S(1)} %get-tuple-element.95.rest_0_, ...), custom_call_target="tpu_custom_call" | custom-call | flops 131072 | bytes 524288 | tf_op jit(solution)/shard_map/pallas_call | solution.py:583
  (7 shorter events, 0.3 us)
Async XLA Ops:
  3.6 7.8 %collective-permute-start.2 = (bf16[144,512]{1,0:T(8,128)(2,1)S(1)}, bf16[144,512]{1,0:T(8,128)(2,1)S(1)}, u32[]{:S(2)}, u32[]{:S(2)}) collective-permute-start(bf16[144,512]{1,0:T(8,128)(2,1)S(1)} %get-tuple-element.57.rest_0_), channel_id=1, source_target_pairs={{0,4},{1,5},{2,6},{3,7},{4,0},{5,1},{6,2},{7,3},{8,12},{9,13},{10,... | collective-permute-start | bytes 442376 | tf_op jit(solution)/shard_map/ppermute | solution.py:488
  6.7 8.9 %collective-permute-start.1 = (bf16[128,512]{1,0:T(8,128)(2,1)S(1)}, bf16[128,512]{1,0:T(8,128)(2,1)S(1)}, u32[]{:S(2)}, u32[]{:S(2)}) collective-permute-start(bf16[128,512]{1,0:T(8,128)(2,1)S(1)} %get-tuple-element.56.rest_1_), channel_id=1, source_target_pairs={{0,4},{1,5},{2,6},{3,7},{4,0},{5,1},{6,2},{7,3},{8,12},{9,13},{10,... | collective-permute-start | bytes 393224 | tf_op jit(solution)/shard_map/ppermute | solution.py:488
  11.5 5.9 %collective-permute-start.5 = (bf16[144,512]{1,0:T(8,128)(2,1)S(1)}, bf16[144,512]{1,0:T(8,128)(2,1)S(1)}, u32[]{:S(2)}, u32[]{:S(2)}) collective-permute-start(bf16[144,512]{1,0:T(8,128)(2,1)S(1)} %get-tuple-element.70.rest_0_.rest_4_), channel_id=1, source_target_pairs={{0,1},{1,0},{2,3},{3,2},{4,8},{5,9},{6,10},{7,11},{8,4},{9,5},{10,... | collective-permute-start | bytes 442376 | tf_op jit(solution)/shard_map/ppermute | solution.py:488
  11.5 7.6 %collective-permute-start.4 = (bf16[128,512]{1,0:T(8,128)(2,1)S(1)}, bf16[128,512]{1,0:T(8,128)(2,1)S(1)}, u32[]{:S(2)}, u32[]{:S(2)}) collective-permute-start(bf16[128,512]{1,0:T(8,128)(2,1)S(1)} %get-tuple-element.73.rest_2_), channel_id=1, source_target_pairs={{0,4},{1,5},{2,6},{3,7},{4,0},{5,1},{6,2},{7,3},{8,12},{9,13},{10,... | collective-permute-start | bytes 393224 | tf_op jit(solution)/shard_map/ppermute | solution.py:488
  15.6 3.6 %collective-permute-start.3 = (bf16[128,512]{1,0:T(8,128)(2,1)S(1)}, bf16[128,512]{1,0:T(8,128)(2,1)S(1)}, u32[]{:S(2)}, u32[]{:S(2)}) collective-permute-start(bf16[128,512]{1,0:T(8,128)(2,1)S(1)} %get-tuple-element.72.rest_5_), channel_id=1, source_target_pairs={{0,1},{1,0},{2,3},{3,2},{4,8},{5,9},{6,10},{7,11},{8,4},{9,5},{10,... | collective-permute-start | bytes 393224 | tf_op jit(solution)/shard_map/ppermute | solution.py:488
  15.7 6.4 %collective-permute-start = (bf16[128,512]{1,0:T(8,128)(2,1)S(1)}, bf16[128,512]{1,0:T(8,128)(2,1)S(1)}, u32[]{:S(2)}, u32[]{:S(2)}) collective-permute-start(bf16[128,512]{1,0:T(8,128)(2,1)S(1)} %get-tuple-element.53.rest_3_), channel_id=1, source_target_pairs={{0,4},{1,5},{2,6},{3,7},{4,0},{5,1},{6,2},{7,3},{8,12},{9,13},{10,... | collective-permute-start | bytes 393224 | tf_op jit(solution)/shard_map/ppermute | solution.py:488
  17.4 7.8 %collective-permute-start.8 = (bf16[144,512]{1,0:T(8,128)(2,1)S(1)}, bf16[144,512]{1,0:T(8,128)(2,1)S(1)}, u32[]{:S(2)}, u32[]{:S(2)}) collective-permute-start(bf16[144,512]{1,0:T(8,128)(2,1)S(1)} %get-tuple-element.81.rest_8_), channel_id=1, source_target_pairs={{0,4},{1,5},{2,6},{3,7},{4,0},{5,1},{6,2},{7,3},{8,12},{9,13},{10,... | collective-permute-start | bytes 442376 | tf_op jit(solution)/shard_map/ppermute | solution.py:488
  19.2 7.0 %collective-permute-start.7 = (bf16[128,512]{1,0:T(8,128)(2,1)S(1)}, bf16[128,512]{1,0:T(8,128)(2,1)S(1)}, u32[]{:S(2)}, u32[]{:S(2)}) collective-permute-start(bf16[128,512]{1,0:T(8,128)(2,1)S(1)} %get-tuple-element.79.rest_6_), channel_id=1, source_target_pairs={{0,1},{1,0},{2,3},{3,2},{4,8},{5,9},{6,10},{7,11},{8,4},{9,5},{10,... | collective-permute-start | bytes 393224 | tf_op jit(solution)/shard_map/ppermute | solution.py:488
  19.3 8.3 %collective-permute-start.9 = (bf16[128,512]{1,0:T(8,128)(2,1)S(1)}, bf16[128,512]{1,0:T(8,128)(2,1)S(1)}, u32[]{:S(2)}, u32[]{:S(2)}) collective-permute-start(bf16[128,512]{1,0:T(8,128)(2,1)S(1)} %get-tuple-element.84.rest_9_), channel_id=1, source_target_pairs={{0,4},{1,5},{2,6},{3,7},{4,0},{5,1},{6,2},{7,3},{8,12},{9,13},{10,... | collective-permute-start | bytes 393224 | tf_op jit(solution)/shard_map/ppermute | solution.py:488
  22.1 6.8 %collective-permute-start.6 = (bf16[128,512]{1,0:T(8,128)(2,1)S(1)}, bf16[128,512]{1,0:T(8,128)(2,1)S(1)}, u32[]{:S(2)}, u32[]{:S(2)}) collective-permute-start(bf16[128,512]{1,0:T(8,128)(2,1)S(1)} %get-tuple-element.78.rest_3_.rest_7_), channel_id=1, source_target_pairs={{0,1},{1,0},{2,3},{3,2},{4,8},{5,9},{6,10},{7,11},{8,4},{9,5},{10,... | collective-permute-start | bytes 393224 | tf_op jit(solution)/shard_map/ppermute | solution.py:488
  29.0 6.5 %collective-permute-start.11 = (bf16[128,512]{1,0:T(8,128)(2,1)S(1)}, bf16[128,512]{1,0:T(8,128)(2,1)S(1)}, u32[]{:S(2)}, u32[]{:S(2)}) collective-permute-start(bf16[128,512]{1,0:T(8,128)(2,1)S(1)} %get-tuple-element.88.rest_11_), channel_id=1, source_target_pairs={{0,4},{1,5},{2,6},{3,7},{4,0},{5,1},{6,2},{7,3},{8,12},{9,13},{10,... | collective-permute-start | bytes 393224 | tf_op jit(solution)/shard_map/ppermute | solution.py:488
  30.4 8.0 %collective-permute-start.10 = (bf16[128,512]{1,0:T(8,128)(2,1)S(1)}, bf16[128,512]{1,0:T(8,128)(2,1)S(1)}, u32[]{:S(2)}, u32[]{:S(2)}) collective-permute-start(bf16[128,512]{1,0:T(8,128)(2,1)S(1)} %get-tuple-element.87.rest_10_), channel_id=1, source_target_pairs={{0,4},{1,5},{2,6},{3,7},{4,0},{5,1},{6,2},{7,3},{8,12},{9,13},{10,... | collective-permute-start | bytes 393224 | tf_op jit(solution)/shard_map/ppermute | solution.py:488
  31.4 8.3 %collective-permute-start.12 = (f32[4,4224]{1,0:T(4,128)S(1)}, f32[4,4224]{1,0:T(4,128)S(1)}, u32[]{:S(2)}, u32[]{:S(2)}) collective-permute-start(f32[4,4224]{1,0:T(4,128)S(1)} %get-tuple-element.96), channel_id=1, source_target_pairs={{0,12},{4,0},{8,4},{12,8},{1,13},{5,1},{9,5},{13,9},{2,14},{6,2},{... | collective-permute-start | bytes 202760 | tf_op jit(solution)/shard_map/ppermute | solution.py:491
  34.2 6.0 %collective-permute-start.13 = (f32[4,4224]{1,0:T(4,128)S(1)}, f32[4,4224]{1,0:T(4,128)S(1)}, u32[]{:S(2)}, u32[]{:S(2)}) collective-permute-start(f32[4,4224]{1,0:T(4,128)S(1)} %get-tuple-element.97), channel_id=1, source_target_pairs={{0,8},{4,12},{8,0},{12,4},{1,9},{5,13},{9,1},{13,5},{2,10},{6,14},... | collective-permute-start | bytes 202760 | tf_op jit(solution)/shard_map/ppermute | solution.py:491
  34.2 8.1 %collective-permute-start.14 = (f32[4,4224]{1,0:T(4,128)S(1)}, f32[4,4224]{1,0:T(4,128)S(1)}, u32[]{:S(2)}, u32[]{:S(2)}) collective-permute-start(f32[4,4224]{1,0:T(4,128)S(1)} %get-tuple-element.98), channel_id=1, source_target_pairs={{0,4},{4,8},{8,12},{12,0},{1,5},{5,9},{9,13},{13,1},{2,6},{6,10},{... | collective-permute-start | bytes 202760 | tf_op jit(solution)/shard_map/ppermute | solution.py:491

commit v6 on v5

--- a/solution.py
+++ b/solution.py
@@ -68,12 +68,12 @@
     return pltpu.with_memory_space_constraint(value, space)
 
 
-def call(kernel, out_shape, flops, moved, **options):
+def call(kernel, out_shape, **options):
     return pl.pallas_call(
         kernel,
         out_shape=out_shape,
         compiler_params=pltpu.CompilerParams(vmem_limit_bytes=VMEM_LIMIT),
-        cost_estimate=pl.CostEstimate(flops=flops, bytes_accessed=moved, transcendentals=0),
+        cost_estimate=pl.CostEstimate(flops=1, bytes_accessed=1, transcendentals=0),
         **options,
     )
 
@@ -84,28 +84,31 @@
     return jnp.where(keep(row, column), 1.0, 0.0).astype(BF16)
 
 
-def state_kernel(kept, chunks, ride, *refs):
+def chunk_total(k, x_ref, turned, weight, whole, total_ref, sent_ref, decay_ref):
+    width = total_ref.shape[1]
+    first = k * width
+    scaled = x_ref[:, first : first + width].astype(F32) * over_lanes(weight, first, width)
+    total = dot(turned, scaled.astype(BF16))
+    total_ref[...] = total
+    sent_ref[:N] = total.astype(BF16)
+    decay_ref[...] = over_lanes(whole, first, width, 3)
+
+
+def first_kernel(kept, ride, *refs):
     hbm, refs = refs[: kept + 1], refs[kept + 1 :]
     here, refs = refs[:kept], refs[kept:]
-    total_ref, decay_ref, cum_ref, row_ref = refs[:4]
-    sent_refs, (dt_ref, sems) = refs[4 : 4 + chunks], refs[4 + chunks :]
+    cum_ref, row_ref, weight_ref, whole_ref, turned_ref = refs[:5]
+    total_ref, sent_ref, decay_ref, dt_ref, sems = refs[5:]
     x_ref, b_ref, a_ref, asked_ref = here[:4]
     heads, tokens = dt_ref.shape
     spans = tokens // SPAN
-    width = total_ref.shape[2]
-    per_group = H // G
-    groups = heads // per_group
-    group_lanes = per_group * P_SIZE
+    width = total_ref.shape[1]
     dt_copy = pltpu.make_async_copy(hbm[kept], dt_ref, sems.at[0])
-    copies = [
-        pltpu.make_async_copy(hbm[i], here[i], sems.at[i]) for i in range(1, kept)
+    copies = [pltpu.make_async_copy(hbm[i], here[i], sems.at[i]) for i in range(1, kept)]
+    x_copies = [
+        pltpu.make_async_copy(hbm[0].at[:, lanes], x_ref.at[:, lanes], sems.at[kept + i])
+        for i, lanes in enumerate((slice(0, width), slice(width, x_ref.shape[1])))
     ]
-    x_copies = []
-    for g in range(groups):
-        lanes = slice(g * group_lanes, (g + 1) * group_lanes)
-        x_copies.append(
-            pltpu.make_async_copy(hbm[0].at[:, lanes], x_ref.at[:, lanes], sems.at[kept + g])
-        )
     for copy in [dt_copy, copies[1], copies[0], *x_copies, *copies[2:]]:
         copy.start()
     upper = triangle(lambda s, t: s <= t)
@@ -126,28 +129,32 @@
         weights[i] = jnp.exp2(after - cums[i]) * step[:, i * SPAN : (i + 1) * SPAN]
     weight = jnp.concatenate(weights, axis=1).T
     whole = jnp.sum(jnp.where(eye, jnp.exp2(after), 0.0), axis=0, keepdims=True)
+    weight_ref[...] = weight
+    whole_ref[...] = whole
+    copies[0].wait()
+    turned = b_ref[:, :N].astype(F32).T.astype(BF16)
+    x_copies[0].wait()
+    chunk_total(0, x_ref, turned, weight, whole, total_ref, sent_ref, decay_ref)
+    turned_ref[0] = turned
+    for g in range(1, turned_ref.shape[0]):
+        turned_ref[g] = b_ref[:, g * N : (g + 1) * N].astype(F32).T.astype(BF16)
     cum = jnp.concatenate(cums, axis=1)
     cum_ref[...] = cum
     row_ref[...] = jnp.log2(step) - cum
-    copies[0].wait()
-    for g in range(groups):
-        turned = b_ref[:, g * N : (g + 1) * N].astype(F32).T.astype(BF16)
-        x_copies[g].wait()
-        for k in range(chunks):
-            first = k * width
-            if first // group_lanes != g:
-                continue
-            lanes = slice(first, first + width)
-            scaled = (x_ref[:, lanes].astype(F32) * over_lanes(weight, first, width)).astype(BF16)
-            total = dot(turned, scaled)
-            total_ref[k] = total
-            sent_refs[k][:N] = total.astype(BF16)
-            decay_ref[k] = over_lanes(whole, first, width, 3)
+    x_copies[1].wait()
     for copy in copies[2:]:
         copy.wait()
     if ride:
         own = flat(asked_ref).astype(BF16)
-        sent_refs[0][N:] = jnp.concatenate([own, own], axis=1)
+        sent_ref[N:] = jnp.concatenate([own, own], axis=1)
+
+
+def state_kernel(k, x_ref, turned_ref, weight_ref, whole_ref, *rest):
+    total_ref, sent_ref, decay_ref = rest[-3:]
+    g = k * total_ref.shape[1] // (H // G * P_SIZE)
+    chunk_total(
+        k, x_ref, turned_ref[g], weight_ref[...], whole_ref[...], total_ref, sent_ref, decay_ref
+    )
 
 
 def flat(ref):
@@ -160,7 +167,7 @@
     if hop == 1 and k == 0:
         carry_ref[...] = jnp.zeros_like(carry_ref)
     got = got_ref[:N]
-    moving_ref[:N] = (total_ref[k] + decay_ref[k] * got.astype(F32)).astype(BF16)
+    moving_ref[:N] = (total_ref[...] + decay_ref[...] * got.astype(F32)).astype(BF16)
 
     @pl.when(me == hop)
     def _():
@@ -193,9 +200,6 @@
 
 def inner_kernel(g, x_ref, b_ref, c_ref, cum_ref, row_ref, d_ref, *rest):
     inner_ref = rest[-1]
-    if len(rest) > 1:
-        asked_ref, handed_ref, inner_ref = rest
-        handed_ref[...] = asked_ref[...]
     heads, tokens = cum_ref.shape
     spans = tokens // SPAN
     per_group = H // G
@@ -241,7 +245,7 @@
 
 
 def ask_kernel(count, ride, x_ref, b_ref, cum_ref, row_ref, len_ref, owner_ref, *rest):
-    local_ref, gain_ref, next_ref = rest[-3:]
+    local_ref, gain_ref, asked_ref = rest[-3:]
     heads, tokens = cum_ref.shape
     spans = tokens // SPAN
     asks = local_ref.shape[0]
@@ -260,18 +264,12 @@
     row = lax.broadcasted_iota(jnp.int32, (asks, asks * count), 0)
     column = lax.broadcasted_iota(jnp.int32, (asks, asks * count), 1)
     place = row // STEPS
-    if ride:
-        place = lax.rem(me + count - place, count)
-
-    def of_source(source):
-        wanted = place * asks + source * STEPS + row % STEPS
-        return dot(jnp.where(column == wanted, 1.0, 0.0).astype(BF16), blocks).astype(BF16)
-
-    asked = of_source(me)
-    next_ref[...] = of_source(lax.rem(me + 1, count))
+    wanted = place * asks + me * STEPS + row % STEPS
+    asked = dot(jnp.where(column == wanted, 1.0, 0.0).astype(BF16), blocks).astype(BF16)
+    asked_ref[...] = asked
     block = lax.broadcasted_iota(jnp.int32, (asks, 1), 0) // STEPS
     spot = len_ref[...] - 1 - me * tokens
-    mine = (owner_ref[...] == lax.rem(me + count - block, count)) & (spot >= 0) & (spot < tokens)
+    mine = (owner_ref[...] == (block if ride else lax.rem(me + count - block, count))) & (spot >= 0) & (spot < tokens)
     spot = jnp.sum(jnp.where(mine, spot, 0).astype(F32), axis=1, keepdims=True).astype(jnp.int32)
     position = lax.broadcasted_iota(jnp.int32, (asks, tokens), 1)
     picked = jnp.where(position == spot, 1.0, 0.0).astype(BF16)
@@ -283,8 +281,7 @@
     ask_start = starts[0]
     for i in range(1, spans):
         ask_start = jnp.where(spot >= i * SPAN, starts[i], ask_start)
-    gain = near_ask + ask_start
-    gain_ref[...] = jnp.concatenate([gain] * (gain_ref.shape[1] // heads), axis=1)
+    gain_ref[...] = jnp.exp2(near_ask + ask_start)
     columns = []
     for j in range(spans):
         column = near_ask
@@ -307,35 +304,58 @@
             local_ref[:, lanes] = dot(jnp.concatenate(parts, axis=1), right)
 
 
-def message_kernel(count, chunks, local_ref, gain_ref, next_ref, *rest):
-    moving_refs, message_refs = rest[:-count], rest[-count:]
+def read_kernel(count, chunks, ops, final, local_ref, gain_ref, asked_ref, carry_ref, *rest):
+    got_refs, rest = rest[: chunks * final], rest[chunks * final :]
+    read_refs = rest[-(len(ops) + final) :]
     me = lax.axis_index("seq")
     lanes = local_ref.shape[1]
     width = lanes // chunks
     for k in range(chunks):
         first = k * width
+        here = slice(first, first + width)
         g = first // (H // G * P_SIZE)
-        state = moving_refs[k][:N].astype(F32)
-        for hop in range(1, count - 1):
-            state = jnp.where(me == hop, moving_refs[hop * chunks + k][:N].astype(F32), state)
-        reading = dot(next_ref[:, g * N : (g + 1) * N], state.astype(BF16))
-        for r in range(count):
-            message_refs[r][:, first : first + width] = reading[r * STEPS : (r + 1) * STEPS]
-    for r in range(count):
-        mine = slice(r * STEPS, (r + 1) * STEPS)
-        message_refs[r][:, lanes : 2 * lanes] = local_ref[mine]
-        message_refs[r][:, 2 * lanes :] = gain_ref[mine]
-
-
-def outer_kernel(chunks, count, c_ref, cum_ref, carry_ref, *rest):
-    got_refs = rest[: len(chunks)]
-    inner_refs = rest[len(chunks) :]
-    out_hbm, token_ref, out_ref, sems = rest[-4:]
-    token_ref[...] = jnp.zeros_like(token_ref)
+        state = carry_ref[k]
+        if final:
+            state = jnp.where(me == count - 1, got_refs[k][:N], state)
+        carried = dot(asked_ref[:, g * N : (g + 1) * N], state)
+        reading = local_ref[:, here] + over_lanes(gain_ref[...], first, width) * carried
+        parts = [reading[r * STEPS : (r + 1) * STEPS] for r in range(count)]
+        for (one, other), read_ref in zip(ops, read_refs):
+            part = parts[other]
+            if one != other:
+                part = jnp.where(me == one, part, parts[one])
+            read_ref[:, here] = part
+        if final:
+            own = parts[0]
+            for r in range(1, count):
+                own = jnp.where(me == r, parts[r], own)
+            read_refs[-1][:, here] = own
+
+
+def outer_kernel(parts, count, c_ref, cum_ref, carry_ref, *rest):
+    final = len(parts) > 1
+    part = parts[-1]
+    got_refs = rest[: len(part)]
+    inner_refs = rest[len(part) : len(part) + cum_ref.shape[0] // (H // G)]
+    if final:
+        early_ref, out_hbm, token_ref, out_ref, sems = rest[-5:]
+        token_ref[...] = jnp.zeros_like(token_ref)
+    else:
+        out_ref = rest[-1]
     heads, tokens = cum_ref.shape
     spans = tokens // SPAN
     width = got_refs[0].shape[1]
     group_lanes = H // G * P_SIZE
+    copies = []
+
+    def send(source, k):
+        lanes = slice(k * width, (k + 1) * width)
+        copies.append(pltpu.make_async_copy(source, out_hbm.at[:, lanes], sems.at[k]))
+        copies[-1].start()
+
+    if final:
+        for i, k in enumerate(parts[0]):
+            send(early_ref.at[i], k)
     last = lax.axis_index("seq") == count - 1
     start = jnp.zeros((heads, 1), F32)
     gains = []
@@ -344,18 +364,15 @@
         gains.append(jnp.exp2(cum + start))
         start = start + cum[:, SPAN - 1 : SPAN]
     gain = jnp.concatenate(gains, axis=1).T
-    copies = []
-    for i, k in enumerate(chunks):
+    for i, k in enumerate(part):
         first = k * width
         g = first // group_lanes
         state = jnp.where(last, got_refs[i][:N], carry_ref[k])
         carried = dot(c_ref[:, g * N : (g + 1) * N], state)
         inner = inner_refs[g][:, first - g * group_lanes : first - g * group_lanes + width]
         out_ref[i] = (inner + over_lanes(gain, first, width) * carried).astype(BF16)
-        copies.append(
-            pltpu.make_async_copy(out_ref.at[i], out_hbm.at[:, first : first + width], sems.at[i])
-        )
-        copies[i].start()
+        if final:
+            send(out_ref.at[i], k)
     for copy in copies:
         copy.wait()
 
@@ -406,20 +423,28 @@
         held_ref[i] = held[i * STEPS : (i + 1) * STEPS]
 
 
-def finish_kernel(keep_ref, fresh_ref, held_ref, *rest):
-    back_refs, out_ref = rest[:-2], rest[-1]
-    count = len(back_refs)
-    lanes = keep_ref.shape[2]
+def finish_kernel(ops, keep_ref, fresh_ref, held_ref, *rest):
+    count = keep_ref.shape[0]
+    back_refs, own_ref, out_ref = rest[: len(ops)], rest[len(ops)], rest[-1]
     me = lax.axis_index("seq")
-    gain = jnp.concatenate([ref[:, 2 * lanes :] for ref in back_refs], axis=0)
-    gain = over_lanes(jnp.exp2(gain[:, : lanes // P_SIZE]), 0, lanes)
-    for r in range(count):
-        source = lax.rem(me + r, count)
-        carried = gain[r * STEPS : (r + 1) * STEPS] * back_refs[r - 1][:, :lanes]
-        reading = back_refs[r][:, lanes : 2 * lanes] + jnp.where(source > 0, carried, 0.0)
+
+    def finish(source, reading):
         value = reading * keep_ref[source] + fresh_ref[source]
         held = held_ref[source][:, :1] > 0.0
         out_ref[source] = jnp.where(held, value, 0.0).astype(BF16)
+
+    if isinstance(ops[0], tuple):
+        for source in range(count):
+            reading = own_ref[...]
+            for (one, other), back_ref in zip(ops, back_refs):
+                if source in (one, other):
+                    owner = one + other - source
+                    reading = jnp.where(me == owner, back_ref[...], reading)
+            finish(source, reading)
+    else:
+        finish(me, own_ref[...])
+        for r, back_ref in zip(ops, back_refs):
+            finish(lax.rem(me + r, count), back_ref[...])
 
 
 def shards(
@@ -456,65 +481,69 @@
         dec_b[0],
         dec_dt[0],
     ]
+    chunk_shapes = [
+        (shape((N, width)), sent_shape(k), shape((1, width))) for k in range(chunks)
+    ]
     results = call(
-        functools.partial(state_kernel, len(inputs), chunks, ride),
+        functools.partial(first_kernel, len(inputs), ride),
         tuple(shape(value.shape, value.dtype) for value in inputs)
         + (
-            shape((chunks, N, width)),
-            shape((chunks, 1, width)),
             shape((heads, tokens)),
             shape((heads, tokens)),
+            shape((tokens, heads)),
+            shape((1, heads)),
+            shape((groups, N, tokens), BF16),
         )
-        + tuple(sent_shape(k) for k in range(chunks)),
-        2 * tokens * N * lanes,
-        4 * tokens * lanes,
+        + chunk_shapes[0],
         in_specs=[in_hbm] * (len(inputs) + 1),
         scratch_shapes=[
             pltpu.VMEM((heads, tokens), BF16),
-            pltpu.SemaphoreType.DMA((len(inputs) + groups,)),
+            pltpu.SemaphoreType.DMA((len(inputs) + 2,)),
         ],
     )(*[pinned(value, pltpu.HBM) for value in inputs + [dt_raw.T]])
     x, b, a_row, asked_here, c, d_row, len_row, owner_row, x_dec, b_dec, dt_dec = results[:11]
-    total, decay, cum, row, *sent = results[11:]
-
-    def forward(value, hop):
+    cum, row, weight, whole, turned = results[11:16]
+    total, sent, decay = ([value] for value in results[16:])
+
+    def state_part(k, tie):
+        part = call(
+            functools.partial(state_kernel, k),
+            chunk_shapes[k],
+            in_specs=[in_vmem] * 4 + [anywhere],
+        )(x, turned, weight, whole, tie)
+        for values, value in zip((total, sent, decay), part):
+            values.append(value)
+
+    def swap(value, *couples):
+        partner = {}
+        for one, other in couples:
+            partner.update({one: other, other: one})
         pairs = []
         for d in range(count):
-            other = d + 1 if (d - hop) % 2 else d - 1
             for t in range(tensor):
-                alone = not 0 <= other < count
-                there = d * tensor + (t ^ 1) if alone else other * tensor + t
+                there = partner[d] * tensor + t if d in partner else d * tensor + (t ^ 1)
                 pairs.append((d * tensor + t, there))
         return lax.ppermute(value, ("seq", "tp"), pairs)
 
+    def forward(value, hop, k):
+        rides = ride and k == 0 and hop != 2
+        return swap(value, *([(0, 1), (2, 3)] if rides else [(hop - 1, hop)]))
+
     def shift(value, by):
         return lax.ppermute(value, "seq", [(d, (d + by) % count) for d in range(count)])
 
-    got = {(1, k): forward(sent[k], 1) for k in range(chunks)}
-    moving = {(1, k): sent[k] for k in range(chunks)}
-
-    def inner_part(g):
-        more = (asked_here,) if g == 0 and not ride else ()
-        inner_shape = shape((tokens, group_lanes))
+    def inner_part(g, *after):
         return call(
             functools.partial(inner_kernel, g),
-            (shape(asked_here.shape, BF16), inner_shape) if more else inner_shape,
-            2 * tokens * tokens * group_lanes,
-            16 * tokens * group_lanes,
-        )(x, b, c, cum, row, d_row, *more)
-
-    inner = [inner_part(g) for g in range(groups)]
-    if not ride:
-        handed, inner[0] = inner[0]
-        asks = [handed] + [shift(handed, r) for r in range(1, count)]
+            shape((tokens, group_lanes)),
+            in_specs=[in_vmem] * 6 + [anywhere] * len(after),
+        )(x, b, c, cum, row, d_row, *after)
 
     def ask_part(*after):
         blocks = (moving[2, 0], got[2, 0], got[3, 0]) if ride else asks
         return call(
             functools.partial(ask_kernel, count, ride),
-            (shape((rows, lanes)), shape((rows, 128)), shape((rows, names), BF16)),
-            2 * rows * tokens * lanes,
-            4 * tokens * lanes,
+            (shape((rows, lanes)), shape((rows, heads)), shape((rows, names), BF16)),
             in_specs=[in_vmem] * (6 + len(blocks)) + [anywhere] * len(after),
         )(x, b, cum, row, len_row, owner_row, *blocks, *after)
 
@@ -522,71 +551,88 @@
         return call(
             functools.partial(fresh_kernel, tokens),
             (shape((count, STEPS, lanes)),) * 2 + (shape((count, STEPS, 128)),),
-            64 * rows * lanes,
-            16 * rows * lanes,
             in_specs=[in_vmem] * 8 + [anywhere] * len(after),
         )(x_dec, b_dec, asked_here, dt_dec, a_row, d_row, len_row, owner_row, *after)
 
-    def outer_part(part, carry, before):
+    def outer_part(parts, carry, before, *after):
+        part = parts[-1]
+        out = shape((len(part), tokens, width), BF16)
+        operands = [c, cum, carry, *[got[count - 1, k] for k in part], *inner, *before]
         return call(
-            functools.partial(outer_kernel, part, count),
-            (pltpu.HBM((tokens, lanes), BF16), shape((8, 128))),
-            2 * tokens * N * lanes,
-            8 * tokens * lanes,
-            in_specs=[in_vmem] * (3 + len(part) + groups) + [in_hbm] * len(before),
-            out_specs=(in_hbm, in_vmem),
-            scratch_shapes=[
-                pltpu.VMEM((len(part), tokens, width), BF16),
-                pltpu.SemaphoreType.DMA((len(part),)),
-            ],
-            input_output_aliases={3 + len(part) + groups: 0} if before else {},
-        )(c, cum, carry, *[got[count - 1, k] for k in part], *inner, *before)
-
+            functools.partial(outer_kernel, parts, count),
+            (pltpu.HBM((tokens, lanes), BF16), shape((8, 128))) if before else out,
+            in_specs=[in_vmem] * len(operands) + [anywhere] * len(after),
+            out_specs=(in_hbm, in_vmem) if before else in_vmem,
+            scratch_shapes=[out, pltpu.SemaphoreType.DMA((chunks,))] if before else [],
+        )(*operands, *after)
+
+    def read_part(ops, final, *after):
+        arrived = [got[count - 1, k] for k in range(chunks)] if final else []
+        operands = [local, gain, asked, carry, *arrived]
+        return call(
+            functools.partial(read_kernel, count, chunks, ops, final),
+            (shape((STEPS, lanes)),) * (len(ops) + final),
+            in_specs=[in_vmem] * len(operands) + [anywhere] * len(after),
+        )(*operands, *after)
+
+    got = {(1, 0): forward(sent[0], 1, 0)}
+    moving = {}
+    inner = [inner_part(0)]
+    state_part(1, inner[0])
+    got[1, 1] = forward(sent[1], 1, 1)
+    inner += [inner_part(g, sent[1]) for g in range(1, groups)]
+    if not ride:
+        asks = [asked_here] + [shift(asked_here, r) for r in range(1, count)]
     order = sorted((k + hop, hop, k) for hop in range(1, count - 1) for k in range(chunks))
     early, late = tuple(range(chunks // 2)), tuple(range(chunks // 2, chunks))
-    after = inner
+    after = inner[-1:]
     carry = tie = None
     for _, hop, k in order:
         if (hop, k) == (1, 1):
             keep, fresh, held = fresh_part(tie)
             after = [keep]
         if (hop, k) == (count - 2, chunks - 2):
-            local, gain, asked_next = ask_part(tie)
+            local, gain, asked = ask_part(tie)
             after = [gain]
         if (hop, k) == (count - 2, chunks - 1):
-            prefill, token = outer_part(early, carry, [])
-            after = [token]
+            outer = outer_part((early,), carry, [], tie)
+            after = [outer]
         tail = [sent[0]] if ride and (hop, k) == (1, 0) else []
         filed = [] if carry is None else [carry]
         moving[hop + 1, k], carry = call(
             functools.partial(pass_kernel, hop, k, ride),
             (sent_shape(k), shape((chunks, N, width), BF16)),
-            2 * N * width,
-            8 * N * width,
             in_specs=[in_vmem] * (3 + len(filed) + len(tail)) + [anywhere] * len(after),
             input_output_aliases={3: 1} if filed else {},
-        )(got[hop, k], total, decay, *filed, *tail, *after)
-        got[hop + 1, k] = forward(moving[hop + 1, k], hop + 1)
+        )(got[hop, k], total[k], decay[k], *filed, *tail, *after)
+        got[hop + 1, k] = forward(moving[hop + 1, k], hop + 1, k)
         tie, after = moving[hop + 1, k], []
-
-    message = call(
-        functools.partial(message_kernel, count, chunks),
-        (shape((STEPS, 2 * lanes + 128)),) * count,
-        2 * rows * N * lanes,
-        4 * N * lanes,
-    )(local, gain, asked_next, *[moving[hop, k] for hop in range(1, count) for k in range(chunks)])
-    back = [message[0]] + [None] * (count - 1)
-    for r in reversed(range(1, count)):
-        back[r] = shift(message[r], -r)
-    prefill, token = outer_part(late, carry, [prefill])
+        if hop == 1 and k + 2 < chunks:
+            state_part(k + 2, tie)
+            got[1, k + 2] = forward(sent[k + 2], 1, k + 2)
+
+    back = []
+    if ride:
+        ops = [(0, 1), (0, 2), (1, 2)]
+        first_readings = read_part(ops, False, tie, got[count - 1, chunks - 2])
+        for (one, other), value in zip(ops, first_readings):
+            back.append(swap(value, (one, other)))
+        ends = [(0, 3), (1, 3), (2, 3)]
+        *reading, own = read_part(ends, True, first_readings[0])
+        for (one, other), value in zip(ends, reading):
+            back.append(swap(value, (one, other)))
+        ops = ops + ends
+    else:
+        *reading, own = read_part([(r, r) for r in range(count)], True)
+        ops = list(range(1, count))
+        back, own = [shift(reading[r], -r) for r in ops], reading[0]
+    prefill, token = outer_part((early, late), carry, [outer])
 
     decoded = call(
-        finish_kernel,
+        functools.partial(finish_kernel, ops),
         jax.ShapeDtypeStruct((count, STEPS, lanes), BF16),
-        4 * rows * lanes,
-        16 * rows * lanes,
-        in_specs=[in_vmem] * (3 + count) + [anywhere],
-    )(keep, fresh, held, *back, token)
+        in_specs=[in_vmem] * (4 + len(ops)) + [anywhere],
+    )(keep, fresh, held, *back, own, token)
     return (prefill, decoded[None])
 
 

time: 43.4 us -> 40.9 us (0.942)
  waiting for transfers between devices: 13 us -> 7.17 us
  starting transfers between devices: 18.6 us -> 22.5 us
  Pallas kernels: 10.8 us -> 10.2 us
    ppermute x15 -> x18, waiting for transfers between devices: 13 us -> 7.17 us  [swap(): return lax.ppermute(value, ('seq', 'tp'), pairs)]
    ppermute x15 -> x18, starting transfers between devices: 18.6 us -> 22.5 us  [swap(): return lax.ppermute(value, ('seq', 'tp'), pairs)]
    pallas_call x7 -> x11, Pallas kernels: 9.05 us -> 8.51 us  [the longest x2 2.04 us: inner_part(): call(functools.partial(inner_kernel, g), shape((tokens, group_lanes)), in...]
  transfers between devices with their start and end apart: 15 -> 18, of which waited for: 8 -> 6; matrix products, arithmetic and copies ran while one was open for 0% -> 0% of each run, Pallas kernels for 16% -> 18%
where the time goes in v6:
time: 40.9 us; the launch traced here: 40.7 us
  starting transfers between devices  22.5 us (55%)
  Pallas kernels  10.2 us (25%)
  waiting for transfers between devices  7.17 us (18%)
  between operations  0.85 us (2%)
    ppermute x18, starting transfers between devices, swap(): return lax.ppermute(value, ('seq', 'tp'), pairs)  22.5 us
    ppermute x18, waiting for transfers between devices, swap(): return lax.ppermute(value, ('seq', 'tp'), pairs)  7.17 us
    pallas_call x2, Pallas kernels, inner_part(): call(functools.partial(inner_kernel, g), shape((tokens, group_lanes)), in...  2.04 us
    pallas_call x2, Pallas kernels, outer_part(): call(functools.partial(outer_kernel, parts, count), (pltpu.HBM((tokens, l...  1.96 us
    pallas_call x1, Pallas kernels, shards(): call(functools.partial(first_kernel, len(inputs), ride), tuple((shape(val...  1.9 us
    pallas_call x3, Pallas kernels, state_part(): call(functools.partial(state_kernel, k), chunk_shapes[k], in_specs=[in_vm...  1.36 us
    pallas_call x1, Pallas kernels, ask_part(): call(functools.partial(ask_kernel, count, ride), (shape((rows, lanes)), s...  0.88 us
  transfers between devices with their start and end apart: 18, of which 6 were waited for; matrix products, arithmetic and copies ran while one was open for 0% of the time, Pallas kernels for 18%

profile of v6, /device:TPU:0, one launch (start us, length us, event | category | flops | bytes accessed | tf_op | source)
XLA Modules:
  0.0 40.7 jit_solution(6403942146213495313)
XLA Ops:
  0.6 1.9 %shard_map.131 = (bf16[256,2048]{1,0:T(8,128)(2,1)S(1)}, bf16[256,256]{1,0:T(8,128)(2,1)S(1)}, f32[1,32]{1,0:T(1,128)S(1)}, bf16[4,4,256]{2,1,0:T(4,128)(2,1)S(1...) custom-call(bf16[256,2048]{1,0:T(8,128)(2,1)} %refs_0_.1, ...), custom_call_target="tpu_custom_call" | custom-call | flops 1 | bytes 1 | tf_op jit(solution)/shard_map/pallas_call | solution.py:487
  2.5 3.1 %collective-permute-start.1 = (bf16[144,512]{1,0:T(8,128)(2,1)S(1)}, bf16[144,512]{1,0:T(8,128)(2,1)S(1)}, u32[]{:S(2)}, u32[]{:S(2)}) collective-permute-start(bf16[144,512]{1,0:T(8,128)(2,1)S(1)} %get-tuple-element.73.rest_0_), channel_id=1, source_target_pairs={{0,4},{1,5},{2,6},{3,7},{4,0},{5,1},{6,2},{7,3},{8,12},{9,13},{10,... | collective-permute-start | bytes 442376 | tf_op jit(solution)/shard_map/ppermute | solution.py:526
  5.6 1.0 %shard_map.132.rest_0_.rest_2_ = f32[256,1024]{1,0:T(8,128)S(1)} custom-call(bf16[256,2048]{1,0:T(8,128)(2,1)S(1)} %get-tuple-element.63.x_ref, bf16[256,256]{1,0:T(8,128)(2,1)S(1)} %get-tuple-element.67.b_ref, bf16[256,256]{1,0:T(8,128)(2,1)S(1)} %get-tuple-element.61.c_ref, f32[32,256]{1,0:T(8,128)S(1)} %get-tuple-element.62.cum_ref, ...), custom_call_target="tpu_custom_call" | custom-call | flops 1 | bytes 1 | tf_op jit(solution)/shard_map/pallas_call | solution.py:536
  6.7 0.5 %shard_map.133 = (f32[128,512]{1,0:T(8,128)S(1)}, bf16[128,512]{1,0:T(8,128)(2,1)S(1)}, f32[1,512]{1,0:T(1,128)S(1)}) custom-call(bf16[256,2048]{1,0:T(8,128)(2,1)S(1)} %get-tuple-element.63.x_ref, bf16[2,128,256]{2,1,0:T(8,128)(2,1)S(1)} %get-tuple-element.64.turned_ref, f32[256,32]{1,0:T(8,128)S(1)} %get-tuple-element.65.weight_ref, ...), custom_call_target="tpu_custom_call" | custom-call | flops 1 | bytes 1 | tf_op jit(solution)/shard_map/pallas_call | solution.py:509
  7.1 0.1 collective-permute-start
  7.2 1.0 %shard_map.134.rest_1_.rest_3_ = f32[256,1024]{1,0:T(8,128)S(1)} custom-call(bf16[256,2048]{1,0:T(8,128)(2,1)S(1)} %get-tuple-element.63.x_ref, bf16[256,256]{1,0:T(8,128)(2,1)S(1)} %get-tuple-element.67.b_ref, bf16[256,256]{1,0:T(8,128)(2,1)S(1)} %get-tuple-element.61.c_ref, f32[32,256]{1,0:T(8,128)S(1)} %get-tuple-element.62.cum_ref, ...), custom_call_target="tpu_custom_call" | custom-call | flops 1 | bytes 1 | tf_op jit(solution)/shard_map/pallas_call | solution.py:536
  8.2 1.7 %collective-permute-done.1.got_ref = bf16[144,512]{1,0:T(8,128)(2,1)S(1)} collective-permute-done((bf16[144,512]{1,0:T(8,128)(2,1)S(1)}, bf16[144,512]{1,0:T(8,128)(2,1)S(1)}, u32[]{:S(2)}, u32[]{:S(2)}) %collective-permute-start.1) | collective-permute-done | bytes 147488 | tf_op jit(solution)/shard_map/ppermute | solution.py:526
  9.9 0.1 shard_map.135
  10.0 0.1 collective-permute-start.5
  10.0 0.5 %shard_map.139 = (f32[128,512]{1,0:T(8,128)S(1)}, bf16[128,512]{1,0:T(8,128)(2,1)S(1)}, f32[1,512]{1,0:T(1,128)S(1)}) custom-call(bf16[256,2048]{1,0:T(8,128)(2,1)S(1)} %get-tuple-element.63.x_ref, bf16[2,128,256]{2,1,0:T(8,128)(2,1)S(1)} %get-tuple-element.64.turned_ref, f32[256,32]{1,0:T(8,128)S(1)} %get-tuple-element.65.weight_ref, ...), custom_call_target="tpu_custom_call" | custom-call | flops 1 | bytes 1 | tf_op jit(solution)/shard_map/pallas_call | solution.py:509
  10.5 2.9 %collective-permute-start.4 = (bf16[128,512]{1,0:T(8,128)(2,1)S(1)}, bf16[128,512]{1,0:T(8,128)(2,1)S(1)}, u32[]{:S(2)}, u32[]{:S(2)}) collective-permute-start(bf16[128,512]{1,0:T(8,128)(2,1)S(1)} %get-tuple-element.90), channel_id=1, source_target_pairs={{0,4},{1,5},{2,6},{3,7},{4,0},{5,1},{6,2},{7,3},{8,9},{9,8},{10,11... | collective-permute-start | bytes 393224 | tf_op jit(solution)/shard_map/ppermute | solution.py:526
  13.4 0.4 %shard_map.136 = (f32[4,4,2048]{2,1,0:T(4,128)S(1)}, f32[4,4,2048]{2,1,0:T(4,128)S(1)}, f32[4,4,128]{2,1,0:T(4,128)S(1)}) custom-call(bf16[4,4,2048]{2,1,0:T(4,128)(2,1)S(1)} %get-tuple-element.77.x_ref, bf16[4,4,256]{2,1,0:T(4,128)(2,1)S(1)} %get-tuple-element.78.b_ref, bf16[4,4,256]{2,1,0:T(4,128)(2,1)S(1)} %get-tuple-element.79.c_ref, ...), custom_call_target="tpu_custom_call" | custom-call | flops 1 | bytes 1 | tf_op jit(solution)/shard_map/pallas_call | solution.py:551
  13.9 0.0 collective-permute-done.got_ref
  13.9 0.1 collective-permute-start.3
  14.0 0.5 %shard_map.138 = (f32[128,512]{1,0:T(8,128)S(1)}, bf16[128,512]{1,0:T(8,128)(2,1)S(1)}, f32[1,512]{1,0:T(1,128)S(1)}) custom-call(bf16[256,2048]{1,0:T(8,128)(2,1)S(1)} %get-tuple-element.63.x_ref, bf16[2,128,256]{2,1,0:T(8,128)(2,1)S(1)} %get-tuple-element.64.turned_ref, f32[256,32]{1,0:T(8,128)S(1)} %get-tuple-element.65.weight_ref, ...), custom_call_target="tpu_custom_call" | custom-call | flops 1 | bytes 1 | tf_op jit(solution)/shard_map/pallas_call | solution.py:509
  14.5 1.7 %collective-permute-start.2 = (bf16[128,512]{1,0:T(8,128)(2,1)S(1)}, bf16[128,512]{1,0:T(8,128)(2,1)S(1)}, u32[]{:S(2)}, u32[]{:S(2)}) collective-permute-start(bf16[128,512]{1,0:T(8,128)(2,1)S(1)} %get-tuple-element.87), channel_id=1, source_target_pairs={{0,4},{1,5},{2,6},{3,7},{4,0},{5,1},{6,2},{7,3},{8,9},{9,8},{10,11... | collective-permute-start | bytes 393224 | tf_op jit(solution)/shard_map/ppermute | solution.py:526
  16.1 0.0 collective-permute-done.5.got_ref.rest_1_
  16.2 2.3 %collective-permute-start.8 = (bf16[144,512]{1,0:T(8,128)(2,1)S(1)}, bf16[144,512]{1,0:T(8,128)(2,1)S(1)}, u32[]{:S(2)}, u32[]{:S(2)}) collective-permute-start(bf16[144,512]{1,0:T(8,128)(2,1)S(1)} %get-tuple-element.100), channel_id=1, source_target_pairs={{0,4},{1,5},{2,6},{3,7},{4,0},{5,1},{6,2},{7,3},{8,12},{9,13},{10,... | collective-permute-start | bytes 442376 | tf_op jit(solution)/shard_map/ppermute | solution.py:526
  18.5 0.0 collective-permute-done.4.got_ref
  18.5 0.1 collective-permute-start.7
  18.6 0.0 collective-permute-done.3.got_ref
  18.7 0.6 %collective-permute-start.9 = (bf16[128,512]{1,0:T(8,128)(2,1)S(1)}, bf16[128,512]{1,0:T(8,128)(2,1)S(1)}, u32[]{:S(2)}, u32[]{:S(2)}) collective-permute-start(bf16[128,512]{1,0:T(8,128)(2,1)S(1)} %get-tuple-element.103), channel_id=1, source_target_pairs={{0,1},{1,0},{2,3},{3,2},{4,5},{5,4},{6,7},{7,6},{8,12},{9,13},{10,... | collective-permute-start | bytes 393224 | tf_op jit(solution)/shard_map/ppermute | solution.py:526
  19.2 1.6 %collective-permute-done.2.got_ref = bf16[128,512]{1,0:T(8,128)(2,1)S(1)} collective-permute-done((bf16[128,512]{1,0:T(8,128)(2,1)S(1)}, bf16[128,512]{1,0:T(8,128)(2,1)S(1)}, u32[]{:S(2)}, u32[]{:S(2)}) %collective-permute-start.2) | collective-permute-done | bytes 131104 | tf_op jit(solution)/shard_map/ppermute | solution.py:526
  20.8 0.1 collective-permute-start.6
  20.9 2.6 %collective-permute-done.8.rest_2_.rest_0_ = bf16[144,512]{1,0:T(8,128)(2,1)S(1)} collective-permute-done((bf16[144,512]{1,0:T(8,128)(2,1)S(1)}, bf16[144,512]{1,0:T(8,128)(2,1)S(1)}, u32[]{:S(2)}, u32[]{:S(2)}) %collective-permute-start.8) | collective-permute-done | bytes 147488 | tf_op jit(solution)/shard_map/ppermute | solution.py:526
  23.6 0.9 %shard_map.144 = (f32[16,2048]{1,0:T(8,128)S(1)}, f32[16,32]{1,0:T(8,128)S(1)}, bf16[16,256]{1,0:T(8,128)(2,1)S(1)}) custom-call(bf16[256,2048]{1,0:T(8,128)(2,1)S(1)} %get-tuple-element.63.x_ref, bf16[256,256]{1,0:T(8,128)(2,1)S(1)} %get-tuple-element.67.b_ref, f32[32,256]{1,0:T(8,128)S(1)} %get-tuple-element.62.cum_ref, ...), custom_call_target="tpu_custom_call" | custom-call | flops 1 | bytes 1 | tf_op jit(solution)/shard_map/pallas_call | solution.py:544
  24.4 0.0 collective-permute-done.7.got_ref
  24.5 0.1 shard_map.145
  24.5 0.1 collective-permute-start.10
  24.6 0.0 collective-permute-done.9.rest_1_
  24.6 0.6 %shard_map.146.rest_1_.rest_4_ = bf16[2,256,512]{2,1,0:T(8,128)(2,1)S(1)} custom-call(bf16[256,256]{1,0:T(8,128)(2,1)S(1)} %get-tuple-element.61.c_ref, f32[32,256]{1,0:T(8,128)S(1)} %get-tuple-element.62.cum_ref, bf16[4,128,512]{2,1,0:T(8,128)(2,1)S(1)} %get-tuple-element.102.carry_ref.rest_0_, bf16[144,512]{1,0:T(8,128)(2,1)S(1)} %collective-permute-done.8.rest_2_.rest_0_, ...), custom_call_target="tpu_custom_call" | custom-call | flops 1 | bytes 1 | tf_op jit(solution)/shard_map/pallas_call | solution.py:561
  25.2 0.0 collective-permute-done.6.got_ref
  25.3 0.6 %collective-permute-start.11 = (bf16[128,512]{1,0:T(8,128)(2,1)S(1)}, bf16[128,512]{1,0:T(8,128)(2,1)S(1)}, u32[]{:S(2)}, u32[]{:S(2)}) collective-permute-start(bf16[128,512]{1,0:T(8,128)(2,1)S(1)} %get-tuple-element.106.rest_0_), channel_id=1, source_target_pairs={{0,1},{1,0},{2,3},{3,2},{4,5},{5,4},{6,7},{7,6},{8,12},{9,13},{10,... | collective-permute-start | bytes 393224 | tf_op jit(solution)/shard_map/ppermute | solution.py:526
  25.8 0.1 collective-permute-done.10.rest_0_.rest_1_.rest_2_
  25.9 0.2 shard_map.149
  26.2 0.6 %collective-permute-done.11.rest_1_.rest_3_ = bf16[128,512]{1,0:T(8,128)(2,1)S(1)} collective-permute-done((bf16[128,512]{1,0:T(8,128)(2,1)S(1)}, bf16[128,512]{1,0:T(8,128)(2,1)S(1)}, u32[]{:S(2)}, u32[]{:S(2)}) %collective-permute-start.11) | collective-permute-done | bytes 131104 | tf_op jit(solution)/shard_map/ppermute | solution.py:526
  26.8 0.3 shard_map.150
  27.1 6.0 %collective-permute-start.15 = (f32[4,2048]{1,0:T(4,128)S(1)}, f32[4,2048]{1,0:T(4,128)S(1)}, u32[]{:S(2)}, u32[]{:S(2)}) collective-permute-start(f32[4,2048]{1,0:T(4,128)S(1)} %get-tuple-element.115), channel_id=1, source_target_pairs={{0,12},{1,13},{2,14},{3,15},{4,5},{5,4},{6,7},{7,6},{8,9},{9,8},{1... | collective-permute-start | bytes 98312 | tf_op jit(solution)/shard_map/ppermute | solution.py:526
  33.1 0.0 collective-permute-start.12
  33.1 0.0 collective-permute-start.16
  33.1 0.5 %collective-permute-start.17 = (f32[4,2048]{1,0:T(4,128)S(1)}, f32[4,2048]{1,0:T(4,128)S(1)}, u32[]{:S(2)}, u32[]{:S(2)}) collective-permute-start(f32[4,2048]{1,0:T(4,128)S(1)} %get-tuple-element.117), channel_id=1, source_target_pairs={{0,1},{1,0},{2,3},{3,2},{4,5},{5,4},{6,7},{7,6},{8,12},{9,13},{10,... | collective-permute-start | bytes 98312 | tf_op jit(solution)/shard_map/ppermute | solution.py:526
  33.6 4.4 %collective-permute-start.13 = (f32[4,2048]{1,0:T(4,128)S(1)}, f32[4,2048]{1,0:T(4,128)S(1)}, u32[]{:S(2)}, u32[]{:S(2)}) collective-permute-start(f32[4,2048]{1,0:T(4,128)S(1)} %get-tuple-element.113), channel_id=1, source_target_pairs={{0,8},{1,9},{2,10},{3,11},{4,5},{5,4},{6,7},{7,6},{8,0},{9,1},{10,... | collective-permute-start | bytes 98312 | tf_op jit(solution)/shard_map/ppermute | solution.py:526
  38.1 0.0 collective-permute-done.15.rest_3_
  38.1 0.0 collective-permute-start.14
  38.1 1.4 %shard_map.148 = (bf16[256,2048]{1,0:T(8,128)(2,1)}, f32[8,128]{1,0:T(8,128)S(1)}) custom-call(bf16[256,256]{1,0:T(8,128)(2,1)S(1)} %get-tuple-element.61.c_ref, f32[32,256]{1,0:T(8,128)S(1)} %get-tuple-element.62.cum_ref, bf16[4,128,512]{2,1,0:T(8,128)(2,1)S(1)} %get-tuple-element.105.carry_ref, ...), custom_call_target="tpu_custom_call" | custom-call | flops 1 | bytes 1 | tf_op jit(solution)/shard_map/pallas_call | solution.py:561
  39.4 0.0 collective-permute-done.16.rest_4_
  39.4 0.0 collective-permute-done.17.rest_5_
  39.5 0.0 collective-permute-done.12.rest_0_
  39.5 0.5 %collective-permute-done.13.rest_1_ = f32[4,2048]{1,0:T(4,128)S(1)} collective-permute-done((f32[4,2048]{1,0:T(4,128)S(1)}, f32[4,2048]{1,0:T(4,128)S(1)}, u32[]{:S(2)}, u32[]{:S(2)}) %collective-permute-start.13) | collective-permute-done | bytes 32800 | tf_op jit(solution)/shard_map/ppermute | solution.py:526
  40.0 0.0 collective-permute-done.14.rest_2_
  40.0 0.7 %shard_map.151 = bf16[4,4,2048]{2,1,0:T(4,128)(2,1)} custom-call(f32[4,4,2048]{2,1,0:T(4,128)S(1)} %get-tuple-element.85.rest_1_.keep_ref, f32[4,4,2048]{2,1,0:T(4,128)S(1)} %get-tuple-element.108.fresh_ref, f32[4,4,128]{2,1,0:T(4,128)S(1)} %get-tuple-element.109.held_ref, f32[4,2048]{1,0:T(4,128)S(1)} %collective-permute-done.12.rest_0_, ...), custom_call_target="tpu_custom_call" | custom-call | flops 1 | bytes 1 | tf_op jit(solution)/shard_map/pallas_call | solution.py:631
  (6 shorter events, 0.3 us)
Async XLA Ops:
  2.5 7.3 %collective-permute-start.1 = (bf16[144,512]{1,0:T(8,128)(2,1)S(1)}, bf16[144,512]{1,0:T(8,128)(2,1)S(1)}, u32[]{:S(2)}, u32[]{:S(2)}) collective-permute-start(bf16[144,512]{1,0:T(8,128)(2,1)S(1)} %get-tuple-element.73.rest_0_), channel_id=1, source_target_pairs={{0,4},{1,5},{2,6},{3,7},{4,0},{5,1},{6,2},{7,3},{8,12},{9,13},{10,... | collective-permute-start | bytes 442376 | tf_op jit(solution)/shard_map/ppermute | solution.py:526
  7.1 6.8 %collective-permute-start = (bf16[128,512]{1,0:T(8,128)(2,1)S(1)}, bf16[128,512]{1,0:T(8,128)(2,1)S(1)}, u32[]{:S(2)}, u32[]{:S(2)}) collective-permute-start(bf16[128,512]{1,0:T(8,128)(2,1)S(1)} %get-tuple-element.70.rest_0_), channel_id=1, source_target_pairs={{0,4},{1,5},{2,6},{3,7},{4,0},{5,1},{6,2},{7,3},{8,9},{9,8},{10,11... | collective-permute-start | bytes 393224 | tf_op jit(solution)/shard_map/ppermute | solution.py:526
  10.0 6.2 %collective-permute-start.5 = (bf16[144,512]{1,0:T(8,128)(2,1)S(1)}, bf16[144,512]{1,0:T(8,128)(2,1)S(1)}, u32[]{:S(2)}, u32[]{:S(2)}) collective-permute-start(bf16[144,512]{1,0:T(8,128)(2,1)S(1)} %get-tuple-element.84.rest_0_), channel_id=1, source_target_pairs={{0,1},{1,0},{2,3},{3,2},{4,8},{5,9},{6,10},{7,11},{8,4},{9,5},{10,... | collective-permute-start | bytes 442376 | tf_op jit(solution)/shard_map/ppermute | solution.py:526
  10.5 8.0 %collective-permute-start.4 = (bf16[128,512]{1,0:T(8,128)(2,1)S(1)}, bf16[128,512]{1,0:T(8,128)(2,1)S(1)}, u32[]{:S(2)}, u32[]{:S(2)}) collective-permute-start(bf16[128,512]{1,0:T(8,128)(2,1)S(1)} %get-tuple-element.90), channel_id=1, source_target_pairs={{0,4},{1,5},{2,6},{3,7},{4,0},{5,1},{6,2},{7,3},{8,9},{9,8},{10,11... | collective-permute-start | bytes 393224 | tf_op jit(solution)/shard_map/ppermute | solution.py:526
  13.9 4.7 %collective-permute-start.3 = (bf16[128,512]{1,0:T(8,128)(2,1)S(1)}, bf16[128,512]{1,0:T(8,128)(2,1)S(1)}, u32[]{:S(2)}, u32[]{:S(2)}) collective-permute-start(bf16[128,512]{1,0:T(8,128)(2,1)S(1)} %get-tuple-element.86.rest_0_), channel_id=1, source_target_pairs={{0,1},{1,0},{2,3},{3,2},{4,8},{5,9},{6,10},{7,11},{8,4},{9,5},{10,... | collective-permute-start | bytes 393224 | tf_op jit(solution)/shard_map/ppermute | solution.py:526
  14.5 6.3 %collective-permute-start.2 = (bf16[128,512]{1,0:T(8,128)(2,1)S(1)}, bf16[128,512]{1,0:T(8,128)(2,1)S(1)}, u32[]{:S(2)}, u32[]{:S(2)}) collective-permute-start(bf16[128,512]{1,0:T(8,128)(2,1)S(1)} %get-tuple-element.87), channel_id=1, source_target_pairs={{0,4},{1,5},{2,6},{3,7},{4,0},{5,1},{6,2},{7,3},{8,9},{9,8},{10,11... | collective-permute-start | bytes 393224 | tf_op jit(solution)/shard_map/ppermute | solution.py:526
  16.2 7.4 %collective-permute-start.8 = (bf16[144,512]{1,0:T(8,128)(2,1)S(1)}, bf16[144,512]{1,0:T(8,128)(2,1)S(1)}, u32[]{:S(2)}, u32[]{:S(2)}) collective-permute-start(bf16[144,512]{1,0:T(8,128)(2,1)S(1)} %get-tuple-element.100), channel_id=1, source_target_pairs={{0,4},{1,5},{2,6},{3,7},{4,0},{5,1},{6,2},{7,3},{8,12},{9,13},{10,... | collective-permute-start | bytes 442376 | tf_op jit(solution)/shard_map/ppermute | solution.py:526
  18.5 5.9 %collective-permute-start.7 = (bf16[128,512]{1,0:T(8,128)(2,1)S(1)}, bf16[128,512]{1,0:T(8,128)(2,1)S(1)}, u32[]{:S(2)}, u32[]{:S(2)}) collective-permute-start(bf16[128,512]{1,0:T(8,128)(2,1)S(1)} %get-tuple-element.98), channel_id=1, source_target_pairs={{0,1},{1,0},{2,3},{3,2},{4,8},{5,9},{6,10},{7,11},{8,4},{9,5},{10,... | collective-permute-start | bytes 393224 | tf_op jit(solution)/shard_map/ppermute | solution.py:526
  18.7 5.9 %collective-permute-start.9 = (bf16[128,512]{1,0:T(8,128)(2,1)S(1)}, bf16[128,512]{1,0:T(8,128)(2,1)S(1)}, u32[]{:S(2)}, u32[]{:S(2)}) collective-permute-start(bf16[128,512]{1,0:T(8,128)(2,1)S(1)} %get-tuple-element.103), channel_id=1, source_target_pairs={{0,1},{1,0},{2,3},{3,2},{4,5},{5,4},{6,7},{7,6},{8,12},{9,13},{10,... | collective-permute-start | bytes 393224 | tf_op jit(solution)/shard_map/ppermute | solution.py:526
  20.8 4.4 %collective-permute-start.6 = (bf16[128,512]{1,0:T(8,128)(2,1)S(1)}, bf16[128,512]{1,0:T(8,128)(2,1)S(1)}, u32[]{:S(2)}, u32[]{:S(2)}) collective-permute-start(bf16[128,512]{1,0:T(8,128)(2,1)S(1)} %get-tuple-element.97.rest_3_), channel_id=1, source_target_pairs={{0,1},{1,0},{2,3},{3,2},{4,8},{5,9},{6,10},{7,11},{8,4},{9,5},{10,... | collective-permute-start | bytes 393224 | tf_op jit(solution)/shard_map/ppermute | solution.py:526
  24.5 1.4 %collective-permute-start.10 = (bf16[128,512]{1,0:T(8,128)(2,1)S(1)}, bf16[128,512]{1,0:T(8,128)(2,1)S(1)}, u32[]{:S(2)}, u32[]{:S(2)}) collective-permute-start(bf16[128,512]{1,0:T(8,128)(2,1)S(1)} %get-tuple-element.104.rest_4_), channel_id=1, source_target_pairs={{0,1},{1,0},{2,3},{3,2},{4,5},{5,4},{6,7},{7,6},{8,12},{9,13},{10,... | collective-permute-start | bytes 393224 | tf_op jit(solution)/shard_map/ppermute | solution.py:526
  25.3 1.5 %collective-permute-start.11 = (bf16[128,512]{1,0:T(8,128)(2,1)S(1)}, bf16[128,512]{1,0:T(8,128)(2,1)S(1)}, u32[]{:S(2)}, u32[]{:S(2)}) collective-permute-start(bf16[128,512]{1,0:T(8,128)(2,1)S(1)} %get-tuple-element.106.rest_0_), channel_id=1, source_target_pairs={{0,1},{1,0},{2,3},{3,2},{4,5},{5,4},{6,7},{7,6},{8,12},{9,13},{10,... | collective-permute-start | bytes 393224 | tf_op jit(solution)/shard_map/ppermute | solution.py:526
  27.1 11.0 %collective-permute-start.15 = (f32[4,2048]{1,0:T(4,128)S(1)}, f32[4,2048]{1,0:T(4,128)S(1)}, u32[]{:S(2)}, u32[]{:S(2)}) collective-permute-start(f32[4,2048]{1,0:T(4,128)S(1)} %get-tuple-element.115), channel_id=1, source_target_pairs={{0,12},{1,13},{2,14},{3,15},{4,5},{5,4},{6,7},{7,6},{8,9},{9,8},{1... | collective-permute-start | bytes 98312 | tf_op jit(solution)/shard_map/ppermute | solution.py:526
  33.1 6.3 %collective-permute-start.12 = (f32[4,2048]{1,0:T(4,128)S(1)}, f32[4,2048]{1,0:T(4,128)S(1)}, u32[]{:S(2)}, u32[]{:S(2)}) collective-permute-start(f32[4,2048]{1,0:T(4,128)S(1)} %get-tuple-element.112.rest_4_), channel_id=1, source_target_pairs={{0,4},{1,5},{2,6},{3,7},{4,0},{5,1},{6,2},{7,3},{8,9},{9,8},{10,11... | collective-permute-start | bytes 98312 | tf_op jit(solution)/shard_map/ppermute | solution.py:526
  33.1 6.3 %collective-permute-start.16 = (f32[4,2048]{1,0:T(4,128)S(1)}, f32[4,2048]{1,0:T(4,128)S(1)}, u32[]{:S(2)}, u32[]{:S(2)}) collective-permute-start(f32[4,2048]{1,0:T(4,128)S(1)} %get-tuple-element.116), channel_id=1, source_target_pairs={{0,1},{1,0},{2,3},{3,2},{4,12},{5,13},{6,14},{7,15},{8,9},{9,8},{1... | collective-permute-start | bytes 98312 | tf_op jit(solution)/shard_map/ppermute | solution.py:526
  33.1 6.3 %collective-permute-start.17 = (f32[4,2048]{1,0:T(4,128)S(1)}, f32[4,2048]{1,0:T(4,128)S(1)}, u32[]{:S(2)}, u32[]{:S(2)}) collective-permute-start(f32[4,2048]{1,0:T(4,128)S(1)} %get-tuple-element.117), channel_id=1, source_target_pairs={{0,1},{1,0},{2,3},{3,2},{4,5},{5,4},{6,7},{7,6},{8,12},{9,13},{10,... | collective-permute-start | bytes 98312 | tf_op jit(solution)/shard_map/ppermute | solution.py:526
  33.6 6.3 %collective-permute-start.13 = (f32[4,2048]{1,0:T(4,128)S(1)}, f32[4,2048]{1,0:T(4,128)S(1)}, u32[]{:S(2)}, u32[]{:S(2)}) collective-permute-start(f32[4,2048]{1,0:T(4,128)S(1)} %get-tuple-element.113), channel_id=1, source_target_pairs={{0,8},{1,9},{2,10},{3,11},{4,5},{5,4},{6,7},{7,6},{8,0},{9,1},{10,... | collective-permute-start | bytes 98312 | tf_op jit(solution)/shard_map/ppermute | solution.py:526
  38.1 1.9 %collective-permute-start.14 = (f32[4,2048]{1,0:T(4,128)S(1)}, f32[4,2048]{1,0:T(4,128)S(1)}, u32[]{:S(2)}, u32[]{:S(2)}) collective-permute-start(f32[4,2048]{1,0:T(4,128)S(1)} %get-tuple-element.114), channel_id=1, source_target_pairs={{0,1},{1,0},{2,3},{3,2},{4,8},{5,9},{6,10},{7,11},{8,4},{9,5},{10,... | collective-permute-start | bytes 98312 | tf_op jit(solution)/shard_map/ppermute | solution.py:526

commit v7 on v6

--- a/solution.py
+++ b/solution.py
@@ -68,12 +68,12 @@
     return pltpu.with_memory_space_constraint(value, space)
 
 
-def call(kernel, out_shape, **options):
+def call(kernel, out_shape, flops=1, **options):
     return pl.pallas_call(
         kernel,
         out_shape=out_shape,
         compiler_params=pltpu.CompilerParams(vmem_limit_bytes=VMEM_LIMIT),
-        cost_estimate=pl.CostEstimate(flops=1, bytes_accessed=1, transcendentals=0),
+        cost_estimate=pl.CostEstimate(flops=flops, bytes_accessed=1, transcendentals=0),
         **options,
     )
 
@@ -84,13 +84,11 @@
     return jnp.where(keep(row, column), 1.0, 0.0).astype(BF16)
 
 
-def chunk_total(k, x_ref, turned, weight, whole, total_ref, sent_ref, decay_ref):
+def chunk_total(k, x_ref, turned, weight, whole, total_ref, decay_ref):
     width = total_ref.shape[1]
     first = k * width
     scaled = x_ref[:, first : first + width].astype(F32) * over_lanes(weight, first, width)
-    total = dot(turned, scaled.astype(BF16))
-    total_ref[...] = total
-    sent_ref[:N] = total.astype(BF16)
+    total_ref[...] = dot(turned, scaled.astype(BF16))
     decay_ref[...] = over_lanes(whole, first, width, 3)
 
 
@@ -98,7 +96,7 @@
     hbm, refs = refs[: kept + 1], refs[kept + 1 :]
     here, refs = refs[:kept], refs[kept:]
     cum_ref, row_ref, weight_ref, whole_ref, turned_ref = refs[:5]
-    total_ref, sent_ref, decay_ref, dt_ref, sems = refs[5:]
+    total_ref, decay_ref, sent_ref, dt_ref, sems = refs[5:]
     x_ref, b_ref, a_ref, asked_ref = here[:4]
     heads, tokens = dt_ref.shape
     spans = tokens // SPAN
@@ -134,7 +132,8 @@
     copies[0].wait()
     turned = b_ref[:, :N].astype(F32).T.astype(BF16)
     x_copies[0].wait()
-    chunk_total(0, x_ref, turned, weight, whole, total_ref, sent_ref, decay_ref)
+    chunk_total(0, x_ref, turned, weight, whole, total_ref, decay_ref)
+    sent_ref[:N] = total_ref[...].astype(BF16)
     turned_ref[0] = turned
     for g in range(1, turned_ref.shape[0]):
         turned_ref[g] = b_ref[:, g * N : (g + 1) * N].astype(F32).T.astype(BF16)
@@ -149,23 +148,31 @@
         sent_ref[N:] = jnp.concatenate([own, own], axis=1)
 
 
-def state_kernel(k, x_ref, turned_ref, weight_ref, whole_ref, *rest):
-    total_ref, sent_ref, decay_ref = rest[-3:]
-    g = k * total_ref.shape[1] // (H // G * P_SIZE)
-    chunk_total(
-        k, x_ref, turned_ref[g], weight_ref[...], whole_ref[...], total_ref, sent_ref, decay_ref
-    )
+def state_kernel(part, first, x_ref, turned_ref, weight_ref, whole_ref, *rest):
+    results = rest[-2 * len(part) - first :]
+    for i, k in enumerate(part):
+        total_ref, decay_ref = results[2 * i : 2 * i + 2]
+        g = k * total_ref.shape[1] // (H // G * P_SIZE)
+        chunk_total(k, x_ref, turned_ref[g], weight_ref[...], whole_ref[...], total_ref, decay_ref)
+    if first:
+        results[-1][...] = results[0][...].astype(BF16)
 
 
 def flat(ref):
     return jnp.concatenate([ref[i].astype(F32) for i in range(ref.shape[0])], axis=0)
 
 
-def pass_kernel(hop, k, ride, got_ref, total_ref, decay_ref, *rest):
-    moving_ref, carry_ref = rest[-2:]
+def token_kernel(got_ref, tie_ref, token_ref):
+    token_ref[...] = jnp.zeros_like(token_ref)
+
+
+def pass_kernel(hop, k, tail, more, got_ref, total_ref, decay_ref, *rest):
+    extra, (moving_ref, carry_ref) = rest, rest[-2 - more : len(rest) - more]
     me = lax.axis_index("seq")
     if hop == 1 and k == 0:
         carry_ref[...] = jnp.zeros_like(carry_ref)
+    else:
+        extra = extra[1:]
     got = got_ref[:N]
     moving_ref[:N] = (total_ref[...] + decay_ref[...] * got.astype(F32)).astype(BF16)
 
@@ -173,15 +180,16 @@
     def _():
         carry_ref[k] = got
 
-    if ride and k == 0:
-        tail = got_ref[N:]
+    if more:
+        rest[-1][...] = extra[0][...].astype(BF16)
+        extra = extra[1:]
+    if tail:
+        rows = extra[0][N:]
         if hop == 1:
-            own = rest[0][N:]
-            names = tail.shape[1] // 2
-            lane = lax.broadcasted_iota(jnp.int32, tail.shape, 1)
-            mine = (lane // names) == lax.rem(me, 2)
-            tail = jnp.where(mine, own.astype(F32), tail.astype(F32)).astype(BF16)
-        moving_ref[N:] = tail
+            lane = lax.broadcasted_iota(jnp.int32, rows.shape, 1)
+            mine = (lane // (rows.shape[1] // 2)) == lax.rem(me, 2)
+            rows = jnp.where(mine, rows.astype(F32), got_ref[N:].astype(F32)).astype(BF16)
+        moving_ref[N:] = rows
 
 
 def pair_halves(x_part):
@@ -324,7 +332,7 @@
             part = parts[other]
             if one != other:
                 part = jnp.where(me == one, part, parts[one])
-            read_ref[:, here] = part
+            read_ref[:, here] = part.astype(read_ref.dtype)
         if final:
             own = parts[0]
             for r in range(1, count):
@@ -439,12 +447,12 @@
             for (one, other), back_ref in zip(ops, back_refs):
                 if source in (one, other):
                     owner = one + other - source
-                    reading = jnp.where(me == owner, back_ref[...], reading)
+                    reading = jnp.where(me == owner, back_ref[...].astype(F32), reading)
             finish(source, reading)
     else:
         finish(me, own_ref[...])
         for r, back_ref in zip(ops, back_refs):
-            finish(lax.rem(me + r, count), back_ref[...])
+            finish(lax.rem(me + r, count), back_ref[...].astype(F32))
 
 
 def shards(
@@ -465,8 +473,9 @@
     in_vmem = pl.BlockSpec(memory_space=pltpu.VMEM)
     ride = count == 4 and width == 2 * names
 
-    def sent_shape(k):
-        return shape((N + rows * (ride and k == 0), width), BF16)
+    def sent_shape(hop, k):
+        tail = ride and (hop, k) in ((1, 0), (2, 0), (3, 2))
+        return shape((N + rows * tail, width), BF16)
 
     inputs = [
         ssm_input,
@@ -481,9 +490,7 @@
         dec_b[0],
         dec_dt[0],
     ]
-    chunk_shapes = [
-        (shape((N, width)), sent_shape(k), shape((1, width))) for k in range(chunks)
-    ]
+    chunk_shapes = (shape((N, width)), shape((1, width)))
     results = call(
         functools.partial(first_kernel, len(inputs), ride),
         tuple(shape(value.shape, value.dtype) for value in inputs)
@@ -494,7 +501,8 @@
             shape((1, heads)),
             shape((groups, N, tokens), BF16),
         )
-        + chunk_shapes[0],
+        + chunk_shapes
+        + (sent_shape(1, 0),),
         in_specs=[in_hbm] * (len(inputs) + 1),
         scratch_shapes=[
             pltpu.VMEM((heads, tokens), BF16),
@@ -503,16 +511,20 @@
     )(*[pinned(value, pltpu.HBM) for value in inputs + [dt_raw.T]])
     x, b, a_row, asked_here, c, d_row, len_row, owner_row, x_dec, b_dec, dt_dec = results[:11]
     cum, row, weight, whole, turned = results[11:16]
-    total, sent, decay = ([value] for value in results[16:])
-
-    def state_part(k, tie):
-        part = call(
-            functools.partial(state_kernel, k),
-            chunk_shapes[k],
+    total, decay = [results[16]], [results[17]]
+    sent = {0: results[18]}
+
+    def state_part(part, tie):
+        first = part[0] == 1
+        out = call(
+            functools.partial(state_kernel, part, first),
+            chunk_shapes * len(part) + (sent_shape(1, 1),) * first,
             in_specs=[in_vmem] * 4 + [anywhere],
         )(x, turned, weight, whole, tie)
-        for values, value in zip((total, sent, decay), part):
-            values.append(value)
+        total.extend(out[0 : 2 * len(part) : 2])
+        decay.extend(out[1 : 2 * len(part) : 2])
+        if first:
+            sent[1] = out[-1]
 
     def swap(value, *couples):
         partner = {}
@@ -526,7 +538,7 @@
         return lax.ppermute(value, ("seq", "tp"), pairs)
 
     def forward(value, hop, k):
-        rides = ride and k == 0 and hop != 2
+        rides = ride and (hop, k) in ((1, 0), (3, 2))
         return swap(value, *([(0, 1), (2, 3)] if rides else [(hop - 1, hop)]))
 
     def shift(value, by):
@@ -540,7 +552,7 @@
         )(x, b, c, cum, row, d_row, *after)
 
     def ask_part(*after):
-        blocks = (moving[2, 0], got[2, 0], got[3, 0]) if ride else asks
+        blocks = (moving[2, 0], got[2, 0], got[3, 2]) if ride else asks
         return call(
             functools.partial(ask_kernel, count, ride),
             (shape((rows, lanes)), shape((rows, heads)), shape((rows, names), BF16)),
@@ -571,61 +583,69 @@
         operands = [local, gain, asked, carry, *arrived]
         return call(
             functools.partial(read_kernel, count, chunks, ops, final),
-            (shape((STEPS, lanes)),) * (len(ops) + final),
+            (shape((STEPS, lanes), BF16),) * len(ops) + (shape((STEPS, lanes)),) * final,
             in_specs=[in_vmem] * len(operands) + [anywhere] * len(after),
         )(*operands, *after)
 
     got = {(1, 0): forward(sent[0], 1, 0)}
     moving = {}
     inner = [inner_part(0)]
-    state_part(1, inner[0])
+    for g in range(1, groups):
+        inner.append(inner_part(g, inner[-1]))
+    state_part([1], inner[-1])
     got[1, 1] = forward(sent[1], 1, 1)
-    inner += [inner_part(g, sent[1]) for g in range(1, groups)]
+    if chunks > 2:
+        state_part(list(range(2, chunks)), sent[1])
+    keep, fresh, held = fresh_part(total[-1])
     if not ride:
         asks = [asked_here] + [shift(asked_here, r) for r in range(1, count)]
     order = sorted((k + hop, hop, k) for hop in range(1, count - 1) for k in range(chunks))
-    early, late = tuple(range(chunks // 2)), tuple(range(chunks // 2, chunks))
-    after = inner[-1:]
     carry = tie = None
     for _, hop, k in order:
-        if (hop, k) == (1, 1):
-            keep, fresh, held = fresh_part(tie)
-            after = [keep]
-        if (hop, k) == (count - 2, chunks - 2):
-            local, gain, asked = ask_part(tie)
-            after = [gain]
-        if (hop, k) == (count - 2, chunks - 1):
-            outer = outer_part((early,), carry, [], tie)
-            after = [outer]
-        tail = [sent[0]] if ride and (hop, k) == (1, 0) else []
-        filed = [] if carry is None else [carry]
-        moving[hop + 1, k], carry = call(
-            functools.partial(pass_kernel, hop, k, ride),
-            (sent_shape(k), shape((chunks, N, width), BF16)),
-            in_specs=[in_vmem] * (3 + len(filed) + len(tail)) + [anywhere] * len(after),
-            input_output_aliases={3: 1} if filed else {},
-        )(got[hop, k], total[k], decay[k], *filed, *tail, *after)
+        tail = {(1, 0): sent[0], (2, 2): got.get((2, 0))}.get((hop, k)) if ride else None
+        more = hop == 1 and k + 2 < chunks
+        operands = [got[hop, k], total[k], decay[k]]
+        operands += [] if carry is None else [carry]
+        operands += total[k + 2 : k + 3] * more + [tail] * (tail is not None)
+        after = [keep] if carry is None else []
+        if hop == count - 2 and k > 1:
+            after.append(
+                call(
+                    token_kernel, shape((8, 128)), flops=10**9, in_specs=[anywhere] * 2
+                )(got[hop + 1, k - 2], tie)
+            )
+        moving[hop + 1, k], carry, *following = call(
+            functools.partial(pass_kernel, hop, k, tail is not None, more),
+            (sent_shape(hop + 1, k), shape((chunks, N, width), BF16))
+            + (sent_shape(1, k + 2),) * more,
+            in_specs=[in_vmem] * len(operands) + [anywhere] * len(after),
+            input_output_aliases={} if carry is None else {3: 1},
+        )(*operands, *after)
         got[hop + 1, k] = forward(moving[hop + 1, k], hop + 1, k)
-        tie, after = moving[hop + 1, k], []
-        if hop == 1 and k + 2 < chunks:
-            state_part(k + 2, tie)
-            got[1, k + 2] = forward(sent[k + 2], 1, k + 2)
+        tie = moving[hop + 1, k]
+        if more:
+            got[1, k + 2] = forward(following[0], 1, k + 2)
+
+    early, late = tuple(range(chunks // 2)), tuple(range(chunks // 2, chunks))
+    local, gain, asked = ask_part(tie)
 
     back = []
     if ride:
-        ops = [(0, 1), (0, 2), (1, 2)]
-        first_readings = read_part(ops, False, tie, got[count - 1, chunks - 2])
-        for (one, other), value in zip(ops, first_readings):
-            back.append(swap(value, (one, other)))
-        ends = [(0, 3), (1, 3), (2, 3)]
-        *reading, own = read_part(ends, True, first_readings[0])
-        for (one, other), value in zip(ends, reading):
-            back.append(swap(value, (one, other)))
+        ops, ends = [(0, 1), (0, 2), (1, 2)], [(0, 3), (1, 3), (2, 3)]
+        reading = read_part(ops, False)
+        for couple, value in zip(ops, reading):
+            back.append(swap(value, couple))
+        outer = outer_part((early,), carry, [], reading[0])
+        *reading, own = read_part(ends, True, outer, *back)
+        for couple, value in zip(ends, reading):
+            back.append(swap(value, couple))
         ops = ops + ends
     else:
+        outer = outer_part((early,), carry, [])
         *reading, own = read_part([(r, r) for r in range(count)], True)
         ops = list(range(1, count))
-        back, own = [shift(reading[r], -r) for r in ops], reading[0]
+        back = [shift(reading[r], -r) for r in ops]
+        own = reading[0].astype(F32)
     prefill, token = outer_part((early, late), carry, [outer])
 
     decoded = call(

time: 40.9 us -> 42.9 us (1.049)
  waiting for transfers between devices: 7.17 us -> 13.1 us
  starting transfers between devices: 22.5 us -> 18.4 us
    ppermute x18, waiting for transfers between devices: 7.17 us -> 13.1 us  [swap(): return lax.ppermute(value, ('seq', 'tp'), pairs)]
    ppermute x18, starting transfers between devices: 22.5 us -> 18.4 us  [swap(): return lax.ppermute(value, ('seq', 'tp'), pairs)]
    pallas_call x11 -> x12, Pallas kernels: 1.74 us -> 1.61 us  [the longest x2 1.23 us: state_part(): call(functools.partial(state_kernel, part, first), chunk_shapes * len(par...]
  transfers between devices with their start and end apart: 18 -> 18, of which waited for: 6 -> 7; matrix products, arithmetic and copies ran while one was open for 0% -> 0% of each run, Pallas kernels for 18% -> 17%
where the time goes in v7:
time: 42.9 us; the launch traced here: 42.7 us
  starting transfers between devices  18.4 us (43%)
  waiting for transfers between devices  13.1 us (31%)
  Pallas kernels  10.3 us (24%)
  between operations  0.85 us (2%)
    ppermute x18, starting transfers between devices, swap(): return lax.ppermute(value, ('seq', 'tp'), pairs)  18.4 us
    ppermute x18, waiting for transfers between devices, swap(): return lax.ppermute(value, ('seq', 'tp'), pairs)  13.1 us
    pallas_call x2, Pallas kernels, inner_part(): call(functools.partial(inner_kernel, g), shape((tokens, group_lanes)), in...  2.17 us
    pallas_call x2, Pallas kernels, outer_part(): call(functools.partial(outer_kernel, parts, count), (pltpu.HBM((tokens, l...  1.99 us
    pallas_call x1, Pallas kernels, shards(): call(functools.partial(first_kernel, len(inputs), ride), tuple((shape(val...  1.9 us
    pallas_call x2, Pallas kernels, state_part(): call(functools.partial(state_kernel, part, first), chunk_shapes * len(par...  1.23 us
    pallas_call x1, Pallas kernels, ask_part(): call(functools.partial(ask_kernel, count, ride), (shape((rows, lanes)), s...  0.92 us
  transfers between devices with their start and end apart: 18, of which 7 were waited for; matrix products, arithmetic and copies ran while one was open for 0% of the time, Pallas kernels for 17%

profile of v7, /device:TPU:0, one launch (start us, length us, event | category | flops | bytes accessed | tf_op | source)
XLA Modules:
  0.0 42.7 jit_solution(13312263339410375824)
XLA Ops:
  0.6 1.9 %shard_map.131 = (bf16[256,2048]{1,0:T(8,128)(2,1)S(1)}, bf16[256,256]{1,0:T(8,128)(2,1)S(1)}, f32[1,32]{1,0:T(1,128)S(1)}, bf16[4,4,256]{2,1,0:T(4,128)(2,1)S(1...) custom-call(bf16[256,2048]{1,0:T(8,128)(2,1)} %refs_0_.1, ...), custom_call_target="tpu_custom_call" | custom-call | flops 1 | bytes 1 | tf_op jit(solution)/shard_map/pallas_call | solution.py:494
  2.5 3.1 %collective-permute-start.1 = (bf16[144,512]{1,0:T(8,128)(2,1)S(1)}, bf16[144,512]{1,0:T(8,128)(2,1)S(1)}, u32[]{:S(2)}, u32[]{:S(2)}) collective-permute-start(bf16[144,512]{1,0:T(8,128)(2,1)S(1)} %get-tuple-element.73.rest_1_), channel_id=1, source_target_pairs={{0,4},{1,5},{2,6},{3,7},{4,0},{5,1},{6,2},{7,3},{8,12},{9,13},{10,... | collective-permute-start | bytes 442376 | tf_op jit(solution)/shard_map/ppermute | solution.py:538
  5.6 1.1 %shard_map.132.rest_0_.rest_2_ = f32[256,1024]{1,0:T(8,128)S(1)} custom-call(bf16[256,2048]{1,0:T(8,128)(2,1)S(1)} %get-tuple-element.63.x_ref, bf16[256,256]{1,0:T(8,128)(2,1)S(1)} %get-tuple-element.67.b_ref, bf16[256,256]{1,0:T(8,128)(2,1)S(1)} %get-tuple-element.61.c_ref, f32[32,256]{1,0:T(8,128)S(1)} %get-tuple-element.62.cum_ref, ...), custom_call_target="tpu_custom_call" | custom-call | flops 1 | bytes 1 | tf_op jit(solution)/shard_map/pallas_call | solution.py:548
  6.7 1.1 %shard_map.133.rest_0_.rest_3_ = f32[256,1024]{1,0:T(8,128)S(1)} custom-call(bf16[256,2048]{1,0:T(8,128)(2,1)S(1)} %get-tuple-element.63.x_ref, bf16[256,256]{1,0:T(8,128)(2,1)S(1)} %get-tuple-element.67.b_ref, bf16[256,256]{1,0:T(8,128)(2,1)S(1)} %get-tuple-element.61.c_ref, f32[32,256]{1,0:T(8,128)S(1)} %get-tuple-element.62.cum_ref, ...), custom_call_target="tpu_custom_call" | custom-call | flops 1 | bytes 1 | tf_op jit(solution)/shard_map/pallas_call | solution.py:548
  7.8 0.5 %shard_map.134 = (f32[128,512]{1,0:T(8,128)S(1)}, f32[1,512]{1,0:T(1,128)S(1)}, bf16[128,512]{1,0:T(8,128)(2,1)S(1)}) custom-call(bf16[256,2048]{1,0:T(8,128)(2,1)S(1)} %get-tuple-element.63.x_ref, bf16[2,128,256]{2,1,0:T(8,128)(2,1)S(1)} %get-tuple-element.64.turned_ref, f32[256,32]{1,0:T(8,128)S(1)} %get-tuple-element.65.weight_ref, ...), custom_call_target="tpu_custom_call" | custom-call | flops 1 | bytes 1 | tf_op jit(solution)/shard_map/pallas_call | solution.py:519
  8.3 0.1 collective-permute-start
  8.3 0.8 %shard_map.135 = (f32[128,512]{1,0:T(8,128)S(1)}, f32[1,512]{1,0:T(1,128)S(1)}, f32[128,512]{1,0:T(8,128)S(1)}, f32[1,512]{1,0:T(1,128)S(1)}) custom-call(bf16[256,2048]{1,0:T(8,128)(2,1)S(1)} %get-tuple-element.63.x_ref, bf16[2,128,256]{2,1,0:T(8,128)(2,1)S(1)} %get-tuple-element.64.turned_ref, f32[256,32]{1,0:T(8,128)S(1)} %get-tuple-element.65.weight_ref, ...), custom_call_target="tpu_custom_call" | custom-call | flops 1 | bytes 1 | tf_op jit(solution)/shard_map/pallas_call | solution.py:519
  9.1 0.4 shard_map.136
  9.5 0.0 collective-permute-done.1.got_ref
  9.6 0.1 shard_map.137
  9.6 0.1 collective-permute-start.5
  9.7 3.2 %collective-permute-start.4 = (bf16[128,512]{1,0:T(8,128)(2,1)S(1)}, bf16[128,512]{1,0:T(8,128)(2,1)S(1)}, u32[]{:S(2)}, u32[]{:S(2)}) collective-permute-start(bf16[128,512]{1,0:T(8,128)(2,1)S(1)} %get-tuple-element.90), channel_id=1, source_target_pairs={{0,4},{1,5},{2,6},{3,7},{4,0},{5,1},{6,2},{7,3},{8,9},{9,8},{10,11... | collective-permute-start | bytes 393224 | tf_op jit(solution)/shard_map/ppermute | solution.py:538
  12.9 0.4 collective-permute-done.got_ref
  13.3 0.1 collective-permute-start.3
  13.4 0.8 %collective-permute-start.2 = (bf16[128,512]{1,0:T(8,128)(2,1)S(1)}, bf16[128,512]{1,0:T(8,128)(2,1)S(1)}, u32[]{:S(2)}, u32[]{:S(2)}) collective-permute-start(bf16[128,512]{1,0:T(8,128)(2,1)S(1)} %get-tuple-element.87), channel_id=1, source_target_pairs={{0,4},{1,5},{2,6},{3,7},{4,0},{5,1},{6,2},{7,3},{8,9},{9,8},{10,11... | collective-permute-start | bytes 393224 | tf_op jit(solution)/shard_map/ppermute | solution.py:538
  14.2 0.0 collective-permute-done.5.got_ref.rest_1_
  14.3 0.1 collective-permute-start.8
  14.3 2.5 %collective-permute-done.4.got_ref = bf16[128,512]{1,0:T(8,128)(2,1)S(1)} collective-permute-done((bf16[128,512]{1,0:T(8,128)(2,1)S(1)}, bf16[128,512]{1,0:T(8,128)(2,1)S(1)}, u32[]{:S(2)}, u32[]{:S(2)}) %collective-permute-start.4) | collective-permute-done | bytes 131104 | tf_op jit(solution)/shard_map/ppermute | solution.py:538
  16.9 0.1 collective-permute-start.7
  17.0 0.0 collective-permute-done.3.got_ref
  17.1 0.6 %collective-permute-start.9 = (bf16[128,512]{1,0:T(8,128)(2,1)S(1)}, bf16[128,512]{1,0:T(8,128)(2,1)S(1)}, u32[]{:S(2)}, u32[]{:S(2)}) collective-permute-start(bf16[128,512]{1,0:T(8,128)(2,1)S(1)} %get-tuple-element.102), channel_id=1, source_target_pairs={{0,1},{1,0},{2,3},{3,2},{4,5},{5,4},{6,7},{7,6},{8,12},{9,13},{10,... | collective-permute-start | bytes 393224 | tf_op jit(solution)/shard_map/ppermute | solution.py:538
  17.6 1.9 %collective-permute-done.2.got_ref = bf16[128,512]{1,0:T(8,128)(2,1)S(1)} collective-permute-done((bf16[128,512]{1,0:T(8,128)(2,1)S(1)}, bf16[128,512]{1,0:T(8,128)(2,1)S(1)}, u32[]{:S(2)}, u32[]{:S(2)}) %collective-permute-start.2) | collective-permute-done | bytes 131104 | tf_op jit(solution)/shard_map/ppermute | solution.py:538
  19.6 0.1 collective-permute-start.6
  19.7 0.0 collective-permute-done.8.got_ref.rest_0_
  19.7 0.0 collective-permute-done.7.got_ref
  19.8 6.1 %collective-permute-start.10 = (bf16[144,512]{1,0:T(8,128)(2,1)S(1)}, bf16[144,512]{1,0:T(8,128)(2,1)S(1)}, u32[]{:S(2)}, u32[]{:S(2)}) collective-permute-start(bf16[144,512]{1,0:T(8,128)(2,1)S(1)} %get-tuple-element.103.tie_ref), channel_id=1, source_target_pairs={{0,4},{1,5},{2,6},{3,7},{4,0},{5,1},{6,2},{7,3},{8,12},{9,13},{10,... | collective-permute-start | bytes 442376 | tf_op jit(solution)/shard_map/ppermute | solution.py:538
  25.8 0.0 collective-permute-done.9.got_ref.rest_1_
  25.8 0.0 collective-permute-done.6.got_ref
  25.9 0.1 collective-permute-start.11
  26.0 3.0 %collective-permute-done.10.rest_2_.rest_0_ = bf16[144,512]{1,0:T(8,128)(2,1)S(1)} collective-permute-done((bf16[144,512]{1,0:T(8,128)(2,1)S(1)}, bf16[144,512]{1,0:T(8,128)(2,1)S(1)}, u32[]{:S(2)}, u32[]{:S(2)}) %collective-permute-start.10) | collective-permute-done | bytes 147488 | tf_op jit(solution)/shard_map/ppermute | solution.py:538
  28.9 0.9 %shard_map.147 = (f32[16,2048]{1,0:T(8,128)S(1)}, f32[16,32]{1,0:T(8,128)S(1)}, bf16[16,256]{1,0:T(8,128)(2,1)S(1)}) custom-call(bf16[256,2048]{1,0:T(8,128)(2,1)S(1)} %get-tuple-element.63.x_ref, bf16[256,256]{1,0:T(8,128)(2,1)S(1)} %get-tuple-element.67.b_ref, f32[32,256]{1,0:T(8,128)S(1)} %get-tuple-element.62.cum_ref, ...), custom_call_target="tpu_custom_call" | custom-call | flops 1 | bytes 1 | tf_op jit(solution)/shard_map/pallas_call | solution.py:556
  29.9 0.3 shard_map.148
  30.1 2.2 %collective-permute-start.13 = (bf16[4,2048]{1,0:T(4,128)(2,1)S(1)}, bf16[4,2048]{1,0:T(4,128)(2,1)S(1)}, u32[]{:S(2)}, u32[]{:S(2)}) collective-permute-start(bf16[4,2048]{1,0:T(4,128)(2,1)S(1)} %get-tuple-element.113), channel_id=1, source_target_pairs={{0,8},{1,9},{2,10},{3,11},{4,5},{5,4},{6,7},{7,6},{8,0},{9,1},{10,... | collective-permute-start | bytes 49160 | tf_op jit(solution)/shard_map/ppermute | solution.py:538
  32.3 0.0 collective-permute-start.14
  32.3 1.4 %collective-permute-start.12 = (bf16[4,2048]{1,0:T(4,128)(2,1)S(1)}, bf16[4,2048]{1,0:T(4,128)(2,1)S(1)}, u32[]{:S(2)}, u32[]{:S(2)}) collective-permute-start(bf16[4,2048]{1,0:T(4,128)(2,1)S(1)} %get-tuple-element.109.rest_4_), channel_id=1, source_target_pairs={{0,4},{1,5},{2,6},{3,7},{4,0},{5,1},{6,2},{7,3},{8,9},{9,8},{10,11... | collective-permute-start | bytes 49160 | tf_op jit(solution)/shard_map/ppermute | solution.py:538
  33.7 0.6 %shard_map.149.rest_4_ = bf16[2,256,512]{2,1,0:T(8,128)(2,1)S(1)} custom-call(bf16[256,256]{1,0:T(8,128)(2,1)S(1)} %get-tuple-element.61.c_ref, f32[32,256]{1,0:T(8,128)S(1)} %get-tuple-element.62.cum_ref, bf16[4,128,512]{2,1,0:T(8,128)(2,1)S(1)} %get-tuple-element.104.carry_ref, bf16[128,512]{1,0:T(8,128)(2,1)S(1)} %collective-permute-done.8.got_ref.rest_0_, ...), custom_call_target="tpu_custom_call" | custom-call | flops 1 | bytes 1 | tf_op jit(solution)/shard_map/pallas_call | solution.py:573
  34.3 0.0 collective-permute-done.11.rest_1_.rest_3_
  34.3 0.6 %collective-permute-done.13.rest_6_.rest_1_ = bf16[4,2048]{1,0:T(4,128)(2,1)S(1)} collective-permute-done((bf16[4,2048]{1,0:T(4,128)(2,1)S(1)}, bf16[4,2048]{1,0:T(4,128)(2,1)S(1)}, u32[]{:S(2)}, u32[]{:S(2)}) %collective-permute-start.13) | collective-permute-done | bytes 16416 | tf_op jit(solution)/shard_map/ppermute | solution.py:538
  34.9 0.0 collective-permute-done.14.rest_7_.rest_2_
  34.9 1.1 %collective-permute-done.12.rest_5_.rest_0_ = bf16[4,2048]{1,0:T(4,128)(2,1)S(1)} collective-permute-done((bf16[4,2048]{1,0:T(4,128)(2,1)S(1)}, bf16[4,2048]{1,0:T(4,128)(2,1)S(1)}, u32[]{:S(2)}, u32[]{:S(2)}) %collective-permute-start.12) | collective-permute-done | bytes 16416 | tf_op jit(solution)/shard_map/ppermute | solution.py:538
  36.1 0.3 shard_map.151
  36.3 0.1 collective-permute-start.15
  36.4 0.1 collective-permute-start.16
  36.5 0.5 %collective-permute-start.17 = (bf16[4,2048]{1,0:T(4,128)(2,1)S(1)}, bf16[4,2048]{1,0:T(4,128)(2,1)S(1)}, u32[]{:S(2)}, u32[]{:S(2)}) collective-permute-start(bf16[4,2048]{1,0:T(4,128)(2,1)S(1)} %get-tuple-element.117), channel_id=1, source_target_pairs={{0,1},{1,0},{2,3},{3,2},{4,5},{5,4},{6,7},{7,6},{8,12},{9,13},{10,... | collective-permute-start | bytes 49160 | tf_op jit(solution)/shard_map/ppermute | solution.py:538
  37.0 1.4 %shard_map.150 = (bf16[256,2048]{1,0:T(8,128)(2,1)}, f32[8,128]{1,0:T(8,128)S(1)}) custom-call(bf16[256,256]{1,0:T(8,128)(2,1)S(1)} %get-tuple-element.61.c_ref, f32[32,256]{1,0:T(8,128)S(1)} %get-tuple-element.62.cum_ref, bf16[4,128,512]{2,1,0:T(8,128)(2,1)S(1)} %get-tuple-element.104.carry_ref, ...), custom_call_target="tpu_custom_call" | custom-call | flops 1 | bytes 1 | tf_op jit(solution)/shard_map/pallas_call | solution.py:573
  38.4 3.6 %collective-permute-done.15.rest_3_ = bf16[4,2048]{1,0:T(4,128)(2,1)S(1)} collective-permute-done((bf16[4,2048]{1,0:T(4,128)(2,1)S(1)}, bf16[4,2048]{1,0:T(4,128)(2,1)S(1)}, u32[]{:S(2)}, u32[]{:S(2)}) %collective-permute-start.15) | collective-permute-done | bytes 16416 | tf_op jit(solution)/shard_map/ppermute | solution.py:538
  41.9 0.0 collective-permute-done.16.rest_4_
  42.0 0.0 collective-permute-done.17.rest_5_
  42.0 0.7 %shard_map.152 = bf16[4,4,2048]{2,1,0:T(4,128)(2,1)} custom-call(f32[4,4,2048]{2,1,0:T(4,128)S(1)} %get-tuple-element.85.rest_2_.keep_ref, f32[4,4,2048]{2,1,0:T(4,128)S(1)} %get-tuple-element.111.fresh_ref, f32[4,4,128]{2,1,0:T(4,128)S(1)} %get-tuple-element.112.held_ref, bf16[4,2048]{1,0:T(4,128)(2,1)S(1)} %collective-permute-done.12.rest_5_.rest_0_, ...), custom_call_target="tpu_custom_call" | custom-call | flops 1 | bytes 1 | tf_op jit(solution)/shard_map/pallas_call | solution.py:651
  (9 shorter events, 0.3 us)
Async XLA Ops:
  2.5 7.0 %collective-permute-start.1 = (bf16[144,512]{1,0:T(8,128)(2,1)S(1)}, bf16[144,512]{1,0:T(8,128)(2,1)S(1)}, u32[]{:S(2)}, u32[]{:S(2)}) collective-permute-start(bf16[144,512]{1,0:T(8,128)(2,1)S(1)} %get-tuple-element.73.rest_1_), channel_id=1, source_target_pairs={{0,4},{1,5},{2,6},{3,7},{4,0},{5,1},{6,2},{7,3},{8,12},{9,13},{10,... | collective-permute-start | bytes 442376 | tf_op jit(solution)/shard_map/ppermute | solution.py:538
  8.3 5.0 %collective-permute-start = (bf16[128,512]{1,0:T(8,128)(2,1)S(1)}, bf16[128,512]{1,0:T(8,128)(2,1)S(1)}, u32[]{:S(2)}, u32[]{:S(2)}) collective-permute-start(bf16[128,512]{1,0:T(8,128)(2,1)S(1)} %get-tuple-element.70.rest_0_), channel_id=1, source_target_pairs={{0,4},{1,5},{2,6},{3,7},{4,0},{5,1},{6,2},{7,3},{8,9},{9,8},{10,11... | collective-permute-start | bytes 393224 | tf_op jit(solution)/shard_map/ppermute | solution.py:538
  9.6 4.6 %collective-permute-start.5 = (bf16[144,512]{1,0:T(8,128)(2,1)S(1)}, bf16[144,512]{1,0:T(8,128)(2,1)S(1)}, u32[]{:S(2)}, u32[]{:S(2)}) collective-permute-start(bf16[144,512]{1,0:T(8,128)(2,1)S(1)} %get-tuple-element.92.rest_0_), channel_id=1, source_target_pairs={{0,1},{1,0},{2,3},{3,2},{4,8},{5,9},{6,10},{7,11},{8,4},{9,5},{10,... | collective-permute-start | bytes 442376 | tf_op jit(solution)/shard_map/ppermute | solution.py:538
  9.7 7.2 %collective-permute-start.4 = (bf16[128,512]{1,0:T(8,128)(2,1)S(1)}, bf16[128,512]{1,0:T(8,128)(2,1)S(1)}, u32[]{:S(2)}, u32[]{:S(2)}) collective-permute-start(bf16[128,512]{1,0:T(8,128)(2,1)S(1)} %get-tuple-element.90), channel_id=1, source_target_pairs={{0,4},{1,5},{2,6},{3,7},{4,0},{5,1},{6,2},{7,3},{8,9},{9,8},{10,11... | collective-permute-start | bytes 393224 | tf_op jit(solution)/shard_map/ppermute | solution.py:538
  13.3 3.7 %collective-permute-start.3 = (bf16[128,512]{1,0:T(8,128)(2,1)S(1)}, bf16[128,512]{1,0:T(8,128)(2,1)S(1)}, u32[]{:S(2)}, u32[]{:S(2)}) collective-permute-start(bf16[128,512]{1,0:T(8,128)(2,1)S(1)} %get-tuple-element.89), channel_id=1, source_target_pairs={{0,1},{1,0},{2,3},{3,2},{4,8},{5,9},{6,10},{7,11},{8,4},{9,5},{10,... | collective-permute-start | bytes 393224 | tf_op jit(solution)/shard_map/ppermute | solution.py:538
  13.4 6.1 %collective-permute-start.2 = (bf16[128,512]{1,0:T(8,128)(2,1)S(1)}, bf16[128,512]{1,0:T(8,128)(2,1)S(1)}, u32[]{:S(2)}, u32[]{:S(2)}) collective-permute-start(bf16[128,512]{1,0:T(8,128)(2,1)S(1)} %get-tuple-element.87), channel_id=1, source_target_pairs={{0,4},{1,5},{2,6},{3,7},{4,0},{5,1},{6,2},{7,3},{8,9},{9,8},{10,11... | collective-permute-start | bytes 393224 | tf_op jit(solution)/shard_map/ppermute | solution.py:538
  14.3 5.4 %collective-permute-start.8 = (bf16[128,512]{1,0:T(8,128)(2,1)S(1)}, bf16[128,512]{1,0:T(8,128)(2,1)S(1)}, u32[]{:S(2)}, u32[]{:S(2)}) collective-permute-start(bf16[128,512]{1,0:T(8,128)(2,1)S(1)} %get-tuple-element.100), channel_id=1, source_target_pairs={{0,1},{1,0},{2,3},{3,2},{4,5},{5,4},{6,7},{7,6},{8,12},{9,13},{10,... | collective-permute-start | bytes 393224 | tf_op jit(solution)/shard_map/ppermute | solution.py:538
  16.9 2.8 %collective-permute-start.7 = (bf16[128,512]{1,0:T(8,128)(2,1)S(1)}, bf16[128,512]{1,0:T(8,128)(2,1)S(1)}, u32[]{:S(2)}, u32[]{:S(2)}) collective-permute-start(bf16[128,512]{1,0:T(8,128)(2,1)S(1)} %get-tuple-element.98), channel_id=1, source_target_pairs={{0,1},{1,0},{2,3},{3,2},{4,8},{5,9},{6,10},{7,11},{8,4},{9,5},{10,... | collective-permute-start | bytes 393224 | tf_op jit(solution)/shard_map/ppermute | solution.py:538
  17.1 8.7 %collective-permute-start.9 = (bf16[128,512]{1,0:T(8,128)(2,1)S(1)}, bf16[128,512]{1,0:T(8,128)(2,1)S(1)}, u32[]{:S(2)}, u32[]{:S(2)}) collective-permute-start(bf16[128,512]{1,0:T(8,128)(2,1)S(1)} %get-tuple-element.102), channel_id=1, source_target_pairs={{0,1},{1,0},{2,3},{3,2},{4,5},{5,4},{6,7},{7,6},{8,12},{9,13},{10,... | collective-permute-start | bytes 393224 | tf_op jit(solution)/shard_map/ppermute | solution.py:538
  19.6 6.2 %collective-permute-start.6 = (bf16[128,512]{1,0:T(8,128)(2,1)S(1)}, bf16[128,512]{1,0:T(8,128)(2,1)S(1)}, u32[]{:S(2)}, u32[]{:S(2)}) collective-permute-start(bf16[128,512]{1,0:T(8,128)(2,1)S(1)} %get-tuple-element.97.tie_ref), channel_id=1, source_target_pairs={{0,1},{1,0},{2,3},{3,2},{4,8},{5,9},{6,10},{7,11},{8,4},{9,5},{10,... | collective-permute-start | bytes 393224 | tf_op jit(solution)/shard_map/ppermute | solution.py:538
  19.8 9.2 %collective-permute-start.10 = (bf16[144,512]{1,0:T(8,128)(2,1)S(1)}, bf16[144,512]{1,0:T(8,128)(2,1)S(1)}, u32[]{:S(2)}, u32[]{:S(2)}) collective-permute-start(bf16[144,512]{1,0:T(8,128)(2,1)S(1)} %get-tuple-element.103.tie_ref), channel_id=1, source_target_pairs={{0,4},{1,5},{2,6},{3,7},{4,0},{5,1},{6,2},{7,3},{8,12},{9,13},{10,... | collective-permute-start | bytes 442376 | tf_op jit(solution)/shard_map/ppermute | solution.py:538
  25.9 8.5 %collective-permute-start.11 = (bf16[128,512]{1,0:T(8,128)(2,1)S(1)}, bf16[128,512]{1,0:T(8,128)(2,1)S(1)}, u32[]{:S(2)}, u32[]{:S(2)}) collective-permute-start(bf16[128,512]{1,0:T(8,128)(2,1)S(1)} %get-tuple-element.105.rest_3_), channel_id=1, source_target_pairs={{0,1},{1,0},{2,3},{3,2},{4,5},{5,4},{6,7},{7,6},{8,12},{9,13},{10,... | collective-permute-start | bytes 393224 | tf_op jit(solution)/shard_map/ppermute | solution.py:538
  30.1 4.8 %collective-permute-start.13 = (bf16[4,2048]{1,0:T(4,128)(2,1)S(1)}, bf16[4,2048]{1,0:T(4,128)(2,1)S(1)}, u32[]{:S(2)}, u32[]{:S(2)}) collective-permute-start(bf16[4,2048]{1,0:T(4,128)(2,1)S(1)} %get-tuple-element.113), channel_id=1, source_target_pairs={{0,8},{1,9},{2,10},{3,11},{4,5},{5,4},{6,7},{7,6},{8,0},{9,1},{10,... | collective-permute-start | bytes 49160 | tf_op jit(solution)/shard_map/ppermute | solution.py:538
  32.3 2.6 %collective-permute-start.14 = (bf16[4,2048]{1,0:T(4,128)(2,1)S(1)}, bf16[4,2048]{1,0:T(4,128)(2,1)S(1)}, u32[]{:S(2)}, u32[]{:S(2)}) collective-permute-start(bf16[4,2048]{1,0:T(4,128)(2,1)S(1)} %get-tuple-element.114), channel_id=1, source_target_pairs={{0,1},{1,0},{2,3},{3,2},{4,8},{5,9},{6,10},{7,11},{8,4},{9,5},{10,... | collective-permute-start | bytes 49160 | tf_op jit(solution)/shard_map/ppermute | solution.py:538
  32.3 3.7 %collective-permute-start.12 = (bf16[4,2048]{1,0:T(4,128)(2,1)S(1)}, bf16[4,2048]{1,0:T(4,128)(2,1)S(1)}, u32[]{:S(2)}, u32[]{:S(2)}) collective-permute-start(bf16[4,2048]{1,0:T(4,128)(2,1)S(1)} %get-tuple-element.109.rest_4_), channel_id=1, source_target_pairs={{0,4},{1,5},{2,6},{3,7},{4,0},{5,1},{6,2},{7,3},{8,9},{9,8},{10,11... | collective-permute-start | bytes 49160 | tf_op jit(solution)/shard_map/ppermute | solution.py:538
  36.3 5.6 %collective-permute-start.15 = (bf16[4,2048]{1,0:T(4,128)(2,1)S(1)}, bf16[4,2048]{1,0:T(4,128)(2,1)S(1)}, u32[]{:S(2)}, u32[]{:S(2)}) collective-permute-start(bf16[4,2048]{1,0:T(4,128)(2,1)S(1)} %get-tuple-element.115), channel_id=1, source_target_pairs={{0,12},{1,13},{2,14},{3,15},{4,5},{5,4},{6,7},{7,6},{8,9},{9,8},{1... | collective-permute-start | bytes 49160 | tf_op jit(solution)/shard_map/ppermute | solution.py:538
  36.4 5.5 %collective-permute-start.16 = (bf16[4,2048]{1,0:T(4,128)(2,1)S(1)}, bf16[4,2048]{1,0:T(4,128)(2,1)S(1)}, u32[]{:S(2)}, u32[]{:S(2)}) collective-permute-start(bf16[4,2048]{1,0:T(4,128)(2,1)S(1)} %get-tuple-element.116), channel_id=1, source_target_pairs={{0,1},{1,0},{2,3},{3,2},{4,12},{5,13},{6,14},{7,15},{8,9},{9,8},{1... | collective-permute-start | bytes 49160 | tf_op jit(solution)/shard_map/ppermute | solution.py:538
  36.5 5.5 %collective-permute-start.17 = (bf16[4,2048]{1,0:T(4,128)(2,1)S(1)}, bf16[4,2048]{1,0:T(4,128)(2,1)S(1)}, u32[]{:S(2)}, u32[]{:S(2)}) collective-permute-start(bf16[4,2048]{1,0:T(4,128)(2,1)S(1)} %get-tuple-element.117), channel_id=1, source_target_pairs={{0,1},{1,0},{2,3},{3,2},{4,5},{5,4},{6,7},{7,6},{8,12},{9,13},{10,... | collective-permute-start | bytes 49160 | tf_op jit(solution)/shard_map/ppermute | solution.py:538

commit v8 on v7

--- a/solution.py
+++ b/solution.py
@@ -18,6 +18,7 @@
 F32 = jnp.float32
 BF16 = jnp.bfloat16
 CHUNKS = 4
+COSTS = {(2, 2): 10**9}
 VMEM_LIMIT = 32 * 1024 * 1024
 
 
@@ -69,8 +70,10 @@
 
 
 def call(kernel, out_shape, flops=1, **options):
+    name = getattr(kernel, "func", kernel).__name__
     return pl.pallas_call(
         kernel,
+        name=name,
         out_shape=out_shape,
         compiler_params=pltpu.CompilerParams(vmem_limit_bytes=VMEM_LIMIT),
         cost_estimate=pl.CostEstimate(flops=flops, bytes_accessed=1, transcendentals=0),
@@ -92,11 +95,11 @@
     decay_ref[...] = over_lanes(whole, first, width, 3)
 
 
-def first_kernel(kept, ride, *refs):
+def first_kernel(kept, *refs):
     hbm, refs = refs[: kept + 1], refs[kept + 1 :]
     here, refs = refs[:kept], refs[kept:]
     cum_ref, row_ref, weight_ref, whole_ref, turned_ref = refs[:5]
-    total_ref, decay_ref, sent_ref, dt_ref, sems = refs[5:]
+    total_ref, decay_ref, sent_ref, own_ref, dt_ref, sems = refs[5:]
     x_ref, b_ref, a_ref, asked_ref = here[:4]
     heads, tokens = dt_ref.shape
     spans = tokens // SPAN
@@ -133,7 +136,7 @@
     turned = b_ref[:, :N].astype(F32).T.astype(BF16)
     x_copies[0].wait()
     chunk_total(0, x_ref, turned, weight, whole, total_ref, decay_ref)
-    sent_ref[:N] = total_ref[...].astype(BF16)
+    sent_ref[...] = total_ref[...].astype(BF16)
     turned_ref[0] = turned
     for g in range(1, turned_ref.shape[0]):
         turned_ref[g] = b_ref[:, g * N : (g + 1) * N].astype(F32).T.astype(BF16)
@@ -143,19 +146,17 @@
     x_copies[1].wait()
     for copy in copies[2:]:
         copy.wait()
-    if ride:
-        own = flat(asked_ref).astype(BF16)
-        sent_ref[N:] = jnp.concatenate([own, own], axis=1)
-
-
-def state_kernel(part, first, x_ref, turned_ref, weight_ref, whole_ref, *rest):
-    results = rest[-2 * len(part) - first :]
+    own = flat(asked_ref).astype(BF16)
+    own_ref[...] = jnp.concatenate([own, own], axis=1)
+
+
+def state_kernel(part, x_ref, turned_ref, weight_ref, whole_ref, *rest):
+    results = rest[-2 * len(part) - 1 :]
     for i, k in enumerate(part):
         total_ref, decay_ref = results[2 * i : 2 * i + 2]
         g = k * total_ref.shape[1] // (H // G * P_SIZE)
         chunk_total(k, x_ref, turned_ref[g], weight_ref[...], whole_ref[...], total_ref, decay_ref)
-    if first:
-        results[-1][...] = results[0][...].astype(BF16)
+    results[-1][...] = results[0][...].astype(BF16)
 
 
 def flat(ref):
@@ -166,8 +167,9 @@
     token_ref[...] = jnp.zeros_like(token_ref)
 
 
-def pass_kernel(hop, k, tail, more, got_ref, total_ref, decay_ref, *rest):
-    extra, (moving_ref, carry_ref) = rest, rest[-2 - more : len(rest) - more]
+def pass_kernel(hop, k, tail, more, opening, got_ref, total_ref, decay_ref, *rest):
+    results = rest[-2 - more - opening :]
+    extra, (moving_ref, carry_ref) = rest, results[:2]
     me = lax.axis_index("seq")
     if hop == 1 and k == 0:
         carry_ref[...] = jnp.zeros_like(carry_ref)
@@ -181,15 +183,17 @@
         carry_ref[k] = got
 
     if more:
-        rest[-1][...] = extra[0][...].astype(BF16)
+        results[2][...] = extra[0][...].astype(BF16)
         extra = extra[1:]
-    if tail:
-        rows = extra[0][N:]
-        if hop == 1:
-            lane = lax.broadcasted_iota(jnp.int32, rows.shape, 1)
-            mine = (lane // (rows.shape[1] // 2)) == lax.rem(me, 2)
-            rows = jnp.where(mine, rows.astype(F32), got_ref[N:].astype(F32)).astype(BF16)
-        moving_ref[N:] = rows
+    if opening:
+        results[-1][...] = extra[0][...]
+    if tail and hop == 1:
+        own, other = extra[0][...].astype(F32), extra[1][...].astype(F32)
+        lane = lax.broadcasted_iota(jnp.int32, own.shape, 1)
+        mine = (lane // (own.shape[1] // 2)) == lax.rem(me, 2)
+        moving_ref[N:] = jnp.where(mine, own, other).astype(BF16)
+    elif tail:
+        moving_ref[N:] = got_ref[N:]
 
 
 def pair_halves(x_part):
@@ -474,7 +478,7 @@
     ride = count == 4 and width == 2 * names
 
     def sent_shape(hop, k):
-        tail = ride and (hop, k) in ((1, 0), (2, 0), (3, 2))
+        tail = ride and k == 1 and hop > 1
         return shape((N + rows * tail, width), BF16)
 
     inputs = [
@@ -491,8 +495,9 @@
         dec_dt[0],
     ]
     chunk_shapes = (shape((N, width)), shape((1, width)))
+    own_shape = shape((rows, 2 * names), BF16)
     results = call(
-        functools.partial(first_kernel, len(inputs), ride),
+        functools.partial(first_kernel, len(inputs)),
         tuple(shape(value.shape, value.dtype) for value in inputs)
         + (
             shape((heads, tokens)),
@@ -502,7 +507,7 @@
             shape((groups, N, tokens), BF16),
         )
         + chunk_shapes
-        + (sent_shape(1, 0),),
+        + (sent_shape(1, 0), own_shape),
         in_specs=[in_hbm] * (len(inputs) + 1),
         scratch_shapes=[
             pltpu.VMEM((heads, tokens), BF16),
@@ -513,18 +518,17 @@
     cum, row, weight, whole, turned = results[11:16]
     total, decay = [results[16]], [results[17]]
     sent = {0: results[18]}
+    own = results[19]
 
     def state_part(part, tie):
-        first = part[0] == 1
         out = call(
-            functools.partial(state_kernel, part, first),
-            chunk_shapes * len(part) + (sent_shape(1, 1),) * first,
+            functools.partial(state_kernel, part),
+            chunk_shapes * len(part) + (sent_shape(1, 1),),
             in_specs=[in_vmem] * 4 + [anywhere],
         )(x, turned, weight, whole, tie)
         total.extend(out[0 : 2 * len(part) : 2])
         decay.extend(out[1 : 2 * len(part) : 2])
-        if first:
-            sent[1] = out[-1]
+        return out[-1]
 
     def swap(value, *couples):
         partner = {}
@@ -538,8 +542,9 @@
         return lax.ppermute(value, ("seq", "tp"), pairs)
 
     def forward(value, hop, k):
-        rides = ride and (hop, k) in ((1, 0), (3, 2))
-        return swap(value, *([(0, 1), (2, 3)] if rides else [(hop - 1, hop)]))
+        rides = ride and (hop, k) == (3, 1)
+        with jax.named_scope(f"hop{hop}_chunk{k}"):
+            return swap(value, *([(0, 1), (2, 3)] if rides else [(hop - 1, hop)]))
 
     def shift(value, by):
         return lax.ppermute(value, "seq", [(d, (d + by) % count) for d in range(count)])
@@ -552,10 +557,11 @@
         )(x, b, c, cum, row, d_row, *after)
 
     def ask_part(*after):
-        blocks = (moving[2, 0], got[2, 0], got[3, 2]) if ride else asks
+        blocks = (moving[2, 1], got[2, 1], got[3, 1]) if ride else asks
         return call(
             functools.partial(ask_kernel, count, ride),
             (shape((rows, lanes)), shape((rows, heads)), shape((rows, names), BF16)),
+            flops=10**9,
             in_specs=[in_vmem] * (6 + len(blocks)) + [anywhere] * len(after),
         )(x, b, cum, row, len_row, owner_row, *blocks, *after)
 
@@ -592,32 +598,36 @@
     inner = [inner_part(0)]
     for g in range(1, groups):
         inner.append(inner_part(g, inner[-1]))
-    state_part([1], inner[-1])
+    sent[1] = state_part(list(range(1, chunks)), inner[-1])
     got[1, 1] = forward(sent[1], 1, 1)
-    if chunks > 2:
-        state_part(list(range(2, chunks)), sent[1])
-    keep, fresh, held = fresh_part(total[-1])
     if not ride:
         asks = [asked_here] + [shift(asked_here, r) for r in range(1, count)]
     order = sorted((k + hop, hop, k) for hop in range(1, count - 1) for k in range(chunks))
-    carry = tie = None
+    carry = tie = other = None
     for _, hop, k in order:
-        tail = {(1, 0): sent[0], (2, 2): got.get((2, 0))}.get((hop, k)) if ride else None
+        tail = ride and k == 1
         more = hop == 1 and k + 2 < chunks
         operands = [got[hop, k], total[k], decay[k]]
         operands += [] if carry is None else [carry]
-        operands += total[k + 2 : k + 3] * more + [tail] * (tail is not None)
-        after = [keep] if carry is None else []
-        if hop == count - 2 and k > 1:
-            after.append(
+        opening = ride and (hop, k) == (1, 0)
+        operands += total[k + 2 : k + 3] * more + [own] * opening
+        operands += [own, other] * (tail and hop == 1)
+        after = []
+        if hop == count - 2 and k == chunks - 1:
+            local, gain, asked = ask_part(tie)
+            after = [gain]
+        elif hop == count - 2 and k > 1:
+            after = [
                 call(
                     token_kernel, shape((8, 128)), flops=10**9, in_specs=[anywhere] * 2
                 )(got[hop + 1, k - 2], tie)
-            )
+            ]
         moving[hop + 1, k], carry, *following = call(
-            functools.partial(pass_kernel, hop, k, tail is not None, more),
+            functools.partial(pass_kernel, hop, k, tail, more, opening),
             (sent_shape(hop + 1, k), shape((chunks, N, width), BF16))
-            + (sent_shape(1, k + 2),) * more,
+            + (sent_shape(1, k + 2),) * more
+            + (own_shape,) * opening,
+            flops=COSTS.get((hop, k), 1),
             in_specs=[in_vmem] * len(operands) + [anywhere] * len(after),
             input_output_aliases={} if carry is None else {3: 1},
         )(*operands, *after)
@@ -625,9 +635,10 @@
         tie = moving[hop + 1, k]
         if more:
             got[1, k + 2] = forward(following[0], 1, k + 2)
+        if ride and (hop, k) == (1, 0):
+            other = swap(following[-1], (0, 1), (2, 3))
 
     early, late = tuple(range(chunks // 2)), tuple(range(chunks // 2, chunks))
-    local, gain, asked = ask_part(tie)
 
     back = []
     if ride:
@@ -636,23 +647,25 @@
         for couple, value in zip(ops, reading):
             back.append(swap(value, couple))
         outer = outer_part((early,), carry, [], reading[0])
-        *reading, own = read_part(ends, True, outer, *back)
+        keep, fresh, held = fresh_part(outer)
+        *reading, mine = read_part(ends, True, keep, *back)
         for couple, value in zip(ends, reading):
             back.append(swap(value, couple))
         ops = ops + ends
     else:
         outer = outer_part((early,), carry, [])
-        *reading, own = read_part([(r, r) for r in range(count)], True)
+        keep, fresh, held = fresh_part(outer)
+        *reading, mine = read_part([(r, r) for r in range(count)], True)
         ops = list(range(1, count))
         back = [shift(reading[r], -r) for r in ops]
-        own = reading[0].astype(F32)
+        mine = reading[0].astype(F32)
     prefill, token = outer_part((early, late), carry, [outer])
 
     decoded = call(
         functools.partial(finish_kernel, ops),
         jax.ShapeDtypeStruct((count, STEPS, lanes), BF16),
         in_specs=[in_vmem] * (4 + len(ops)) + [anywhere],
-    )(keep, fresh, held, *back, own, token)
+    )(keep, fresh, held, *back, mine, token)
     return (prefill, decoded[None])
 
 

time: 42.9 us -> 43.6 us (1.016)
  waiting for transfers between devices: 13.1 us -> 21.1 us
  starting transfers between devices: 18.4 us -> 11.6 us
    ppermute x18 -> x19, waiting for transfers between devices: 13.1 us -> 21.1 us  [swap(): return lax.ppermute(value, ('seq', 'tp'), pairs)]
    ppermute x18 -> x19, starting transfers between devices: 18.4 us -> 11.6 us  [swap(): return lax.ppermute(value, ('seq', 'tp'), pairs)]
    pallas_call x11 -> x10, Pallas kernels: 3.5 us -> 3.38 us  [the longest x1 1.9 us: shards(): call(functools.partial(first_kernel, len(inputs)), tuple((shape(value.sha...]
  transfers between devices with their start and end apart: 18 -> 19, of which waited for: 7 -> 9; matrix products, arithmetic and copies ran while one was open for 0% -> 0% of each run, Pallas kernels for 17% -> 16%
where the time goes in v8:
time: 43.6 us; the launch traced here: 43.3 us
  waiting for transfers between devices  21.1 us (48%)
  starting transfers between devices  11.6 us (27%)
  Pallas kernels  9.94 us (23%)
  between operations  0.78 us (2%)
    ppermute x19, waiting for transfers between devices, swap(): return lax.ppermute(value, ('seq', 'tp'), pairs)  21.1 us
    ppermute x19, starting transfers between devices, swap(): return lax.ppermute(value, ('seq', 'tp'), pairs)  11.6 us
    pallas_call x2, Pallas kernels, inner_part(): call(functools.partial(inner_kernel, g), shape((tokens, group_lanes)), in...  2.03 us
    pallas_call x2, Pallas kernels, outer_part(): call(functools.partial(outer_kernel, parts, count), (pltpu.HBM((tokens, l...  1.96 us
    pallas_call x1, Pallas kernels, shards(): call(functools.partial(first_kernel, len(inputs)), tuple((shape(value.sha...  1.9 us
    pallas_call x1, Pallas kernels, state_part(): call(functools.partial(state_kernel, part), chunk_shapes * len(part) + (s...  1.09 us
    pallas_call x1, Pallas kernels, ask_part(): call(functools.partial(ask_kernel, count, ride), (shape((rows, lanes)), s...  0.88 us
  transfers between devices with their start and end apart: 19, of which 9 were waited for; matrix products, arithmetic and copies ran while one was open for 0% of the time, Pallas kernels for 16%

profile of v8, /device:TPU:0, one launch (start us, length us, event | category | flops | bytes accessed | tf_op | source)
XLA Modules:
  0.0 43.3 jit_solution(15023408139140134000)
XLA Ops:
  0.6 1.9 %first_kernel.1 = (bf16[256,2048]{1,0:T(8,128)(2,1)S(1)}, bf16[256,256]{1,0:T(8,128)(2,1)S(1)}, f32[1,32]{1,0:T(1,128)S(1)}, bf16[4,4,256]{2,1,0:T(4,128)(2,1)S(...) custom-call(bf16[256,2048]{1,0:T(8,128)(2,1)} %refs_0_.1, ...), custom_call_target="tpu_custom_call" | custom-call | flops 1 | bytes 1 | tf_op jit(solution)/shard_map/first_kernel/pallas_call | solution.py:499
  2.5 3.1 %collective-permute-start.1 = (bf16[128,512]{1,0:T(8,128)(2,1)S(1)}, bf16[128,512]{1,0:T(8,128)(2,1)S(1)}, u32[]{:S(2)}, u32[]{:S(2)}) collective-permute-start(bf16[128,512]{1,0:T(8,128)(2,1)S(1)} %get-tuple-element.75), channel_id=1, source_target_pairs={{0,4},{1,5},{2,6},{3,7},{4,0},{5,1},{6,2},{7,3},{8,9},{9,8},{10,11... | collective-permute-start | bytes 393224 | tf_op jit(solution)/shard_map/hop1_chunk0/ppermute | solution.py:542
  5.6 1.0 %inner_kernel.2.rest_0_.rest_2_ = f32[256,1024]{1,0:T(8,128)S(1)} custom-call(bf16[256,2048]{1,0:T(8,128)(2,1)S(1)} %get-tuple-element.65.x_ref, bf16[256,256]{1,0:T(8,128)(2,1)S(1)} %get-tuple-element.69.b_ref, bf16[256,256]{1,0:T(8,128)(2,1)S(1)} %get-tuple-element.63.c_ref, f32[32,256]{1,0:T(8,128)S(1)} %get-tuple-element.64.cum_ref, ...), custom_call_target="tpu_custom_call" | custom-call | flops 1 | bytes 1 | tf_op jit(solution)/shard_map/inner_kernel/pallas_call | solution.py:553
  6.6 1.0 %inner_kernel.3.rest_0_.rest_3_ = f32[256,1024]{1,0:T(8,128)S(1)} custom-call(bf16[256,2048]{1,0:T(8,128)(2,1)S(1)} %get-tuple-element.65.x_ref, bf16[256,256]{1,0:T(8,128)(2,1)S(1)} %get-tuple-element.69.b_ref, bf16[256,256]{1,0:T(8,128)(2,1)S(1)} %get-tuple-element.63.c_ref, f32[32,256]{1,0:T(8,128)S(1)} %get-tuple-element.64.cum_ref, ...), custom_call_target="tpu_custom_call" | custom-call | flops 1 | bytes 1 | tf_op jit(solution)/shard_map/inner_kernel/pallas_call | solution.py:553
  7.7 1.1 %state_kernel.1 = (f32[128,512]{1,0:T(8,128)S(1)}, f32[1,512]{1,0:T(1,128)S(1)}, f32[128,512]{1,0:T(8,128)S(1)}, f32[1,512]{1,0:T(1,128)S(1)}, f32[128,512]{1,0:...) custom-call(bf16[256,2048]{1,0:T(8,128)(2,1)S(1)} %get-tuple-element.65.x_ref, ...), custom_call_target="tpu_custom_call" | custom-call | flops 1 | bytes 1 | tf_op jit(solution)/shard_map/state_kernel/pallas_call | solution.py:524
  8.8 0.1 collective-permute-start
  8.8 0.3 collective-permute-done.1.got_ref
  9.1 0.1 pass_kernel.8
  9.2 0.1 collective-permute-start.6
  9.3 1.8 %collective-permute-start.5 = (bf16[128,512]{1,0:T(8,128)(2,1)S(1)}, bf16[128,512]{1,0:T(8,128)(2,1)S(1)}, u32[]{:S(2)}, u32[]{:S(2)}) collective-permute-start(bf16[128,512]{1,0:T(8,128)(2,1)S(1)} %get-tuple-element.86), channel_id=1, source_target_pairs={{0,4},{1,5},{2,6},{3,7},{4,0},{5,1},{6,2},{7,3},{8,9},{9,8},{10,11... | collective-permute-start | bytes 393224 | tf_op jit(solution)/shard_map/hop1_chunk2/ppermute | solution.py:542
  11.1 0.3 collective-permute-start.2
  11.4 3.8 %collective-permute-done.got_ref = bf16[128,512]{1,0:T(8,128)(2,1)S(1)} collective-permute-done((bf16[128,512]{1,0:T(8,128)(2,1)S(1)}, bf16[128,512]{1,0:T(8,128)(2,1)S(1)}, u32[]{:S(2)}, u32[]{:S(2)}) %collective-permute-start) | collective-permute-done | bytes 131104 | tf_op jit(solution)/shard_map/hop1_chunk1/ppermute | solution.py:542
  15.2 1.8 %collective-permute-done.2.rest_3_ = bf16[16,512]{1,0:T(8,128)(2,1)S(1)} collective-permute-done((bf16[16,512]{1,0:T(8,128)(2,1)S(1)}, bf16[16,512]{1,0:T(8,128)(2,1)S(1)}, u32[]{:S(2)}, u32[]{:S(2)}) %collective-permute-start.2) | collective-permute-done | bytes 16416 | tf_op jit(solution)/shard_map/ppermute | solution.py:542
  16.9 0.1 pass_kernel.9
  17.0 0.1 collective-permute-start.4
  17.1 0.4 collective-permute-start.3
  17.4 0.0 collective-permute-done.6.got_ref
  17.5 0.2 collective-permute-start.9
  17.7 0.0 collective-permute-done.5.got_ref
  17.7 0.4 collective-permute-start.8
  18.2 0.3 collective-permute-done.4.got_ref.rest_1_
  18.5 4.5 %collective-permute-done.3.got_ref = bf16[128,512]{1,0:T(8,128)(2,1)S(1)} collective-permute-done((bf16[128,512]{1,0:T(8,128)(2,1)S(1)}, bf16[128,512]{1,0:T(8,128)(2,1)S(1)}, u32[]{:S(2)}, u32[]{:S(2)}) %collective-permute-start.3) | collective-permute-done | bytes 131104 | tf_op jit(solution)/shard_map/hop1_chunk3/ppermute | solution.py:542
  23.0 0.1 collective-permute-start.7
  23.1 0.3 collective-permute-start.10
  23.5 0.0 collective-permute-done.9.got_ref.rest_0_
  23.5 0.0 collective-permute-done.8.got_ref
  23.5 0.2 collective-permute-start.11
  23.8 5.6 %collective-permute-done.10.rest_2_.rest_1_ = bf16[144,512]{1,0:T(8,128)(2,1)S(1)} collective-permute-done((bf16[144,512]{1,0:T(8,128)(2,1)S(1)}, bf16[144,512]{1,0:T(8,128)(2,1)S(1)}, u32[]{:S(2)}, u32[]{:S(2)}) %collective-permute-start.10) | collective-permute-done | bytes 147488 | tf_op jit(solution)/shard_map/hop3_chunk1/ppermute | solution.py:542
  29.4 0.9 %ask_kernel.1 = (f32[16,2048]{1,0:T(8,128)S(1)}, f32[16,32]{1,0:T(8,128)S(1)}, bf16[16,256]{1,0:T(8,128)(2,1)S(1)}) custom-call(bf16[256,2048]{1,0:T(8,128)(2,1)S(1)} %get-tuple-element.65.x_ref, bf16[256,256]{1,0:T(8,128)(2,1)S(1)} %get-tuple-element.69.b_ref, f32[32,256]{1,0:T(8,128)S(1)} %get-tuple-element.64.cum_ref, ...), custom_call_target="tpu_custom_call" | custom-call | flops 1000000000 | bytes 1 | tf_op jit(solution)/shard_map/ask_kernel/pallas_call | solution.py:561
  30.3 0.0 collective-permute-done.7.got_ref
  30.3 0.1 pass_kernel.15
  30.3 0.1 collective-permute-start.12
  30.4 0.3 read_kernel.2
  30.7 2.3 %collective-permute-start.14 = (bf16[4,2048]{1,0:T(4,128)(2,1)S(1)}, bf16[4,2048]{1,0:T(4,128)(2,1)S(1)}, u32[]{:S(2)}, u32[]{:S(2)}) collective-permute-start(bf16[4,2048]{1,0:T(4,128)(2,1)S(1)} %get-tuple-element.117), channel_id=1, source_target_pairs={{0,8},{1,9},{2,10},{3,11},{4,5},{5,4},{6,7},{7,6},{8,0},{9,1},{10,... | collective-permute-start | bytes 49160 | tf_op jit(solution)/shard_map/ppermute | solution.py:542
  33.0 0.0 collective-permute-start.15
  33.0 1.3 %collective-permute-start.13 = (bf16[4,2048]{1,0:T(4,128)(2,1)S(1)}, bf16[4,2048]{1,0:T(4,128)(2,1)S(1)}, u32[]{:S(2)}, u32[]{:S(2)}) collective-permute-start(bf16[4,2048]{1,0:T(4,128)(2,1)S(1)} %get-tuple-element.107.rest_4_), channel_id=1, source_target_pairs={{0,4},{1,5},{2,6},{3,7},{4,0},{5,1},{6,2},{7,3},{8,9},{9,8},{10,11... | collective-permute-start | bytes 49160 | tf_op jit(solution)/shard_map/ppermute | solution.py:542
  34.2 0.6 %outer_kernel.2.rest_4_.rest_0_ = bf16[2,256,512]{2,1,0:T(8,128)(2,1)S(1)} custom-call(bf16[256,256]{1,0:T(8,128)(2,1)S(1)} %get-tuple-element.63.c_ref, f32[32,256]{1,0:T(8,128)S(1)} %get-tuple-element.64.cum_ref, bf16[4,128,512]{2,1,0:T(8,128)(2,1)S(1)} %get-tuple-element.103.carry_ref, bf16[128,512]{1,0:T(8,128)(2,1)S(1)} %collective-permute-done.9.got_ref.rest_0_, ...), custom_call_target="tpu_custom_call" | custom-call | flops 1 | bytes 1 | tf_op jit(solution)/shard_map/outer_kernel/pallas_call | solution.py:579
  34.9 0.4 fresh_kernel.1
  35.3 0.1 collective-permute-done.14.rest_6_.rest_1_
  35.4 0.0 collective-permute-done.15.rest_7_.rest_2_
  35.4 1.3 %collective-permute-done.13.rest_5_.rest_0_ = bf16[4,2048]{1,0:T(4,128)(2,1)S(1)} collective-permute-done((bf16[4,2048]{1,0:T(4,128)(2,1)S(1)}, bf16[4,2048]{1,0:T(4,128)(2,1)S(1)}, u32[]{:S(2)}, u32[]{:S(2)}) %collective-permute-start.13) | collective-permute-done | bytes 16416 | tf_op jit(solution)/shard_map/ppermute | solution.py:542
  36.7 0.0 collective-permute-done.11.rest_0_.rest_2_
  36.7 0.0 collective-permute-done.12.rest_1_.rest_3_
  36.7 0.3 read_kernel.3
  37.0 0.4 collective-permute-start.16
  37.4 0.0 collective-permute-start.17
  37.4 0.5 %collective-permute-start.18 = (bf16[4,2048]{1,0:T(4,128)(2,1)S(1)}, bf16[4,2048]{1,0:T(4,128)(2,1)S(1)}, u32[]{:S(2)}, u32[]{:S(2)}) collective-permute-start(bf16[4,2048]{1,0:T(4,128)(2,1)S(1)} %get-tuple-element.121), channel_id=1, source_target_pairs={{0,1},{1,0},{2,3},{3,2},{4,5},{5,4},{6,7},{7,6},{8,12},{9,13},{10,... | collective-permute-start | bytes 49160 | tf_op jit(solution)/shard_map/ppermute | solution.py:542
  37.9 1.4 %outer_kernel.3 = (bf16[256,2048]{1,0:T(8,128)(2,1)}, f32[8,128]{1,0:T(8,128)S(1)}) custom-call(bf16[256,256]{1,0:T(8,128)(2,1)S(1)} %get-tuple-element.63.c_ref, f32[32,256]{1,0:T(8,128)S(1)} %get-tuple-element.64.cum_ref, bf16[4,128,512]{2,1,0:T(8,128)(2,1)S(1)} %get-tuple-element.103.carry_ref, ...), custom_call_target="tpu_custom_call" | custom-call | flops 1 | bytes 1 | tf_op jit(solution)/shard_map/outer_kernel/pallas_call | solution.py:579
  39.3 3.3 %collective-permute-done.16.rest_3_ = bf16[4,2048]{1,0:T(4,128)(2,1)S(1)} collective-permute-done((bf16[4,2048]{1,0:T(4,128)(2,1)S(1)}, bf16[4,2048]{1,0:T(4,128)(2,1)S(1)}, u32[]{:S(2)}, u32[]{:S(2)}) %collective-permute-start.16) | collective-permute-done | bytes 16416 | tf_op jit(solution)/shard_map/ppermute | solution.py:542
  42.6 0.0 collective-permute-done.17.rest_4_
  42.6 0.0 collective-permute-done.18.rest_5_
  42.6 0.7 %finish_kernel.1 = bf16[4,4,2048]{2,1,0:T(4,128)(2,1)} custom-call(f32[4,4,2048]{2,1,0:T(4,128)S(1)} %get-tuple-element.114.rest_4_.keep_ref, f32[4,4,2048]{2,1,0:T(4,128)S(1)} %get-tuple-element.115.fresh_ref, f32[4,4,128]{2,1,0:T(4,128)S(1)} %get-tuple-element.116.held_ref, bf16[4,2048]{1,0:T(4,128)(2,1)S(1)} %collective-permute-done.13.rest_5_.rest_0_, ...), custom_call_target="tpu_custom_call" | custom-call | flops 1 | bytes 1 | tf_op jit(solution)/shard_map/finish_kernel/pallas_call | solution.py:664
  (6 shorter events, 0.2 us)
Async XLA Ops:
  2.5 6.6 %collective-permute-start.1 = (bf16[128,512]{1,0:T(8,128)(2,1)S(1)}, bf16[128,512]{1,0:T(8,128)(2,1)S(1)}, u32[]{:S(2)}, u32[]{:S(2)}) collective-permute-start(bf16[128,512]{1,0:T(8,128)(2,1)S(1)} %get-tuple-element.75), channel_id=1, source_target_pairs={{0,4},{1,5},{2,6},{3,7},{4,0},{5,1},{6,2},{7,3},{8,9},{9,8},{10,11... | collective-permute-start | bytes 393224 | tf_op jit(solution)/shard_map/hop1_chunk0/ppermute | solution.py:542
  8.8 6.4 %collective-permute-start = (bf16[128,512]{1,0:T(8,128)(2,1)S(1)}, bf16[128,512]{1,0:T(8,128)(2,1)S(1)}, u32[]{:S(2)}, u32[]{:S(2)}) collective-permute-start(bf16[128,512]{1,0:T(8,128)(2,1)S(1)} %get-tuple-element.72), channel_id=1, source_target_pairs={{0,4},{1,5},{2,6},{3,7},{4,0},{5,1},{6,2},{7,3},{8,9},{9,8},{10,11... | collective-permute-start | bytes 393224 | tf_op jit(solution)/shard_map/hop1_chunk1/ppermute | solution.py:542
  9.2 8.2 %collective-permute-start.6 = (bf16[128,512]{1,0:T(8,128)(2,1)S(1)}, bf16[128,512]{1,0:T(8,128)(2,1)S(1)}, u32[]{:S(2)}, u32[]{:S(2)}) collective-permute-start(bf16[128,512]{1,0:T(8,128)(2,1)S(1)} %get-tuple-element.88), channel_id=1, source_target_pairs={{0,1},{1,0},{2,3},{3,2},{4,8},{5,9},{6,10},{7,11},{8,4},{9,5},{10,... | collective-permute-start | bytes 393224 | tf_op jit(solution)/shard_map/hop2_chunk0/ppermute | solution.py:542
  9.3 8.4 %collective-permute-start.5 = (bf16[128,512]{1,0:T(8,128)(2,1)S(1)}, bf16[128,512]{1,0:T(8,128)(2,1)S(1)}, u32[]{:S(2)}, u32[]{:S(2)}) collective-permute-start(bf16[128,512]{1,0:T(8,128)(2,1)S(1)} %get-tuple-element.86), channel_id=1, source_target_pairs={{0,4},{1,5},{2,6},{3,7},{4,0},{5,1},{6,2},{7,3},{8,9},{9,8},{10,11... | collective-permute-start | bytes 393224 | tf_op jit(solution)/shard_map/hop1_chunk2/ppermute | solution.py:542
  11.1 5.8 %collective-permute-start.2 = (bf16[16,512]{1,0:T(8,128)(2,1)S(1)}, bf16[16,512]{1,0:T(8,128)(2,1)S(1)}, u32[]{:S(2)}, u32[]{:S(2)}) collective-permute-start(bf16[16,512]{1,0:T(8,128)(2,1)S(1)} %get-tuple-element.82), channel_id=1, source_target_pairs={{0,4},{1,5},{2,6},{3,7},{4,0},{5,1},{6,2},{7,3},{8,12},{9,13},{10,... | collective-permute-start | bytes 49160 | tf_op jit(solution)/shard_map/ppermute | solution.py:542
  17.0 1.4 %collective-permute-start.4 = (bf16[144,512]{1,0:T(8,128)(2,1)S(1)}, bf16[144,512]{1,0:T(8,128)(2,1)S(1)}, u32[]{:S(2)}, u32[]{:S(2)}) collective-permute-start(bf16[144,512]{1,0:T(8,128)(2,1)S(1)} %get-tuple-element.85.rest_0_), channel_id=1, source_target_pairs={{0,1},{1,0},{2,3},{3,2},{4,8},{5,9},{6,10},{7,11},{8,4},{9,5},{10,... | collective-permute-start | bytes 442376 | tf_op jit(solution)/shard_map/hop2_chunk1/ppermute | solution.py:542
  17.1 5.9 %collective-permute-start.3 = (bf16[128,512]{1,0:T(8,128)(2,1)S(1)}, bf16[128,512]{1,0:T(8,128)(2,1)S(1)}, u32[]{:S(2)}, u32[]{:S(2)}) collective-permute-start(bf16[128,512]{1,0:T(8,128)(2,1)S(1)} %get-tuple-element.83), channel_id=1, source_target_pairs={{0,4},{1,5},{2,6},{3,7},{4,0},{5,1},{6,2},{7,3},{8,9},{9,8},{10,11... | collective-permute-start | bytes 393224 | tf_op jit(solution)/shard_map/hop1_chunk3/ppermute | solution.py:542
  17.5 6.0 %collective-permute-start.9 = (bf16[128,512]{1,0:T(8,128)(2,1)S(1)}, bf16[128,512]{1,0:T(8,128)(2,1)S(1)}, u32[]{:S(2)}, u32[]{:S(2)}) collective-permute-start(bf16[128,512]{1,0:T(8,128)(2,1)S(1)} %get-tuple-element.96), channel_id=1, source_target_pairs={{0,1},{1,0},{2,3},{3,2},{4,5},{5,4},{6,7},{7,6},{8,12},{9,13},{10,... | collective-permute-start | bytes 393224 | tf_op jit(solution)/shard_map/hop3_chunk0/ppermute | solution.py:542
  17.7 5.7 %collective-permute-start.8 = (bf16[128,512]{1,0:T(8,128)(2,1)S(1)}, bf16[128,512]{1,0:T(8,128)(2,1)S(1)}, u32[]{:S(2)}, u32[]{:S(2)}) collective-permute-start(bf16[128,512]{1,0:T(8,128)(2,1)S(1)} %get-tuple-element.94), channel_id=1, source_target_pairs={{0,1},{1,0},{2,3},{3,2},{4,8},{5,9},{6,10},{7,11},{8,4},{9,5},{10,... | collective-permute-start | bytes 393224 | tf_op jit(solution)/shard_map/hop2_chunk2/ppermute | solution.py:542
  23.0 7.2 %collective-permute-start.7 = (bf16[128,512]{1,0:T(8,128)(2,1)S(1)}, bf16[128,512]{1,0:T(8,128)(2,1)S(1)}, u32[]{:S(2)}, u32[]{:S(2)}) collective-permute-start(bf16[128,512]{1,0:T(8,128)(2,1)S(1)} %get-tuple-element.93.tie_ref), channel_id=1, source_target_pairs={{0,1},{1,0},{2,3},{3,2},{4,8},{5,9},{6,10},{7,11},{8,4},{9,5},{10,... | collective-permute-start | bytes 393224 | tf_op jit(solution)/shard_map/hop2_chunk3/ppermute | solution.py:542
  23.1 6.3 %collective-permute-start.10 = (bf16[144,512]{1,0:T(8,128)(2,1)S(1)}, bf16[144,512]{1,0:T(8,128)(2,1)S(1)}, u32[]{:S(2)}, u32[]{:S(2)}) collective-permute-start(bf16[144,512]{1,0:T(8,128)(2,1)S(1)} %get-tuple-element.100), channel_id=1, source_target_pairs={{0,4},{1,5},{2,6},{3,7},{4,0},{5,1},{6,2},{7,3},{8,12},{9,13},{10,... | collective-permute-start | bytes 442376 | tf_op jit(solution)/shard_map/hop3_chunk1/ppermute | solution.py:542
  23.5 13.2 %collective-permute-start.11 = (bf16[128,512]{1,0:T(8,128)(2,1)S(1)}, bf16[128,512]{1,0:T(8,128)(2,1)S(1)}, u32[]{:S(2)}, u32[]{:S(2)}) collective-permute-start(bf16[128,512]{1,0:T(8,128)(2,1)S(1)} %get-tuple-element.101.rest_3_), channel_id=1, source_target_pairs={{0,1},{1,0},{2,3},{3,2},{4,5},{5,4},{6,7},{7,6},{8,12},{9,13},{10,... | collective-permute-start | bytes 393224 | tf_op jit(solution)/shard_map/hop3_chunk2/ppermute | solution.py:542
  30.3 6.4 %collective-permute-start.12 = (bf16[128,512]{1,0:T(8,128)(2,1)S(1)}, bf16[128,512]{1,0:T(8,128)(2,1)S(1)}, u32[]{:S(2)}, u32[]{:S(2)}) collective-permute-start(bf16[128,512]{1,0:T(8,128)(2,1)S(1)} %get-tuple-element.104), channel_id=1, source_target_pairs={{0,1},{1,0},{2,3},{3,2},{4,5},{5,4},{6,7},{7,6},{8,12},{9,13},{10,... | collective-permute-start | bytes 393224 | tf_op jit(solution)/shard_map/hop3_chunk3/ppermute | solution.py:542
  30.7 4.7 %collective-permute-start.14 = (bf16[4,2048]{1,0:T(4,128)(2,1)S(1)}, bf16[4,2048]{1,0:T(4,128)(2,1)S(1)}, u32[]{:S(2)}, u32[]{:S(2)}) collective-permute-start(bf16[4,2048]{1,0:T(4,128)(2,1)S(1)} %get-tuple-element.117), channel_id=1, source_target_pairs={{0,8},{1,9},{2,10},{3,11},{4,5},{5,4},{6,7},{7,6},{8,0},{9,1},{10,... | collective-permute-start | bytes 49160 | tf_op jit(solution)/shard_map/ppermute | solution.py:542
  33.0 2.4 %collective-permute-start.15 = (bf16[4,2048]{1,0:T(4,128)(2,1)S(1)}, bf16[4,2048]{1,0:T(4,128)(2,1)S(1)}, u32[]{:S(2)}, u32[]{:S(2)}) collective-permute-start(bf16[4,2048]{1,0:T(4,128)(2,1)S(1)} %get-tuple-element.118), channel_id=1, source_target_pairs={{0,1},{1,0},{2,3},{3,2},{4,8},{5,9},{6,10},{7,11},{8,4},{9,5},{10,... | collective-permute-start | bytes 49160 | tf_op jit(solution)/shard_map/ppermute | solution.py:542
  33.0 3.7 %collective-permute-start.13 = (bf16[4,2048]{1,0:T(4,128)(2,1)S(1)}, bf16[4,2048]{1,0:T(4,128)(2,1)S(1)}, u32[]{:S(2)}, u32[]{:S(2)}) collective-permute-start(bf16[4,2048]{1,0:T(4,128)(2,1)S(1)} %get-tuple-element.107.rest_4_), channel_id=1, source_target_pairs={{0,4},{1,5},{2,6},{3,7},{4,0},{5,1},{6,2},{7,3},{8,9},{9,8},{10,11... | collective-permute-start | bytes 49160 | tf_op jit(solution)/shard_map/ppermute | solution.py:542
  37.0 5.6 %collective-permute-start.16 = (bf16[4,2048]{1,0:T(4,128)(2,1)S(1)}, bf16[4,2048]{1,0:T(4,128)(2,1)S(1)}, u32[]{:S(2)}, u32[]{:S(2)}) collective-permute-start(bf16[4,2048]{1,0:T(4,128)(2,1)S(1)} %get-tuple-element.119), channel_id=1, source_target_pairs={{0,12},{1,13},{2,14},{3,15},{4,5},{5,4},{6,7},{7,6},{8,9},{9,8},{1... | collective-permute-start | bytes 49160 | tf_op jit(solution)/shard_map/ppermute | solution.py:542
  37.4 5.2 %collective-permute-start.17 = (bf16[4,2048]{1,0:T(4,128)(2,1)S(1)}, bf16[4,2048]{1,0:T(4,128)(2,1)S(1)}, u32[]{:S(2)}, u32[]{:S(2)}) collective-permute-start(bf16[4,2048]{1,0:T(4,128)(2,1)S(1)} %get-tuple-element.120), channel_id=1, source_target_pairs={{0,1},{1,0},{2,3},{3,2},{4,12},{5,13},{6,14},{7,15},{8,9},{9,8},{1... | collective-permute-start | bytes 49160 | tf_op jit(solution)/shard_map/ppermute | solution.py:542
  37.4 5.2 %collective-permute-start.18 = (bf16[4,2048]{1,0:T(4,128)(2,1)S(1)}, bf16[4,2048]{1,0:T(4,128)(2,1)S(1)}, u32[]{:S(2)}, u32[]{:S(2)}) collective-permute-start(bf16[4,2048]{1,0:T(4,128)(2,1)S(1)} %get-tuple-element.121), channel_id=1, source_target_pairs={{0,1},{1,0},{2,3},{3,2},{4,5},{5,4},{6,7},{7,6},{8,12},{9,13},{10,... | collective-permute-start | bytes 49160 | tf_op jit(solution)/shard_map/ppermute | solution.py:542

commit v9 on v8

--- a/solution.py
+++ b/solution.py
@@ -18,7 +18,7 @@
 F32 = jnp.float32
 BF16 = jnp.bfloat16
 CHUNKS = 4
-COSTS = {(2, 2): 10**9}
+TOKEN_COST = 5 * 10**8
 VMEM_LIMIT = 32 * 1024 * 1024
 
 
@@ -99,8 +99,8 @@
     hbm, refs = refs[: kept + 1], refs[kept + 1 :]
     here, refs = refs[:kept], refs[kept:]
     cum_ref, row_ref, weight_ref, whole_ref, turned_ref = refs[:5]
-    total_ref, decay_ref, sent_ref, own_ref, dt_ref, sems = refs[5:]
-    x_ref, b_ref, a_ref, asked_ref = here[:4]
+    total_ref, decay_ref, sent_ref, dt_ref, sems = refs[5:]
+    x_ref, b_ref, a_ref = here[:3]
     heads, tokens = dt_ref.shape
     spans = tokens // SPAN
     width = total_ref.shape[1]
@@ -146,8 +146,6 @@
     x_copies[1].wait()
     for copy in copies[2:]:
         copy.wait()
-    own = flat(asked_ref).astype(BF16)
-    own_ref[...] = jnp.concatenate([own, own], axis=1)
 
 
 def state_kernel(part, x_ref, turned_ref, weight_ref, whole_ref, *rest):
@@ -163,37 +161,26 @@
     return jnp.concatenate([ref[i].astype(F32) for i in range(ref.shape[0])], axis=0)
 
 
-def token_kernel(got_ref, tie_ref, token_ref):
-    token_ref[...] = jnp.zeros_like(token_ref)
-
-
-def pass_kernel(hop, k, tail, more, opening, got_ref, total_ref, decay_ref, *rest):
-    results = rest[-2 - more - opening :]
-    extra, (moving_ref, carry_ref) = rest, results[:2]
-    me = lax.axis_index("seq")
+def token_kernel(*refs):
+    refs[-1][...] = jnp.zeros_like(refs[-1])
+
+
+def pass_kernel(hop, k, more, got_ref, total_ref, decay_ref, *rest):
+    moving_ref, carry_ref = rest[len(rest) - 2 - more : len(rest) - more]
     if hop == 1 and k == 0:
+        following_ref = rest[0]
         carry_ref[...] = jnp.zeros_like(carry_ref)
     else:
-        extra = extra[1:]
-    got = got_ref[:N]
-    moving_ref[:N] = (total_ref[...] + decay_ref[...] * got.astype(F32)).astype(BF16)
-
-    @pl.when(me == hop)
+        following_ref = rest[1]
+    got = got_ref[...]
+    moving_ref[...] = (total_ref[...] + decay_ref[...] * got.astype(F32)).astype(BF16)
+
+    @pl.when(lax.axis_index("seq") == hop)
     def _():
         carry_ref[k] = got
 
     if more:
-        results[2][...] = extra[0][...].astype(BF16)
-        extra = extra[1:]
-    if opening:
-        results[-1][...] = extra[0][...]
-    if tail and hop == 1:
-        own, other = extra[0][...].astype(F32), extra[1][...].astype(F32)
-        lane = lax.broadcasted_iota(jnp.int32, own.shape, 1)
-        mine = (lane // (own.shape[1] // 2)) == lax.rem(me, 2)
-        moving_ref[N:] = jnp.where(mine, own, other).astype(BF16)
-    elif tail:
-        moving_ref[N:] = got_ref[N:]
+        rest[-1][...] = following_ref[...].astype(BF16)
 
 
 def pair_halves(x_part):
@@ -256,7 +243,7 @@
             inner_ref[mine, here] = dot(left, right) + skip * x_part[mine].astype(F32)
 
 
-def ask_kernel(count, ride, x_ref, b_ref, cum_ref, row_ref, len_ref, owner_ref, *rest):
+def ask_kernel(x_ref, b_ref, cum_ref, row_ref, len_ref, owner_ref, asked_here_ref, *rest):
     local_ref, gain_ref, asked_ref = rest[-3:]
     heads, tokens = cum_ref.shape
     spans = tokens // SPAN
@@ -264,24 +251,12 @@
     per_group = H // G
     groups = heads // per_group
     me = lax.axis_index("seq")
-    if ride:
-        near, middle, far = [ref[N:].astype(F32) for ref in rest[:3]]
-        far = jnp.where((me == 1) | (me == 2), middle, far)
-        halves = (jnp.where(me < 2, near, far), jnp.where(me < 2, far, near))
-        names = near.shape[1] // 2
-        blocks = [half[:, i * names : (i + 1) * names] for half in halves for i in range(2)]
-    else:
-        blocks = [flat(ref) for ref in rest[:count]]
-    blocks = jnp.concatenate(blocks, axis=0).astype(BF16)
-    row = lax.broadcasted_iota(jnp.int32, (asks, asks * count), 0)
-    column = lax.broadcasted_iota(jnp.int32, (asks, asks * count), 1)
-    place = row // STEPS
-    wanted = place * asks + me * STEPS + row % STEPS
-    asked = dot(jnp.where(column == wanted, 1.0, 0.0).astype(BF16), blocks).astype(BF16)
+    blocks = [asked_here_ref[r, me].astype(F32) for r in range(asks // STEPS)]
+    asked = jnp.concatenate(blocks, axis=0).astype(BF16)
     asked_ref[...] = asked
     block = lax.broadcasted_iota(jnp.int32, (asks, 1), 0) // STEPS
     spot = len_ref[...] - 1 - me * tokens
-    mine = (owner_ref[...] == (block if ride else lax.rem(me + count - block, count))) & (spot >= 0) & (spot < tokens)
+    mine = (owner_ref[...] == block) & (spot >= 0) & (spot < tokens)
     spot = jnp.sum(jnp.where(mine, spot, 0).astype(F32), axis=1, keepdims=True).astype(jnp.int32)
     position = lax.broadcasted_iota(jnp.int32, (asks, tokens), 1)
     picked = jnp.where(position == spot, 1.0, 0.0).astype(BF16)
@@ -328,14 +303,17 @@
         g = first // (H // G * P_SIZE)
         state = carry_ref[k]
         if final:
-            state = jnp.where(me == count - 1, got_refs[k][:N], state)
+            state = jnp.where(me == count - 1, got_refs[k][...], state)
         carried = dot(asked_ref[:, g * N : (g + 1) * N], state)
         reading = local_ref[:, here] + over_lanes(gain_ref[...], first, width) * carried
         parts = [reading[r * STEPS : (r + 1) * STEPS] for r in range(count)]
-        for (one, other), read_ref in zip(ops, read_refs):
-            part = parts[other]
-            if one != other:
-                part = jnp.where(me == one, part, parts[one])
+        for op, read_ref in zip(ops, read_refs):
+            if isinstance(op, tuple):
+                part = jnp.where(me == op[0], parts[op[1]], parts[op[0]])
+            else:
+                part = parts[0]
+                for r in range(1, count):
+                    part = jnp.where(lax.rem(me + count - op, count) == r, parts[r], part)
             read_ref[:, here] = part.astype(read_ref.dtype)
         if final:
             own = parts[0]
@@ -379,7 +357,7 @@
     for i, k in enumerate(part):
         first = k * width
         g = first // group_lanes
-        state = jnp.where(last, got_refs[i][:N], carry_ref[k])
+        state = jnp.where(last, got_refs[i][...], carry_ref[k])
         carried = dot(c_ref[:, g * N : (g + 1) * N], state)
         inner = inner_refs[g][:, first - g * group_lanes : first - g * group_lanes + width]
         out_ref[i] = (inner + over_lanes(gain, first, width) * carried).astype(BF16)
@@ -475,12 +453,7 @@
     anywhere = pl.BlockSpec(memory_space=pl.ANY)
     in_hbm = pl.BlockSpec(memory_space=pltpu.HBM)
     in_vmem = pl.BlockSpec(memory_space=pltpu.VMEM)
-    ride = count == 4 and width == 2 * names
-
-    def sent_shape(hop, k):
-        tail = ride and k == 1 and hop > 1
-        return shape((N + rows * tail, width), BF16)
-
+    sent_shape = shape((N, width), BF16)
     inputs = [
         ssm_input,
         bmat,
@@ -495,7 +468,6 @@
         dec_dt[0],
     ]
     chunk_shapes = (shape((N, width)), shape((1, width)))
-    own_shape = shape((rows, 2 * names), BF16)
     results = call(
         functools.partial(first_kernel, len(inputs)),
         tuple(shape(value.shape, value.dtype) for value in inputs)
@@ -507,7 +479,7 @@
             shape((groups, N, tokens), BF16),
         )
         + chunk_shapes
-        + (sent_shape(1, 0), own_shape),
+        + (sent_shape,),
         in_specs=[in_hbm] * (len(inputs) + 1),
         scratch_shapes=[
             pltpu.VMEM((heads, tokens), BF16),
@@ -517,13 +489,13 @@
     x, b, a_row, asked_here, c, d_row, len_row, owner_row, x_dec, b_dec, dt_dec = results[:11]
     cum, row, weight, whole, turned = results[11:16]
     total, decay = [results[16]], [results[17]]
+    all_asked = lax.all_gather(dec_c[0], "seq")
     sent = {0: results[18]}
-    own = results[19]
 
     def state_part(part, tie):
         out = call(
             functools.partial(state_kernel, part),
-            chunk_shapes * len(part) + (sent_shape(1, 1),),
+            chunk_shapes * len(part) + (sent_shape,),
             in_specs=[in_vmem] * 4 + [anywhere],
         )(x, turned, weight, whole, tie)
         total.extend(out[0 : 2 * len(part) : 2])
@@ -542,9 +514,8 @@
         return lax.ppermute(value, ("seq", "tp"), pairs)
 
     def forward(value, hop, k):
-        rides = ride and (hop, k) == (3, 1)
         with jax.named_scope(f"hop{hop}_chunk{k}"):
-            return swap(value, *([(0, 1), (2, 3)] if rides else [(hop - 1, hop)]))
+            return swap(value, (hop - 1, hop))
 
     def shift(value, by):
         return lax.ppermute(value, "seq", [(d, (d + by) % count) for d in range(count)])
@@ -557,13 +528,16 @@
         )(x, b, c, cum, row, d_row, *after)
 
     def ask_part(*after):
-        blocks = (moving[2, 1], got[2, 1], got[3, 1]) if ride else asks
         return call(
-            functools.partial(ask_kernel, count, ride),
+            ask_kernel,
             (shape((rows, lanes)), shape((rows, heads)), shape((rows, names), BF16)),
-            flops=10**9,
-            in_specs=[in_vmem] * (6 + len(blocks)) + [anywhere] * len(after),
-        )(x, b, cum, row, len_row, owner_row, *blocks, *after)
+            in_specs=[in_vmem] * 7 + [anywhere] * len(after),
+        )(x, b, cum, row, len_row, owner_row, all_asked, *after)
+
+    def token(*after, flops=1):
+        return call(
+            token_kernel, shape((8, 128)), flops=flops, in_specs=[anywhere] * len(after)
+        )(*after)
 
     def fresh_part(*after):
         return call(
@@ -594,78 +568,54 @@
         )(*operands, *after)
 
     got = {(1, 0): forward(sent[0], 1, 0)}
-    moving = {}
     inner = [inner_part(0)]
     for g in range(1, groups):
         inner.append(inner_part(g, inner[-1]))
     sent[1] = state_part(list(range(1, chunks)), inner[-1])
     got[1, 1] = forward(sent[1], 1, 1)
-    if not ride:
-        asks = [asked_here] + [shift(asked_here, r) for r in range(1, count)]
     order = sorted((k + hop, hop, k) for hop in range(1, count - 1) for k in range(chunks))
-    carry = tie = other = None
+    carry = tie = None
     for _, hop, k in order:
-        tail = ride and k == 1
         more = hop == 1 and k + 2 < chunks
         operands = [got[hop, k], total[k], decay[k]]
         operands += [] if carry is None else [carry]
-        opening = ride and (hop, k) == (1, 0)
-        operands += total[k + 2 : k + 3] * more + [own] * opening
-        operands += [own, other] * (tail and hop == 1)
+        operands += total[k + 2 : k + 3] * more
         after = []
-        if hop == count - 2 and k == chunks - 1:
-            local, gain, asked = ask_part(tie)
-            after = [gain]
-        elif hop == count - 2 and k > 1:
-            after = [
-                call(
-                    token_kernel, shape((8, 128)), flops=10**9, in_specs=[anywhere] * 2
-                )(got[hop + 1, k - 2], tie)
-            ]
-        moving[hop + 1, k], carry, *following = call(
-            functools.partial(pass_kernel, hop, k, tail, more, opening),
-            (sent_shape(hop + 1, k), shape((chunks, N, width), BF16))
-            + (sent_shape(1, k + 2),) * more
-            + (own_shape,) * opening,
-            flops=COSTS.get((hop, k), 1),
+        if hop == count - 2 and k > 1:
+            after = [token(got[hop + 1, k - 2], tie, flops=TOKEN_COST)]
+        tie, carry, *following = call(
+            functools.partial(pass_kernel, hop, k, more),
+            (sent_shape, shape((chunks, N, width), BF16)) + (sent_shape,) * more,
             in_specs=[in_vmem] * len(operands) + [anywhere] * len(after),
             input_output_aliases={} if carry is None else {3: 1},
         )(*operands, *after)
-        got[hop + 1, k] = forward(moving[hop + 1, k], hop + 1, k)
-        tie = moving[hop + 1, k]
+        got[hop + 1, k] = forward(tie, hop + 1, k)
         if more:
             got[1, k + 2] = forward(following[0], 1, k + 2)
-        if ride and (hop, k) == (1, 0):
-            other = swap(following[-1], (0, 1), (2, 3))
 
     early, late = tuple(range(chunks // 2)), tuple(range(chunks // 2, chunks))
-
-    back = []
-    if ride:
-        ops, ends = [(0, 1), (0, 2), (1, 2)], [(0, 3), (1, 3), (2, 3)]
+    four = count == 4
+    local, gain, asked = ask_part(tie)
+    back, ops = [], [(0, 2), (1, 2), (0, 1)] if four else []
+    if four:
         reading = read_part(ops, False)
         for couple, value in zip(ops, reading):
             back.append(swap(value, couple))
-        outer = outer_part((early,), carry, [], reading[0])
-        keep, fresh, held = fresh_part(outer)
-        *reading, mine = read_part(ends, True, keep, *back)
-        for couple, value in zip(ends, reading):
-            back.append(swap(value, couple))
-        ops = ops + ends
-    else:
-        outer = outer_part((early,), carry, [])
-        keep, fresh, held = fresh_part(outer)
-        *reading, mine = read_part([(r, r) for r in range(count)], True)
-        ops = list(range(1, count))
-        back = [shift(reading[r], -r) for r in ops]
-        mine = reading[0].astype(F32)
-    prefill, token = outer_part((early, late), carry, [outer])
+    outer = outer_part((early,), carry, [], reading[0] if four else asked)
+    keep, fresh, held = fresh_part(outer)
+    order_token = token(got[count - 1, chunks - 2], keep, flops=TOKEN_COST)
+    ends = [(0, 3), (1, 3), (2, 3)] if four else list(range(1, count))
+    *reading, mine = read_part(ends, True, order_token, *back)
+    for op, value in zip(ends, reading):
+        back.append(swap(value, op) if four else shift(value, -op))
+    ops = ops + ends
+    prefill, end_token = outer_part((early, late), carry, [outer])
 
     decoded = call(
         functools.partial(finish_kernel, ops),
         jax.ShapeDtypeStruct((count, STEPS, lanes), BF16),
         in_specs=[in_vmem] * (4 + len(ops)) + [anywhere],
-    )(keep, fresh, held, *back, mine, token)
+    )(keep, fresh, held, *back, mine, end_token)
     return (prefill, decoded[None])
 
 

time: 43.6 us -> 51.7 us (1.19)
  blocking collectives: 0 us -> 14.8 us
  waiting for transfers between devices: 21.1 us -> 14 us
    all_gather x0 -> x1, blocking collectives: none -> 14.8 us  [shards(): all_asked = lax.all_gather(dec_c[0], 'seq')]
    ppermute x19 -> x18, waiting for transfers between devices: 21.1 us -> 14 us  [swap(): return lax.ppermute(value, ('seq', 'tp'), pairs)]
    ppermute x19 -> x18, starting transfers between devices: 11.6 us -> 11.3 us  [swap(): return lax.ppermute(value, ('seq', 'tp'), pairs)]
    pallas_call x10 -> x12, Pallas kernels: 1.26 us -> 1.26 us  [the longest x1 0.89 us: ask_part(): call(ask_kernel, (shape((rows, lanes)), shape((rows, heads)), shape((rows...]
  transfers between devices with their start and end apart: 19 -> 18, of which waited for: 9 -> 8; matrix products, arithmetic and copies ran while one was open for 0% -> 0% of each run, Pallas kernels for 16% -> 14%
where the time goes in v9:
time: 51.7 us; the launch traced here: 51.4 us
  blocking collectives  14.8 us (29%)
  waiting for transfers between devices  14 us (27%)
  starting transfers between devices  11.3 us (22%)
  Pallas kernels  9.94 us (19%)
  between operations  0.85 us (2%)
    all_gather x1, blocking collectives, shards(): all_asked = lax.all_gather(dec_c[0], 'seq')  14.8 us
    ppermute x18, waiting for transfers between devices, swap(): return lax.ppermute(value, ('seq', 'tp'), pairs)  14 us
    ppermute x18, starting transfers between devices, swap(): return lax.ppermute(value, ('seq', 'tp'), pairs)  11.3 us
    pallas_call x2, Pallas kernels, inner_part(): call(functools.partial(inner_kernel, g), shape((tokens, group_lanes)), in...  2.05 us
    pallas_call x2, Pallas kernels, outer_part(): call(functools.partial(outer_kernel, parts, count), (pltpu.HBM((tokens, l...  1.95 us
    pallas_call x1, Pallas kernels, shards(): call(functools.partial(first_kernel, len(inputs)), tuple((shape(value.sha...  1.89 us
    pallas_call x1, Pallas kernels, state_part(): call(functools.partial(state_kernel, part), chunk_shapes * len(part) + (s...  1.1 us
  transfers between devices with their start and end apart: 18, of which 8 were waited for; matrix products, arithmetic and copies ran while one was open for 0% of the time, Pallas kernels for 14%

profile of v9, /device:TPU:0, one launch (start us, length us, event | category | flops | bytes accessed | tf_op | source)
XLA Modules:
  0.0 51.4 jit_solution(9130701725700492190)
XLA Ops:
  0.6 1.9 %first_kernel.1 = (bf16[256,2048]{1,0:T(8,128)(2,1)S(1)}, bf16[256,256]{1,0:T(8,128)(2,1)S(1)}, f32[1,32]{1,0:T(1,128)S(1)}, bf16[4,4,256]{2,1,0:T(4,128)(2,1)S(...) custom-call(bf16[256,2048]{1,0:T(8,128)(2,1)} %refs_0_.1, ...), custom_call_target="tpu_custom_call" | custom-call | flops 1 | bytes 1 | tf_op jit(solution)/shard_map/first_kernel/pallas_call | solution.py:471
  2.5 3.1 %collective-permute-start.1 = (bf16[128,512]{1,0:T(8,128)(2,1)S(1)}, bf16[128,512]{1,0:T(8,128)(2,1)S(1)}, u32[]{:S(2)}, u32[]{:S(2)}) collective-permute-start(bf16[128,512]{1,0:T(8,128)(2,1)S(1)} %get-tuple-element.73), channel_id=1, source_target_pairs={{0,4},{1,5},{2,6},{3,7},{4,0},{5,1},{6,2},{7,3},{8,9},{9,8},{10,11... | collective-permute-start | bytes 393224 | tf_op jit(solution)/shard_map/hop1_chunk0/ppermute | solution.py:514
  5.6 1.0 %inner_kernel.2.rest_0_.rest_2_ = f32[256,1024]{1,0:T(8,128)S(1)} custom-call(bf16[256,2048]{1,0:T(8,128)(2,1)S(1)} %get-tuple-element.63.x_ref, bf16[256,256]{1,0:T(8,128)(2,1)S(1)} %get-tuple-element.67.b_ref, bf16[256,256]{1,0:T(8,128)(2,1)S(1)} %get-tuple-element.61.c_ref, f32[32,256]{1,0:T(8,128)S(1)} %get-tuple-element.62.cum_ref, ...), custom_call_target="tpu_custom_call" | custom-call | flops 1 | bytes 1 | tf_op jit(solution)/shard_map/inner_kernel/pallas_call | solution.py:524
  6.7 1.0 %inner_kernel.3.rest_0_.rest_3_ = f32[256,1024]{1,0:T(8,128)S(1)} custom-call(bf16[256,2048]{1,0:T(8,128)(2,1)S(1)} %get-tuple-element.63.x_ref, bf16[256,256]{1,0:T(8,128)(2,1)S(1)} %get-tuple-element.67.b_ref, bf16[256,256]{1,0:T(8,128)(2,1)S(1)} %get-tuple-element.61.c_ref, f32[32,256]{1,0:T(8,128)S(1)} %get-tuple-element.62.cum_ref, ...), custom_call_target="tpu_custom_call" | custom-call | flops 1 | bytes 1 | tf_op jit(solution)/shard_map/inner_kernel/pallas_call | solution.py:524
  7.7 1.1 %state_kernel.1 = (f32[128,512]{1,0:T(8,128)S(1)}, f32[1,512]{1,0:T(1,128)S(1)}, f32[128,512]{1,0:T(8,128)S(1)}, f32[1,512]{1,0:T(1,128)S(1)}, f32[128,512]{1,0:...) custom-call(bf16[256,2048]{1,0:T(8,128)(2,1)S(1)} %get-tuple-element.63.x_ref, ...), custom_call_target="tpu_custom_call" | custom-call | flops 1 | bytes 1 | tf_op jit(solution)/shard_map/state_kernel/pallas_call | solution.py:496
  8.8 0.1 collective-permute-start
  8.8 0.3 collective-permute-done.1.got_ref
  9.1 0.1 pass_kernel.8
  9.2 0.1 collective-permute-start.5
  9.3 1.8 %collective-permute-start.4 = (bf16[128,512]{1,0:T(8,128)(2,1)S(1)}, bf16[128,512]{1,0:T(8,128)(2,1)S(1)}, u32[]{:S(2)}, u32[]{:S(2)}) collective-permute-start(bf16[128,512]{1,0:T(8,128)(2,1)S(1)} %get-tuple-element.82), channel_id=1, source_target_pairs={{0,4},{1,5},{2,6},{3,7},{4,0},{5,1},{6,2},{7,3},{8,9},{9,8},{10,11... | collective-permute-start | bytes 393224 | tf_op jit(solution)/shard_map/hop1_chunk2/ppermute | solution.py:514
  11.1 4.1 %collective-permute-done.got_ref = bf16[128,512]{1,0:T(8,128)(2,1)S(1)} collective-permute-done((bf16[128,512]{1,0:T(8,128)(2,1)S(1)}, bf16[128,512]{1,0:T(8,128)(2,1)S(1)}, u32[]{:S(2)}, u32[]{:S(2)}) %collective-permute-start) | collective-permute-done | bytes 131104 | tf_op jit(solution)/shard_map/hop1_chunk1/ppermute | solution.py:514
  15.3 0.1 collective-permute-start.3
  15.3 0.1 collective-permute-start.2
  15.4 0.0 collective-permute-done.5.got_ref
  15.5 0.5 collective-permute-start.8
  15.9 0.7 %collective-permute-done.4.got_ref = bf16[128,512]{1,0:T(8,128)(2,1)S(1)} collective-permute-done((bf16[128,512]{1,0:T(8,128)(2,1)S(1)}, bf16[128,512]{1,0:T(8,128)(2,1)S(1)}, u32[]{:S(2)}, u32[]{:S(2)}) %collective-permute-start.4) | collective-permute-done | bytes 131104 | tf_op jit(solution)/shard_map/hop1_chunk2/ppermute | solution.py:514
  16.6 0.1 collective-permute-start.7
  16.7 0.0 collective-permute-done.3.got_ref
  16.8 0.5 %collective-permute-start.9 = (bf16[128,512]{1,0:T(8,128)(2,1)S(1)}, bf16[128,512]{1,0:T(8,128)(2,1)S(1)}, u32[]{:S(2)}, u32[]{:S(2)}) collective-permute-start(bf16[128,512]{1,0:T(8,128)(2,1)S(1)} %get-tuple-element.94), channel_id=1, source_target_pairs={{0,1},{1,0},{2,3},{3,2},{4,5},{5,4},{6,7},{7,6},{8,12},{9,13},{10,... | collective-permute-start | bytes 393224 | tf_op jit(solution)/shard_map/hop3_chunk1/ppermute | solution.py:514
  17.3 3.9 %collective-permute-done.2.got_ref = bf16[128,512]{1,0:T(8,128)(2,1)S(1)} collective-permute-done((bf16[128,512]{1,0:T(8,128)(2,1)S(1)}, bf16[128,512]{1,0:T(8,128)(2,1)S(1)}, u32[]{:S(2)}, u32[]{:S(2)}) %collective-permute-start.2) | collective-permute-done | bytes 131104 | tf_op jit(solution)/shard_map/hop1_chunk3/ppermute | solution.py:514
  21.3 0.1 collective-permute-start.6
  21.4 0.0 collective-permute-done.8.refs_0_.rest_0_
  21.4 0.0 collective-permute-done.7.got_ref
  21.4 0.5 %collective-permute-start.10 = (bf16[128,512]{1,0:T(8,128)(2,1)S(1)}, bf16[128,512]{1,0:T(8,128)(2,1)S(1)}, u32[]{:S(2)}, u32[]{:S(2)}) collective-permute-start(bf16[128,512]{1,0:T(8,128)(2,1)S(1)} %get-tuple-element.95.refs_1_), channel_id=1, source_target_pairs={{0,1},{1,0},{2,3},{3,2},{4,5},{5,4},{6,7},{7,6},{8,12},{9,13},{10,... | collective-permute-start | bytes 393224 | tf_op jit(solution)/shard_map/hop3_chunk2/ppermute | solution.py:514
  22.0 0.0 collective-permute-done.9.refs_0_.rest_1_
  22.0 0.7 %collective-permute-done.6.got_ref = bf16[128,512]{1,0:T(8,128)(2,1)S(1)} collective-permute-done((bf16[128,512]{1,0:T(8,128)(2,1)S(1)}, bf16[128,512]{1,0:T(8,128)(2,1)S(1)}, u32[]{:S(2)}, u32[]{:S(2)}) %collective-permute-start.6) | collective-permute-done | bytes 131104 | tf_op jit(solution)/shard_map/hop2_chunk3/ppermute | solution.py:514
  22.7 0.0 copy-start
  22.7 0.2 collective-permute-start.11
  23.0 0.4 copy-done
  23.4 14.8 %all_gather.3.asked_here_ref = bf16[4,4,4,256]{3,2,1,0:T(4,128)(2,1)S(1)} all-gather(bf16[1,4,4,256]{3,2,1,0:T(4,128)(2,1)S(1)} %copy-done), channel_id=1, replica_groups=mesh['grp'=2,'seq'=4,'tp'=4] {'seq'}, dimensions={0}, use_global_device_ids=true | all-gather | bytes 40960 | tf_op jit(solution)/shard_map/all_gather | solution.py:492
  38.2 0.9 %ask_kernel.1 = (f32[16,2048]{1,0:T(8,128)S(1)}, f32[16,32]{1,0:T(8,128)S(1)}, bf16[16,256]{1,0:T(8,128)(2,1)S(1)}) custom-call(bf16[256,2048]{1,0:T(8,128)(2,1)S(1)} %get-tuple-element.63.x_ref, bf16[256,256]{1,0:T(8,128)(2,1)S(1)} %get-tuple-element.67.b_ref, f32[32,256]{1,0:T(8,128)S(1)} %get-tuple-element.62.cum_ref, ...), custom_call_target="tpu_custom_call" | custom-call | flops 1 | bytes 1 | tf_op jit(solution)/shard_map/ask_kernel/pallas_call | solution.py:531
  39.1 0.3 read_kernel.2
  39.4 0.6 %collective-permute-start.12 = (bf16[4,2048]{1,0:T(4,128)(2,1)S(1)}, bf16[4,2048]{1,0:T(4,128)(2,1)S(1)}, u32[]{:S(2)}, u32[]{:S(2)}) collective-permute-start(bf16[4,2048]{1,0:T(4,128)(2,1)S(1)} %get-tuple-element.103.rest_4_), channel_id=1, source_target_pairs={{0,8},{1,9},{2,10},{3,11},{4,5},{5,4},{6,7},{7,6},{8,0},{9,1},{10,... | collective-permute-start | bytes 49160 | tf_op jit(solution)/shard_map/ppermute | solution.py:514
  40.0 0.0 collective-permute-start.13
  40.0 2.9 %collective-permute-start.14 = (bf16[4,2048]{1,0:T(4,128)(2,1)S(1)}, bf16[4,2048]{1,0:T(4,128)(2,1)S(1)}, u32[]{:S(2)}, u32[]{:S(2)}) collective-permute-start(bf16[4,2048]{1,0:T(4,128)(2,1)S(1)} %get-tuple-element.114), channel_id=1, source_target_pairs={{0,4},{1,5},{2,6},{3,7},{4,0},{5,1},{6,2},{7,3},{8,9},{9,8},{10,11... | collective-permute-start | bytes 49160 | tf_op jit(solution)/shard_map/ppermute | solution.py:514
  43.0 0.6 %outer_kernel.2.rest_4_.rest_0_ = bf16[2,256,512]{2,1,0:T(8,128)(2,1)S(1)} custom-call(bf16[256,256]{1,0:T(8,128)(2,1)S(1)} %get-tuple-element.61.c_ref, f32[32,256]{1,0:T(8,128)S(1)} %get-tuple-element.62.cum_ref, bf16[4,128,512]{2,1,0:T(8,128)(2,1)S(1)} %get-tuple-element.96.carry_ref, bf16[128,512]{1,0:T(8,128)(2,1)S(1)} %collective-permute-done.8.refs_0_.rest_0_, ...), custom_call_target="tpu_custom_call" | custom-call | flops 1 | bytes 1 | tf_op jit(solution)/shard_map/outer_kernel/pallas_call | solution.py:553
  43.6 0.4 fresh_kernel.1
  44.0 0.0 collective-permute-done.10.rest_0_.refs_0_.rest_2_
  44.0 0.1 collective-permute-done.12.rest_5_.rest_0_
  44.1 0.0 collective-permute-done.13.rest_6_.rest_1_
  44.1 0.6 %collective-permute-done.14.rest_7_.rest_2_ = bf16[4,2048]{1,0:T(4,128)(2,1)S(1)} collective-permute-done((bf16[4,2048]{1,0:T(4,128)(2,1)S(1)}, bf16[4,2048]{1,0:T(4,128)(2,1)S(1)}, u32[]{:S(2)}, u32[]{:S(2)}) %collective-permute-start.14) | collective-permute-done | bytes 16416 | tf_op jit(solution)/shard_map/ppermute | solution.py:514
  44.7 0.0 collective-permute-done.11.rest_1_.rest_3_
  44.7 0.3 read_kernel.3
  45.0 0.1 collective-permute-start.15
  45.0 0.1 collective-permute-start.16
  45.1 0.5 collective-permute-start.17
  45.6 1.3 %outer_kernel.3 = (bf16[256,2048]{1,0:T(8,128)(2,1)}, f32[8,128]{1,0:T(8,128)S(1)}) custom-call(bf16[256,256]{1,0:T(8,128)(2,1)S(1)} %get-tuple-element.61.c_ref, f32[32,256]{1,0:T(8,128)S(1)} %get-tuple-element.62.cum_ref, bf16[4,128,512]{2,1,0:T(8,128)(2,1)S(1)} %get-tuple-element.96.carry_ref, ...), custom_call_target="tpu_custom_call" | custom-call | flops 1 | bytes 1 | tf_op jit(solution)/shard_map/outer_kernel/pallas_call | solution.py:553
  47.0 3.6 %collective-permute-done.15.rest_3_ = bf16[4,2048]{1,0:T(4,128)(2,1)S(1)} collective-permute-done((bf16[4,2048]{1,0:T(4,128)(2,1)S(1)}, bf16[4,2048]{1,0:T(4,128)(2,1)S(1)}, u32[]{:S(2)}, u32[]{:S(2)}) %collective-permute-start.15) | collective-permute-done | bytes 16416 | tf_op jit(solution)/shard_map/ppermute | solution.py:514
  50.6 0.0 collective-permute-done.16.rest_4_
  50.6 0.0 collective-permute-done.17.rest_5_
  50.6 0.7 %finish_kernel.1 = bf16[4,4,2048]{2,1,0:T(4,128)(2,1)} custom-call(f32[4,4,2048]{2,1,0:T(4,128)S(1)} %get-tuple-element.110.refs_1_.keep_ref, f32[4,4,2048]{2,1,0:T(4,128)S(1)} %get-tuple-element.111.fresh_ref, f32[4,4,128]{2,1,0:T(4,128)S(1)} %get-tuple-element.112.held_ref, bf16[4,2048]{1,0:T(4,128)(2,1)S(1)} %collective-permute-done.12.rest_5_.rest_0_, ...), custom_call_target="tpu_custom_call" | custom-call | flops 1 | bytes 1 | tf_op jit(solution)/shard_map/finish_kernel/pallas_call | solution.py:614
  (10 shorter events, 0.3 us)
Async XLA Ops:
  2.5 6.6 %collective-permute-start.1 = (bf16[128,512]{1,0:T(8,128)(2,1)S(1)}, bf16[128,512]{1,0:T(8,128)(2,1)S(1)}, u32[]{:S(2)}, u32[]{:S(2)}) collective-permute-start(bf16[128,512]{1,0:T(8,128)(2,1)S(1)} %get-tuple-element.73), channel_id=1, source_target_pairs={{0,4},{1,5},{2,6},{3,7},{4,0},{5,1},{6,2},{7,3},{8,9},{9,8},{10,11... | collective-permute-start | bytes 393224 | tf_op jit(solution)/shard_map/hop1_chunk0/ppermute | solution.py:514
  8.8 6.4 %collective-permute-start = (bf16[128,512]{1,0:T(8,128)(2,1)S(1)}, bf16[128,512]{1,0:T(8,128)(2,1)S(1)}, u32[]{:S(2)}, u32[]{:S(2)}) collective-permute-start(bf16[128,512]{1,0:T(8,128)(2,1)S(1)} %get-tuple-element.70), channel_id=1, source_target_pairs={{0,4},{1,5},{2,6},{3,7},{4,0},{5,1},{6,2},{7,3},{8,9},{9,8},{10,11... | collective-permute-start | bytes 393224 | tf_op jit(solution)/shard_map/hop1_chunk1/ppermute | solution.py:514
  9.2 6.2 %collective-permute-start.5 = (bf16[128,512]{1,0:T(8,128)(2,1)S(1)}, bf16[128,512]{1,0:T(8,128)(2,1)S(1)}, u32[]{:S(2)}, u32[]{:S(2)}) collective-permute-start(bf16[128,512]{1,0:T(8,128)(2,1)S(1)} %get-tuple-element.84), channel_id=1, source_target_pairs={{0,1},{1,0},{2,3},{3,2},{4,8},{5,9},{6,10},{7,11},{8,4},{9,5},{10,... | collective-permute-start | bytes 393224 | tf_op jit(solution)/shard_map/hop2_chunk0/ppermute | solution.py:514
  9.3 7.3 %collective-permute-start.4 = (bf16[128,512]{1,0:T(8,128)(2,1)S(1)}, bf16[128,512]{1,0:T(8,128)(2,1)S(1)}, u32[]{:S(2)}, u32[]{:S(2)}) collective-permute-start(bf16[128,512]{1,0:T(8,128)(2,1)S(1)} %get-tuple-element.82), channel_id=1, source_target_pairs={{0,4},{1,5},{2,6},{3,7},{4,0},{5,1},{6,2},{7,3},{8,9},{9,8},{10,11... | collective-permute-start | bytes 393224 | tf_op jit(solution)/shard_map/hop1_chunk2/ppermute | solution.py:514
  15.3 1.5 %collective-permute-start.3 = (bf16[128,512]{1,0:T(8,128)(2,1)S(1)}, bf16[128,512]{1,0:T(8,128)(2,1)S(1)}, u32[]{:S(2)}, u32[]{:S(2)}) collective-permute-start(bf16[128,512]{1,0:T(8,128)(2,1)S(1)} %get-tuple-element.81), channel_id=1, source_target_pairs={{0,1},{1,0},{2,3},{3,2},{4,8},{5,9},{6,10},{7,11},{8,4},{9,5},{10,... | collective-permute-start | bytes 393224 | tf_op jit(solution)/shard_map/hop2_chunk1/ppermute | solution.py:514
  15.3 5.9 %collective-permute-start.2 = (bf16[128,512]{1,0:T(8,128)(2,1)S(1)}, bf16[128,512]{1,0:T(8,128)(2,1)S(1)}, u32[]{:S(2)}, u32[]{:S(2)}) collective-permute-start(bf16[128,512]{1,0:T(8,128)(2,1)S(1)} %get-tuple-element.79), channel_id=1, source_target_pairs={{0,4},{1,5},{2,6},{3,7},{4,0},{5,1},{6,2},{7,3},{8,9},{9,8},{10,11... | collective-permute-start | bytes 393224 | tf_op jit(solution)/shard_map/hop1_chunk3/ppermute | solution.py:514
  15.5 5.9 %collective-permute-start.8 = (bf16[128,512]{1,0:T(8,128)(2,1)S(1)}, bf16[128,512]{1,0:T(8,128)(2,1)S(1)}, u32[]{:S(2)}, u32[]{:S(2)}) collective-permute-start(bf16[128,512]{1,0:T(8,128)(2,1)S(1)} %get-tuple-element.92), channel_id=1, source_target_pairs={{0,1},{1,0},{2,3},{3,2},{4,5},{5,4},{6,7},{7,6},{8,12},{9,13},{10,... | collective-permute-start | bytes 393224 | tf_op jit(solution)/shard_map/hop3_chunk0/ppermute | solution.py:514
  16.6 4.7 %collective-permute-start.7 = (bf16[128,512]{1,0:T(8,128)(2,1)S(1)}, bf16[128,512]{1,0:T(8,128)(2,1)S(1)}, u32[]{:S(2)}, u32[]{:S(2)}) collective-permute-start(bf16[128,512]{1,0:T(8,128)(2,1)S(1)} %get-tuple-element.90), channel_id=1, source_target_pairs={{0,1},{1,0},{2,3},{3,2},{4,8},{5,9},{6,10},{7,11},{8,4},{9,5},{10,... | collective-permute-start | bytes 393224 | tf_op jit(solution)/shard_map/hop2_chunk2/ppermute | solution.py:514
  16.8 5.2 %collective-permute-start.9 = (bf16[128,512]{1,0:T(8,128)(2,1)S(1)}, bf16[128,512]{1,0:T(8,128)(2,1)S(1)}, u32[]{:S(2)}, u32[]{:S(2)}) collective-permute-start(bf16[128,512]{1,0:T(8,128)(2,1)S(1)} %get-tuple-element.94), channel_id=1, source_target_pairs={{0,1},{1,0},{2,3},{3,2},{4,5},{5,4},{6,7},{7,6},{8,12},{9,13},{10,... | collective-permute-start | bytes 393224 | tf_op jit(solution)/shard_map/hop3_chunk1/ppermute | solution.py:514
  21.3 1.4 %collective-permute-start.6 = (bf16[128,512]{1,0:T(8,128)(2,1)S(1)}, bf16[128,512]{1,0:T(8,128)(2,1)S(1)}, u32[]{:S(2)}, u32[]{:S(2)}) collective-permute-start(bf16[128,512]{1,0:T(8,128)(2,1)S(1)} %get-tuple-element.89.refs_1_), channel_id=1, source_target_pairs={{0,1},{1,0},{2,3},{3,2},{4,8},{5,9},{6,10},{7,11},{8,4},{9,5},{10,... | collective-permute-start | bytes 393224 | tf_op jit(solution)/shard_map/hop2_chunk3/ppermute | solution.py:514
  21.4 22.5 %collective-permute-start.10 = (bf16[128,512]{1,0:T(8,128)(2,1)S(1)}, bf16[128,512]{1,0:T(8,128)(2,1)S(1)}, u32[]{:S(2)}, u32[]{:S(2)}) collective-permute-start(bf16[128,512]{1,0:T(8,128)(2,1)S(1)} %get-tuple-element.95.refs_1_), channel_id=1, source_target_pairs={{0,1},{1,0},{2,3},{3,2},{4,5},{5,4},{6,7},{7,6},{8,12},{9,13},{10,... | collective-permute-start | bytes 393224 | tf_op jit(solution)/shard_map/hop3_chunk2/ppermute | solution.py:514
  22.7 0.7 %copy-start = (bf16[1,4,4,256]{3,2,1,0:T(4,128)(2,1)S(1)}, bf16[1,4,4,256]{3,2,1,0:T(4,128)(2,1)}, u32[]{:S(2)}) copy-start(bf16[1,4,4,256]{3,2,1,0:T(4,128)(2,1)} %param.22) | copy-start | bytes 24580
  22.7 21.9 %collective-permute-start.11 = (bf16[128,512]{1,0:T(8,128)(2,1)S(1)}, bf16[128,512]{1,0:T(8,128)(2,1)S(1)}, u32[]{:S(2)}, u32[]{:S(2)}) collective-permute-start(bf16[128,512]{1,0:T(8,128)(2,1)S(1)} %get-tuple-element.97.rest_0_), channel_id=1, source_target_pairs={{0,1},{1,0},{2,3},{3,2},{4,5},{5,4},{6,7},{7,6},{8,12},{9,13},{10,... | collective-permute-start | bytes 393224 | tf_op jit(solution)/shard_map/hop3_chunk3/ppermute | solution.py:514
  39.4 4.7 %collective-permute-start.12 = (bf16[4,2048]{1,0:T(4,128)(2,1)S(1)}, bf16[4,2048]{1,0:T(4,128)(2,1)S(1)}, u32[]{:S(2)}, u32[]{:S(2)}) collective-permute-start(bf16[4,2048]{1,0:T(4,128)(2,1)S(1)} %get-tuple-element.103.rest_4_), channel_id=1, source_target_pairs={{0,8},{1,9},{2,10},{3,11},{4,5},{5,4},{6,7},{7,6},{8,0},{9,1},{10,... | collective-permute-start | bytes 49160 | tf_op jit(solution)/shard_map/ppermute | solution.py:514
  40.0 4.1 %collective-permute-start.13 = (bf16[4,2048]{1,0:T(4,128)(2,1)S(1)}, bf16[4,2048]{1,0:T(4,128)(2,1)S(1)}, u32[]{:S(2)}, u32[]{:S(2)}) collective-permute-start(bf16[4,2048]{1,0:T(4,128)(2,1)S(1)} %get-tuple-element.113), channel_id=1, source_target_pairs={{0,1},{1,0},{2,3},{3,2},{4,8},{5,9},{6,10},{7,11},{8,4},{9,5},{10,... | collective-permute-start | bytes 49160 | tf_op jit(solution)/shard_map/ppermute | solution.py:514
  40.0 4.6 %collective-permute-start.14 = (bf16[4,2048]{1,0:T(4,128)(2,1)S(1)}, bf16[4,2048]{1,0:T(4,128)(2,1)S(1)}, u32[]{:S(2)}, u32[]{:S(2)}) collective-permute-start(bf16[4,2048]{1,0:T(4,128)(2,1)S(1)} %get-tuple-element.114), channel_id=1, source_target_pairs={{0,4},{1,5},{2,6},{3,7},{4,0},{5,1},{6,2},{7,3},{8,9},{9,8},{10,11... | collective-permute-start | bytes 49160 | tf_op jit(solution)/shard_map/ppermute | solution.py:514
  45.0 5.7 %collective-permute-start.15 = (bf16[4,2048]{1,0:T(4,128)(2,1)S(1)}, bf16[4,2048]{1,0:T(4,128)(2,1)S(1)}, u32[]{:S(2)}, u32[]{:S(2)}) collective-permute-start(bf16[4,2048]{1,0:T(4,128)(2,1)S(1)} %get-tuple-element.115), channel_id=1, source_target_pairs={{0,12},{1,13},{2,14},{3,15},{4,5},{5,4},{6,7},{7,6},{8,9},{9,8},{1... | collective-permute-start | bytes 49160 | tf_op jit(solution)/shard_map/ppermute | solution.py:514
  45.0 5.6 %collective-permute-start.16 = (bf16[4,2048]{1,0:T(4,128)(2,1)S(1)}, bf16[4,2048]{1,0:T(4,128)(2,1)S(1)}, u32[]{:S(2)}, u32[]{:S(2)}) collective-permute-start(bf16[4,2048]{1,0:T(4,128)(2,1)S(1)} %get-tuple-element.116), channel_id=1, source_target_pairs={{0,1},{1,0},{2,3},{3,2},{4,12},{5,13},{6,14},{7,15},{8,9},{9,8},{1... | collective-permute-start | bytes 49160 | tf_op jit(solution)/shard_map/ppermute | solution.py:514
  45.1 5.5 %collective-permute-start.17 = (bf16[4,2048]{1,0:T(4,128)(2,1)S(1)}, bf16[4,2048]{1,0:T(4,128)(2,1)S(1)}, u32[]{:S(2)}, u32[]{:S(2)}) collective-permute-start(bf16[4,2048]{1,0:T(4,128)(2,1)S(1)} %get-tuple-element.117), channel_id=1, source_target_pairs={{0,1},{1,0},{2,3},{3,2},{4,5},{5,4},{6,7},{7,6},{8,12},{9,13},{10,... | collective-permute-start | bytes 49160 | tf_op jit(solution)/shard_map/ppermute | solution.py:514

commit v10 on v9

--- a/solution.py
+++ b/solution.py
@@ -19,6 +19,7 @@
 BF16 = jnp.bfloat16
 CHUNKS = 4
 TOKEN_COST = 5 * 10**8
+PASS_COST = 5 * 10**8
 VMEM_LIMIT = 32 * 1024 * 1024
 
 
@@ -148,13 +149,16 @@
         copy.wait()
 
 
-def state_kernel(part, x_ref, turned_ref, weight_ref, whole_ref, *rest):
+def state_kernel(part, x_ref, turned_ref, weight_ref, whole_ref, asked_ref, *rest):
     results = rest[-2 * len(part) - 1 :]
     for i, k in enumerate(part):
         total_ref, decay_ref = results[2 * i : 2 * i + 2]
         g = k * total_ref.shape[1] // (H // G * P_SIZE)
         chunk_total(k, x_ref, turned_ref[g], weight_ref[...], whole_ref[...], total_ref, decay_ref)
-    results[-1][...] = results[0][...].astype(BF16)
+    results[-1][:N] = results[0][...].astype(BF16)
+    if results[-1].shape[0] > N:
+        own = flat(asked_ref).astype(BF16)
+        results[-1][N:] = jnp.concatenate([own, own], axis=1)
 
 
 def flat(ref):
@@ -167,15 +171,24 @@
 
 def pass_kernel(hop, k, more, got_ref, total_ref, decay_ref, *rest):
     moving_ref, carry_ref = rest[len(rest) - 2 - more : len(rest) - more]
+    me = lax.axis_index("seq")
     if hop == 1 and k == 0:
         following_ref = rest[0]
         carry_ref[...] = jnp.zeros_like(carry_ref)
     else:
         following_ref = rest[1]
-    got = got_ref[...]
-    moving_ref[...] = (total_ref[...] + decay_ref[...] * got.astype(F32)).astype(BF16)
-
-    @pl.when(lax.axis_index("seq") == hop)
+    got = got_ref[:N]
+    moving_ref[:N] = (total_ref[...] + decay_ref[...] * got.astype(F32)).astype(BF16)
+    if got_ref.shape[0] > N:
+        tail = got_ref[N:]
+        if hop == 1:
+            own = rest[1 + more][N:].astype(F32)
+            lane = lax.broadcasted_iota(jnp.int32, own.shape, 1)
+            mine = (lane // (own.shape[1] // 2)) == lax.rem(me, 2)
+            tail = jnp.where(mine, own, tail.astype(F32)).astype(BF16)
+        moving_ref[N:] = tail
+
+    @pl.when(me == hop)
     def _():
         carry_ref[k] = got
 
@@ -243,7 +256,7 @@
             inner_ref[mine, here] = dot(left, right) + skip * x_part[mine].astype(F32)
 
 
-def ask_kernel(x_ref, b_ref, cum_ref, row_ref, len_ref, owner_ref, asked_here_ref, *rest):
+def ask_kernel(ride, x_ref, b_ref, cum_ref, row_ref, len_ref, owner_ref, *rest):
     local_ref, gain_ref, asked_ref = rest[-3:]
     heads, tokens = cum_ref.shape
     spans = tokens // SPAN
@@ -251,8 +264,20 @@
     per_group = H // G
     groups = heads // per_group
     me = lax.axis_index("seq")
-    blocks = [asked_here_ref[r, me].astype(F32) for r in range(asks // STEPS)]
-    asked = jnp.concatenate(blocks, axis=0).astype(BF16)
+    if ride:
+        near, middle, far = [ref[N:].astype(F32) for ref in rest[:3]]
+        far = jnp.where((me == 1) | (me == 2), middle, far)
+        halves = (jnp.where(me < 2, near, far), jnp.where(me < 2, far, near))
+        names = near.shape[1] // 2
+        blocks = [half[:, i * names : (i + 1) * names] for half in halves for i in range(2)]
+        blocks = jnp.concatenate(blocks, axis=0).astype(BF16)
+        row = lax.broadcasted_iota(jnp.int32, (asks, blocks.shape[0]), 0)
+        column = lax.broadcasted_iota(jnp.int32, (asks, blocks.shape[0]), 1)
+        wanted = row // STEPS * asks + me * STEPS + row % STEPS
+        asked = dot(jnp.where(column == wanted, 1.0, 0.0).astype(BF16), blocks).astype(BF16)
+    else:
+        blocks = [rest[0][r, me].astype(F32) for r in range(asks // STEPS)]
+        asked = jnp.concatenate(blocks, axis=0).astype(BF16)
     asked_ref[...] = asked
     block = lax.broadcasted_iota(jnp.int32, (asks, 1), 0) // STEPS
     spot = len_ref[...] - 1 - me * tokens
@@ -303,7 +328,7 @@
         g = first // (H // G * P_SIZE)
         state = carry_ref[k]
         if final:
-            state = jnp.where(me == count - 1, got_refs[k][...], state)
+            state = jnp.where(me == count - 1, got_refs[k][:N], state)
         carried = dot(asked_ref[:, g * N : (g + 1) * N], state)
         reading = local_ref[:, here] + over_lanes(gain_ref[...], first, width) * carried
         parts = [reading[r * STEPS : (r + 1) * STEPS] for r in range(count)]
@@ -357,7 +382,7 @@
     for i, k in enumerate(part):
         first = k * width
         g = first // group_lanes
-        state = jnp.where(last, got_refs[i][...], carry_ref[k])
+        state = jnp.where(last, got_refs[i][:N], carry_ref[k])
         carried = dot(c_ref[:, g * N : (g + 1) * N], state)
         inner = inner_refs[g][:, first - g * group_lanes : first - g * group_lanes + width]
         out_ref[i] = (inner + over_lanes(gain, first, width) * carried).astype(BF16)
@@ -453,7 +478,11 @@
     anywhere = pl.BlockSpec(memory_space=pl.ANY)
     in_hbm = pl.BlockSpec(memory_space=pltpu.HBM)
     in_vmem = pl.BlockSpec(memory_space=pltpu.VMEM)
-    sent_shape = shape((N, width), BF16)
+    ride = count == 4 and width == 2 * names
+
+    def sent_shape(k):
+        return shape((N + rows * (ride and k == 1), width), BF16)
+
     inputs = [
         ssm_input,
         bmat,
@@ -479,7 +508,7 @@
             shape((groups, N, tokens), BF16),
         )
         + chunk_shapes
-        + (sent_shape,),
+        + (sent_shape(0),),
         in_specs=[in_hbm] * (len(inputs) + 1),
         scratch_shapes=[
             pltpu.VMEM((heads, tokens), BF16),
@@ -489,15 +518,15 @@
     x, b, a_row, asked_here, c, d_row, len_row, owner_row, x_dec, b_dec, dt_dec = results[:11]
     cum, row, weight, whole, turned = results[11:16]
     total, decay = [results[16]], [results[17]]
-    all_asked = lax.all_gather(dec_c[0], "seq")
+    all_asked = None if ride else lax.all_gather(dec_c[0], "seq")
     sent = {0: results[18]}
 
     def state_part(part, tie):
         out = call(
             functools.partial(state_kernel, part),
-            chunk_shapes * len(part) + (sent_shape,),
-            in_specs=[in_vmem] * 4 + [anywhere],
-        )(x, turned, weight, whole, tie)
+            chunk_shapes * len(part) + (sent_shape(1),),
+            in_specs=[in_vmem] * 5 + [anywhere],
+        )(x, turned, weight, whole, asked_here, tie)
         total.extend(out[0 : 2 * len(part) : 2])
         decay.extend(out[1 : 2 * len(part) : 2])
         return out[-1]
@@ -515,7 +544,8 @@
 
     def forward(value, hop, k):
         with jax.named_scope(f"hop{hop}_chunk{k}"):
-            return swap(value, (hop - 1, hop))
+            rides = ride and k == 1 and hop != 2
+            return swap(value, *([(0, 1), (2, 3)] if rides else [(hop - 1, hop)]))
 
     def shift(value, by):
         return lax.ppermute(value, "seq", [(d, (d + by) % count) for d in range(count)])
@@ -528,11 +558,12 @@
         )(x, b, c, cum, row, d_row, *after)
 
     def ask_part(*after):
+        blocks = (moving[2, 1], got[2, 1], got[3, 1]) if ride else (all_asked,)
         return call(
-            ask_kernel,
+            functools.partial(ask_kernel, ride),
             (shape((rows, lanes)), shape((rows, heads)), shape((rows, names), BF16)),
-            in_specs=[in_vmem] * 7 + [anywhere] * len(after),
-        )(x, b, cum, row, len_row, owner_row, all_asked, *after)
+            in_specs=[in_vmem] * (6 + len(blocks)) + [anywhere] * len(after),
+        )(x, b, cum, row, len_row, owner_row, *blocks, *after)
 
     def token(*after, flops=1):
         return call(
@@ -574,21 +605,24 @@
     sent[1] = state_part(list(range(1, chunks)), inner[-1])
     got[1, 1] = forward(sent[1], 1, 1)
     order = sorted((k + hop, hop, k) for hop in range(1, count - 1) for k in range(chunks))
+    moving = {}
     carry = tie = None
     for _, hop, k in order:
         more = hop == 1 and k + 2 < chunks
         operands = [got[hop, k], total[k], decay[k]]
         operands += [] if carry is None else [carry]
-        operands += total[k + 2 : k + 3] * more
+        operands += total[k + 2 : k + 3] * more + [sent[1]] * (ride and (hop, k) == (1, 1))
         after = []
         if hop == count - 2 and k > 1:
             after = [token(got[hop + 1, k - 2], tie, flops=TOKEN_COST)]
         tie, carry, *following = call(
             functools.partial(pass_kernel, hop, k, more),
-            (sent_shape, shape((chunks, N, width), BF16)) + (sent_shape,) * more,
+            (sent_shape(k), shape((chunks, N, width), BF16)) + (sent_shape(k + 2),) * more,
+            flops=PASS_COST if k % 2 == 0 else 1,
             in_specs=[in_vmem] * len(operands) + [anywhere] * len(after),
             input_output_aliases={} if carry is None else {3: 1},
         )(*operands, *after)
+        moving[hop + 1, k] = tie
         got[hop + 1, k] = forward(tie, hop + 1, k)
         if more:
             got[1, k + 2] = forward(following[0], 1, k + 2)

time: 51.7 us -> 42.3 us (0.82)
  blocking collectives: 14.8 us -> 0 us
  starting transfers between devices: 11.3 us -> 17.3 us
    all_gather x1 -> x0, blocking collectives: 14.8 us -> none  [shards(): all_asked = lax.all_gather(dec_c[0], 'seq')]
    ppermute x18, starting transfers between devices: 11.3 us -> 17.3 us  [swap(): return lax.ppermute(value, ('seq', 'tp'), pairs)]
  transfers between devices with their start and end apart: 18 -> 18, of which waited for: 8 -> 7; matrix products, arithmetic and copies ran while one was open for 0% -> 0% of each run, Pallas kernels for 14% -> 17%
where the time goes in v10:
time: 42.3 us; the launch traced here: 42.1 us
  starting transfers between devices  17.3 us (41%)
  waiting for transfers between devices  14 us (33%)
  Pallas kernels  9.97 us (24%)
  between operations  0.85 us (2%)
    ppermute x18, starting transfers between devices, swap(): return lax.ppermute(value, ('seq', 'tp'), pairs)  17.3 us
    ppermute x18, waiting for transfers between devices, swap(): return lax.ppermute(value, ('seq', 'tp'), pairs)  14 us
    pallas_call x2, Pallas kernels, inner_part(): call(functools.partial(inner_kernel, g), shape((tokens, group_lanes)), in...  2.05 us
    pallas_call x2, Pallas kernels, outer_part(): call(functools.partial(outer_kernel, parts, count), (pltpu.HBM((tokens, l...  1.95 us
    pallas_call x1, Pallas kernels, shards(): call(functools.partial(first_kernel, len(inputs)), tuple((shape(value.sha...  1.9 us
    pallas_call x1, Pallas kernels, state_part(): call(functools.partial(state_kernel, part), chunk_shapes * len(part) + (s...  1.1 us
    pallas_call x1, Pallas kernels, ask_part(): call(functools.partial(ask_kernel, ride), (shape((rows, lanes)), shape((r...  0.89 us
  transfers between devices with their start and end apart: 18, of which 7 were waited for; matrix products, arithmetic and copies ran while one was open for 0% of the time, Pallas kernels for 17%

profile of v10, /device:TPU:0, one launch (start us, length us, event | category | flops | bytes accessed | tf_op | source)
XLA Modules:
  0.0 42.1 jit_solution(11068534217296583243)
XLA Ops:
  0.6 1.9 %first_kernel.1 = (bf16[256,2048]{1,0:T(8,128)(2,1)S(1)}, bf16[256,256]{1,0:T(8,128)(2,1)S(1)}, f32[1,32]{1,0:T(1,128)S(1)}, bf16[4,4,256]{2,1,0:T(4,128)(2,1)S(...) custom-call(bf16[256,2048]{1,0:T(8,128)(2,1)} %refs_0_.1, ...), custom_call_target="tpu_custom_call" | custom-call | flops 1 | bytes 1 | tf_op jit(solution)/shard_map/first_kernel/pallas_call | solution.py:500
  2.5 3.1 %collective-permute-start.1 = (bf16[128,512]{1,0:T(8,128)(2,1)S(1)}, bf16[128,512]{1,0:T(8,128)(2,1)S(1)}, u32[]{:S(2)}, u32[]{:S(2)}) collective-permute-start(bf16[128,512]{1,0:T(8,128)(2,1)S(1)} %get-tuple-element.74), channel_id=1, source_target_pairs={{0,4},{1,5},{2,6},{3,7},{4,0},{5,1},{6,2},{7,3},{8,9},{9,8},{10,11... | collective-permute-start | bytes 393224 | tf_op jit(solution)/shard_map/hop1_chunk0/ppermute | solution.py:543
  5.6 1.0 %inner_kernel.2.rest_0_.rest_2_ = f32[256,1024]{1,0:T(8,128)S(1)} custom-call(bf16[256,2048]{1,0:T(8,128)(2,1)S(1)} %get-tuple-element.63.x_ref, bf16[256,256]{1,0:T(8,128)(2,1)S(1)} %get-tuple-element.68.b_ref, bf16[256,256]{1,0:T(8,128)(2,1)S(1)} %get-tuple-element.61.c_ref, f32[32,256]{1,0:T(8,128)S(1)} %get-tuple-element.62.cum_ref, ...), custom_call_target="tpu_custom_call" | custom-call | flops 1 | bytes 1 | tf_op jit(solution)/shard_map/inner_kernel/pallas_call | solution.py:554
  6.7 1.0 %inner_kernel.3.rest_0_.rest_3_ = f32[256,1024]{1,0:T(8,128)S(1)} custom-call(bf16[256,2048]{1,0:T(8,128)(2,1)S(1)} %get-tuple-element.63.x_ref, bf16[256,256]{1,0:T(8,128)(2,1)S(1)} %get-tuple-element.68.b_ref, bf16[256,256]{1,0:T(8,128)(2,1)S(1)} %get-tuple-element.61.c_ref, f32[32,256]{1,0:T(8,128)S(1)} %get-tuple-element.62.cum_ref, ...), custom_call_target="tpu_custom_call" | custom-call | flops 1 | bytes 1 | tf_op jit(solution)/shard_map/inner_kernel/pallas_call | solution.py:554
  7.7 1.1 %state_kernel.1 = (f32[128,512]{1,0:T(8,128)S(1)}, f32[1,512]{1,0:T(1,128)S(1)}, f32[128,512]{1,0:T(8,128)S(1)}, f32[1,512]{1,0:T(1,128)S(1)}, f32[128,512]{1,0:...) custom-call(bf16[256,2048]{1,0:T(8,128)(2,1)S(1)} %get-tuple-element.63.x_ref, ...), custom_call_target="tpu_custom_call" | custom-call | flops 1 | bytes 1 | tf_op jit(solution)/shard_map/state_kernel/pallas_call | solution.py:525
  8.8 0.1 collective-permute-start
  8.8 0.3 collective-permute-done.1.got_ref
  9.1 0.1 pass_kernel.8
  9.2 0.1 collective-permute-start.5
  9.3 2.9 %collective-permute-start.4 = (bf16[128,512]{1,0:T(8,128)(2,1)S(1)}, bf16[128,512]{1,0:T(8,128)(2,1)S(1)}, u32[]{:S(2)}, u32[]{:S(2)}) collective-permute-start(bf16[128,512]{1,0:T(8,128)(2,1)S(1)} %get-tuple-element.83), channel_id=1, source_target_pairs={{0,4},{1,5},{2,6},{3,7},{4,0},{5,1},{6,2},{7,3},{8,9},{9,8},{10,11... | collective-permute-start | bytes 393224 | tf_op jit(solution)/shard_map/hop1_chunk2/ppermute | solution.py:543
  12.1 3.3 %collective-permute-done.got_ref = bf16[144,512]{1,0:T(8,128)(2,1)S(1)} collective-permute-done((bf16[144,512]{1,0:T(8,128)(2,1)S(1)}, bf16[144,512]{1,0:T(8,128)(2,1)S(1)}, u32[]{:S(2)}, u32[]{:S(2)}) %collective-permute-start) | collective-permute-done | bytes 147488 | tf_op jit(solution)/shard_map/hop1_chunk1/ppermute | solution.py:543
  15.4 0.1 pass_kernel.9
  15.5 0.1 collective-permute-start.3
  15.5 1.2 %collective-permute-start.2 = (bf16[128,512]{1,0:T(8,128)(2,1)S(1)}, bf16[128,512]{1,0:T(8,128)(2,1)S(1)}, u32[]{:S(2)}, u32[]{:S(2)}) collective-permute-start(bf16[128,512]{1,0:T(8,128)(2,1)S(1)} %get-tuple-element.80), channel_id=1, source_target_pairs={{0,4},{1,5},{2,6},{3,7},{4,0},{5,1},{6,2},{7,3},{8,9},{9,8},{10,11... | collective-permute-start | bytes 393224 | tf_op jit(solution)/shard_map/hop1_chunk3/ppermute | solution.py:543
  16.8 0.0 collective-permute-done.5.got_ref
  16.8 0.1 collective-permute-start.8
  16.9 0.0 collective-permute-done.4.got_ref
  17.0 0.5 %collective-permute-start.7 = (bf16[128,512]{1,0:T(8,128)(2,1)S(1)}, bf16[128,512]{1,0:T(8,128)(2,1)S(1)}, u32[]{:S(2)}, u32[]{:S(2)}) collective-permute-start(bf16[128,512]{1,0:T(8,128)(2,1)S(1)} %get-tuple-element.91), channel_id=1, source_target_pairs={{0,1},{1,0},{2,3},{3,2},{4,8},{5,9},{6,10},{7,11},{8,4},{9,5},{10,... | collective-permute-start | bytes 393224 | tf_op jit(solution)/shard_map/hop2_chunk2/ppermute | solution.py:543
  17.5 0.0 collective-permute-done.3.got_ref.rest_1_
  17.6 3.1 %collective-permute-start.9 = (bf16[144,512]{1,0:T(8,128)(2,1)S(1)}, bf16[144,512]{1,0:T(8,128)(2,1)S(1)}, u32[]{:S(2)}, u32[]{:S(2)}) collective-permute-start(bf16[144,512]{1,0:T(8,128)(2,1)S(1)} %get-tuple-element.95), channel_id=1, source_target_pairs={{0,4},{1,5},{2,6},{3,7},{4,0},{5,1},{6,2},{7,3},{8,12},{9,13},{10,... | collective-permute-start | bytes 442376 | tf_op jit(solution)/shard_map/hop3_chunk1/ppermute | solution.py:543
  20.6 1.3 %collective-permute-done.2.got_ref = bf16[128,512]{1,0:T(8,128)(2,1)S(1)} collective-permute-done((bf16[128,512]{1,0:T(8,128)(2,1)S(1)}, bf16[128,512]{1,0:T(8,128)(2,1)S(1)}, u32[]{:S(2)}, u32[]{:S(2)}) %collective-permute-start.2) | collective-permute-done | bytes 131104 | tf_op jit(solution)/shard_map/hop1_chunk3/ppermute | solution.py:543
  22.0 0.1 collective-permute-start.6
  22.0 0.0 collective-permute-done.8.refs_0_.rest_0_
  22.1 0.0 collective-permute-done.7.got_ref
  22.1 0.5 %collective-permute-start.10 = (bf16[128,512]{1,0:T(8,128)(2,1)S(1)}, bf16[128,512]{1,0:T(8,128)(2,1)S(1)}, u32[]{:S(2)}, u32[]{:S(2)}) collective-permute-start(bf16[128,512]{1,0:T(8,128)(2,1)S(1)} %get-tuple-element.96.refs_1_), channel_id=1, source_target_pairs={{0,1},{1,0},{2,3},{3,2},{4,5},{5,4},{6,7},{7,6},{8,12},{9,13},{10,... | collective-permute-start | bytes 393224 | tf_op jit(solution)/shard_map/hop3_chunk2/ppermute | solution.py:543
  22.6 2.0 %collective-permute-done.9.refs_0_.rest_2_.rest_1_ = bf16[144,512]{1,0:T(8,128)(2,1)S(1)} collective-permute-done((bf16[144,512]{1,0:T(8,128)(2,1)S(1)}, bf16[144,512]{1,0:T(8,128)(2,1)S(1)}, u32[]{:S(2)}, u32[]{:S(2)}) %collective-permute-start.9) | collective-permute-done | bytes 147488 | tf_op jit(solution)/shard_map/hop3_chunk1/ppermute | solution.py:543
  24.6 0.0 collective-permute-done.6.got_ref
  24.7 0.1 collective-permute-start.11
  24.7 0.9 %ask_kernel.1 = (f32[16,2048]{1,0:T(8,128)S(1)}, f32[16,32]{1,0:T(8,128)S(1)}, bf16[16,256]{1,0:T(8,128)(2,1)S(1)}) custom-call(bf16[256,2048]{1,0:T(8,128)(2,1)S(1)} %get-tuple-element.63.x_ref, bf16[256,256]{1,0:T(8,128)(2,1)S(1)} %get-tuple-element.68.b_ref, f32[32,256]{1,0:T(8,128)S(1)} %get-tuple-element.62.cum_ref, ...), custom_call_target="tpu_custom_call" | custom-call | flops 1 | bytes 1 | tf_op jit(solution)/shard_map/ask_kernel/pallas_call | solution.py:562
  25.6 0.3 read_kernel.2
  25.9 0.6 %collective-permute-start.13 = (bf16[4,2048]{1,0:T(4,128)(2,1)S(1)}, bf16[4,2048]{1,0:T(4,128)(2,1)S(1)}, u32[]{:S(2)}, u32[]{:S(2)}) collective-permute-start(bf16[4,2048]{1,0:T(4,128)(2,1)S(1)} %get-tuple-element.113), channel_id=1, source_target_pairs={{0,1},{1,0},{2,3},{3,2},{4,8},{5,9},{6,10},{7,11},{8,4},{9,5},{10,... | collective-permute-start | bytes 49160 | tf_op jit(solution)/shard_map/ppermute | solution.py:543
  26.5 4.3 %collective-permute-start.14 = (bf16[4,2048]{1,0:T(4,128)(2,1)S(1)}, bf16[4,2048]{1,0:T(4,128)(2,1)S(1)}, u32[]{:S(2)}, u32[]{:S(2)}) collective-permute-start(bf16[4,2048]{1,0:T(4,128)(2,1)S(1)} %get-tuple-element.114), channel_id=1, source_target_pairs={{0,4},{1,5},{2,6},{3,7},{4,0},{5,1},{6,2},{7,3},{8,9},{9,8},{10,11... | collective-permute-start | bytes 49160 | tf_op jit(solution)/shard_map/ppermute | solution.py:543
  30.8 0.0 collective-permute-start.12
  30.8 0.6 %outer_kernel.2.rest_4_.rest_0_ = bf16[2,256,512]{2,1,0:T(8,128)(2,1)S(1)} custom-call(bf16[256,256]{1,0:T(8,128)(2,1)S(1)} %get-tuple-element.61.c_ref, f32[32,256]{1,0:T(8,128)S(1)} %get-tuple-element.62.cum_ref, bf16[4,128,512]{2,1,0:T(8,128)(2,1)S(1)} %get-tuple-element.97.carry_ref, bf16[128,512]{1,0:T(8,128)(2,1)S(1)} %collective-permute-done.8.refs_0_.rest_0_, ...), custom_call_target="tpu_custom_call" | custom-call | flops 1 | bytes 1 | tf_op jit(solution)/shard_map/outer_kernel/pallas_call | solution.py:584
  31.4 0.4 fresh_kernel.1
  31.9 0.0 collective-permute-done.10.rest_0_.refs_0_.rest_2_
  31.9 0.0 collective-permute-done.13.rest_6_.rest_1_
  31.9 0.6 %collective-permute-done.14.rest_7_.rest_2_ = bf16[4,2048]{1,0:T(4,128)(2,1)S(1)} collective-permute-done((bf16[4,2048]{1,0:T(4,128)(2,1)S(1)}, bf16[4,2048]{1,0:T(4,128)(2,1)S(1)}, u32[]{:S(2)}, u32[]{:S(2)}) %collective-permute-start.14) | collective-permute-done | bytes 16416 | tf_op jit(solution)/shard_map/ppermute | solution.py:543
  32.5 2.9 %collective-permute-done.12.rest_5_.rest_0_ = bf16[4,2048]{1,0:T(4,128)(2,1)S(1)} collective-permute-done((bf16[4,2048]{1,0:T(4,128)(2,1)S(1)}, bf16[4,2048]{1,0:T(4,128)(2,1)S(1)}, u32[]{:S(2)}, u32[]{:S(2)}) %collective-permute-start.12) | collective-permute-done | bytes 16416 | tf_op jit(solution)/shard_map/ppermute | solution.py:543
  35.4 0.0 collective-permute-done.11.rest_1_.rest_3_
  35.5 0.3 read_kernel.3
  35.7 0.1 collective-permute-start.15
  35.8 0.1 collective-permute-start.16
  35.9 0.5 %collective-permute-start.17 = (bf16[4,2048]{1,0:T(4,128)(2,1)S(1)}, bf16[4,2048]{1,0:T(4,128)(2,1)S(1)}, u32[]{:S(2)}, u32[]{:S(2)}) collective-permute-start(bf16[4,2048]{1,0:T(4,128)(2,1)S(1)} %get-tuple-element.117), channel_id=1, source_target_pairs={{0,1},{1,0},{2,3},{3,2},{4,5},{5,4},{6,7},{7,6},{8,12},{9,13},{10,... | collective-permute-start | bytes 49160 | tf_op jit(solution)/shard_map/ppermute | solution.py:543
  36.4 1.3 %outer_kernel.3 = (bf16[256,2048]{1,0:T(8,128)(2,1)}, f32[8,128]{1,0:T(8,128)S(1)}) custom-call(bf16[256,256]{1,0:T(8,128)(2,1)S(1)} %get-tuple-element.61.c_ref, f32[32,256]{1,0:T(8,128)S(1)} %get-tuple-element.62.cum_ref, bf16[4,128,512]{2,1,0:T(8,128)(2,1)S(1)} %get-tuple-element.97.carry_ref, ...), custom_call_target="tpu_custom_call" | custom-call | flops 1 | bytes 1 | tf_op jit(solution)/shard_map/outer_kernel/pallas_call | solution.py:584
  37.8 3.6 %collective-permute-done.15.rest_3_ = bf16[4,2048]{1,0:T(4,128)(2,1)S(1)} collective-permute-done((bf16[4,2048]{1,0:T(4,128)(2,1)S(1)}, bf16[4,2048]{1,0:T(4,128)(2,1)S(1)}, u32[]{:S(2)}, u32[]{:S(2)}) %collective-permute-start.15) | collective-permute-done | bytes 16416 | tf_op jit(solution)/shard_map/ppermute | solution.py:543
  41.4 0.0 collective-permute-done.16.rest_4_
  41.4 0.0 collective-permute-done.17.rest_5_
  41.4 0.7 %finish_kernel.1 = bf16[4,4,2048]{2,1,0:T(4,128)(2,1)} custom-call(f32[4,4,2048]{2,1,0:T(4,128)S(1)} %get-tuple-element.110.refs_1_.keep_ref, f32[4,4,2048]{2,1,0:T(4,128)S(1)} %get-tuple-element.111.fresh_ref, f32[4,4,128]{2,1,0:T(4,128)S(1)} %get-tuple-element.112.held_ref, bf16[4,2048]{1,0:T(4,128)(2,1)S(1)} %collective-permute-done.12.rest_5_.rest_0_, ...), custom_call_target="tpu_custom_call" | custom-call | flops 1 | bytes 1 | tf_op jit(solution)/shard_map/finish_kernel/pallas_call | solution.py:648
  (9 shorter events, 0.2 us)
Async XLA Ops:
  2.5 6.6 %collective-permute-start.1 = (bf16[128,512]{1,0:T(8,128)(2,1)S(1)}, bf16[128,512]{1,0:T(8,128)(2,1)S(1)}, u32[]{:S(2)}, u32[]{:S(2)}) collective-permute-start(bf16[128,512]{1,0:T(8,128)(2,1)S(1)} %get-tuple-element.74), channel_id=1, source_target_pairs={{0,4},{1,5},{2,6},{3,7},{4,0},{5,1},{6,2},{7,3},{8,9},{9,8},{10,11... | collective-permute-start | bytes 393224 | tf_op jit(solution)/shard_map/hop1_chunk0/ppermute | solution.py:543
  8.8 6.6 %collective-permute-start = (bf16[144,512]{1,0:T(8,128)(2,1)S(1)}, bf16[144,512]{1,0:T(8,128)(2,1)S(1)}, u32[]{:S(2)}, u32[]{:S(2)}) collective-permute-start(bf16[144,512]{1,0:T(8,128)(2,1)S(1)} %get-tuple-element.71.rest_2_), channel_id=1, source_target_pairs={{0,4},{1,5},{2,6},{3,7},{4,0},{5,1},{6,2},{7,3},{8,12},{9,13},{10,... | collective-permute-start | bytes 442376 | tf_op jit(solution)/shard_map/hop1_chunk1/ppermute | solution.py:543
  9.2 7.6 %collective-permute-start.5 = (bf16[128,512]{1,0:T(8,128)(2,1)S(1)}, bf16[128,512]{1,0:T(8,128)(2,1)S(1)}, u32[]{:S(2)}, u32[]{:S(2)}) collective-permute-start(bf16[128,512]{1,0:T(8,128)(2,1)S(1)} %get-tuple-element.85), channel_id=1, source_target_pairs={{0,1},{1,0},{2,3},{3,2},{4,8},{5,9},{6,10},{7,11},{8,4},{9,5},{10,... | collective-permute-start | bytes 393224 | tf_op jit(solution)/shard_map/hop2_chunk0/ppermute | solution.py:543
  9.3 7.7 %collective-permute-start.4 = (bf16[128,512]{1,0:T(8,128)(2,1)S(1)}, bf16[128,512]{1,0:T(8,128)(2,1)S(1)}, u32[]{:S(2)}, u32[]{:S(2)}) collective-permute-start(bf16[128,512]{1,0:T(8,128)(2,1)S(1)} %get-tuple-element.83), channel_id=1, source_target_pairs={{0,4},{1,5},{2,6},{3,7},{4,0},{5,1},{6,2},{7,3},{8,9},{9,8},{10,11... | collective-permute-start | bytes 393224 | tf_op jit(solution)/shard_map/hop1_chunk2/ppermute | solution.py:543
  15.5 2.1 %collective-permute-start.3 = (bf16[144,512]{1,0:T(8,128)(2,1)S(1)}, bf16[144,512]{1,0:T(8,128)(2,1)S(1)}, u32[]{:S(2)}, u32[]{:S(2)}) collective-permute-start(bf16[144,512]{1,0:T(8,128)(2,1)S(1)} %get-tuple-element.82.rest_0_), channel_id=1, source_target_pairs={{0,1},{1,0},{2,3},{3,2},{4,8},{5,9},{6,10},{7,11},{8,4},{9,5},{10,... | collective-permute-start | bytes 442376 | tf_op jit(solution)/shard_map/hop2_chunk1/ppermute | solution.py:543
  15.5 6.4 %collective-permute-start.2 = (bf16[128,512]{1,0:T(8,128)(2,1)S(1)}, bf16[128,512]{1,0:T(8,128)(2,1)S(1)}, u32[]{:S(2)}, u32[]{:S(2)}) collective-permute-start(bf16[128,512]{1,0:T(8,128)(2,1)S(1)} %get-tuple-element.80), channel_id=1, source_target_pairs={{0,4},{1,5},{2,6},{3,7},{4,0},{5,1},{6,2},{7,3},{8,9},{9,8},{10,11... | collective-permute-start | bytes 393224 | tf_op jit(solution)/shard_map/hop1_chunk3/ppermute | solution.py:543
  16.8 5.2 %collective-permute-start.8 = (bf16[128,512]{1,0:T(8,128)(2,1)S(1)}, bf16[128,512]{1,0:T(8,128)(2,1)S(1)}, u32[]{:S(2)}, u32[]{:S(2)}) collective-permute-start(bf16[128,512]{1,0:T(8,128)(2,1)S(1)} %get-tuple-element.93), channel_id=1, source_target_pairs={{0,1},{1,0},{2,3},{3,2},{4,5},{5,4},{6,7},{7,6},{8,12},{9,13},{10,... | collective-permute-start | bytes 393224 | tf_op jit(solution)/shard_map/hop3_chunk0/ppermute | solution.py:543
  17.0 5.1 %collective-permute-start.7 = (bf16[128,512]{1,0:T(8,128)(2,1)S(1)}, bf16[128,512]{1,0:T(8,128)(2,1)S(1)}, u32[]{:S(2)}, u32[]{:S(2)}) collective-permute-start(bf16[128,512]{1,0:T(8,128)(2,1)S(1)} %get-tuple-element.91), channel_id=1, source_target_pairs={{0,1},{1,0},{2,3},{3,2},{4,8},{5,9},{6,10},{7,11},{8,4},{9,5},{10,... | collective-permute-start | bytes 393224 | tf_op jit(solution)/shard_map/hop2_chunk2/ppermute | solution.py:543
  17.6 7.0 %collective-permute-start.9 = (bf16[144,512]{1,0:T(8,128)(2,1)S(1)}, bf16[144,512]{1,0:T(8,128)(2,1)S(1)}, u32[]{:S(2)}, u32[]{:S(2)}) collective-permute-start(bf16[144,512]{1,0:T(8,128)(2,1)S(1)} %get-tuple-element.95), channel_id=1, source_target_pairs={{0,4},{1,5},{2,6},{3,7},{4,0},{5,1},{6,2},{7,3},{8,12},{9,13},{10,... | collective-permute-start | bytes 442376 | tf_op jit(solution)/shard_map/hop3_chunk1/ppermute | solution.py:543
  22.0 2.7 %collective-permute-start.6 = (bf16[128,512]{1,0:T(8,128)(2,1)S(1)}, bf16[128,512]{1,0:T(8,128)(2,1)S(1)}, u32[]{:S(2)}, u32[]{:S(2)}) collective-permute-start(bf16[128,512]{1,0:T(8,128)(2,1)S(1)} %get-tuple-element.90.refs_1_), channel_id=1, source_target_pairs={{0,1},{1,0},{2,3},{3,2},{4,8},{5,9},{6,10},{7,11},{8,4},{9,5},{10,... | collective-permute-start | bytes 393224 | tf_op jit(solution)/shard_map/hop2_chunk3/ppermute | solution.py:543
  22.1 9.8 %collective-permute-start.10 = (bf16[128,512]{1,0:T(8,128)(2,1)S(1)}, bf16[128,512]{1,0:T(8,128)(2,1)S(1)}, u32[]{:S(2)}, u32[]{:S(2)}) collective-permute-start(bf16[128,512]{1,0:T(8,128)(2,1)S(1)} %get-tuple-element.96.refs_1_), channel_id=1, source_target_pairs={{0,1},{1,0},{2,3},{3,2},{4,5},{5,4},{6,7},{7,6},{8,12},{9,13},{10,... | collective-permute-start | bytes 393224 | tf_op jit(solution)/shard_map/hop3_chunk2/ppermute | solution.py:543
  24.7 10.8 %collective-permute-start.11 = (bf16[128,512]{1,0:T(8,128)(2,1)S(1)}, bf16[128,512]{1,0:T(8,128)(2,1)S(1)}, u32[]{:S(2)}, u32[]{:S(2)}) collective-permute-start(bf16[128,512]{1,0:T(8,128)(2,1)S(1)} %get-tuple-element.98.rest_3_), channel_id=1, source_target_pairs={{0,1},{1,0},{2,3},{3,2},{4,5},{5,4},{6,7},{7,6},{8,12},{9,13},{10,... | collective-permute-start | bytes 393224 | tf_op jit(solution)/shard_map/hop3_chunk3/ppermute | solution.py:543
  25.9 6.0 %collective-permute-start.13 = (bf16[4,2048]{1,0:T(4,128)(2,1)S(1)}, bf16[4,2048]{1,0:T(4,128)(2,1)S(1)}, u32[]{:S(2)}, u32[]{:S(2)}) collective-permute-start(bf16[4,2048]{1,0:T(4,128)(2,1)S(1)} %get-tuple-element.113), channel_id=1, source_target_pairs={{0,1},{1,0},{2,3},{3,2},{4,8},{5,9},{6,10},{7,11},{8,4},{9,5},{10,... | collective-permute-start | bytes 49160 | tf_op jit(solution)/shard_map/ppermute | solution.py:543
  26.5 6.1 %collective-permute-start.14 = (bf16[4,2048]{1,0:T(4,128)(2,1)S(1)}, bf16[4,2048]{1,0:T(4,128)(2,1)S(1)}, u32[]{:S(2)}, u32[]{:S(2)}) collective-permute-start(bf16[4,2048]{1,0:T(4,128)(2,1)S(1)} %get-tuple-element.114), channel_id=1, source_target_pairs={{0,4},{1,5},{2,6},{3,7},{4,0},{5,1},{6,2},{7,3},{8,9},{9,8},{10,11... | collective-permute-start | bytes 49160 | tf_op jit(solution)/shard_map/ppermute | solution.py:543
  30.8 4.6 %collective-permute-start.12 = (bf16[4,2048]{1,0:T(4,128)(2,1)S(1)}, bf16[4,2048]{1,0:T(4,128)(2,1)S(1)}, u32[]{:S(2)}, u32[]{:S(2)}) collective-permute-start(bf16[4,2048]{1,0:T(4,128)(2,1)S(1)} %get-tuple-element.104.rest_4_), channel_id=1, source_target_pairs={{0,8},{1,9},{2,10},{3,11},{4,5},{5,4},{6,7},{7,6},{8,0},{9,1},{10,... | collective-permute-start | bytes 49160 | tf_op jit(solution)/shard_map/ppermute | solution.py:543
  35.7 5.6 %collective-permute-start.15 = (bf16[4,2048]{1,0:T(4,128)(2,1)S(1)}, bf16[4,2048]{1,0:T(4,128)(2,1)S(1)}, u32[]{:S(2)}, u32[]{:S(2)}) collective-permute-start(bf16[4,2048]{1,0:T(4,128)(2,1)S(1)} %get-tuple-element.115), channel_id=1, source_target_pairs={{0,12},{1,13},{2,14},{3,15},{4,5},{5,4},{6,7},{7,6},{8,9},{9,8},{1... | collective-permute-start | bytes 49160 | tf_op jit(solution)/shard_map/ppermute | solution.py:543
  35.8 5.5 %collective-permute-start.16 = (bf16[4,2048]{1,0:T(4,128)(2,1)S(1)}, bf16[4,2048]{1,0:T(4,128)(2,1)S(1)}, u32[]{:S(2)}, u32[]{:S(2)}) collective-permute-start(bf16[4,2048]{1,0:T(4,128)(2,1)S(1)} %get-tuple-element.116), channel_id=1, source_target_pairs={{0,1},{1,0},{2,3},{3,2},{4,12},{5,13},{6,14},{7,15},{8,9},{9,8},{1... | collective-permute-start | bytes 49160 | tf_op jit(solution)/shard_map/ppermute | solution.py:543
  35.9 5.5 %collective-permute-start.17 = (bf16[4,2048]{1,0:T(4,128)(2,1)S(1)}, bf16[4,2048]{1,0:T(4,128)(2,1)S(1)}, u32[]{:S(2)}, u32[]{:S(2)}) collective-permute-start(bf16[4,2048]{1,0:T(4,128)(2,1)S(1)} %get-tuple-element.117), channel_id=1, source_target_pairs={{0,1},{1,0},{2,3},{3,2},{4,5},{5,4},{6,7},{7,6},{8,12},{9,13},{10,... | collective-permute-start | bytes 49160 | tf_op jit(solution)/shard_map/ppermute | solution.py:543

commit v11 on v10

--- a/solution.py
+++ b/solution.py
@@ -18,7 +18,7 @@
 F32 = jnp.float32
 BF16 = jnp.bfloat16
 CHUNKS = 4
-TOKEN_COST = 5 * 10**8
+TOKEN_COST = 10**8
 PASS_COST = 5 * 10**8
 VMEM_LIMIT = 32 * 1024 * 1024
 
@@ -137,7 +137,7 @@
     turned = b_ref[:, :N].astype(F32).T.astype(BF16)
     x_copies[0].wait()
     chunk_total(0, x_ref, turned, weight, whole, total_ref, decay_ref)
-    sent_ref[...] = total_ref[...].astype(BF16)
+    sent_ref[:N] = total_ref[...].astype(BF16)
     turned_ref[0] = turned
     for g in range(1, turned_ref.shape[0]):
         turned_ref[g] = b_ref[:, g * N : (g + 1) * N].astype(F32).T.astype(BF16)
@@ -147,18 +147,18 @@
     x_copies[1].wait()
     for copy in copies[2:]:
         copy.wait()
-
-
-def state_kernel(part, x_ref, turned_ref, weight_ref, whole_ref, asked_ref, *rest):
+    if sent_ref.shape[0] > N:
+        own = flat(here[3]).astype(BF16)
+        sent_ref[N:] = jnp.concatenate([own, own], axis=1)
+
+
+def state_kernel(part, x_ref, turned_ref, weight_ref, whole_ref, *rest):
     results = rest[-2 * len(part) - 1 :]
     for i, k in enumerate(part):
         total_ref, decay_ref = results[2 * i : 2 * i + 2]
         g = k * total_ref.shape[1] // (H // G * P_SIZE)
         chunk_total(k, x_ref, turned_ref[g], weight_ref[...], whole_ref[...], total_ref, decay_ref)
-    results[-1][:N] = results[0][...].astype(BF16)
-    if results[-1].shape[0] > N:
-        own = flat(asked_ref).astype(BF16)
-        results[-1][N:] = jnp.concatenate([own, own], axis=1)
+    results[-1][...] = results[0][...].astype(BF16)
 
 
 def flat(ref):
@@ -179,14 +179,13 @@
         following_ref = rest[1]
     got = got_ref[:N]
     moving_ref[:N] = (total_ref[...] + decay_ref[...] * got.astype(F32)).astype(BF16)
-    if got_ref.shape[0] > N:
-        tail = got_ref[N:]
-        if hop == 1:
-            own = rest[1 + more][N:].astype(F32)
-            lane = lax.broadcasted_iota(jnp.int32, own.shape, 1)
-            mine = (lane // (own.shape[1] // 2)) == lax.rem(me, 2)
-            tail = jnp.where(mine, own, tail.astype(F32)).astype(BF16)
-        moving_ref[N:] = tail
+    if moving_ref.shape[0] > N and hop == 1:
+        own, other = [ref[N:].astype(F32) for ref in rest[1 + more : 3 + more]]
+        lane = lax.broadcasted_iota(jnp.int32, own.shape, 1)
+        mine = (lane // (own.shape[1] // 2)) == lax.rem(me, 2)
+        moving_ref[N:] = jnp.where(mine, own, other).astype(BF16)
+    elif moving_ref.shape[0] > N:
+        moving_ref[N:] = got_ref[N:]
 
     @pl.when(me == hop)
     def _():
@@ -480,8 +479,8 @@
     in_vmem = pl.BlockSpec(memory_space=pltpu.VMEM)
     ride = count == 4 and width == 2 * names
 
-    def sent_shape(k):
-        return shape((N + rows * (ride and k == 1), width), BF16)
+    def sent_shape(hop, k):
+        return shape((N + rows * (ride and (hop, k) in ((1, 0), (2, 1), (3, 1))), width), BF16)
 
     inputs = [
         ssm_input,
@@ -508,7 +507,7 @@
             shape((groups, N, tokens), BF16),
         )
         + chunk_shapes
-        + (sent_shape(0),),
+        + (sent_shape(1, 0),),
         in_specs=[in_hbm] * (len(inputs) + 1),
         scratch_shapes=[
             pltpu.VMEM((heads, tokens), BF16),
@@ -524,9 +523,9 @@
     def state_part(part, tie):
         out = call(
             functools.partial(state_kernel, part),
-            chunk_shapes * len(part) + (sent_shape(1),),
-            in_specs=[in_vmem] * 5 + [anywhere],
-        )(x, turned, weight, whole, asked_here, tie)
+            chunk_shapes * len(part) + (sent_shape(1, 1),),
+            in_specs=[in_vmem] * 4 + [anywhere],
+        )(x, turned, weight, whole, tie)
         total.extend(out[0 : 2 * len(part) : 2])
         decay.extend(out[1 : 2 * len(part) : 2])
         return out[-1]
@@ -544,7 +543,7 @@
 
     def forward(value, hop, k):
         with jax.named_scope(f"hop{hop}_chunk{k}"):
-            rides = ride and k == 1 and hop != 2
+            rides = ride and (hop, k) in ((1, 0), (3, 1))
             return swap(value, *([(0, 1), (2, 3)] if rides else [(hop - 1, hop)]))
 
     def shift(value, by):
@@ -611,13 +610,14 @@
         more = hop == 1 and k + 2 < chunks
         operands = [got[hop, k], total[k], decay[k]]
         operands += [] if carry is None else [carry]
-        operands += total[k + 2 : k + 3] * more + [sent[1]] * (ride and (hop, k) == (1, 1))
+        operands += total[k + 2 : k + 3] * more + [sent[0], got[1, 0]] * (ride and (hop, k) == (1, 1))
         after = []
         if hop == count - 2 and k > 1:
             after = [token(got[hop + 1, k - 2], tie, flops=TOKEN_COST)]
         tie, carry, *following = call(
             functools.partial(pass_kernel, hop, k, more),
-            (sent_shape(k), shape((chunks, N, width), BF16)) + (sent_shape(k + 2),) * more,
+            (sent_shape(hop + 1, k), shape((chunks, N, width), BF16))
+            + (sent_shape(1, k + 2),) * more,
             flops=PASS_COST if k % 2 == 0 else 1,
             in_specs=[in_vmem] * len(operands) + [anywhere] * len(after),
             input_output_aliases={} if carry is None else {3: 1},
@@ -630,20 +630,23 @@
     early, late = tuple(range(chunks // 2)), tuple(range(chunks // 2, chunks))
     four = count == 4
     local, gain, asked = ask_part(tie)
-    back, ops = [], [(0, 2), (1, 2), (0, 1)] if four else []
+    back, ops = [], [(0, 1), (0, 2), (1, 2)] if four else []
     if four:
         reading = read_part(ops, False)
         for couple, value in zip(ops, reading):
             back.append(swap(value, couple))
-    outer = outer_part((early,), carry, [], reading[0] if four else asked)
-    keep, fresh, held = fresh_part(outer)
-    order_token = token(got[count - 1, chunks - 2], keep, flops=TOKEN_COST)
-    ends = [(0, 3), (1, 3), (2, 3)] if four else list(range(1, count))
-    *reading, mine = read_part(ends, True, order_token, *back)
-    for op, value in zip(ends, reading):
-        back.append(swap(value, op) if four else shift(value, -op))
-    ops = ops + ends
+    ends = [(2, 3), (1, 3), (0, 3)] if four else list(range(1, count))
+    before = reading[0] if four else asked
+    order_token = token(got[count - 1, chunks - 2], before, flops=TOKEN_COST)
+    *reading, mine = read_part(ends, True, order_token)
+    last_back = [
+        swap(value, op) if four else shift(value, -op) for op, value in zip(ends, reading)
+    ]
+    outer = outer_part((early,), carry, [], mine)
     prefill, end_token = outer_part((early, late), carry, [outer])
+    keep, fresh, held = fresh_part(end_token)
+    end_token = token(keep, *back, flops=TOKEN_COST)
+    ops, back = ops + ends, back + last_back
 
     decoded = call(
         functools.partial(finish_kernel, ops),

time: 42.3 us -> 38.7 us (0.915)
  waiting for transfers between devices: 14 us -> 6.94 us
  starting transfers between devices: 17.3 us -> 20.7 us
    ppermute x18, waiting for transfers between devices: 14 us -> 6.94 us  [swap(): return lax.ppermute(value, ('seq', 'tp'), pairs)]
    ppermute x18, starting transfers between devices: 17.3 us -> 20.7 us  [swap(): return lax.ppermute(value, ('seq', 'tp'), pairs)]
  transfers between devices with their start and end apart: 18 -> 18, of which waited for: 7 -> 6; matrix products, arithmetic and copies ran while one was open for 0% -> 0% of each run, Pallas kernels for 17% -> 19%
where the time goes in v11:
time: 38.7 us; the launch traced here: 38.5 us
  starting transfers between devices  20.7 us (53%)
  Pallas kernels  9.98 us (26%)
  waiting for transfers between devices  6.94 us (18%)
  between operations  0.88 us (2%)
    ppermute x18, starting transfers between devices, swap(): return lax.ppermute(value, ('seq', 'tp'), pairs)  20.7 us
    ppermute x18, waiting for transfers between devices, swap(): return lax.ppermute(value, ('seq', 'tp'), pairs)  6.94 us
    pallas_call x2, Pallas kernels, inner_part(): call(functools.partial(inner_kernel, g), shape((tokens, group_lanes)), in...  2.04 us
    pallas_call x2, Pallas kernels, outer_part(): call(functools.partial(outer_kernel, parts, count), (pltpu.HBM((tokens, l...  1.96 us
    pallas_call x1, Pallas kernels, shards(): call(functools.partial(first_kernel, len(inputs)), tuple((shape(value.sha...  1.9 us
    pallas_call x1, Pallas kernels, state_part(): call(functools.partial(state_kernel, part), chunk_shapes * len(part) + (s...  1.09 us
    pallas_call x1, Pallas kernels, ask_part(): call(functools.partial(ask_kernel, ride), (shape((rows, lanes)), shape((r...  0.89 us
  transfers between devices with their start and end apart: 18, of which 6 were waited for; matrix products, arithmetic and copies ran while one was open for 0% of the time, Pallas kernels for 19%

profile of v11, /device:TPU:0, one launch (start us, length us, event | category | flops | bytes accessed | tf_op | source)
XLA Modules:
  0.0 38.5 jit_solution(1791787352319905655)
XLA Ops:
  0.6 1.9 %first_kernel.1 = (bf16[256,2048]{1,0:T(8,128)(2,1)S(1)}, bf16[256,256]{1,0:T(8,128)(2,1)S(1)}, f32[1,32]{1,0:T(1,128)S(1)}, bf16[4,4,256]{2,1,0:T(4,128)(2,1)S(...) custom-call(bf16[256,2048]{1,0:T(8,128)(2,1)} %refs_0_.1, ...), custom_call_target="tpu_custom_call" | custom-call | flops 1 | bytes 1 | tf_op jit(solution)/shard_map/first_kernel/pallas_call | solution.py:499
  2.5 3.1 %collective-permute-start.1 = (bf16[144,512]{1,0:T(8,128)(2,1)S(1)}, bf16[144,512]{1,0:T(8,128)(2,1)S(1)}, u32[]{:S(2)}, u32[]{:S(2)}) collective-permute-start(bf16[144,512]{1,0:T(8,128)(2,1)S(1)} %get-tuple-element.73.rest_2_), channel_id=1, source_target_pairs={{0,4},{1,5},{2,6},{3,7},{4,0},{5,1},{6,2},{7,3},{8,12},{9,13},{10,... | collective-permute-start | bytes 442376 | tf_op jit(solution)/shard_map/hop1_chunk0/ppermute | solution.py:542
  5.6 1.0 %inner_kernel.2.rest_0_.rest_2_ = f32[256,1024]{1,0:T(8,128)S(1)} custom-call(bf16[256,2048]{1,0:T(8,128)(2,1)S(1)} %get-tuple-element.63.x_ref, bf16[256,256]{1,0:T(8,128)(2,1)S(1)} %get-tuple-element.67.b_ref, bf16[256,256]{1,0:T(8,128)(2,1)S(1)} %get-tuple-element.61.c_ref, f32[32,256]{1,0:T(8,128)S(1)} %get-tuple-element.62.cum_ref, ...), custom_call_target="tpu_custom_call" | custom-call | flops 1 | bytes 1 | tf_op jit(solution)/shard_map/inner_kernel/pallas_call | solution.py:553
  6.6 1.0 %inner_kernel.3.rest_0_.rest_3_ = f32[256,1024]{1,0:T(8,128)S(1)} custom-call(bf16[256,2048]{1,0:T(8,128)(2,1)S(1)} %get-tuple-element.63.x_ref, bf16[256,256]{1,0:T(8,128)(2,1)S(1)} %get-tuple-element.67.b_ref, bf16[256,256]{1,0:T(8,128)(2,1)S(1)} %get-tuple-element.61.c_ref, f32[32,256]{1,0:T(8,128)S(1)} %get-tuple-element.62.cum_ref, ...), custom_call_target="tpu_custom_call" | custom-call | flops 1 | bytes 1 | tf_op jit(solution)/shard_map/inner_kernel/pallas_call | solution.py:553
  7.7 1.1 %state_kernel.1 = (f32[128,512]{1,0:T(8,128)S(1)}, f32[1,512]{1,0:T(1,128)S(1)}, f32[128,512]{1,0:T(8,128)S(1)}, f32[1,512]{1,0:T(1,128)S(1)}, f32[128,512]{1,0:...) custom-call(bf16[256,2048]{1,0:T(8,128)(2,1)S(1)} %get-tuple-element.63.x_ref, ...), custom_call_target="tpu_custom_call" | custom-call | flops 1 | bytes 1 | tf_op jit(solution)/shard_map/state_kernel/pallas_call | solution.py:524
  8.8 0.1 collective-permute-start
  8.8 0.6 %collective-permute-done.1.got_ref.rest_3_ = bf16[144,512]{1,0:T(8,128)(2,1)S(1)} collective-permute-done((bf16[144,512]{1,0:T(8,128)(2,1)S(1)}, bf16[144,512]{1,0:T(8,128)(2,1)S(1)}, u32[]{:S(2)}, u32[]{:S(2)}) %collective-permute-start.1) | collective-permute-done | bytes 147488 | tf_op jit(solution)/shard_map/hop1_chunk0/ppermute | solution.py:542
  9.5 0.1 pass_kernel.8
  9.6 0.1 collective-permute-start.5
  9.6 3.3 %collective-permute-start.4 = (bf16[128,512]{1,0:T(8,128)(2,1)S(1)}, bf16[128,512]{1,0:T(8,128)(2,1)S(1)}, u32[]{:S(2)}, u32[]{:S(2)}) collective-permute-start(bf16[128,512]{1,0:T(8,128)(2,1)S(1)} %get-tuple-element.82), channel_id=1, source_target_pairs={{0,4},{1,5},{2,6},{3,7},{4,0},{5,1},{6,2},{7,3},{8,9},{9,8},{10,11... | collective-permute-start | bytes 393224 | tf_op jit(solution)/shard_map/hop1_chunk2/ppermute | solution.py:542
  12.9 1.5 %collective-permute-done.got_ref = bf16[128,512]{1,0:T(8,128)(2,1)S(1)} collective-permute-done((bf16[128,512]{1,0:T(8,128)(2,1)S(1)}, bf16[128,512]{1,0:T(8,128)(2,1)S(1)}, u32[]{:S(2)}, u32[]{:S(2)}) %collective-permute-start) | collective-permute-done | bytes 131104 | tf_op jit(solution)/shard_map/hop1_chunk1/ppermute | solution.py:542
  14.4 0.1 pass_kernel.9
  14.5 0.1 collective-permute-start.3
  14.5 0.1 collective-permute-start.2
  14.6 0.0 collective-permute-done.5.got_ref
  14.7 0.5 %collective-permute-start.8 = (bf16[128,512]{1,0:T(8,128)(2,1)S(1)}, bf16[128,512]{1,0:T(8,128)(2,1)S(1)}, u32[]{:S(2)}, u32[]{:S(2)}) collective-permute-start(bf16[128,512]{1,0:T(8,128)(2,1)S(1)} %get-tuple-element.92), channel_id=1, source_target_pairs={{0,1},{1,0},{2,3},{3,2},{4,5},{5,4},{6,7},{7,6},{8,12},{9,13},{10,... | collective-permute-start | bytes 393224 | tf_op jit(solution)/shard_map/hop3_chunk0/ppermute | solution.py:542
  15.1 1.4 %collective-permute-done.4.got_ref = bf16[128,512]{1,0:T(8,128)(2,1)S(1)} collective-permute-done((bf16[128,512]{1,0:T(8,128)(2,1)S(1)}, bf16[128,512]{1,0:T(8,128)(2,1)S(1)}, u32[]{:S(2)}, u32[]{:S(2)}) %collective-permute-start.4) | collective-permute-done | bytes 131104 | tf_op jit(solution)/shard_map/hop1_chunk2/ppermute | solution.py:542
  16.6 0.1 collective-permute-start.7
  16.7 0.0 collective-permute-done.3.got_ref.rest_1_
  16.8 2.9 %collective-permute-start.9 = (bf16[144,512]{1,0:T(8,128)(2,1)S(1)}, bf16[144,512]{1,0:T(8,128)(2,1)S(1)}, u32[]{:S(2)}, u32[]{:S(2)}) collective-permute-start(bf16[144,512]{1,0:T(8,128)(2,1)S(1)} %get-tuple-element.94), channel_id=1, source_target_pairs={{0,4},{1,5},{2,6},{3,7},{4,0},{5,1},{6,2},{7,3},{8,12},{9,13},{10,... | collective-permute-start | bytes 442376 | tf_op jit(solution)/shard_map/hop3_chunk1/ppermute | solution.py:542
  19.7 1.2 %collective-permute-done.2.got_ref = bf16[128,512]{1,0:T(8,128)(2,1)S(1)} collective-permute-done((bf16[128,512]{1,0:T(8,128)(2,1)S(1)}, bf16[128,512]{1,0:T(8,128)(2,1)S(1)}, u32[]{:S(2)}, u32[]{:S(2)}) %collective-permute-start.2) | collective-permute-done | bytes 131104 | tf_op jit(solution)/shard_map/hop1_chunk3/ppermute | solution.py:542
  20.9 0.1 collective-permute-start.6
  21.0 0.0 collective-permute-done.8.refs_0_.rest_0_
  21.0 0.0 collective-permute-done.7.got_ref
  21.1 0.5 %collective-permute-start.10 = (bf16[128,512]{1,0:T(8,128)(2,1)S(1)}, bf16[128,512]{1,0:T(8,128)(2,1)S(1)}, u32[]{:S(2)}, u32[]{:S(2)}) collective-permute-start(bf16[128,512]{1,0:T(8,128)(2,1)S(1)} %get-tuple-element.95.refs_1_), channel_id=1, source_target_pairs={{0,1},{1,0},{2,3},{3,2},{4,5},{5,4},{6,7},{7,6},{8,12},{9,13},{10,... | collective-permute-start | bytes 393224 | tf_op jit(solution)/shard_map/hop3_chunk2/ppermute | solution.py:542
  21.6 2.0 %collective-permute-done.9.refs_0_.rest_2_.rest_1_ = bf16[144,512]{1,0:T(8,128)(2,1)S(1)} collective-permute-done((bf16[144,512]{1,0:T(8,128)(2,1)S(1)}, bf16[144,512]{1,0:T(8,128)(2,1)S(1)}, u32[]{:S(2)}, u32[]{:S(2)}) %collective-permute-start.9) | collective-permute-done | bytes 147488 | tf_op jit(solution)/shard_map/hop3_chunk1/ppermute | solution.py:542
  23.6 0.0 collective-permute-done.6.got_ref
  23.7 0.1 collective-permute-start.11
  23.7 0.9 %ask_kernel.1 = (f32[16,2048]{1,0:T(8,128)S(1)}, f32[16,32]{1,0:T(8,128)S(1)}, bf16[16,256]{1,0:T(8,128)(2,1)S(1)}) custom-call(bf16[256,2048]{1,0:T(8,128)(2,1)S(1)} %get-tuple-element.63.x_ref, bf16[256,256]{1,0:T(8,128)(2,1)S(1)} %get-tuple-element.67.b_ref, f32[32,256]{1,0:T(8,128)S(1)} %get-tuple-element.62.cum_ref, ...), custom_call_target="tpu_custom_call" | custom-call | flops 1 | bytes 1 | tf_op jit(solution)/shard_map/ask_kernel/pallas_call | solution.py:561
  24.6 0.3 read_kernel.2
  24.9 4.8 %collective-permute-start.13 = (bf16[4,2048]{1,0:T(4,128)(2,1)S(1)}, bf16[4,2048]{1,0:T(4,128)(2,1)S(1)}, u32[]{:S(2)}, u32[]{:S(2)}) collective-permute-start(bf16[4,2048]{1,0:T(4,128)(2,1)S(1)} %get-tuple-element.115), channel_id=1, source_target_pairs={{0,8},{1,9},{2,10},{3,11},{4,5},{5,4},{6,7},{7,6},{8,0},{9,1},{10,... | collective-permute-start | bytes 49160 | tf_op jit(solution)/shard_map/ppermute | solution.py:542
  29.7 0.0 collective-permute-start.14
  29.7 0.6 %collective-permute-start.12 = (bf16[4,2048]{1,0:T(4,128)(2,1)S(1)}, bf16[4,2048]{1,0:T(4,128)(2,1)S(1)}, u32[]{:S(2)}, u32[]{:S(2)}) collective-permute-start(bf16[4,2048]{1,0:T(4,128)(2,1)S(1)} %get-tuple-element.103.refs_1_), channel_id=1, source_target_pairs={{0,4},{1,5},{2,6},{3,7},{4,0},{5,1},{6,2},{7,3},{8,9},{9,8},{10,11... | collective-permute-start | bytes 49160 | tf_op jit(solution)/shard_map/ppermute | solution.py:542
  30.4 0.0 collective-permute-done.10.refs_0_.rest_2_.rest_0_
  30.4 0.0 collective-permute-done.11.rest_3_.rest_1_
  30.4 0.3 read_kernel.3
  30.7 0.1 collective-permute-start.15
  30.8 0.5 %collective-permute-start.16 = (bf16[4,2048]{1,0:T(4,128)(2,1)S(1)}, bf16[4,2048]{1,0:T(4,128)(2,1)S(1)}, u32[]{:S(2)}, u32[]{:S(2)}) collective-permute-start(bf16[4,2048]{1,0:T(4,128)(2,1)S(1)} %get-tuple-element.118), channel_id=1, source_target_pairs={{0,1},{1,0},{2,3},{3,2},{4,12},{5,13},{6,14},{7,15},{8,9},{9,8},{1... | collective-permute-start | bytes 49160 | tf_op jit(solution)/shard_map/ppermute | solution.py:542
  31.3 0.2 collective-permute-done.13.refs_2_.rest_1_
  31.4 3.8 %collective-permute-start.17 = (bf16[4,2048]{1,0:T(4,128)(2,1)S(1)}, bf16[4,2048]{1,0:T(4,128)(2,1)S(1)}, u32[]{:S(2)}, u32[]{:S(2)}) collective-permute-start(bf16[4,2048]{1,0:T(4,128)(2,1)S(1)} %get-tuple-element.119), channel_id=1, source_target_pairs={{0,12},{1,13},{2,14},{3,15},{4,5},{5,4},{6,7},{7,6},{8,9},{9,8},{1... | collective-permute-start | bytes 49160 | tf_op jit(solution)/shard_map/ppermute | solution.py:542
  35.3 0.6 %outer_kernel.2.rest_4_ = bf16[2,256,512]{2,1,0:T(8,128)(2,1)S(1)} custom-call(bf16[256,256]{1,0:T(8,128)(2,1)S(1)} %get-tuple-element.61.c_ref, f32[32,256]{1,0:T(8,128)S(1)} %get-tuple-element.62.cum_ref, bf16[4,128,512]{2,1,0:T(8,128)(2,1)S(1)} %get-tuple-element.96.carry_ref, bf16[128,512]{1,0:T(8,128)(2,1)S(1)} %collective-permute-done.8.refs_0_.rest_0_, ...), custom_call_target="tpu_custom_call" | custom-call | flops 1 | bytes 1 | tf_op jit(solution)/shard_map/outer_kernel/pallas_call | solution.py:583
  35.9 1.4 %outer_kernel.3 = (bf16[256,2048]{1,0:T(8,128)(2,1)}, f32[8,128]{1,0:T(8,128)S(1)}) custom-call(bf16[256,256]{1,0:T(8,128)(2,1)S(1)} %get-tuple-element.61.c_ref, f32[32,256]{1,0:T(8,128)S(1)} %get-tuple-element.62.cum_ref, bf16[4,128,512]{2,1,0:T(8,128)(2,1)S(1)} %get-tuple-element.96.carry_ref, ...), custom_call_target="tpu_custom_call" | custom-call | flops 1 | bytes 1 | tf_op jit(solution)/shard_map/outer_kernel/pallas_call | solution.py:583
  37.3 0.4 %fresh_kernel.1 = (f32[4,4,2048]{2,1,0:T(4,128)S(1)}, f32[4,4,2048]{2,1,0:T(4,128)S(1)}, f32[4,4,128]{2,1,0:T(4,128)S(1)}) custom-call(bf16[4,4,2048]{2,1,0:T(4,128)(2,1)S(1)} %get-tuple-element.106.x_ref, bf16[4,4,256]{2,1,0:T(4,128)(2,1)S(1)} %get-tuple-element.107.b_ref, bf16[4,4,256]{2,1,0:T(4,128)(2,1)S(1)} %get-tuple-element.108.c_ref, ...), custom_call_target="tpu_custom_call" | custom-call | flops 1 | bytes 1 | tf_op jit(solution)/shard_map/fresh_kernel/pallas_call | solution.py:573
  37.7 0.0 collective-permute-done.14.refs_3_.rest_2_
  37.7 0.0 collective-permute-done.12.refs_1_.rest_0_
  37.7 0.0 collective-permute-done.15.rest_3_
  37.7 0.0 collective-permute-done.16.rest_4_
  37.7 0.0 collective-permute-done.17.rest_5_
  37.8 0.7 %finish_kernel.1 = bf16[4,4,2048]{2,1,0:T(4,128)(2,1)} custom-call(f32[4,4,2048]{2,1,0:T(4,128)S(1)} %get-tuple-element.112.refs_0_.keep_ref, f32[4,4,2048]{2,1,0:T(4,128)S(1)} %get-tuple-element.113.fresh_ref, f32[4,4,128]{2,1,0:T(4,128)S(1)} %get-tuple-element.114.held_ref, bf16[4,2048]{1,0:T(4,128)(2,1)S(1)} %collective-permute-done.12.refs_1_.rest_0_, ...), custom_call_target="tpu_custom_call" | custom-call | flops 1 | bytes 1 | tf_op jit(solution)/shard_map/finish_kernel/pallas_call | solution.py:651
  (10 shorter events, 0.3 us)
Async XLA Ops:
  2.5 6.9 %collective-permute-start.1 = (bf16[144,512]{1,0:T(8,128)(2,1)S(1)}, bf16[144,512]{1,0:T(8,128)(2,1)S(1)}, u32[]{:S(2)}, u32[]{:S(2)}) collective-permute-start(bf16[144,512]{1,0:T(8,128)(2,1)S(1)} %get-tuple-element.73.rest_2_), channel_id=1, source_target_pairs={{0,4},{1,5},{2,6},{3,7},{4,0},{5,1},{6,2},{7,3},{8,12},{9,13},{10,... | collective-permute-start | bytes 442376 | tf_op jit(solution)/shard_map/hop1_chunk0/ppermute | solution.py:542
  8.8 5.6 %collective-permute-start = (bf16[128,512]{1,0:T(8,128)(2,1)S(1)}, bf16[128,512]{1,0:T(8,128)(2,1)S(1)}, u32[]{:S(2)}, u32[]{:S(2)}) collective-permute-start(bf16[128,512]{1,0:T(8,128)(2,1)S(1)} %get-tuple-element.70), channel_id=1, source_target_pairs={{0,4},{1,5},{2,6},{3,7},{4,0},{5,1},{6,2},{7,3},{8,9},{9,8},{10,11... | collective-permute-start | bytes 393224 | tf_op jit(solution)/shard_map/hop1_chunk1/ppermute | solution.py:542
  9.6 5.1 %collective-permute-start.5 = (bf16[128,512]{1,0:T(8,128)(2,1)S(1)}, bf16[128,512]{1,0:T(8,128)(2,1)S(1)}, u32[]{:S(2)}, u32[]{:S(2)}) collective-permute-start(bf16[128,512]{1,0:T(8,128)(2,1)S(1)} %get-tuple-element.84), channel_id=1, source_target_pairs={{0,1},{1,0},{2,3},{3,2},{4,8},{5,9},{6,10},{7,11},{8,4},{9,5},{10,... | collective-permute-start | bytes 393224 | tf_op jit(solution)/shard_map/hop2_chunk0/ppermute | solution.py:542
  9.6 7.0 %collective-permute-start.4 = (bf16[128,512]{1,0:T(8,128)(2,1)S(1)}, bf16[128,512]{1,0:T(8,128)(2,1)S(1)}, u32[]{:S(2)}, u32[]{:S(2)}) collective-permute-start(bf16[128,512]{1,0:T(8,128)(2,1)S(1)} %get-tuple-element.82), channel_id=1, source_target_pairs={{0,4},{1,5},{2,6},{3,7},{4,0},{5,1},{6,2},{7,3},{8,9},{9,8},{10,11... | collective-permute-start | bytes 393224 | tf_op jit(solution)/shard_map/hop1_chunk2/ppermute | solution.py:542
  14.5 2.3 %collective-permute-start.3 = (bf16[144,512]{1,0:T(8,128)(2,1)S(1)}, bf16[144,512]{1,0:T(8,128)(2,1)S(1)}, u32[]{:S(2)}, u32[]{:S(2)}) collective-permute-start(bf16[144,512]{1,0:T(8,128)(2,1)S(1)} %get-tuple-element.81.rest_0_), channel_id=1, source_target_pairs={{0,1},{1,0},{2,3},{3,2},{4,8},{5,9},{6,10},{7,11},{8,4},{9,5},{10,... | collective-permute-start | bytes 442376 | tf_op jit(solution)/shard_map/hop2_chunk1/ppermute | solution.py:542
  14.5 6.4 %collective-permute-start.2 = (bf16[128,512]{1,0:T(8,128)(2,1)S(1)}, bf16[128,512]{1,0:T(8,128)(2,1)S(1)}, u32[]{:S(2)}, u32[]{:S(2)}) collective-permute-start(bf16[128,512]{1,0:T(8,128)(2,1)S(1)} %get-tuple-element.79), channel_id=1, source_target_pairs={{0,4},{1,5},{2,6},{3,7},{4,0},{5,1},{6,2},{7,3},{8,9},{9,8},{10,11... | collective-permute-start | bytes 393224 | tf_op jit(solution)/shard_map/hop1_chunk3/ppermute | solution.py:542
  14.7 6.4 %collective-permute-start.8 = (bf16[128,512]{1,0:T(8,128)(2,1)S(1)}, bf16[128,512]{1,0:T(8,128)(2,1)S(1)}, u32[]{:S(2)}, u32[]{:S(2)}) collective-permute-start(bf16[128,512]{1,0:T(8,128)(2,1)S(1)} %get-tuple-element.92), channel_id=1, source_target_pairs={{0,1},{1,0},{2,3},{3,2},{4,5},{5,4},{6,7},{7,6},{8,12},{9,13},{10,... | collective-permute-start | bytes 393224 | tf_op jit(solution)/shard_map/hop3_chunk0/ppermute | solution.py:542
  16.6 4.4 %collective-permute-start.7 = (bf16[128,512]{1,0:T(8,128)(2,1)S(1)}, bf16[128,512]{1,0:T(8,128)(2,1)S(1)}, u32[]{:S(2)}, u32[]{:S(2)}) collective-permute-start(bf16[128,512]{1,0:T(8,128)(2,1)S(1)} %get-tuple-element.90), channel_id=1, source_target_pairs={{0,1},{1,0},{2,3},{3,2},{4,8},{5,9},{6,10},{7,11},{8,4},{9,5},{10,... | collective-permute-start | bytes 393224 | tf_op jit(solution)/shard_map/hop2_chunk2/ppermute | solution.py:542
  16.8 6.8 %collective-permute-start.9 = (bf16[144,512]{1,0:T(8,128)(2,1)S(1)}, bf16[144,512]{1,0:T(8,128)(2,1)S(1)}, u32[]{:S(2)}, u32[]{:S(2)}) collective-permute-start(bf16[144,512]{1,0:T(8,128)(2,1)S(1)} %get-tuple-element.94), channel_id=1, source_target_pairs={{0,4},{1,5},{2,6},{3,7},{4,0},{5,1},{6,2},{7,3},{8,12},{9,13},{10,... | collective-permute-start | bytes 442376 | tf_op jit(solution)/shard_map/hop3_chunk1/ppermute | solution.py:542
  20.9 2.7 %collective-permute-start.6 = (bf16[128,512]{1,0:T(8,128)(2,1)S(1)}, bf16[128,512]{1,0:T(8,128)(2,1)S(1)}, u32[]{:S(2)}, u32[]{:S(2)}) collective-permute-start(bf16[128,512]{1,0:T(8,128)(2,1)S(1)} %get-tuple-element.89.refs_1_), channel_id=1, source_target_pairs={{0,1},{1,0},{2,3},{3,2},{4,8},{5,9},{6,10},{7,11},{8,4},{9,5},{10,... | collective-permute-start | bytes 393224 | tf_op jit(solution)/shard_map/hop2_chunk3/ppermute | solution.py:542
  21.1 9.3 %collective-permute-start.10 = (bf16[128,512]{1,0:T(8,128)(2,1)S(1)}, bf16[128,512]{1,0:T(8,128)(2,1)S(1)}, u32[]{:S(2)}, u32[]{:S(2)}) collective-permute-start(bf16[128,512]{1,0:T(8,128)(2,1)S(1)} %get-tuple-element.95.refs_1_), channel_id=1, source_target_pairs={{0,1},{1,0},{2,3},{3,2},{4,5},{5,4},{6,7},{7,6},{8,12},{9,13},{10,... | collective-permute-start | bytes 393224 | tf_op jit(solution)/shard_map/hop3_chunk2/ppermute | solution.py:542
  23.7 6.7 %collective-permute-start.11 = (bf16[128,512]{1,0:T(8,128)(2,1)S(1)}, bf16[128,512]{1,0:T(8,128)(2,1)S(1)}, u32[]{:S(2)}, u32[]{:S(2)}) collective-permute-start(bf16[128,512]{1,0:T(8,128)(2,1)S(1)} %get-tuple-element.97.rest_3_), channel_id=1, source_target_pairs={{0,1},{1,0},{2,3},{3,2},{4,5},{5,4},{6,7},{7,6},{8,12},{9,13},{10,... | collective-permute-start | bytes 393224 | tf_op jit(solution)/shard_map/hop3_chunk3/ppermute | solution.py:542
  24.9 6.5 %collective-permute-start.13 = (bf16[4,2048]{1,0:T(4,128)(2,1)S(1)}, bf16[4,2048]{1,0:T(4,128)(2,1)S(1)}, u32[]{:S(2)}, u32[]{:S(2)}) collective-permute-start(bf16[4,2048]{1,0:T(4,128)(2,1)S(1)} %get-tuple-element.115), channel_id=1, source_target_pairs={{0,8},{1,9},{2,10},{3,11},{4,5},{5,4},{6,7},{7,6},{8,0},{9,1},{10,... | collective-permute-start | bytes 49160 | tf_op jit(solution)/shard_map/ppermute | solution.py:542
  29.7 8.0 %collective-permute-start.14 = (bf16[4,2048]{1,0:T(4,128)(2,1)S(1)}, bf16[4,2048]{1,0:T(4,128)(2,1)S(1)}, u32[]{:S(2)}, u32[]{:S(2)}) collective-permute-start(bf16[4,2048]{1,0:T(4,128)(2,1)S(1)} %get-tuple-element.116), channel_id=1, source_target_pairs={{0,1},{1,0},{2,3},{3,2},{4,8},{5,9},{6,10},{7,11},{8,4},{9,5},{10,... | collective-permute-start | bytes 49160 | tf_op jit(solution)/shard_map/ppermute | solution.py:542
  29.7 8.0 %collective-permute-start.12 = (bf16[4,2048]{1,0:T(4,128)(2,1)S(1)}, bf16[4,2048]{1,0:T(4,128)(2,1)S(1)}, u32[]{:S(2)}, u32[]{:S(2)}) collective-permute-start(bf16[4,2048]{1,0:T(4,128)(2,1)S(1)} %get-tuple-element.103.refs_1_), channel_id=1, source_target_pairs={{0,4},{1,5},{2,6},{3,7},{4,0},{5,1},{6,2},{7,3},{8,9},{9,8},{10,11... | collective-permute-start | bytes 49160 | tf_op jit(solution)/shard_map/ppermute | solution.py:542
  30.7 7.1 %collective-permute-start.15 = (bf16[4,2048]{1,0:T(4,128)(2,1)S(1)}, bf16[4,2048]{1,0:T(4,128)(2,1)S(1)}, u32[]{:S(2)}, u32[]{:S(2)}) collective-permute-start(bf16[4,2048]{1,0:T(4,128)(2,1)S(1)} %get-tuple-element.117), channel_id=1, source_target_pairs={{0,1},{1,0},{2,3},{3,2},{4,5},{5,4},{6,7},{7,6},{8,12},{9,13},{10,... | collective-permute-start | bytes 49160 | tf_op jit(solution)/shard_map/ppermute | solution.py:542
  30.8 7.0 %collective-permute-start.16 = (bf16[4,2048]{1,0:T(4,128)(2,1)S(1)}, bf16[4,2048]{1,0:T(4,128)(2,1)S(1)}, u32[]{:S(2)}, u32[]{:S(2)}) collective-permute-start(bf16[4,2048]{1,0:T(4,128)(2,1)S(1)} %get-tuple-element.118), channel_id=1, source_target_pairs={{0,1},{1,0},{2,3},{3,2},{4,12},{5,13},{6,14},{7,15},{8,9},{9,8},{1... | collective-permute-start | bytes 49160 | tf_op jit(solution)/shard_map/ppermute | solution.py:542
  31.4 6.3 %collective-permute-start.17 = (bf16[4,2048]{1,0:T(4,128)(2,1)S(1)}, bf16[4,2048]{1,0:T(4,128)(2,1)S(1)}, u32[]{:S(2)}, u32[]{:S(2)}) collective-permute-start(bf16[4,2048]{1,0:T(4,128)(2,1)S(1)} %get-tuple-element.119), channel_id=1, source_target_pairs={{0,12},{1,13},{2,14},{3,15},{4,5},{5,4},{6,7},{7,6},{8,9},{9,8},{1... | collective-permute-start | bytes 49160 | tf_op jit(solution)/shard_map/ppermute | solution.py:542

commit v12 on v11

--- a/solution.py
+++ b/solution.py
@@ -612,6 +612,9 @@
         operands += [] if carry is None else [carry]
         operands += total[k + 2 : k + 3] * more + [sent[0], got[1, 0]] * (ride and (hop, k) == (1, 1))
         after = []
+        if (hop, k) == (1, 1):
+            keep, fresh, held = fresh_part(tie)
+            after = [keep]
         if hop == count - 2 and k > 1:
             after = [token(got[hop + 1, k - 2], tie, flops=TOKEN_COST)]
         tie, carry, *following = call(
@@ -635,7 +638,7 @@
         reading = read_part(ops, False)
         for couple, value in zip(ops, reading):
             back.append(swap(value, couple))
-    ends = [(2, 3), (1, 3), (0, 3)] if four else list(range(1, count))
+    ends = [(0, 3), (1, 3), (2, 3)] if four else list(range(1, count))
     before = reading[0] if four else asked
     order_token = token(got[count - 1, chunks - 2], before, flops=TOKEN_COST)
     *reading, mine = read_part(ends, True, order_token)
@@ -644,8 +647,7 @@
     ]
     outer = outer_part((early,), carry, [], mine)
     prefill, end_token = outer_part((early, late), carry, [outer])
-    keep, fresh, held = fresh_part(end_token)
-    end_token = token(keep, *back, flops=TOKEN_COST)
+    end_token = token(end_token, *back, flops=TOKEN_COST)
     ops, back = ops + ends, back + last_back
 
     decoded = call(

time: 38.7 us -> 37 us (0.956)
  starting transfers between devices: 20.7 us -> 19 us
    ppermute x18, starting transfers between devices: 20.7 us -> 19 us  [swap(): return lax.ppermute(value, ('seq', 'tp'), pairs)]
  transfers between devices with their start and end apart: 18 -> 18, of which waited for: 6 -> 6; matrix products, arithmetic and copies ran while one was open for 0% -> 0% of each run, Pallas kernels for 19% -> 20%
where the time goes in v12:
time: 37 us; the launch traced here: 36.8 us
  starting transfers between devices  19 us (51%)
  Pallas kernels  9.97 us (27%)
  waiting for transfers between devices  6.93 us (19%)
  between operations  0.85 us (2%)
    ppermute x18, starting transfers between devices, swap(): return lax.ppermute(value, ('seq', 'tp'), pairs)  19 us
    ppermute x18, waiting for transfers between devices, swap(): return lax.ppermute(value, ('seq', 'tp'), pairs)  6.93 us
    pallas_call x2, Pallas kernels, inner_part(): call(functools.partial(inner_kernel, g), shape((tokens, group_lanes)), in...  2.04 us
    pallas_call x2, Pallas kernels, outer_part(): call(functools.partial(outer_kernel, parts, count), (pltpu.HBM((tokens, l...  1.95 us
    pallas_call x1, Pallas kernels, shards(): call(functools.partial(first_kernel, len(inputs)), tuple((shape(value.sha...  1.9 us
    pallas_call x1, Pallas kernels, state_part(): call(functools.partial(state_kernel, part), chunk_shapes * len(part) + (s...  1.09 us
    pallas_call x1, Pallas kernels, ask_part(): call(functools.partial(ask_kernel, ride), (shape((rows, lanes)), shape((r...  0.89 us
  transfers between devices with their start and end apart: 18, of which 6 were waited for; matrix products, arithmetic and copies ran while one was open for 0% of the time, Pallas kernels for 20%

profile of v12, /device:TPU:0, one launch (start us, length us, event | category | flops | bytes accessed | tf_op | source)
XLA Modules:
  0.0 36.8 jit_solution(1491117694054111993)
XLA Ops:
  0.6 1.9 %first_kernel.1 = (bf16[256,2048]{1,0:T(8,128)(2,1)S(1)}, bf16[256,256]{1,0:T(8,128)(2,1)S(1)}, f32[1,32]{1,0:T(1,128)S(1)}, bf16[4,4,256]{2,1,0:T(4,128)(2,1)S(...) custom-call(bf16[256,2048]{1,0:T(8,128)(2,1)} %refs_0_.1, ...), custom_call_target="tpu_custom_call" | custom-call | flops 1 | bytes 1 | tf_op jit(solution)/shard_map/first_kernel/pallas_call | solution.py:499
  2.5 3.1 %collective-permute-start.1 = (bf16[144,512]{1,0:T(8,128)(2,1)S(1)}, bf16[144,512]{1,0:T(8,128)(2,1)S(1)}, u32[]{:S(2)}, u32[]{:S(2)}) collective-permute-start(bf16[144,512]{1,0:T(8,128)(2,1)S(1)} %get-tuple-element.73.rest_2_), channel_id=1, source_target_pairs={{0,4},{1,5},{2,6},{3,7},{4,0},{5,1},{6,2},{7,3},{8,12},{9,13},{10,... | collective-permute-start | bytes 442376 | tf_op jit(solution)/shard_map/hop1_chunk0/ppermute | solution.py:542
  5.6 1.0 %inner_kernel.2.rest_0_.rest_2_ = f32[256,1024]{1,0:T(8,128)S(1)} custom-call(bf16[256,2048]{1,0:T(8,128)(2,1)S(1)} %get-tuple-element.63.x_ref, bf16[256,256]{1,0:T(8,128)(2,1)S(1)} %get-tuple-element.67.b_ref, bf16[256,256]{1,0:T(8,128)(2,1)S(1)} %get-tuple-element.61.c_ref, f32[32,256]{1,0:T(8,128)S(1)} %get-tuple-element.62.cum_ref, ...), custom_call_target="tpu_custom_call" | custom-call | flops 1 | bytes 1 | tf_op jit(solution)/shard_map/inner_kernel/pallas_call | solution.py:553
  6.6 1.0 %inner_kernel.3.rest_0_.rest_3_ = f32[256,1024]{1,0:T(8,128)S(1)} custom-call(bf16[256,2048]{1,0:T(8,128)(2,1)S(1)} %get-tuple-element.63.x_ref, bf16[256,256]{1,0:T(8,128)(2,1)S(1)} %get-tuple-element.67.b_ref, bf16[256,256]{1,0:T(8,128)(2,1)S(1)} %get-tuple-element.61.c_ref, f32[32,256]{1,0:T(8,128)S(1)} %get-tuple-element.62.cum_ref, ...), custom_call_target="tpu_custom_call" | custom-call | flops 1 | bytes 1 | tf_op jit(solution)/shard_map/inner_kernel/pallas_call | solution.py:553
  7.7 1.1 %state_kernel.1 = (f32[128,512]{1,0:T(8,128)S(1)}, f32[1,512]{1,0:T(1,128)S(1)}, f32[128,512]{1,0:T(8,128)S(1)}, f32[1,512]{1,0:T(1,128)S(1)}, f32[128,512]{1,0:...) custom-call(bf16[256,2048]{1,0:T(8,128)(2,1)S(1)} %get-tuple-element.63.x_ref, ...), custom_call_target="tpu_custom_call" | custom-call | flops 1 | bytes 1 | tf_op jit(solution)/shard_map/state_kernel/pallas_call | solution.py:524
  8.8 0.1 collective-permute-start
  8.8 0.6 %collective-permute-done.1.got_ref.rest_3_ = bf16[144,512]{1,0:T(8,128)(2,1)S(1)} collective-permute-done((bf16[144,512]{1,0:T(8,128)(2,1)S(1)}, bf16[144,512]{1,0:T(8,128)(2,1)S(1)}, u32[]{:S(2)}, u32[]{:S(2)}) %collective-permute-start.1) | collective-permute-done | bytes 147488 | tf_op jit(solution)/shard_map/hop1_chunk0/ppermute | solution.py:542
  9.5 0.1 pass_kernel.8
  9.6 0.1 collective-permute-start.5
  9.6 3.3 %collective-permute-start.4 = (bf16[128,512]{1,0:T(8,128)(2,1)S(1)}, bf16[128,512]{1,0:T(8,128)(2,1)S(1)}, u32[]{:S(2)}, u32[]{:S(2)}) collective-permute-start(bf16[128,512]{1,0:T(8,128)(2,1)S(1)} %get-tuple-element.91), channel_id=1, source_target_pairs={{0,4},{1,5},{2,6},{3,7},{4,0},{5,1},{6,2},{7,3},{8,9},{9,8},{10,11... | collective-permute-start | bytes 393224 | tf_op jit(solution)/shard_map/hop1_chunk2/ppermute | solution.py:542
  12.9 0.4 %fresh_kernel.1 = (f32[4,4,2048]{2,1,0:T(4,128)S(1)}, f32[4,4,2048]{2,1,0:T(4,128)S(1)}, f32[4,4,128]{2,1,0:T(4,128)S(1)}) custom-call(bf16[4,4,2048]{2,1,0:T(4,128)(2,1)S(1)} %get-tuple-element.79.x_ref, bf16[4,4,256]{2,1,0:T(4,128)(2,1)S(1)} %get-tuple-element.80.b_ref, bf16[4,4,256]{2,1,0:T(4,128)(2,1)S(1)} %get-tuple-element.81.c_ref, ...), custom_call_target="tpu_custom_call" | custom-call | flops 1 | bytes 1 | tf_op jit(solution)/shard_map/fresh_kernel/pallas_call | solution.py:573
  13.4 1.0 %collective-permute-done.got_ref = bf16[128,512]{1,0:T(8,128)(2,1)S(1)} collective-permute-done((bf16[128,512]{1,0:T(8,128)(2,1)S(1)}, bf16[128,512]{1,0:T(8,128)(2,1)S(1)}, u32[]{:S(2)}, u32[]{:S(2)}) %collective-permute-start) | collective-permute-done | bytes 131104 | tf_op jit(solution)/shard_map/hop1_chunk1/ppermute | solution.py:542
  14.4 0.1 pass_kernel.9
  14.5 0.1 collective-permute-start.3
  14.5 0.1 collective-permute-start.2
  14.6 0.0 collective-permute-done.5.got_ref
  14.7 0.5 %collective-permute-start.8 = (bf16[128,512]{1,0:T(8,128)(2,1)S(1)}, bf16[128,512]{1,0:T(8,128)(2,1)S(1)}, u32[]{:S(2)}, u32[]{:S(2)}) collective-permute-start(bf16[128,512]{1,0:T(8,128)(2,1)S(1)} %get-tuple-element.100), channel_id=1, source_target_pairs={{0,1},{1,0},{2,3},{3,2},{4,5},{5,4},{6,7},{7,6},{8,12},{9,13},{10,... | collective-permute-start | bytes 393224 | tf_op jit(solution)/shard_map/hop3_chunk0/ppermute | solution.py:542
  15.2 1.4 %collective-permute-done.4.got_ref = bf16[128,512]{1,0:T(8,128)(2,1)S(1)} collective-permute-done((bf16[128,512]{1,0:T(8,128)(2,1)S(1)}, bf16[128,512]{1,0:T(8,128)(2,1)S(1)}, u32[]{:S(2)}, u32[]{:S(2)}) %collective-permute-start.4) | collective-permute-done | bytes 131104 | tf_op jit(solution)/shard_map/hop1_chunk2/ppermute | solution.py:542
  16.6 0.1 collective-permute-start.7
  16.7 0.0 collective-permute-done.3.got_ref.rest_1_
  16.8 2.8 %collective-permute-start.9 = (bf16[144,512]{1,0:T(8,128)(2,1)S(1)}, bf16[144,512]{1,0:T(8,128)(2,1)S(1)}, u32[]{:S(2)}, u32[]{:S(2)}) collective-permute-start(bf16[144,512]{1,0:T(8,128)(2,1)S(1)} %get-tuple-element.102), channel_id=1, source_target_pairs={{0,4},{1,5},{2,6},{3,7},{4,0},{5,1},{6,2},{7,3},{8,12},{9,13},{10,... | collective-permute-start | bytes 442376 | tf_op jit(solution)/shard_map/hop3_chunk1/ppermute | solution.py:542
  19.6 1.3 %collective-permute-done.2.got_ref = bf16[128,512]{1,0:T(8,128)(2,1)S(1)} collective-permute-done((bf16[128,512]{1,0:T(8,128)(2,1)S(1)}, bf16[128,512]{1,0:T(8,128)(2,1)S(1)}, u32[]{:S(2)}, u32[]{:S(2)}) %collective-permute-start.2) | collective-permute-done | bytes 131104 | tf_op jit(solution)/shard_map/hop1_chunk3/ppermute | solution.py:542
  20.9 0.1 collective-permute-start.6
  21.0 0.0 collective-permute-done.8.refs_0_.rest_0_
  21.0 0.0 collective-permute-done.7.got_ref
  21.1 0.5 %collective-permute-start.10 = (bf16[128,512]{1,0:T(8,128)(2,1)S(1)}, bf16[128,512]{1,0:T(8,128)(2,1)S(1)}, u32[]{:S(2)}, u32[]{:S(2)}) collective-permute-start(bf16[128,512]{1,0:T(8,128)(2,1)S(1)} %get-tuple-element.103.refs_1_), channel_id=1, source_target_pairs={{0,1},{1,0},{2,3},{3,2},{4,5},{5,4},{6,7},{7,6},{8,12},{9,13},{10,... | collective-permute-start | bytes 393224 | tf_op jit(solution)/shard_map/hop3_chunk2/ppermute | solution.py:542
  21.6 2.0 %collective-permute-done.9.refs_0_.rest_2_.rest_1_ = bf16[144,512]{1,0:T(8,128)(2,1)S(1)} collective-permute-done((bf16[144,512]{1,0:T(8,128)(2,1)S(1)}, bf16[144,512]{1,0:T(8,128)(2,1)S(1)}, u32[]{:S(2)}, u32[]{:S(2)}) %collective-permute-start.9) | collective-permute-done | bytes 147488 | tf_op jit(solution)/shard_map/hop3_chunk1/ppermute | solution.py:542
  23.6 0.0 collective-permute-done.6.got_ref
  23.7 0.1 collective-permute-start.11
  23.7 0.9 %ask_kernel.1 = (f32[16,2048]{1,0:T(8,128)S(1)}, f32[16,32]{1,0:T(8,128)S(1)}, bf16[16,256]{1,0:T(8,128)(2,1)S(1)}) custom-call(bf16[256,2048]{1,0:T(8,128)(2,1)S(1)} %get-tuple-element.63.x_ref, bf16[256,256]{1,0:T(8,128)(2,1)S(1)} %get-tuple-element.67.b_ref, f32[32,256]{1,0:T(8,128)S(1)} %get-tuple-element.62.cum_ref, ...), custom_call_target="tpu_custom_call" | custom-call | flops 1 | bytes 1 | tf_op jit(solution)/shard_map/ask_kernel/pallas_call | solution.py:561
  24.6 0.3 read_kernel.2
  24.9 4.6 %collective-permute-start.13 = (bf16[4,2048]{1,0:T(4,128)(2,1)S(1)}, bf16[4,2048]{1,0:T(4,128)(2,1)S(1)}, u32[]{:S(2)}, u32[]{:S(2)}) collective-permute-start(bf16[4,2048]{1,0:T(4,128)(2,1)S(1)} %get-tuple-element.114), channel_id=1, source_target_pairs={{0,8},{1,9},{2,10},{3,11},{4,5},{5,4},{6,7},{7,6},{8,0},{9,1},{10,... | collective-permute-start | bytes 49160 | tf_op jit(solution)/shard_map/ppermute | solution.py:542
  29.5 0.0 collective-permute-start.14
  29.5 0.6 %collective-permute-start.12 = (bf16[4,2048]{1,0:T(4,128)(2,1)S(1)}, bf16[4,2048]{1,0:T(4,128)(2,1)S(1)}, u32[]{:S(2)}, u32[]{:S(2)}) collective-permute-start(bf16[4,2048]{1,0:T(4,128)(2,1)S(1)} %get-tuple-element.109.refs_1_), channel_id=1, source_target_pairs={{0,4},{1,5},{2,6},{3,7},{4,0},{5,1},{6,2},{7,3},{8,9},{9,8},{10,11... | collective-permute-start | bytes 49160 | tf_op jit(solution)/shard_map/ppermute | solution.py:542
  30.1 0.0 collective-permute-done.10.refs_0_.rest_2_.rest_0_
  30.1 0.0 collective-permute-done.11.rest_3_.rest_1_
  30.1 0.3 read_kernel.3
  30.4 2.6 %collective-permute-start.15 = (bf16[4,2048]{1,0:T(4,128)(2,1)S(1)}, bf16[4,2048]{1,0:T(4,128)(2,1)S(1)}, u32[]{:S(2)}, u32[]{:S(2)}) collective-permute-start(bf16[4,2048]{1,0:T(4,128)(2,1)S(1)} %get-tuple-element.116), channel_id=1, source_target_pairs={{0,12},{1,13},{2,14},{3,15},{4,5},{5,4},{6,7},{7,6},{8,9},{9,8},{1... | collective-permute-start | bytes 49160 | tf_op jit(solution)/shard_map/ppermute | solution.py:542
  33.0 0.0 collective-permute-start.16
  33.0 0.0 collective-permute-done.13.refs_2_.rest_1_
  33.0 0.5 %collective-permute-start.17 = (bf16[4,2048]{1,0:T(4,128)(2,1)S(1)}, bf16[4,2048]{1,0:T(4,128)(2,1)S(1)}, u32[]{:S(2)}, u32[]{:S(2)}) collective-permute-start(bf16[4,2048]{1,0:T(4,128)(2,1)S(1)} %get-tuple-element.118), channel_id=1, source_target_pairs={{0,1},{1,0},{2,3},{3,2},{4,5},{5,4},{6,7},{7,6},{8,12},{9,13},{10,... | collective-permute-start | bytes 49160 | tf_op jit(solution)/shard_map/ppermute | solution.py:542
  33.5 0.6 %outer_kernel.2.rest_4_ = bf16[2,256,512]{2,1,0:T(8,128)(2,1)S(1)} custom-call(bf16[256,256]{1,0:T(8,128)(2,1)S(1)} %get-tuple-element.61.c_ref, f32[32,256]{1,0:T(8,128)S(1)} %get-tuple-element.62.cum_ref, bf16[4,128,512]{2,1,0:T(8,128)(2,1)S(1)} %get-tuple-element.104.carry_ref, bf16[128,512]{1,0:T(8,128)(2,1)S(1)} %collective-permute-done.8.refs_0_.rest_0_, ...), custom_call_target="tpu_custom_call" | custom-call | flops 1 | bytes 1 | tf_op jit(solution)/shard_map/outer_kernel/pallas_call | solution.py:583
  34.1 1.3 %outer_kernel.3 = (bf16[256,2048]{1,0:T(8,128)(2,1)}, f32[8,128]{1,0:T(8,128)S(1)}) custom-call(bf16[256,256]{1,0:T(8,128)(2,1)S(1)} %get-tuple-element.61.c_ref, f32[32,256]{1,0:T(8,128)S(1)} %get-tuple-element.62.cum_ref, bf16[4,128,512]{2,1,0:T(8,128)(2,1)S(1)} %get-tuple-element.104.carry_ref, ...), custom_call_target="tpu_custom_call" | custom-call | flops 1 | bytes 1 | tf_op jit(solution)/shard_map/outer_kernel/pallas_call | solution.py:583
  35.5 0.0 collective-permute-done.14.refs_3_.rest_2_
  35.5 0.0 collective-permute-done.12.refs_1_.rest_0_
  35.5 0.5 %collective-permute-done.15.rest_3_ = bf16[4,2048]{1,0:T(4,128)(2,1)S(1)} collective-permute-done((bf16[4,2048]{1,0:T(4,128)(2,1)S(1)}, bf16[4,2048]{1,0:T(4,128)(2,1)S(1)}, u32[]{:S(2)}, u32[]{:S(2)}) %collective-permute-start.15) | collective-permute-done | bytes 16416 | tf_op jit(solution)/shard_map/ppermute | solution.py:542
  36.0 0.0 collective-permute-done.16.rest_4_
  36.0 0.0 collective-permute-done.17.rest_5_
  36.0 0.7 %finish_kernel.1 = bf16[4,4,2048]{2,1,0:T(4,128)(2,1)} custom-call(f32[4,4,2048]{2,1,0:T(4,128)S(1)} %get-tuple-element.87.rest_4_.keep_ref, f32[4,4,2048]{2,1,0:T(4,128)S(1)} %get-tuple-element.112.fresh_ref, f32[4,4,128]{2,1,0:T(4,128)S(1)} %get-tuple-element.113.held_ref, bf16[4,2048]{1,0:T(4,128)(2,1)S(1)} %collective-permute-done.12.refs_1_.rest_0_, ...), custom_call_target="tpu_custom_call" | custom-call | flops 1 | bytes 1 | tf_op jit(solution)/shard_map/finish_kernel/pallas_call | solution.py:653
  (10 shorter events, 0.3 us)
Async XLA Ops:
  2.5 6.9 %collective-permute-start.1 = (bf16[144,512]{1,0:T(8,128)(2,1)S(1)}, bf16[144,512]{1,0:T(8,128)(2,1)S(1)}, u32[]{:S(2)}, u32[]{:S(2)}) collective-permute-start(bf16[144,512]{1,0:T(8,128)(2,1)S(1)} %get-tuple-element.73.rest_2_), channel_id=1, source_target_pairs={{0,4},{1,5},{2,6},{3,7},{4,0},{5,1},{6,2},{7,3},{8,12},{9,13},{10,... | collective-permute-start | bytes 442376 | tf_op jit(solution)/shard_map/hop1_chunk0/ppermute | solution.py:542
  8.8 5.6 %collective-permute-start = (bf16[128,512]{1,0:T(8,128)(2,1)S(1)}, bf16[128,512]{1,0:T(8,128)(2,1)S(1)}, u32[]{:S(2)}, u32[]{:S(2)}) collective-permute-start(bf16[128,512]{1,0:T(8,128)(2,1)S(1)} %get-tuple-element.70), channel_id=1, source_target_pairs={{0,4},{1,5},{2,6},{3,7},{4,0},{5,1},{6,2},{7,3},{8,9},{9,8},{10,11... | collective-permute-start | bytes 393224 | tf_op jit(solution)/shard_map/hop1_chunk1/ppermute | solution.py:542
  9.6 5.1 %collective-permute-start.5 = (bf16[128,512]{1,0:T(8,128)(2,1)S(1)}, bf16[128,512]{1,0:T(8,128)(2,1)S(1)}, u32[]{:S(2)}, u32[]{:S(2)}) collective-permute-start(bf16[128,512]{1,0:T(8,128)(2,1)S(1)} %get-tuple-element.86.rest_0_), channel_id=1, source_target_pairs={{0,1},{1,0},{2,3},{3,2},{4,8},{5,9},{6,10},{7,11},{8,4},{9,5},{10,... | collective-permute-start | bytes 393224 | tf_op jit(solution)/shard_map/hop2_chunk0/ppermute | solution.py:542
  9.6 7.0 %collective-permute-start.4 = (bf16[128,512]{1,0:T(8,128)(2,1)S(1)}, bf16[128,512]{1,0:T(8,128)(2,1)S(1)}, u32[]{:S(2)}, u32[]{:S(2)}) collective-permute-start(bf16[128,512]{1,0:T(8,128)(2,1)S(1)} %get-tuple-element.91), channel_id=1, source_target_pairs={{0,4},{1,5},{2,6},{3,7},{4,0},{5,1},{6,2},{7,3},{8,9},{9,8},{10,11... | collective-permute-start | bytes 393224 | tf_op jit(solution)/shard_map/hop1_chunk2/ppermute | solution.py:542
  14.5 2.3 %collective-permute-start.3 = (bf16[144,512]{1,0:T(8,128)(2,1)S(1)}, bf16[144,512]{1,0:T(8,128)(2,1)S(1)}, u32[]{:S(2)}, u32[]{:S(2)}) collective-permute-start(bf16[144,512]{1,0:T(8,128)(2,1)S(1)} %get-tuple-element.90.rest_0_), channel_id=1, source_target_pairs={{0,1},{1,0},{2,3},{3,2},{4,8},{5,9},{6,10},{7,11},{8,4},{9,5},{10,... | collective-permute-start | bytes 442376 | tf_op jit(solution)/shard_map/hop2_chunk1/ppermute | solution.py:542
  14.5 6.4 %collective-permute-start.2 = (bf16[128,512]{1,0:T(8,128)(2,1)S(1)}, bf16[128,512]{1,0:T(8,128)(2,1)S(1)}, u32[]{:S(2)}, u32[]{:S(2)}) collective-permute-start(bf16[128,512]{1,0:T(8,128)(2,1)S(1)} %get-tuple-element.88), channel_id=1, source_target_pairs={{0,4},{1,5},{2,6},{3,7},{4,0},{5,1},{6,2},{7,3},{8,9},{9,8},{10,11... | collective-permute-start | bytes 393224 | tf_op jit(solution)/shard_map/hop1_chunk3/ppermute | solution.py:542
  14.7 6.4 %collective-permute-start.8 = (bf16[128,512]{1,0:T(8,128)(2,1)S(1)}, bf16[128,512]{1,0:T(8,128)(2,1)S(1)}, u32[]{:S(2)}, u32[]{:S(2)}) collective-permute-start(bf16[128,512]{1,0:T(8,128)(2,1)S(1)} %get-tuple-element.100), channel_id=1, source_target_pairs={{0,1},{1,0},{2,3},{3,2},{4,5},{5,4},{6,7},{7,6},{8,12},{9,13},{10,... | collective-permute-start | bytes 393224 | tf_op jit(solution)/shard_map/hop3_chunk0/ppermute | solution.py:542
  16.6 4.4 %collective-permute-start.7 = (bf16[128,512]{1,0:T(8,128)(2,1)S(1)}, bf16[128,512]{1,0:T(8,128)(2,1)S(1)}, u32[]{:S(2)}, u32[]{:S(2)}) collective-permute-start(bf16[128,512]{1,0:T(8,128)(2,1)S(1)} %get-tuple-element.98), channel_id=1, source_target_pairs={{0,1},{1,0},{2,3},{3,2},{4,8},{5,9},{6,10},{7,11},{8,4},{9,5},{10,... | collective-permute-start | bytes 393224 | tf_op jit(solution)/shard_map/hop2_chunk2/ppermute | solution.py:542
  16.8 6.8 %collective-permute-start.9 = (bf16[144,512]{1,0:T(8,128)(2,1)S(1)}, bf16[144,512]{1,0:T(8,128)(2,1)S(1)}, u32[]{:S(2)}, u32[]{:S(2)}) collective-permute-start(bf16[144,512]{1,0:T(8,128)(2,1)S(1)} %get-tuple-element.102), channel_id=1, source_target_pairs={{0,4},{1,5},{2,6},{3,7},{4,0},{5,1},{6,2},{7,3},{8,12},{9,13},{10,... | collective-permute-start | bytes 442376 | tf_op jit(solution)/shard_map/hop3_chunk1/ppermute | solution.py:542
  20.9 2.7 %collective-permute-start.6 = (bf16[128,512]{1,0:T(8,128)(2,1)S(1)}, bf16[128,512]{1,0:T(8,128)(2,1)S(1)}, u32[]{:S(2)}, u32[]{:S(2)}) collective-permute-start(bf16[128,512]{1,0:T(8,128)(2,1)S(1)} %get-tuple-element.97.refs_1_), channel_id=1, source_target_pairs={{0,1},{1,0},{2,3},{3,2},{4,8},{5,9},{6,10},{7,11},{8,4},{9,5},{10,... | collective-permute-start | bytes 393224 | tf_op jit(solution)/shard_map/hop2_chunk3/ppermute | solution.py:542
  21.1 9.0 %collective-permute-start.10 = (bf16[128,512]{1,0:T(8,128)(2,1)S(1)}, bf16[128,512]{1,0:T(8,128)(2,1)S(1)}, u32[]{:S(2)}, u32[]{:S(2)}) collective-permute-start(bf16[128,512]{1,0:T(8,128)(2,1)S(1)} %get-tuple-element.103.refs_1_), channel_id=1, source_target_pairs={{0,1},{1,0},{2,3},{3,2},{4,5},{5,4},{6,7},{7,6},{8,12},{9,13},{10,... | collective-permute-start | bytes 393224 | tf_op jit(solution)/shard_map/hop3_chunk2/ppermute | solution.py:542
  23.7 6.5 %collective-permute-start.11 = (bf16[128,512]{1,0:T(8,128)(2,1)S(1)}, bf16[128,512]{1,0:T(8,128)(2,1)S(1)}, u32[]{:S(2)}, u32[]{:S(2)}) collective-permute-start(bf16[128,512]{1,0:T(8,128)(2,1)S(1)} %get-tuple-element.105.rest_3_), channel_id=1, source_target_pairs={{0,1},{1,0},{2,3},{3,2},{4,5},{5,4},{6,7},{7,6},{8,12},{9,13},{10,... | collective-permute-start | bytes 393224 | tf_op jit(solution)/shard_map/hop3_chunk3/ppermute | solution.py:542
  24.9 8.1 %collective-permute-start.13 = (bf16[4,2048]{1,0:T(4,128)(2,1)S(1)}, bf16[4,2048]{1,0:T(4,128)(2,1)S(1)}, u32[]{:S(2)}, u32[]{:S(2)}) collective-permute-start(bf16[4,2048]{1,0:T(4,128)(2,1)S(1)} %get-tuple-element.114), channel_id=1, source_target_pairs={{0,8},{1,9},{2,10},{3,11},{4,5},{5,4},{6,7},{7,6},{8,0},{9,1},{10,... | collective-permute-start | bytes 49160 | tf_op jit(solution)/shard_map/ppermute | solution.py:542
  29.5 6.0 %collective-permute-start.14 = (bf16[4,2048]{1,0:T(4,128)(2,1)S(1)}, bf16[4,2048]{1,0:T(4,128)(2,1)S(1)}, u32[]{:S(2)}, u32[]{:S(2)}) collective-permute-start(bf16[4,2048]{1,0:T(4,128)(2,1)S(1)} %get-tuple-element.115), channel_id=1, source_target_pairs={{0,1},{1,0},{2,3},{3,2},{4,8},{5,9},{6,10},{7,11},{8,4},{9,5},{10,... | collective-permute-start | bytes 49160 | tf_op jit(solution)/shard_map/ppermute | solution.py:542
  29.5 6.0 %collective-permute-start.12 = (bf16[4,2048]{1,0:T(4,128)(2,1)S(1)}, bf16[4,2048]{1,0:T(4,128)(2,1)S(1)}, u32[]{:S(2)}, u32[]{:S(2)}) collective-permute-start(bf16[4,2048]{1,0:T(4,128)(2,1)S(1)} %get-tuple-element.109.refs_1_), channel_id=1, source_target_pairs={{0,4},{1,5},{2,6},{3,7},{4,0},{5,1},{6,2},{7,3},{8,9},{9,8},{10,11... | collective-permute-start | bytes 49160 | tf_op jit(solution)/shard_map/ppermute | solution.py:542
  30.4 5.6 %collective-permute-start.15 = (bf16[4,2048]{1,0:T(4,128)(2,1)S(1)}, bf16[4,2048]{1,0:T(4,128)(2,1)S(1)}, u32[]{:S(2)}, u32[]{:S(2)}) collective-permute-start(bf16[4,2048]{1,0:T(4,128)(2,1)S(1)} %get-tuple-element.116), channel_id=1, source_target_pairs={{0,12},{1,13},{2,14},{3,15},{4,5},{5,4},{6,7},{7,6},{8,9},{9,8},{1... | collective-permute-start | bytes 49160 | tf_op jit(solution)/shard_map/ppermute | solution.py:542
  33.0 3.0 %collective-permute-start.16 = (bf16[4,2048]{1,0:T(4,128)(2,1)S(1)}, bf16[4,2048]{1,0:T(4,128)(2,1)S(1)}, u32[]{:S(2)}, u32[]{:S(2)}) collective-permute-start(bf16[4,2048]{1,0:T(4,128)(2,1)S(1)} %get-tuple-element.117), channel_id=1, source_target_pairs={{0,1},{1,0},{2,3},{3,2},{4,12},{5,13},{6,14},{7,15},{8,9},{9,8},{1... | collective-permute-start | bytes 49160 | tf_op jit(solution)/shard_map/ppermute | solution.py:542
  33.0 3.0 %collective-permute-start.17 = (bf16[4,2048]{1,0:T(4,128)(2,1)S(1)}, bf16[4,2048]{1,0:T(4,128)(2,1)S(1)}, u32[]{:S(2)}, u32[]{:S(2)}) collective-permute-start(bf16[4,2048]{1,0:T(4,128)(2,1)S(1)} %get-tuple-element.118), channel_id=1, source_target_pairs={{0,1},{1,0},{2,3},{3,2},{4,5},{5,4},{6,7},{7,6},{8,12},{9,13},{10,... | collective-permute-start | bytes 49160 | tf_op jit(solution)/shard_map/ppermute | solution.py:542

commit v13 on v12

--- a/solution.py
+++ b/solution.py
@@ -19,7 +19,7 @@
 BF16 = jnp.bfloat16
 CHUNKS = 4
 TOKEN_COST = 10**8
-PASS_COST = 5 * 10**8
+PASS_COST = 8 * 10**8
 VMEM_LIMIT = 32 * 1024 * 1024
 
 
@@ -88,19 +88,17 @@
     return jnp.where(keep(row, column), 1.0, 0.0).astype(BF16)
 
 
-def chunk_total(k, x_ref, turned, weight, whole, total_ref, decay_ref):
+def chunk_total(first, x_ref, turned, weight, total_ref):
     width = total_ref.shape[1]
-    first = k * width
     scaled = x_ref[:, first : first + width].astype(F32) * over_lanes(weight, first, width)
     total_ref[...] = dot(turned, scaled.astype(BF16))
-    decay_ref[...] = over_lanes(whole, first, width, 3)
 
 
 def first_kernel(kept, *refs):
     hbm, refs = refs[: kept + 1], refs[kept + 1 :]
     here, refs = refs[:kept], refs[kept:]
-    cum_ref, row_ref, weight_ref, whole_ref, turned_ref = refs[:5]
-    total_ref, decay_ref, sent_ref, dt_ref, sems = refs[5:]
+    cum_ref, row_ref, weight_ref, whole_ref = refs[:4]
+    total_ref, sent_ref, dt_ref, sems = refs[4:]
     x_ref, b_ref, a_ref = here[:3]
     heads, tokens = dt_ref.shape
     spans = tokens // SPAN
@@ -136,11 +134,8 @@
     copies[0].wait()
     turned = b_ref[:, :N].astype(F32).T.astype(BF16)
     x_copies[0].wait()
-    chunk_total(0, x_ref, turned, weight, whole, total_ref, decay_ref)
+    chunk_total(0, x_ref, turned, weight, total_ref)
     sent_ref[:N] = total_ref[...].astype(BF16)
-    turned_ref[0] = turned
-    for g in range(1, turned_ref.shape[0]):
-        turned_ref[g] = b_ref[:, g * N : (g + 1) * N].astype(F32).T.astype(BF16)
     cum = jnp.concatenate(cums, axis=1)
     cum_ref[...] = cum
     row_ref[...] = jnp.log2(step) - cum
@@ -149,16 +144,25 @@
         copy.wait()
     if sent_ref.shape[0] > N:
         own = flat(here[3]).astype(BF16)
-        sent_ref[N:] = jnp.concatenate([own, own], axis=1)
-
-
-def state_kernel(part, x_ref, turned_ref, weight_ref, whole_ref, *rest):
-    results = rest[-2 * len(part) - 1 :]
-    for i, k in enumerate(part):
-        total_ref, decay_ref = results[2 * i : 2 * i + 2]
-        g = k * total_ref.shape[1] // (H // G * P_SIZE)
-        chunk_total(k, x_ref, turned_ref[g], weight_ref[...], whole_ref[...], total_ref, decay_ref)
-    results[-1][...] = results[0][...].astype(BF16)
+        padding = jnp.zeros((own.shape[0], sent_ref.shape[1] - own.shape[1]), BF16)
+        sent_ref[N:] = jnp.concatenate([own, padding], axis=1)
+
+
+def state_kernel(bounds, x_ref, b_ref, weight_ref, whole_ref, *rest):
+    chunks = len(bounds) - 1
+    results = rest[-2 * chunks :]
+    decay_refs, total_refs, sent_ref = results[:chunks], results[chunks:-1], results[-1]
+    turned = [
+        b_ref[:, g * N : (g + 1) * N].astype(F32).T.astype(BF16)
+        for g in range(b_ref.shape[1] // N)
+    ]
+    for k in range(chunks):
+        first = bounds[k]
+        decay_refs[k][...] = over_lanes(whole_ref[...], first, bounds[k + 1] - first, 3)
+        if k:
+            g = first // (H // G * P_SIZE)
+            chunk_total(first, x_ref, turned[g], weight_ref[...], total_refs[k - 1])
+    sent_ref[...] = total_refs[0][...].astype(BF16)
 
 
 def flat(ref):
@@ -169,10 +173,11 @@
     refs[-1][...] = jnp.zeros_like(refs[-1])
 
 
-def pass_kernel(hop, k, more, got_ref, total_ref, decay_ref, *rest):
+def pass_kernel(hop, first, more, got_ref, total_ref, decay_ref, *rest):
     moving_ref, carry_ref = rest[len(rest) - 2 - more : len(rest) - more]
     me = lax.axis_index("seq")
-    if hop == 1 and k == 0:
+    groups = carry_ref.shape[1] // (H // G * P_SIZE)
+    if hop == 1 and first == 0:
         following_ref = rest[0]
         carry_ref[...] = jnp.zeros_like(carry_ref)
     else:
@@ -180,16 +185,18 @@
     got = got_ref[:N]
     moving_ref[:N] = (total_ref[...] + decay_ref[...] * got.astype(F32)).astype(BF16)
     if moving_ref.shape[0] > N and hop == 1:
-        own, other = [ref[N:].astype(F32) for ref in rest[1 + more : 3 + more]]
-        lane = lax.broadcasted_iota(jnp.int32, own.shape, 1)
-        mine = (lane // (own.shape[1] // 2)) == lax.rem(me, 2)
-        moving_ref[N:] = jnp.where(mine, own, other).astype(BF16)
+        names = groups * N
+        own, other = [ref[N:, :names].astype(F32) for ref in rest[1 + more : 3 + more]]
+        even = lax.rem(me, 2) == 0
+        padding = jnp.zeros((own.shape[0], moving_ref.shape[1] - 2 * names), F32)
+        pair = [jnp.where(even, own, other), jnp.where(even, other, own), padding]
+        moving_ref[N:] = jnp.concatenate(pair, axis=1).astype(BF16)
     elif moving_ref.shape[0] > N:
         moving_ref[N:] = got_ref[N:]
 
     @pl.when(me == hop)
     def _():
-        carry_ref[k] = got
+        carry_ref[:, first : first + got.shape[1]] = got
 
     if more:
         rest[-1][...] = following_ref[...].astype(BF16)
@@ -267,7 +274,7 @@
         near, middle, far = [ref[N:].astype(F32) for ref in rest[:3]]
         far = jnp.where((me == 1) | (me == 2), middle, far)
         halves = (jnp.where(me < 2, near, far), jnp.where(me < 2, far, near))
-        names = near.shape[1] // 2
+        names = b_ref.shape[1]
         blocks = [half[:, i * names : (i + 1) * names] for half in halves for i in range(2)]
         blocks = jnp.concatenate(blocks, axis=0).astype(BF16)
         row = lax.broadcasted_iota(jnp.int32, (asks, blocks.shape[0]), 0)
@@ -315,17 +322,17 @@
             local_ref[:, lanes] = dot(jnp.concatenate(parts, axis=1), right)
 
 
-def read_kernel(count, chunks, ops, final, local_ref, gain_ref, asked_ref, carry_ref, *rest):
+def read_kernel(count, bounds, ops, final, local_ref, gain_ref, asked_ref, carry_ref, *rest):
+    chunks = len(bounds) - 1
     got_refs, rest = rest[: chunks * final], rest[chunks * final :]
     read_refs = rest[-(len(ops) + final) :]
     me = lax.axis_index("seq")
-    lanes = local_ref.shape[1]
-    width = lanes // chunks
     for k in range(chunks):
-        first = k * width
+        first = bounds[k]
+        width = bounds[k + 1] - first
         here = slice(first, first + width)
         g = first // (H // G * P_SIZE)
-        state = carry_ref[k]
+        state = carry_ref[:, here]
         if final:
             state = jnp.where(me == count - 1, got_refs[k][:N], state)
         carried = dot(asked_ref[:, g * N : (g + 1) * N], state)
@@ -346,7 +353,7 @@
             read_refs[-1][:, here] = own
 
 
-def outer_kernel(parts, count, c_ref, cum_ref, carry_ref, *rest):
+def outer_kernel(parts, bounds, count, c_ref, cum_ref, carry_ref, *rest):
     final = len(parts) > 1
     part = parts[-1]
     got_refs = rest[: len(part)]
@@ -358,18 +365,16 @@
         out_ref = rest[-1]
     heads, tokens = cum_ref.shape
     spans = tokens // SPAN
-    width = got_refs[0].shape[1]
     group_lanes = H // G * P_SIZE
     copies = []
 
-    def send(source, k):
-        lanes = slice(k * width, (k + 1) * width)
-        copies.append(pltpu.make_async_copy(source, out_hbm.at[:, lanes], sems.at[k]))
+    def send(source, first, width):
+        lanes = slice(first, first + width)
+        copies.append(pltpu.make_async_copy(source, out_hbm.at[:, lanes], sems.at[len(copies)]))
         copies[-1].start()
 
     if final:
-        for i, k in enumerate(parts[0]):
-            send(early_ref.at[i], k)
+        send(early_ref, 0, early_ref.shape[1])
     last = lax.axis_index("seq") == count - 1
     start = jnp.zeros((heads, 1), F32)
     gains = []
@@ -379,14 +384,16 @@
         start = start + cum[:, SPAN - 1 : SPAN]
     gain = jnp.concatenate(gains, axis=1).T
     for i, k in enumerate(part):
-        first = k * width
+        first = bounds[k]
+        width = bounds[k + 1] - first
         g = first // group_lanes
-        state = jnp.where(last, got_refs[i][:N], carry_ref[k])
+        state = jnp.where(last, got_refs[i][:N], carry_ref[:, first : first + width])
         carried = dot(c_ref[:, g * N : (g + 1) * N], state)
         inner = inner_refs[g][:, first - g * group_lanes : first - g * group_lanes + width]
-        out_ref[i] = (inner + over_lanes(gain, first, width) * carried).astype(BF16)
+        here = slice(first - bounds[part[0]], first - bounds[part[0]] + width)
+        out_ref[:, here] = (inner + over_lanes(gain, first, width) * carried).astype(BF16)
         if final:
-            send(out_ref.at[i], k)
+            send(out_ref.at[:, here], first, width)
     for copy in copies:
         copy.wait()
 
@@ -473,14 +480,17 @@
     group_lanes = lanes // groups
     rows = count * STEPS
     chunks = CHUNKS if count <= 4 else groups
-    width = lanes // chunks
+    bounds = tuple(lanes * k // chunks for k in range(chunks + 1))
+    if chunks > groups:
+        bounds = bounds[:1] + (bounds[1] - 128,) + bounds[2:]
+    widths = [bounds[k + 1] - bounds[k] for k in range(chunks)]
     anywhere = pl.BlockSpec(memory_space=pl.ANY)
     in_hbm = pl.BlockSpec(memory_space=pltpu.HBM)
     in_vmem = pl.BlockSpec(memory_space=pltpu.VMEM)
-    ride = count == 4 and width == 2 * names
+    ride = count == 4 and widths[0] >= names and widths[1] >= 2 * names
 
     def sent_shape(hop, k):
-        return shape((N + rows * (ride and (hop, k) in ((1, 0), (2, 1), (3, 1))), width), BF16)
+        return shape((N + rows * (ride and (hop, k) in ((1, 0), (2, 1), (3, 1))), widths[k]), BF16)
 
     inputs = [
         ssm_input,
@@ -495,7 +505,8 @@
         dec_b[0],
         dec_dt[0],
     ]
-    chunk_shapes = (shape((N, width)), shape((1, width)))
+    total_shapes = tuple(shape((N, width)) for width in widths)
+    decay_shapes = tuple(shape((1, width)) for width in widths)
     results = call(
         functools.partial(first_kernel, len(inputs)),
         tuple(shape(value.shape, value.dtype) for value in inputs)
@@ -504,10 +515,9 @@
             shape((heads, tokens)),
             shape((tokens, heads)),
             shape((1, heads)),
-            shape((groups, N, tokens), BF16),
-        )
-        + chunk_shapes
-        + (sent_shape(1, 0),),
+            total_shapes[0],
+            sent_shape(1, 0),
+        ),
         in_specs=[in_hbm] * (len(inputs) + 1),
         scratch_shapes=[
             pltpu.VMEM((heads, tokens), BF16),
@@ -515,20 +525,16 @@
         ],
     )(*[pinned(value, pltpu.HBM) for value in inputs + [dt_raw.T]])
     x, b, a_row, asked_here, c, d_row, len_row, owner_row, x_dec, b_dec, dt_dec = results[:11]
-    cum, row, weight, whole, turned = results[11:16]
-    total, decay = [results[16]], [results[17]]
+    cum, row, weight, whole = results[11:15]
+    total, sent = [results[15]], {0: results[16]}
     all_asked = None if ride else lax.all_gather(dec_c[0], "seq")
-    sent = {0: results[18]}
-
-    def state_part(part, tie):
-        out = call(
-            functools.partial(state_kernel, part),
-            chunk_shapes * len(part) + (sent_shape(1, 1),),
+
+    def state_part(tie):
+        return call(
+            functools.partial(state_kernel, bounds),
+            decay_shapes + total_shapes[1:] + (sent_shape(1, 1),),
             in_specs=[in_vmem] * 4 + [anywhere],
-        )(x, turned, weight, whole, tie)
-        total.extend(out[0 : 2 * len(part) : 2])
-        decay.extend(out[1 : 2 * len(part) : 2])
-        return out[-1]
+        )(x, b, weight, whole, tie)
 
     def swap(value, *couples):
         partner = {}
@@ -578,10 +584,10 @@
 
     def outer_part(parts, carry, before, *after):
         part = parts[-1]
-        out = shape((len(part), tokens, width), BF16)
+        out = shape((tokens, sum(widths[k] for k in part)), BF16)
         operands = [c, cum, carry, *[got[count - 1, k] for k in part], *inner, *before]
         return call(
-            functools.partial(outer_kernel, parts, count),
+            functools.partial(outer_kernel, parts, bounds, count),
             (pltpu.HBM((tokens, lanes), BF16), shape((8, 128))) if before else out,
             in_specs=[in_vmem] * len(operands) + [anywhere] * len(after),
             out_specs=(in_hbm, in_vmem) if before else in_vmem,
@@ -592,7 +598,7 @@
         arrived = [got[count - 1, k] for k in range(chunks)] if final else []
         operands = [local, gain, asked, carry, *arrived]
         return call(
-            functools.partial(read_kernel, count, chunks, ops, final),
+            functools.partial(read_kernel, count, bounds, ops, final),
             (shape((STEPS, lanes), BF16),) * len(ops) + (shape((STEPS, lanes)),) * final,
             in_specs=[in_vmem] * len(operands) + [anywhere] * len(after),
         )(*operands, *after)
@@ -601,7 +607,8 @@
     inner = [inner_part(0)]
     for g in range(1, groups):
         inner.append(inner_part(g, inner[-1]))
-    sent[1] = state_part(list(range(1, chunks)), inner[-1])
+    *parts, sent[1] = state_part(inner[-1])
+    decay, total = parts[:chunks], total + parts[chunks:]
     got[1, 1] = forward(sent[1], 1, 1)
     order = sorted((k + hop, hop, k) for hop in range(1, count - 1) for k in range(chunks))
     moving = {}
@@ -616,11 +623,11 @@
             keep, fresh, held = fresh_part(tie)
             after = [keep]
         if hop == count - 2 and k > 1:
-            after = [token(got[hop + 1, k - 2], tie, flops=TOKEN_COST)]
+            after = [token(got[hop + 1, k - 2], tie, flops=5 * TOKEN_COST)]
         tie, carry, *following = call(
-            functools.partial(pass_kernel, hop, k, more),
-            (sent_shape(hop + 1, k), shape((chunks, N, width), BF16))
-            + (sent_shape(1, k + 2),) * more,
+            functools.partial(pass_kernel, hop, bounds[k], more),
+            (sent_shape(hop + 1, k), shape((N, lanes), BF16))
+            + ((sent_shape(1, k + 2),) if more else ()),
             flops=PASS_COST if k % 2 == 0 else 1,
             in_specs=[in_vmem] * len(operands) + [anywhere] * len(after),
             input_output_aliases={} if carry is None else {3: 1},
@@ -638,7 +645,7 @@
         reading = read_part(ops, False)
         for couple, value in zip(ops, reading):
             back.append(swap(value, couple))
-    ends = [(0, 3), (1, 3), (2, 3)] if four else list(range(1, count))
+    ends = [(0, 3), (2, 3), (1, 3)] if four else list(range(1, count))
     before = reading[0] if four else asked
     order_token = token(got[count - 1, chunks - 2], before, flops=TOKEN_COST)
     *reading, mine = read_part(ends, True, order_token)

time: 37 us -> 37.7 us (1.019)
  waiting for transfers between devices: 6.93 us -> 9.62 us
  starting transfers between devices: 19 us -> 16.8 us
    ppermute x18, waiting for transfers between devices: 6.93 us -> 9.62 us  [swap(): return lax.ppermute(value, ('seq', 'tp'), pairs)]
    ppermute x18, starting transfers between devices: 19 us -> 16.8 us  [swap(): return lax.ppermute(value, ('seq', 'tp'), pairs)]
  transfers between devices with their start and end apart: 18 -> 18, of which waited for: 6 -> 5; matrix products, arithmetic and copies ran while one was open for 0% -> 0% of each run, Pallas kernels for 20% -> 20%
where the time goes in v13:
time: 37.7 us; the launch traced here: 37.5 us
  starting transfers between devices  16.8 us (45%)
  Pallas kernels  10.2 us (27%)
  waiting for transfers between devices  9.62 us (26%)
  between operations  0.86 us (2%)
    ppermute x18, starting transfers between devices, swap(): return lax.ppermute(value, ('seq', 'tp'), pairs)  16.8 us
    ppermute x18, waiting for transfers between devices, swap(): return lax.ppermute(value, ('seq', 'tp'), pairs)  9.62 us
    pallas_call x2, Pallas kernels, inner_part(): call(functools.partial(inner_kernel, g), shape((tokens, group_lanes)), in...  2.15 us
    pallas_call x2, Pallas kernels, outer_part(): call(functools.partial(outer_kernel, parts, bounds, count), (pltpu.HBM((t...  2.05 us
    pallas_call x1, Pallas kernels, shards(): call(functools.partial(first_kernel, len(inputs)), tuple((shape(value.sha...  1.89 us
    pallas_call x1, Pallas kernels, state_part(): call(functools.partial(state_kernel, bounds), decay_shapes + total_shapes...  1.17 us
    pallas_call x1, Pallas kernels, ask_part(): call(functools.partial(ask_kernel, ride), (shape((rows, lanes)), shape((r...  0.92 us
  transfers between devices with their start and end apart: 18, of which 5 were waited for; matrix products, arithmetic and copies ran while one was open for 0% of the time, Pallas kernels for 20%

profile of v13, /device:TPU:0, one launch (start us, length us, event | category | flops | bytes accessed | tf_op | source)
XLA Modules:
  0.0 37.5 jit_solution(15441827596137766944)
XLA Ops:
  0.6 1.9 %first_kernel.1 = (bf16[256,2048]{1,0:T(8,128)(2,1)S(1)}, bf16[256,256]{1,0:T(8,128)(2,1)S(1)}, f32[1,32]{1,0:T(1,128)S(1)}, bf16[4,4,256]{2,1,0:T(4,128)(2,1)S(...) custom-call(bf16[256,2048]{1,0:T(8,128)(2,1)} %refs_0_.1, ...), custom_call_target="tpu_custom_call" | custom-call | flops 1 | bytes 1 | tf_op jit(solution)/shard_map/first_kernel/pallas_call | solution.py:510
  2.5 3.1 %collective-permute-start.1 = (bf16[144,384]{1,0:T(8,128)(2,1)S(1)}, bf16[144,384]{1,0:T(8,128)(2,1)S(1)}, u32[]{:S(2)}, u32[]{:S(2)}) collective-permute-start(bf16[144,384]{1,0:T(8,128)(2,1)S(1)} %get-tuple-element.71.rest_2_), channel_id=1, source_target_pairs={{0,4},{1,5},{2,6},{3,7},{4,0},{5,1},{6,2},{7,3},{8,12},{9,13},{10,... | collective-permute-start | bytes 331784 | tf_op jit(solution)/shard_map/hop1_chunk0/ppermute | solution.py:548
  5.6 1.1 %inner_kernel.2.rest_0_.rest_2_ = f32[256,1024]{1,0:T(8,128)S(1)} custom-call(bf16[256,2048]{1,0:T(8,128)(2,1)S(1)} %get-tuple-element.62.x_ref, bf16[256,256]{1,0:T(8,128)(2,1)S(1)} %get-tuple-element.63.b_ref, bf16[256,256]{1,0:T(8,128)(2,1)S(1)} %get-tuple-element.60.c_ref, f32[32,256]{1,0:T(8,128)S(1)} %get-tuple-element.61.cum_ref, ...), custom_call_target="tpu_custom_call" | custom-call | flops 1 | bytes 1 | tf_op jit(solution)/shard_map/inner_kernel/pallas_call | solution.py:559
  6.7 1.1 %inner_kernel.3.rest_0_.rest_3_ = f32[256,1024]{1,0:T(8,128)S(1)} custom-call(bf16[256,2048]{1,0:T(8,128)(2,1)S(1)} %get-tuple-element.62.x_ref, bf16[256,256]{1,0:T(8,128)(2,1)S(1)} %get-tuple-element.63.b_ref, bf16[256,256]{1,0:T(8,128)(2,1)S(1)} %get-tuple-element.60.c_ref, f32[32,256]{1,0:T(8,128)S(1)} %get-tuple-element.61.cum_ref, ...), custom_call_target="tpu_custom_call" | custom-call | flops 1 | bytes 1 | tf_op jit(solution)/shard_map/inner_kernel/pallas_call | solution.py:559
  7.8 1.2 %state_kernel.1 = (f32[1,384]{1,0:T(1,128)S(1)}, f32[1,640]{1,0:T(1,128)S(1)}, f32[1,512]{1,0:T(1,128)S(1)}, f32[1,512]{1,0:T(1,128)S(1)}, f32[128,640]{1,0:T(8,...) custom-call(bf16[256,2048]{1,0:T(8,128)(2,1)S(1)} %get-tuple-element.62.x_ref, ...), custom_call_target="tpu_custom_call" | custom-call | flops 1 | bytes 1 | tf_op jit(solution)/shard_map/state_kernel/pallas_call | solution.py:533
  8.9 0.1 collective-permute-start
  9.0 0.0 collective-permute-done.1.got_ref.rest_3_
  9.0 0.1 pass_kernel.8
  9.1 0.1 collective-permute-start.5
  9.2 3.1 %collective-permute-start.4 = (bf16[128,512]{1,0:T(8,128)(2,1)S(1)}, bf16[128,512]{1,0:T(8,128)(2,1)S(1)}, u32[]{:S(2)}, u32[]{:S(2)}) collective-permute-start(bf16[128,512]{1,0:T(8,128)(2,1)S(1)} %get-tuple-element.89), channel_id=1, source_target_pairs={{0,4},{1,5},{2,6},{3,7},{4,0},{5,1},{6,2},{7,3},{8,9},{9,8},{10,11... | collective-permute-start | bytes 393224 | tf_op jit(solution)/shard_map/hop1_chunk2/ppermute | solution.py:548
  12.3 0.4 %fresh_kernel.1 = (f32[4,4,2048]{2,1,0:T(4,128)S(1)}, f32[4,4,2048]{2,1,0:T(4,128)S(1)}, f32[4,4,128]{2,1,0:T(4,128)S(1)}) custom-call(bf16[4,4,2048]{2,1,0:T(4,128)(2,1)S(1)} %get-tuple-element.77.x_ref, bf16[4,4,256]{2,1,0:T(4,128)(2,1)S(1)} %get-tuple-element.78.b_ref, bf16[4,4,256]{2,1,0:T(4,128)(2,1)S(1)} %get-tuple-element.79.c_ref, ...), custom_call_target="tpu_custom_call" | custom-call | flops 1 | bytes 1 | tf_op jit(solution)/shard_map/fresh_kernel/pallas_call | solution.py:579
  12.8 3.2 %collective-permute-done.got_ref = bf16[128,640]{1,0:T(8,128)(2,1)S(1)} collective-permute-done((bf16[128,640]{1,0:T(8,128)(2,1)S(1)}, bf16[128,640]{1,0:T(8,128)(2,1)S(1)}, u32[]{:S(2)}, u32[]{:S(2)}) %collective-permute-start) | collective-permute-done | bytes 163872 | tf_op jit(solution)/shard_map/hop1_chunk1/ppermute | solution.py:548
  16.0 0.1 pass_kernel.9
  16.1 0.1 collective-permute-start.3
  16.1 0.1 collective-permute-start.2
  16.2 0.0 collective-permute-done.5.got_ref
  16.3 0.5 %collective-permute-start.8 = (bf16[128,384]{1,0:T(8,128)(2,1)S(1)}, bf16[128,384]{1,0:T(8,128)(2,1)S(1)}, u32[]{:S(2)}, u32[]{:S(2)}) collective-permute-start(bf16[128,384]{1,0:T(8,128)(2,1)S(1)} %get-tuple-element.98), channel_id=1, source_target_pairs={{0,1},{1,0},{2,3},{3,2},{4,5},{5,4},{6,7},{7,6},{8,12},{9,13},{10,... | collective-permute-start | bytes 294920 | tf_op jit(solution)/shard_map/hop3_chunk0/ppermute | solution.py:548
  16.7 0.7 %collective-permute-done.4.got_ref = bf16[128,512]{1,0:T(8,128)(2,1)S(1)} collective-permute-done((bf16[128,512]{1,0:T(8,128)(2,1)S(1)}, bf16[128,512]{1,0:T(8,128)(2,1)S(1)}, u32[]{:S(2)}, u32[]{:S(2)}) %collective-permute-start.4) | collective-permute-done | bytes 131104 | tf_op jit(solution)/shard_map/hop1_chunk2/ppermute | solution.py:548
  17.5 0.1 collective-permute-start.7
  17.6 0.0 collective-permute-done.3.got_ref.rest_1_
  17.6 0.1 pass_kernel.12
  17.7 3.7 %collective-permute-start.9 = (bf16[144,640]{1,0:T(8,128)(2,1)S(1)}, bf16[144,640]{1,0:T(8,128)(2,1)S(1)}, u32[]{:S(2)}, u32[]{:S(2)}) collective-permute-start(bf16[144,640]{1,0:T(8,128)(2,1)S(1)} %get-tuple-element.100), channel_id=1, source_target_pairs={{0,4},{1,5},{2,6},{3,7},{4,0},{5,1},{6,2},{7,3},{8,12},{9,13},{10,... | collective-permute-start | bytes 552968 | tf_op jit(solution)/shard_map/hop3_chunk1/ppermute | solution.py:548
  21.3 1.2 %collective-permute-done.2.got_ref = bf16[128,512]{1,0:T(8,128)(2,1)S(1)} collective-permute-done((bf16[128,512]{1,0:T(8,128)(2,1)S(1)}, bf16[128,512]{1,0:T(8,128)(2,1)S(1)}, u32[]{:S(2)}, u32[]{:S(2)}) %collective-permute-start.2) | collective-permute-done | bytes 131104 | tf_op jit(solution)/shard_map/hop1_chunk3/ppermute | solution.py:548
  22.5 0.1 collective-permute-start.6
  22.6 0.0 collective-permute-done.8.refs_0_.rest_0_
  22.6 0.0 collective-permute-done.7.got_ref
  22.7 0.5 %collective-permute-start.10 = (bf16[128,512]{1,0:T(8,128)(2,1)S(1)}, bf16[128,512]{1,0:T(8,128)(2,1)S(1)}, u32[]{:S(2)}, u32[]{:S(2)}) collective-permute-start(bf16[128,512]{1,0:T(8,128)(2,1)S(1)} %get-tuple-element.101.refs_1_), channel_id=1, source_target_pairs={{0,1},{1,0},{2,3},{3,2},{4,5},{5,4},{6,7},{7,6},{8,12},{9,13},{10,... | collective-permute-start | bytes 393224 | tf_op jit(solution)/shard_map/hop3_chunk2/ppermute | solution.py:548
  23.2 2.8 %collective-permute-done.9.refs_0_.rest_2_.rest_1_ = bf16[144,640]{1,0:T(8,128)(2,1)S(1)} collective-permute-done((bf16[144,640]{1,0:T(8,128)(2,1)S(1)}, bf16[144,640]{1,0:T(8,128)(2,1)S(1)}, u32[]{:S(2)}, u32[]{:S(2)}) %collective-permute-start.9) | collective-permute-done | bytes 184352 | tf_op jit(solution)/shard_map/hop3_chunk1/ppermute | solution.py:548
  26.0 0.0 collective-permute-done.6.got_ref
  26.0 0.1 collective-permute-start.11
  26.1 0.9 %ask_kernel.1 = (f32[16,2048]{1,0:T(8,128)S(1)}, f32[16,32]{1,0:T(8,128)S(1)}, bf16[16,256]{1,0:T(8,128)(2,1)S(1)}) custom-call(bf16[256,2048]{1,0:T(8,128)(2,1)S(1)} %get-tuple-element.62.x_ref, bf16[256,256]{1,0:T(8,128)(2,1)S(1)} %get-tuple-element.63.b_ref, f32[32,256]{1,0:T(8,128)S(1)} %get-tuple-element.61.cum_ref, ...), custom_call_target="tpu_custom_call" | custom-call | flops 1 | bytes 1 | tf_op jit(solution)/shard_map/ask_kernel/pallas_call | solution.py:567
  27.0 0.3 read_kernel.2
  27.3 1.5 %collective-permute-start.13 = (bf16[4,2048]{1,0:T(4,128)(2,1)S(1)}, bf16[4,2048]{1,0:T(4,128)(2,1)S(1)}, u32[]{:S(2)}, u32[]{:S(2)}) collective-permute-start(bf16[4,2048]{1,0:T(4,128)(2,1)S(1)} %get-tuple-element.112), channel_id=1, source_target_pairs={{0,8},{1,9},{2,10},{3,11},{4,5},{5,4},{6,7},{7,6},{8,0},{9,1},{10,... | collective-permute-start | bytes 49160 | tf_op jit(solution)/shard_map/ppermute | solution.py:548
  28.8 0.0 collective-permute-start.14
  28.8 2.1 %collective-permute-start.12 = (bf16[4,2048]{1,0:T(4,128)(2,1)S(1)}, bf16[4,2048]{1,0:T(4,128)(2,1)S(1)}, u32[]{:S(2)}, u32[]{:S(2)}) collective-permute-start(bf16[4,2048]{1,0:T(4,128)(2,1)S(1)} %get-tuple-element.107.refs_1_), channel_id=1, source_target_pairs={{0,4},{1,5},{2,6},{3,7},{4,0},{5,1},{6,2},{7,3},{8,9},{9,8},{10,11... | collective-permute-start | bytes 49160 | tf_op jit(solution)/shard_map/ppermute | solution.py:548
  30.9 0.0 collective-permute-done.10.refs_0_.rest_2_.rest_0_
  30.9 0.0 collective-permute-done.11.rest_3_.rest_1_
  30.9 0.3 read_kernel.3
  31.2 1.3 %collective-permute-start.15 = (bf16[4,2048]{1,0:T(4,128)(2,1)S(1)}, bf16[4,2048]{1,0:T(4,128)(2,1)S(1)}, u32[]{:S(2)}, u32[]{:S(2)}) collective-permute-start(bf16[4,2048]{1,0:T(4,128)(2,1)S(1)} %get-tuple-element.114), channel_id=1, source_target_pairs={{0,12},{1,13},{2,14},{3,15},{4,5},{5,4},{6,7},{7,6},{8,9},{9,8},{1... | collective-permute-start | bytes 49160 | tf_op jit(solution)/shard_map/ppermute | solution.py:548
  32.5 0.0 collective-permute-start.16
  32.5 0.0 collective-permute-done.13.refs_2_.rest_1_
  32.5 0.5 %collective-permute-start.17 = (bf16[4,2048]{1,0:T(4,128)(2,1)S(1)}, bf16[4,2048]{1,0:T(4,128)(2,1)S(1)}, u32[]{:S(2)}, u32[]{:S(2)}) collective-permute-start(bf16[4,2048]{1,0:T(4,128)(2,1)S(1)} %get-tuple-element.116), channel_id=1, source_target_pairs={{0,1},{1,0},{2,3},{3,2},{4,12},{5,13},{6,14},{7,15},{8,9},{9,8},{1... | collective-permute-start | bytes 49160 | tf_op jit(solution)/shard_map/ppermute | solution.py:548
  33.0 0.7 %outer_kernel.2.rest_4_ = bf16[256,1024]{1,0:T(8,128)(2,1)S(1)} custom-call(bf16[256,256]{1,0:T(8,128)(2,1)S(1)} %get-tuple-element.60.c_ref, f32[32,256]{1,0:T(8,128)S(1)} %get-tuple-element.61.cum_ref, bf16[128,2048]{1,0:T(8,128)(2,1)S(1)} %get-tuple-element.102.carry_ref, bf16[128,384]{1,0:T(8,128)(2,1)S(1)} %collective-permute-done.8.refs_0_.rest_0_, ...), custom_call_target="tpu_custom_call" | custom-call | flops 1 | bytes 1 | tf_op jit(solution)/shard_map/outer_kernel/pallas_call | solution.py:589
  33.7 1.4 %outer_kernel.3 = (bf16[256,2048]{1,0:T(8,128)(2,1)}, f32[8,128]{1,0:T(8,128)S(1)}) custom-call(bf16[256,256]{1,0:T(8,128)(2,1)S(1)} %get-tuple-element.60.c_ref, f32[32,256]{1,0:T(8,128)S(1)} %get-tuple-element.61.cum_ref, bf16[128,2048]{1,0:T(8,128)(2,1)S(1)} %get-tuple-element.102.carry_ref, ...), custom_call_target="tpu_custom_call" | custom-call | flops 1 | bytes 1 | tf_op jit(solution)/shard_map/outer_kernel/pallas_call | solution.py:589
  35.1 0.0 collective-permute-done.14.refs_3_.rest_2_
  35.1 0.0 collective-permute-done.12.refs_1_.rest_0_
  35.1 1.7 %collective-permute-done.15.rest_3_ = bf16[4,2048]{1,0:T(4,128)(2,1)S(1)} collective-permute-done((bf16[4,2048]{1,0:T(4,128)(2,1)S(1)}, bf16[4,2048]{1,0:T(4,128)(2,1)S(1)}, u32[]{:S(2)}, u32[]{:S(2)}) %collective-permute-start.15) | collective-permute-done | bytes 16416 | tf_op jit(solution)/shard_map/ppermute | solution.py:548
  36.8 0.0 collective-permute-done.16.rest_4_
  36.8 0.0 collective-permute-done.17.rest_5_
  36.8 0.7 %finish_kernel.1 = bf16[4,4,2048]{2,1,0:T(4,128)(2,1)} custom-call(f32[4,4,2048]{2,1,0:T(4,128)S(1)} %get-tuple-element.85.rest_4_.keep_ref, f32[4,4,2048]{2,1,0:T(4,128)S(1)} %get-tuple-element.110.fresh_ref, f32[4,4,128]{2,1,0:T(4,128)S(1)} %get-tuple-element.111.held_ref, bf16[4,2048]{1,0:T(4,128)(2,1)S(1)} %collective-permute-done.12.refs_1_.rest_0_, ...), custom_call_target="tpu_custom_call" | custom-call | flops 1 | bytes 1 | tf_op jit(solution)/shard_map/finish_kernel/pallas_call | solution.py:660
  (9 shorter events, 0.2 us)
Async XLA Ops:
  2.5 6.5 %collective-permute-start.1 = (bf16[144,384]{1,0:T(8,128)(2,1)S(1)}, bf16[144,384]{1,0:T(8,128)(2,1)S(1)}, u32[]{:S(2)}, u32[]{:S(2)}) collective-permute-start(bf16[144,384]{1,0:T(8,128)(2,1)S(1)} %get-tuple-element.71.rest_2_), channel_id=1, source_target_pairs={{0,4},{1,5},{2,6},{3,7},{4,0},{5,1},{6,2},{7,3},{8,12},{9,13},{10,... | collective-permute-start | bytes 331784 | tf_op jit(solution)/shard_map/hop1_chunk0/ppermute | solution.py:548
  8.9 7.0 %collective-permute-start = (bf16[128,640]{1,0:T(8,128)(2,1)S(1)}, bf16[128,640]{1,0:T(8,128)(2,1)S(1)}, u32[]{:S(2)}, u32[]{:S(2)}) collective-permute-start(bf16[128,640]{1,0:T(8,128)(2,1)S(1)} %get-tuple-element.68), channel_id=1, source_target_pairs={{0,4},{1,5},{2,6},{3,7},{4,0},{5,1},{6,2},{7,3},{8,9},{9,8},{10,11... | collective-permute-start | bytes 491528 | tf_op jit(solution)/shard_map/hop1_chunk1/ppermute | solution.py:548
  9.1 7.1 %collective-permute-start.5 = (bf16[128,384]{1,0:T(8,128)(2,1)S(1)}, bf16[128,384]{1,0:T(8,128)(2,1)S(1)}, u32[]{:S(2)}, u32[]{:S(2)}) collective-permute-start(bf16[128,384]{1,0:T(8,128)(2,1)S(1)} %get-tuple-element.84.rest_0_), channel_id=1, source_target_pairs={{0,1},{1,0},{2,3},{3,2},{4,8},{5,9},{6,10},{7,11},{8,4},{9,5},{10,... | collective-permute-start | bytes 294920 | tf_op jit(solution)/shard_map/hop2_chunk0/ppermute | solution.py:548
  9.2 8.3 %collective-permute-start.4 = (bf16[128,512]{1,0:T(8,128)(2,1)S(1)}, bf16[128,512]{1,0:T(8,128)(2,1)S(1)}, u32[]{:S(2)}, u32[]{:S(2)}) collective-permute-start(bf16[128,512]{1,0:T(8,128)(2,1)S(1)} %get-tuple-element.89), channel_id=1, source_target_pairs={{0,4},{1,5},{2,6},{3,7},{4,0},{5,1},{6,2},{7,3},{8,9},{9,8},{10,11... | collective-permute-start | bytes 393224 | tf_op jit(solution)/shard_map/hop1_chunk2/ppermute | solution.py:548
  16.1 1.5 %collective-permute-start.3 = (bf16[144,640]{1,0:T(8,128)(2,1)S(1)}, bf16[144,640]{1,0:T(8,128)(2,1)S(1)}, u32[]{:S(2)}, u32[]{:S(2)}) collective-permute-start(bf16[144,640]{1,0:T(8,128)(2,1)S(1)} %get-tuple-element.88.rest_0_), channel_id=1, source_target_pairs={{0,1},{1,0},{2,3},{3,2},{4,8},{5,9},{6,10},{7,11},{8,4},{9,5},{10,... | collective-permute-start | bytes 552968 | tf_op jit(solution)/shard_map/hop2_chunk1/ppermute | solution.py:548
  16.1 6.4 %collective-permute-start.2 = (bf16[128,512]{1,0:T(8,128)(2,1)S(1)}, bf16[128,512]{1,0:T(8,128)(2,1)S(1)}, u32[]{:S(2)}, u32[]{:S(2)}) collective-permute-start(bf16[128,512]{1,0:T(8,128)(2,1)S(1)} %get-tuple-element.86), channel_id=1, source_target_pairs={{0,4},{1,5},{2,6},{3,7},{4,0},{5,1},{6,2},{7,3},{8,9},{9,8},{10,11... | collective-permute-start | bytes 393224 | tf_op jit(solution)/shard_map/hop1_chunk3/ppermute | solution.py:548
  16.3 6.4 %collective-permute-start.8 = (bf16[128,384]{1,0:T(8,128)(2,1)S(1)}, bf16[128,384]{1,0:T(8,128)(2,1)S(1)}, u32[]{:S(2)}, u32[]{:S(2)}) collective-permute-start(bf16[128,384]{1,0:T(8,128)(2,1)S(1)} %get-tuple-element.98), channel_id=1, source_target_pairs={{0,1},{1,0},{2,3},{3,2},{4,5},{5,4},{6,7},{7,6},{8,12},{9,13},{10,... | collective-permute-start | bytes 294920 | tf_op jit(solution)/shard_map/hop3_chunk0/ppermute | solution.py:548
  17.5 5.1 %collective-permute-start.7 = (bf16[128,512]{1,0:T(8,128)(2,1)S(1)}, bf16[128,512]{1,0:T(8,128)(2,1)S(1)}, u32[]{:S(2)}, u32[]{:S(2)}) collective-permute-start(bf16[128,512]{1,0:T(8,128)(2,1)S(1)} %get-tuple-element.96), channel_id=1, source_target_pairs={{0,1},{1,0},{2,3},{3,2},{4,8},{5,9},{6,10},{7,11},{8,4},{9,5},{10,... | collective-permute-start | bytes 393224 | tf_op jit(solution)/shard_map/hop2_chunk2/ppermute | solution.py:548
  17.7 8.3 %collective-permute-start.9 = (bf16[144,640]{1,0:T(8,128)(2,1)S(1)}, bf16[144,640]{1,0:T(8,128)(2,1)S(1)}, u32[]{:S(2)}, u32[]{:S(2)}) collective-permute-start(bf16[144,640]{1,0:T(8,128)(2,1)S(1)} %get-tuple-element.100), channel_id=1, source_target_pairs={{0,4},{1,5},{2,6},{3,7},{4,0},{5,1},{6,2},{7,3},{8,12},{9,13},{10,... | collective-permute-start | bytes 552968 | tf_op jit(solution)/shard_map/hop3_chunk1/ppermute | solution.py:548
  22.5 3.5 %collective-permute-start.6 = (bf16[128,512]{1,0:T(8,128)(2,1)S(1)}, bf16[128,512]{1,0:T(8,128)(2,1)S(1)}, u32[]{:S(2)}, u32[]{:S(2)}) collective-permute-start(bf16[128,512]{1,0:T(8,128)(2,1)S(1)} %get-tuple-element.95.refs_1_), channel_id=1, source_target_pairs={{0,1},{1,0},{2,3},{3,2},{4,8},{5,9},{6,10},{7,11},{8,4},{9,5},{10,... | collective-permute-start | bytes 393224 | tf_op jit(solution)/shard_map/hop2_chunk3/ppermute | solution.py:548
  22.7 8.2 %collective-permute-start.10 = (bf16[128,512]{1,0:T(8,128)(2,1)S(1)}, bf16[128,512]{1,0:T(8,128)(2,1)S(1)}, u32[]{:S(2)}, u32[]{:S(2)}) collective-permute-start(bf16[128,512]{1,0:T(8,128)(2,1)S(1)} %get-tuple-element.101.refs_1_), channel_id=1, source_target_pairs={{0,1},{1,0},{2,3},{3,2},{4,5},{5,4},{6,7},{7,6},{8,12},{9,13},{10,... | collective-permute-start | bytes 393224 | tf_op jit(solution)/shard_map/hop3_chunk2/ppermute | solution.py:548
  26.0 4.8 %collective-permute-start.11 = (bf16[128,512]{1,0:T(8,128)(2,1)S(1)}, bf16[128,512]{1,0:T(8,128)(2,1)S(1)}, u32[]{:S(2)}, u32[]{:S(2)}) collective-permute-start(bf16[128,512]{1,0:T(8,128)(2,1)S(1)} %get-tuple-element.103.rest_3_), channel_id=1, source_target_pairs={{0,1},{1,0},{2,3},{3,2},{4,5},{5,4},{6,7},{7,6},{8,12},{9,13},{10,... | collective-permute-start | bytes 393224 | tf_op jit(solution)/shard_map/hop3_chunk3/ppermute | solution.py:548
  27.3 5.2 %collective-permute-start.13 = (bf16[4,2048]{1,0:T(4,128)(2,1)S(1)}, bf16[4,2048]{1,0:T(4,128)(2,1)S(1)}, u32[]{:S(2)}, u32[]{:S(2)}) collective-permute-start(bf16[4,2048]{1,0:T(4,128)(2,1)S(1)} %get-tuple-element.112), channel_id=1, source_target_pairs={{0,8},{1,9},{2,10},{3,11},{4,5},{5,4},{6,7},{7,6},{8,0},{9,1},{10,... | collective-permute-start | bytes 49160 | tf_op jit(solution)/shard_map/ppermute | solution.py:548
  28.8 6.3 %collective-permute-start.14 = (bf16[4,2048]{1,0:T(4,128)(2,1)S(1)}, bf16[4,2048]{1,0:T(4,128)(2,1)S(1)}, u32[]{:S(2)}, u32[]{:S(2)}) collective-permute-start(bf16[4,2048]{1,0:T(4,128)(2,1)S(1)} %get-tuple-element.113), channel_id=1, source_target_pairs={{0,1},{1,0},{2,3},{3,2},{4,8},{5,9},{6,10},{7,11},{8,4},{9,5},{10,... | collective-permute-start | bytes 49160 | tf_op jit(solution)/shard_map/ppermute | solution.py:548
  28.8 6.3 %collective-permute-start.12 = (bf16[4,2048]{1,0:T(4,128)(2,1)S(1)}, bf16[4,2048]{1,0:T(4,128)(2,1)S(1)}, u32[]{:S(2)}, u32[]{:S(2)}) collective-permute-start(bf16[4,2048]{1,0:T(4,128)(2,1)S(1)} %get-tuple-element.107.refs_1_), channel_id=1, source_target_pairs={{0,4},{1,5},{2,6},{3,7},{4,0},{5,1},{6,2},{7,3},{8,9},{9,8},{10,11... | collective-permute-start | bytes 49160 | tf_op jit(solution)/shard_map/ppermute | solution.py:548
  31.2 5.6 %collective-permute-start.15 = (bf16[4,2048]{1,0:T(4,128)(2,1)S(1)}, bf16[4,2048]{1,0:T(4,128)(2,1)S(1)}, u32[]{:S(2)}, u32[]{:S(2)}) collective-permute-start(bf16[4,2048]{1,0:T(4,128)(2,1)S(1)} %get-tuple-element.114), channel_id=1, source_target_pairs={{0,12},{1,13},{2,14},{3,15},{4,5},{5,4},{6,7},{7,6},{8,9},{9,8},{1... | collective-permute-start | bytes 49160 | tf_op jit(solution)/shard_map/ppermute | solution.py:548
  32.5 4.3 %collective-permute-start.16 = (bf16[4,2048]{1,0:T(4,128)(2,1)S(1)}, bf16[4,2048]{1,0:T(4,128)(2,1)S(1)}, u32[]{:S(2)}, u32[]{:S(2)}) collective-permute-start(bf16[4,2048]{1,0:T(4,128)(2,1)S(1)} %get-tuple-element.115), channel_id=1, source_target_pairs={{0,1},{1,0},{2,3},{3,2},{4,5},{5,4},{6,7},{7,6},{8,12},{9,13},{10,... | collective-permute-start | bytes 49160 | tf_op jit(solution)/shard_map/ppermute | solution.py:548
  32.5 4.3 %collective-permute-start.17 = (bf16[4,2048]{1,0:T(4,128)(2,1)S(1)}, bf16[4,2048]{1,0:T(4,128)(2,1)S(1)}, u32[]{:S(2)}, u32[]{:S(2)}) collective-permute-start(bf16[4,2048]{1,0:T(4,128)(2,1)S(1)} %get-tuple-element.116), channel_id=1, source_target_pairs={{0,1},{1,0},{2,3},{3,2},{4,12},{5,13},{6,14},{7,15},{8,9},{9,8},{1... | collective-permute-start | bytes 49160 | tf_op jit(solution)/shard_map/ppermute | solution.py:548

commit v14 on v13

--- a/solution.py
+++ b/solution.py
@@ -605,8 +605,6 @@
 
     got = {(1, 0): forward(sent[0], 1, 0)}
     inner = [inner_part(0)]
-    for g in range(1, groups):
-        inner.append(inner_part(g, inner[-1]))
     *parts, sent[1] = state_part(inner[-1])
     decay, total = parts[:chunks], total + parts[chunks:]
     got[1, 1] = forward(sent[1], 1, 1)
@@ -620,7 +618,9 @@
         operands += total[k + 2 : k + 3] * more + [sent[0], got[1, 0]] * (ride and (hop, k) == (1, 1))
         after = []
         if (hop, k) == (1, 1):
-            keep, fresh, held = fresh_part(tie)
+            for g in range(1, groups):
+                inner.append(inner_part(g, tie))
+            keep, fresh, held = fresh_part(inner[-1])
             after = [keep]
         if hop == count - 2 and k > 1:
             after = [token(got[hop + 1, k - 2], tie, flops=5 * TOKEN_COST)]
@@ -645,7 +645,7 @@
         reading = read_part(ops, False)
         for couple, value in zip(ops, reading):
             back.append(swap(value, couple))
-    ends = [(0, 3), (2, 3), (1, 3)] if four else list(range(1, count))
+    ends = [(0, 3), (1, 3), (2, 3)] if four else list(range(1, count))
     before = reading[0] if four else asked
     order_token = token(got[count - 1, chunks - 2], before, flops=TOKEN_COST)
     *reading, mine = read_part(ends, True, order_token)

time: 37.7 us -> 36.8 us (0.976)
  waiting for transfers between devices: 9.62 us -> 7.13 us
  starting transfers between devices: 16.8 us -> 18.3 us
    ppermute x18, waiting for transfers between devices: 9.62 us -> 7.13 us  [swap(): return lax.ppermute(value, ('seq', 'tp'), pairs)]
    ppermute x18, starting transfers between devices: 16.8 us -> 18.3 us  [swap(): return lax.ppermute(value, ('seq', 'tp'), pairs)]
  transfers between devices with their start and end apart: 18 -> 18, of which waited for: 5 -> 6; matrix products, arithmetic and copies ran while one was open for 0% -> 0% of each run, Pallas kernels for 20% -> 21%
where the time goes in v14:
time: 36.8 us; the launch traced here: 36.6 us
  starting transfers between devices  18.3 us (50%)
  Pallas kernels  10.3 us (28%)
  waiting for transfers between devices  7.13 us (19%)
  between operations  0.86 us (2%)
    ppermute x18, starting transfers between devices, swap(): return lax.ppermute(value, ('seq', 'tp'), pairs)  18.3 us
    ppermute x18, waiting for transfers between devices, swap(): return lax.ppermute(value, ('seq', 'tp'), pairs)  7.13 us
    pallas_call x2, Pallas kernels, inner_part(): call(functools.partial(inner_kernel, g), shape((tokens, group_lanes)), in...  2.15 us
    pallas_call x2, Pallas kernels, outer_part(): call(functools.partial(outer_kernel, parts, bounds, count), (pltpu.HBM((t...  2.06 us
    pallas_call x1, Pallas kernels, shards(): call(functools.partial(first_kernel, len(inputs)), tuple((shape(value.sha...  1.89 us
    pallas_call x1, Pallas kernels, state_part(): call(functools.partial(state_kernel, bounds), decay_shapes + total_shapes...  1.17 us
    pallas_call x1, Pallas kernels, ask_part(): call(functools.partial(ask_kernel, ride), (shape((rows, lanes)), shape((r...  0.92 us
  transfers between devices with their start and end apart: 18, of which 6 were waited for; matrix products, arithmetic and copies ran while one was open for 0% of the time, Pallas kernels for 21%

profile of v14, /device:TPU:0, one launch (start us, length us, event | category | flops | bytes accessed | tf_op | source)
XLA Modules:
  0.0 36.6 jit_solution(7935569590953665293)
XLA Ops:
  0.6 1.9 %first_kernel.1 = (bf16[256,2048]{1,0:T(8,128)(2,1)S(1)}, bf16[256,256]{1,0:T(8,128)(2,1)S(1)}, f32[1,32]{1,0:T(1,128)S(1)}, bf16[4,4,256]{2,1,0:T(4,128)(2,1)S(...) custom-call(bf16[256,2048]{1,0:T(8,128)(2,1)} %refs_0_.1, ...), custom_call_target="tpu_custom_call" | custom-call | flops 1 | bytes 1 | tf_op jit(solution)/shard_map/first_kernel/pallas_call | solution.py:510
  2.5 3.1 %collective-permute-start.1 = (bf16[144,384]{1,0:T(8,128)(2,1)S(1)}, bf16[144,384]{1,0:T(8,128)(2,1)S(1)}, u32[]{:S(2)}, u32[]{:S(2)}) collective-permute-start(bf16[144,384]{1,0:T(8,128)(2,1)S(1)} %get-tuple-element.71.rest_2_), channel_id=1, source_target_pairs={{0,4},{1,5},{2,6},{3,7},{4,0},{5,1},{6,2},{7,3},{8,12},{9,13},{10,... | collective-permute-start | bytes 331784 | tf_op jit(solution)/shard_map/hop1_chunk0/ppermute | solution.py:548
  5.6 1.1 %inner_kernel.2.rest_0_.rest_2_ = f32[256,1024]{1,0:T(8,128)S(1)} custom-call(bf16[256,2048]{1,0:T(8,128)(2,1)S(1)} %get-tuple-element.62.x_ref, bf16[256,256]{1,0:T(8,128)(2,1)S(1)} %get-tuple-element.63.b_ref, bf16[256,256]{1,0:T(8,128)(2,1)S(1)} %get-tuple-element.60.c_ref, f32[32,256]{1,0:T(8,128)S(1)} %get-tuple-element.61.cum_ref, ...), custom_call_target="tpu_custom_call" | custom-call | flops 1 | bytes 1 | tf_op jit(solution)/shard_map/inner_kernel/pallas_call | solution.py:559
  6.7 1.2 %state_kernel.1 = (f32[1,384]{1,0:T(1,128)S(1)}, f32[1,640]{1,0:T(1,128)S(1)}, f32[1,512]{1,0:T(1,128)S(1)}, f32[1,512]{1,0:T(1,128)S(1)}, f32[128,640]{1,0:T(8,...) custom-call(bf16[256,2048]{1,0:T(8,128)(2,1)S(1)} %get-tuple-element.62.x_ref, ...), custom_call_target="tpu_custom_call" | custom-call | flops 1 | bytes 1 | tf_op jit(solution)/shard_map/state_kernel/pallas_call | solution.py:533
  7.9 0.1 collective-permute-start
  7.9 0.7 %collective-permute-done.1.got_ref.rest_3_ = bf16[144,384]{1,0:T(8,128)(2,1)S(1)} collective-permute-done((bf16[144,384]{1,0:T(8,128)(2,1)S(1)}, bf16[144,384]{1,0:T(8,128)(2,1)S(1)}, u32[]{:S(2)}, u32[]{:S(2)}) %collective-permute-start.1) | collective-permute-done | bytes 110624 | tf_op jit(solution)/shard_map/hop1_chunk0/ppermute | solution.py:548
  8.7 0.1 pass_kernel.8
  8.7 0.1 collective-permute-start.5
  8.8 3.3 %collective-permute-start.4 = (bf16[128,512]{1,0:T(8,128)(2,1)S(1)}, bf16[128,512]{1,0:T(8,128)(2,1)S(1)}, u32[]{:S(2)}, u32[]{:S(2)}) collective-permute-start(bf16[128,512]{1,0:T(8,128)(2,1)S(1)} %get-tuple-element.89), channel_id=1, source_target_pairs={{0,4},{1,5},{2,6},{3,7},{4,0},{5,1},{6,2},{7,3},{8,9},{9,8},{10,11... | collective-permute-start | bytes 393224 | tf_op jit(solution)/shard_map/hop1_chunk2/ppermute | solution.py:548
  12.1 1.1 %inner_kernel.3.rest_0_.rest_3_ = f32[256,1024]{1,0:T(8,128)S(1)} custom-call(bf16[256,2048]{1,0:T(8,128)(2,1)S(1)} %get-tuple-element.62.x_ref, bf16[256,256]{1,0:T(8,128)(2,1)S(1)} %get-tuple-element.63.b_ref, bf16[256,256]{1,0:T(8,128)(2,1)S(1)} %get-tuple-element.60.c_ref, f32[32,256]{1,0:T(8,128)S(1)} %get-tuple-element.61.cum_ref, ...), custom_call_target="tpu_custom_call" | custom-call | flops 1 | bytes 1 | tf_op jit(solution)/shard_map/inner_kernel/pallas_call | solution.py:559
  13.2 0.4 %fresh_kernel.1 = (f32[4,4,2048]{2,1,0:T(4,128)S(1)}, f32[4,4,2048]{2,1,0:T(4,128)S(1)}, f32[4,4,128]{2,1,0:T(4,128)S(1)}) custom-call(bf16[4,4,2048]{2,1,0:T(4,128)(2,1)S(1)} %get-tuple-element.77.x_ref, bf16[4,4,256]{2,1,0:T(4,128)(2,1)S(1)} %get-tuple-element.78.b_ref, bf16[4,4,256]{2,1,0:T(4,128)(2,1)S(1)} %get-tuple-element.79.c_ref, ...), custom_call_target="tpu_custom_call" | custom-call | flops 1 | bytes 1 | tf_op jit(solution)/shard_map/fresh_kernel/pallas_call | solution.py:579
  13.6 1.3 %collective-permute-done.got_ref = bf16[128,640]{1,0:T(8,128)(2,1)S(1)} collective-permute-done((bf16[128,640]{1,0:T(8,128)(2,1)S(1)}, bf16[128,640]{1,0:T(8,128)(2,1)S(1)}, u32[]{:S(2)}, u32[]{:S(2)}) %collective-permute-start) | collective-permute-done | bytes 163872 | tf_op jit(solution)/shard_map/hop1_chunk1/ppermute | solution.py:548
  14.9 0.1 pass_kernel.9
  15.0 0.1 collective-permute-start.3
  15.1 0.1 collective-permute-start.2
  15.1 0.0 collective-permute-done.5.got_ref
  15.2 0.5 %collective-permute-start.8 = (bf16[128,384]{1,0:T(8,128)(2,1)S(1)}, bf16[128,384]{1,0:T(8,128)(2,1)S(1)}, u32[]{:S(2)}, u32[]{:S(2)}) collective-permute-start(bf16[128,384]{1,0:T(8,128)(2,1)S(1)} %get-tuple-element.98), channel_id=1, source_target_pairs={{0,1},{1,0},{2,3},{3,2},{4,5},{5,4},{6,7},{7,6},{8,12},{9,13},{10,... | collective-permute-start | bytes 294920 | tf_op jit(solution)/shard_map/hop3_chunk0/ppermute | solution.py:548
  15.7 0.7 %collective-permute-done.4.got_ref = bf16[128,512]{1,0:T(8,128)(2,1)S(1)} collective-permute-done((bf16[128,512]{1,0:T(8,128)(2,1)S(1)}, bf16[128,512]{1,0:T(8,128)(2,1)S(1)}, u32[]{:S(2)}, u32[]{:S(2)}) %collective-permute-start.4) | collective-permute-done | bytes 131104 | tf_op jit(solution)/shard_map/hop1_chunk2/ppermute | solution.py:548
  16.4 0.1 collective-permute-start.7
  16.5 0.0 collective-permute-done.3.got_ref.rest_1_
  16.5 0.1 pass_kernel.12
  16.6 3.7 %collective-permute-start.9 = (bf16[144,640]{1,0:T(8,128)(2,1)S(1)}, bf16[144,640]{1,0:T(8,128)(2,1)S(1)}, u32[]{:S(2)}, u32[]{:S(2)}) collective-permute-start(bf16[144,640]{1,0:T(8,128)(2,1)S(1)} %get-tuple-element.100), channel_id=1, source_target_pairs={{0,4},{1,5},{2,6},{3,7},{4,0},{5,1},{6,2},{7,3},{8,12},{9,13},{10,... | collective-permute-start | bytes 552968 | tf_op jit(solution)/shard_map/hop3_chunk1/ppermute | solution.py:548
  20.2 1.2 %collective-permute-done.2.got_ref = bf16[128,512]{1,0:T(8,128)(2,1)S(1)} collective-permute-done((bf16[128,512]{1,0:T(8,128)(2,1)S(1)}, bf16[128,512]{1,0:T(8,128)(2,1)S(1)}, u32[]{:S(2)}, u32[]{:S(2)}) %collective-permute-start.2) | collective-permute-done | bytes 131104 | tf_op jit(solution)/shard_map/hop1_chunk3/ppermute | solution.py:548
  21.5 0.1 collective-permute-start.6
  21.5 0.0 collective-permute-done.8.refs_0_.rest_0_
  21.6 0.0 collective-permute-done.7.got_ref
  21.6 0.5 %collective-permute-start.10 = (bf16[128,512]{1,0:T(8,128)(2,1)S(1)}, bf16[128,512]{1,0:T(8,128)(2,1)S(1)}, u32[]{:S(2)}, u32[]{:S(2)}) collective-permute-start(bf16[128,512]{1,0:T(8,128)(2,1)S(1)} %get-tuple-element.101.refs_1_), channel_id=1, source_target_pairs={{0,1},{1,0},{2,3},{3,2},{4,5},{5,4},{6,7},{7,6},{8,12},{9,13},{10,... | collective-permute-start | bytes 393224 | tf_op jit(solution)/shard_map/hop3_chunk2/ppermute | solution.py:548
  22.2 2.8 %collective-permute-done.9.refs_0_.rest_2_.rest_1_ = bf16[144,640]{1,0:T(8,128)(2,1)S(1)} collective-permute-done((bf16[144,640]{1,0:T(8,128)(2,1)S(1)}, bf16[144,640]{1,0:T(8,128)(2,1)S(1)}, u32[]{:S(2)}, u32[]{:S(2)}) %collective-permute-start.9) | collective-permute-done | bytes 184352 | tf_op jit(solution)/shard_map/hop3_chunk1/ppermute | solution.py:548
  24.9 0.0 collective-permute-done.6.got_ref
  25.0 0.1 collective-permute-start.11
  25.0 0.9 %ask_kernel.1 = (f32[16,2048]{1,0:T(8,128)S(1)}, f32[16,32]{1,0:T(8,128)S(1)}, bf16[16,256]{1,0:T(8,128)(2,1)S(1)}) custom-call(bf16[256,2048]{1,0:T(8,128)(2,1)S(1)} %get-tuple-element.62.x_ref, bf16[256,256]{1,0:T(8,128)(2,1)S(1)} %get-tuple-element.63.b_ref, f32[32,256]{1,0:T(8,128)S(1)} %get-tuple-element.61.cum_ref, ...), custom_call_target="tpu_custom_call" | custom-call | flops 1 | bytes 1 | tf_op jit(solution)/shard_map/ask_kernel/pallas_call | solution.py:567
  26.0 0.3 read_kernel.2
  26.2 3.0 %collective-permute-start.13 = (bf16[4,2048]{1,0:T(4,128)(2,1)S(1)}, bf16[4,2048]{1,0:T(4,128)(2,1)S(1)}, u32[]{:S(2)}, u32[]{:S(2)}) collective-permute-start(bf16[4,2048]{1,0:T(4,128)(2,1)S(1)} %get-tuple-element.112), channel_id=1, source_target_pairs={{0,8},{1,9},{2,10},{3,11},{4,5},{5,4},{6,7},{7,6},{8,0},{9,1},{10,... | collective-permute-start | bytes 49160 | tf_op jit(solution)/shard_map/ppermute | solution.py:548
  29.3 0.0 collective-permute-start.14
  29.3 0.6 %collective-permute-start.12 = (bf16[4,2048]{1,0:T(4,128)(2,1)S(1)}, bf16[4,2048]{1,0:T(4,128)(2,1)S(1)}, u32[]{:S(2)}, u32[]{:S(2)}) collective-permute-start(bf16[4,2048]{1,0:T(4,128)(2,1)S(1)} %get-tuple-element.107.refs_1_), channel_id=1, source_target_pairs={{0,4},{1,5},{2,6},{3,7},{4,0},{5,1},{6,2},{7,3},{8,9},{9,8},{10,11... | collective-permute-start | bytes 49160 | tf_op jit(solution)/shard_map/ppermute | solution.py:548
  29.9 0.0 collective-permute-done.10.refs_0_.rest_2_.rest_0_
  29.9 0.0 collective-permute-done.11.rest_3_.rest_1_
  29.9 0.3 read_kernel.3
  30.2 2.5 %collective-permute-start.15 = (bf16[4,2048]{1,0:T(4,128)(2,1)S(1)}, bf16[4,2048]{1,0:T(4,128)(2,1)S(1)}, u32[]{:S(2)}, u32[]{:S(2)}) collective-permute-start(bf16[4,2048]{1,0:T(4,128)(2,1)S(1)} %get-tuple-element.114), channel_id=1, source_target_pairs={{0,12},{1,13},{2,14},{3,15},{4,5},{5,4},{6,7},{7,6},{8,9},{9,8},{1... | collective-permute-start | bytes 49160 | tf_op jit(solution)/shard_map/ppermute | solution.py:548
  32.8 0.0 collective-permute-start.16
  32.8 0.0 collective-permute-done.13.refs_2_.rest_1_
  32.8 0.5 %collective-permute-start.17 = (bf16[4,2048]{1,0:T(4,128)(2,1)S(1)}, bf16[4,2048]{1,0:T(4,128)(2,1)S(1)}, u32[]{:S(2)}, u32[]{:S(2)}) collective-permute-start(bf16[4,2048]{1,0:T(4,128)(2,1)S(1)} %get-tuple-element.116), channel_id=1, source_target_pairs={{0,1},{1,0},{2,3},{3,2},{4,5},{5,4},{6,7},{7,6},{8,12},{9,13},{10,... | collective-permute-start | bytes 49160 | tf_op jit(solution)/shard_map/ppermute | solution.py:548
  33.3 0.7 %outer_kernel.2.rest_4_ = bf16[256,1024]{1,0:T(8,128)(2,1)S(1)} custom-call(bf16[256,256]{1,0:T(8,128)(2,1)S(1)} %get-tuple-element.60.c_ref, f32[32,256]{1,0:T(8,128)S(1)} %get-tuple-element.61.cum_ref, bf16[128,2048]{1,0:T(8,128)(2,1)S(1)} %get-tuple-element.102.carry_ref, bf16[128,384]{1,0:T(8,128)(2,1)S(1)} %collective-permute-done.8.refs_0_.rest_0_, ...), custom_call_target="tpu_custom_call" | custom-call | flops 1 | bytes 1 | tf_op jit(solution)/shard_map/outer_kernel/pallas_call | solution.py:589
  34.0 1.4 %outer_kernel.3 = (bf16[256,2048]{1,0:T(8,128)(2,1)}, f32[8,128]{1,0:T(8,128)S(1)}) custom-call(bf16[256,256]{1,0:T(8,128)(2,1)S(1)} %get-tuple-element.60.c_ref, f32[32,256]{1,0:T(8,128)S(1)} %get-tuple-element.61.cum_ref, bf16[128,2048]{1,0:T(8,128)(2,1)S(1)} %get-tuple-element.102.carry_ref, ...), custom_call_target="tpu_custom_call" | custom-call | flops 1 | bytes 1 | tf_op jit(solution)/shard_map/outer_kernel/pallas_call | solution.py:589
  35.3 0.0 collective-permute-done.14.refs_3_.rest_2_
  35.4 0.0 collective-permute-done.12.refs_1_.rest_0_
  35.4 0.4 %collective-permute-done.15.rest_3_ = bf16[4,2048]{1,0:T(4,128)(2,1)S(1)} collective-permute-done((bf16[4,2048]{1,0:T(4,128)(2,1)S(1)}, bf16[4,2048]{1,0:T(4,128)(2,1)S(1)}, u32[]{:S(2)}, u32[]{:S(2)}) %collective-permute-start.15) | collective-permute-done | bytes 16416 | tf_op jit(solution)/shard_map/ppermute | solution.py:548
  35.8 0.0 collective-permute-done.16.rest_4_
  35.8 0.0 collective-permute-done.17.rest_5_
  35.8 0.7 %finish_kernel.1 = bf16[4,4,2048]{2,1,0:T(4,128)(2,1)} custom-call(f32[4,4,2048]{2,1,0:T(4,128)S(1)} %get-tuple-element.85.rest_4_.keep_ref, f32[4,4,2048]{2,1,0:T(4,128)S(1)} %get-tuple-element.110.fresh_ref, f32[4,4,128]{2,1,0:T(4,128)S(1)} %get-tuple-element.111.held_ref, bf16[4,2048]{1,0:T(4,128)(2,1)S(1)} %collective-permute-done.12.refs_1_.rest_0_, ...), custom_call_target="tpu_custom_call" | custom-call | flops 1 | bytes 1 | tf_op jit(solution)/shard_map/finish_kernel/pallas_call | solution.py:660
  (9 shorter events, 0.2 us)
Async XLA Ops:
  2.5 6.1 %collective-permute-start.1 = (bf16[144,384]{1,0:T(8,128)(2,1)S(1)}, bf16[144,384]{1,0:T(8,128)(2,1)S(1)}, u32[]{:S(2)}, u32[]{:S(2)}) collective-permute-start(bf16[144,384]{1,0:T(8,128)(2,1)S(1)} %get-tuple-element.71.rest_2_), channel_id=1, source_target_pairs={{0,4},{1,5},{2,6},{3,7},{4,0},{5,1},{6,2},{7,3},{8,12},{9,13},{10,... | collective-permute-start | bytes 331784 | tf_op jit(solution)/shard_map/hop1_chunk0/ppermute | solution.py:548
  7.9 7.0 %collective-permute-start = (bf16[128,640]{1,0:T(8,128)(2,1)S(1)}, bf16[128,640]{1,0:T(8,128)(2,1)S(1)}, u32[]{:S(2)}, u32[]{:S(2)}) collective-permute-start(bf16[128,640]{1,0:T(8,128)(2,1)S(1)} %get-tuple-element.68), channel_id=1, source_target_pairs={{0,4},{1,5},{2,6},{3,7},{4,0},{5,1},{6,2},{7,3},{8,9},{9,8},{10,11... | collective-permute-start | bytes 491528 | tf_op jit(solution)/shard_map/hop1_chunk1/ppermute | solution.py:548
  8.7 6.4 %collective-permute-start.5 = (bf16[128,384]{1,0:T(8,128)(2,1)S(1)}, bf16[128,384]{1,0:T(8,128)(2,1)S(1)}, u32[]{:S(2)}, u32[]{:S(2)}) collective-permute-start(bf16[128,384]{1,0:T(8,128)(2,1)S(1)} %get-tuple-element.84.rest_0_), channel_id=1, source_target_pairs={{0,1},{1,0},{2,3},{3,2},{4,8},{5,9},{6,10},{7,11},{8,4},{9,5},{10,... | collective-permute-start | bytes 294920 | tf_op jit(solution)/shard_map/hop2_chunk0/ppermute | solution.py:548
  8.8 7.6 %collective-permute-start.4 = (bf16[128,512]{1,0:T(8,128)(2,1)S(1)}, bf16[128,512]{1,0:T(8,128)(2,1)S(1)}, u32[]{:S(2)}, u32[]{:S(2)}) collective-permute-start(bf16[128,512]{1,0:T(8,128)(2,1)S(1)} %get-tuple-element.89), channel_id=1, source_target_pairs={{0,4},{1,5},{2,6},{3,7},{4,0},{5,1},{6,2},{7,3},{8,9},{9,8},{10,11... | collective-permute-start | bytes 393224 | tf_op jit(solution)/shard_map/hop1_chunk2/ppermute | solution.py:548
  15.0 1.5 %collective-permute-start.3 = (bf16[144,640]{1,0:T(8,128)(2,1)S(1)}, bf16[144,640]{1,0:T(8,128)(2,1)S(1)}, u32[]{:S(2)}, u32[]{:S(2)}) collective-permute-start(bf16[144,640]{1,0:T(8,128)(2,1)S(1)} %get-tuple-element.88.rest_0_), channel_id=1, source_target_pairs={{0,1},{1,0},{2,3},{3,2},{4,8},{5,9},{6,10},{7,11},{8,4},{9,5},{10,... | collective-permute-start | bytes 552968 | tf_op jit(solution)/shard_map/hop2_chunk1/ppermute | solution.py:548
  15.1 6.4 %collective-permute-start.2 = (bf16[128,512]{1,0:T(8,128)(2,1)S(1)}, bf16[128,512]{1,0:T(8,128)(2,1)S(1)}, u32[]{:S(2)}, u32[]{:S(2)}) collective-permute-start(bf16[128,512]{1,0:T(8,128)(2,1)S(1)} %get-tuple-element.86), channel_id=1, source_target_pairs={{0,4},{1,5},{2,6},{3,7},{4,0},{5,1},{6,2},{7,3},{8,9},{9,8},{10,11... | collective-permute-start | bytes 393224 | tf_op jit(solution)/shard_map/hop1_chunk3/ppermute | solution.py:548
  15.2 6.4 %collective-permute-start.8 = (bf16[128,384]{1,0:T(8,128)(2,1)S(1)}, bf16[128,384]{1,0:T(8,128)(2,1)S(1)}, u32[]{:S(2)}, u32[]{:S(2)}) collective-permute-start(bf16[128,384]{1,0:T(8,128)(2,1)S(1)} %get-tuple-element.98), channel_id=1, source_target_pairs={{0,1},{1,0},{2,3},{3,2},{4,5},{5,4},{6,7},{7,6},{8,12},{9,13},{10,... | collective-permute-start | bytes 294920 | tf_op jit(solution)/shard_map/hop3_chunk0/ppermute | solution.py:548
  16.4 5.1 %collective-permute-start.7 = (bf16[128,512]{1,0:T(8,128)(2,1)S(1)}, bf16[128,512]{1,0:T(8,128)(2,1)S(1)}, u32[]{:S(2)}, u32[]{:S(2)}) collective-permute-start(bf16[128,512]{1,0:T(8,128)(2,1)S(1)} %get-tuple-element.96), channel_id=1, source_target_pairs={{0,1},{1,0},{2,3},{3,2},{4,8},{5,9},{6,10},{7,11},{8,4},{9,5},{10,... | collective-permute-start | bytes 393224 | tf_op jit(solution)/shard_map/hop2_chunk2/ppermute | solution.py:548
  16.6 8.3 %collective-permute-start.9 = (bf16[144,640]{1,0:T(8,128)(2,1)S(1)}, bf16[144,640]{1,0:T(8,128)(2,1)S(1)}, u32[]{:S(2)}, u32[]{:S(2)}) collective-permute-start(bf16[144,640]{1,0:T(8,128)(2,1)S(1)} %get-tuple-element.100), channel_id=1, source_target_pairs={{0,4},{1,5},{2,6},{3,7},{4,0},{5,1},{6,2},{7,3},{8,12},{9,13},{10,... | collective-permute-start | bytes 552968 | tf_op jit(solution)/shard_map/hop3_chunk1/ppermute | solution.py:548
  21.5 3.5 %collective-permute-start.6 = (bf16[128,512]{1,0:T(8,128)(2,1)S(1)}, bf16[128,512]{1,0:T(8,128)(2,1)S(1)}, u32[]{:S(2)}, u32[]{:S(2)}) collective-permute-start(bf16[128,512]{1,0:T(8,128)(2,1)S(1)} %get-tuple-element.95.refs_1_), channel_id=1, source_target_pairs={{0,1},{1,0},{2,3},{3,2},{4,8},{5,9},{6,10},{7,11},{8,4},{9,5},{10,... | collective-permute-start | bytes 393224 | tf_op jit(solution)/shard_map/hop2_chunk3/ppermute | solution.py:548
  21.6 8.3 %collective-permute-start.10 = (bf16[128,512]{1,0:T(8,128)(2,1)S(1)}, bf16[128,512]{1,0:T(8,128)(2,1)S(1)}, u32[]{:S(2)}, u32[]{:S(2)}) collective-permute-start(bf16[128,512]{1,0:T(8,128)(2,1)S(1)} %get-tuple-element.101.refs_1_), channel_id=1, source_target_pairs={{0,1},{1,0},{2,3},{3,2},{4,5},{5,4},{6,7},{7,6},{8,12},{9,13},{10,... | collective-permute-start | bytes 393224 | tf_op jit(solution)/shard_map/hop3_chunk2/ppermute | solution.py:548
  25.0 5.0 %collective-permute-start.11 = (bf16[128,512]{1,0:T(8,128)(2,1)S(1)}, bf16[128,512]{1,0:T(8,128)(2,1)S(1)}, u32[]{:S(2)}, u32[]{:S(2)}) collective-permute-start(bf16[128,512]{1,0:T(8,128)(2,1)S(1)} %get-tuple-element.103.rest_3_), channel_id=1, source_target_pairs={{0,1},{1,0},{2,3},{3,2},{4,5},{5,4},{6,7},{7,6},{8,12},{9,13},{10,... | collective-permute-start | bytes 393224 | tf_op jit(solution)/shard_map/hop3_chunk3/ppermute | solution.py:548
  26.2 6.5 %collective-permute-start.13 = (bf16[4,2048]{1,0:T(4,128)(2,1)S(1)}, bf16[4,2048]{1,0:T(4,128)(2,1)S(1)}, u32[]{:S(2)}, u32[]{:S(2)}) collective-permute-start(bf16[4,2048]{1,0:T(4,128)(2,1)S(1)} %get-tuple-element.112), channel_id=1, source_target_pairs={{0,8},{1,9},{2,10},{3,11},{4,5},{5,4},{6,7},{7,6},{8,0},{9,1},{10,... | collective-permute-start | bytes 49160 | tf_op jit(solution)/shard_map/ppermute | solution.py:548
  29.3 6.1 %collective-permute-start.14 = (bf16[4,2048]{1,0:T(4,128)(2,1)S(1)}, bf16[4,2048]{1,0:T(4,128)(2,1)S(1)}, u32[]{:S(2)}, u32[]{:S(2)}) collective-permute-start(bf16[4,2048]{1,0:T(4,128)(2,1)S(1)} %get-tuple-element.113), channel_id=1, source_target_pairs={{0,1},{1,0},{2,3},{3,2},{4,8},{5,9},{6,10},{7,11},{8,4},{9,5},{10,... | collective-permute-start | bytes 49160 | tf_op jit(solution)/shard_map/ppermute | solution.py:548
  29.3 6.1 %collective-permute-start.12 = (bf16[4,2048]{1,0:T(4,128)(2,1)S(1)}, bf16[4,2048]{1,0:T(4,128)(2,1)S(1)}, u32[]{:S(2)}, u32[]{:S(2)}) collective-permute-start(bf16[4,2048]{1,0:T(4,128)(2,1)S(1)} %get-tuple-element.107.refs_1_), channel_id=1, source_target_pairs={{0,4},{1,5},{2,6},{3,7},{4,0},{5,1},{6,2},{7,3},{8,9},{9,8},{10,11... | collective-permute-start | bytes 49160 | tf_op jit(solution)/shard_map/ppermute | solution.py:548
  30.2 5.6 %collective-permute-start.15 = (bf16[4,2048]{1,0:T(4,128)(2,1)S(1)}, bf16[4,2048]{1,0:T(4,128)(2,1)S(1)}, u32[]{:S(2)}, u32[]{:S(2)}) collective-permute-start(bf16[4,2048]{1,0:T(4,128)(2,1)S(1)} %get-tuple-element.114), channel_id=1, source_target_pairs={{0,12},{1,13},{2,14},{3,15},{4,5},{5,4},{6,7},{7,6},{8,9},{9,8},{1... | collective-permute-start | bytes 49160 | tf_op jit(solution)/shard_map/ppermute | solution.py:548
  32.8 3.1 %collective-permute-start.16 = (bf16[4,2048]{1,0:T(4,128)(2,1)S(1)}, bf16[4,2048]{1,0:T(4,128)(2,1)S(1)}, u32[]{:S(2)}, u32[]{:S(2)}) collective-permute-start(bf16[4,2048]{1,0:T(4,128)(2,1)S(1)} %get-tuple-element.115), channel_id=1, source_target_pairs={{0,1},{1,0},{2,3},{3,2},{4,12},{5,13},{6,14},{7,15},{8,9},{9,8},{1... | collective-permute-start | bytes 49160 | tf_op jit(solution)/shard_map/ppermute | solution.py:548
  32.8 3.1 %collective-permute-start.17 = (bf16[4,2048]{1,0:T(4,128)(2,1)S(1)}, bf16[4,2048]{1,0:T(4,128)(2,1)S(1)}, u32[]{:S(2)}, u32[]{:S(2)}) collective-permute-start(bf16[4,2048]{1,0:T(4,128)(2,1)S(1)} %get-tuple-element.116), channel_id=1, source_target_pairs={{0,1},{1,0},{2,3},{3,2},{4,5},{5,4},{6,7},{7,6},{8,12},{9,13},{10,... | collective-permute-start | bytes 49160 | tf_op jit(solution)/shard_map/ppermute | solution.py:548

commit v15 on v14

--- a/solution.py
+++ b/solution.py
@@ -19,7 +19,14 @@
 BF16 = jnp.bfloat16
 CHUNKS = 4
 TOKEN_COST = 10**8
-PASS_COST = 8 * 10**8
+PASS_COSTS = {
+    (1, 0): 8 * 10**8,
+    (2, 0): 5 * 10**8,
+    (1, 2): 8 * 10**8,
+    (2, 1): 4 * 10**8,
+    (2, 2): 4 * 10**8,
+}
+GAP_COSTS = (8 * 10**8, 5 * 10**8)
 VMEM_LIMIT = 32 * 1024 * 1024
 
 
@@ -88,10 +95,21 @@
     return jnp.where(keep(row, column), 1.0, 0.0).astype(BF16)
 
 
+def by_group(first, last):
+    group_lanes = H // G * P_SIZE
+    pieces = []
+    while first < last:
+        g = first // group_lanes
+        end = min(last, (g + 1) * group_lanes)
+        pieces.append((g, first, end))
+        first = end
+    return pieces
+
+
 def chunk_total(first, x_ref, turned, weight, total_ref):
-    width = total_ref.shape[1]
-    scaled = x_ref[:, first : first + width].astype(F32) * over_lanes(weight, first, width)
-    total_ref[...] = dot(turned, scaled.astype(BF16))
+    for g, start, end in by_group(first, first + total_ref.shape[1]):
+        scaled = x_ref[:, start:end].astype(F32) * over_lanes(weight, start, end - start)
+        total_ref[:, start - first : end - first] = dot(turned[g], scaled.astype(BF16))
 
 
 def first_kernel(kept, *refs):
@@ -134,7 +152,7 @@
     copies[0].wait()
     turned = b_ref[:, :N].astype(F32).T.astype(BF16)
     x_copies[0].wait()
-    chunk_total(0, x_ref, turned, weight, total_ref)
+    chunk_total(0, x_ref, [turned], weight, total_ref)
     sent_ref[:N] = total_ref[...].astype(BF16)
     cum = jnp.concatenate(cums, axis=1)
     cum_ref[...] = cum
@@ -144,8 +162,7 @@
         copy.wait()
     if sent_ref.shape[0] > N:
         own = flat(here[3]).astype(BF16)
-        padding = jnp.zeros((own.shape[0], sent_ref.shape[1] - own.shape[1]), BF16)
-        sent_ref[N:] = jnp.concatenate([own, padding], axis=1)
+        sent_ref[N:, : own.shape[1]] = own
 
 
 def state_kernel(bounds, x_ref, b_ref, weight_ref, whole_ref, *rest):
@@ -160,8 +177,7 @@
         first = bounds[k]
         decay_refs[k][...] = over_lanes(whole_ref[...], first, bounds[k + 1] - first, 3)
         if k:
-            g = first // (H // G * P_SIZE)
-            chunk_total(first, x_ref, turned[g], weight_ref[...], total_refs[k - 1])
+            chunk_total(first, x_ref, turned, weight_ref[...], total_refs[k - 1])
     sent_ref[...] = total_refs[0][...].astype(BF16)
 
 
@@ -188,9 +204,8 @@
         names = groups * N
         own, other = [ref[N:, :names].astype(F32) for ref in rest[1 + more : 3 + more]]
         even = lax.rem(me, 2) == 0
-        padding = jnp.zeros((own.shape[0], moving_ref.shape[1] - 2 * names), F32)
-        pair = [jnp.where(even, own, other), jnp.where(even, other, own), padding]
-        moving_ref[N:] = jnp.concatenate(pair, axis=1).astype(BF16)
+        moving_ref[N:, :names] = jnp.where(even, own, other).astype(BF16)
+        moving_ref[N:, names : 2 * names] = jnp.where(even, other, own).astype(BF16)
     elif moving_ref.shape[0] > N:
         moving_ref[N:] = got_ref[N:]
 
@@ -331,11 +346,14 @@
         first = bounds[k]
         width = bounds[k + 1] - first
         here = slice(first, first + width)
-        g = first // (H // G * P_SIZE)
         state = carry_ref[:, here]
         if final:
             state = jnp.where(me == count - 1, got_refs[k][:N], state)
-        carried = dot(asked_ref[:, g * N : (g + 1) * N], state)
+        carried = [
+            dot(asked_ref[:, g * N : (g + 1) * N], state[:, start - first : end - first])
+            for g, start, end in by_group(first, first + width)
+        ]
+        carried = jnp.concatenate(carried, axis=1)
         reading = local_ref[:, here] + over_lanes(gain_ref[...], first, width) * carried
         parts = [reading[r * STEPS : (r + 1) * STEPS] for r in range(count)]
         for op, read_ref in zip(ops, read_refs):
@@ -385,15 +403,15 @@
     gain = jnp.concatenate(gains, axis=1).T
     for i, k in enumerate(part):
         first = bounds[k]
-        width = bounds[k + 1] - first
-        g = first // group_lanes
-        state = jnp.where(last, got_refs[i][:N], carry_ref[:, first : first + width])
-        carried = dot(c_ref[:, g * N : (g + 1) * N], state)
-        inner = inner_refs[g][:, first - g * group_lanes : first - g * group_lanes + width]
-        here = slice(first - bounds[part[0]], first - bounds[part[0]] + width)
-        out_ref[:, here] = (inner + over_lanes(gain, first, width) * carried).astype(BF16)
-        if final:
-            send(out_ref.at[:, here], first, width)
+        state = jnp.where(last, got_refs[i][:N], carry_ref[:, first : bounds[k + 1]])
+        for g, start, end in by_group(first, bounds[k + 1]):
+            carried = dot(c_ref[:, g * N : (g + 1) * N], state[:, start - first : end - first])
+            inner = inner_refs[g][:, start - g * group_lanes : end - g * group_lanes]
+            here = slice(start - bounds[part[0]], end - bounds[part[0]])
+            out = inner + over_lanes(gain, start, end - start) * carried
+            out_ref[:, here] = out.astype(BF16)
+            if final:
+                send(out_ref.at[:, here], start, end - start)
     for copy in copies:
         copy.wait()
 
@@ -482,7 +500,7 @@
     chunks = CHUNKS if count <= 4 else groups
     bounds = tuple(lanes * k // chunks for k in range(chunks + 1))
     if chunks > groups:
-        bounds = bounds[:1] + (bounds[1] - 128,) + bounds[2:]
+        bounds = bounds[:1] + (bounds[1] - 128, bounds[2] - 128) + bounds[3:]
     widths = [bounds[k + 1] - bounds[k] for k in range(chunks)]
     anywhere = pl.BlockSpec(memory_space=pl.ANY)
     in_hbm = pl.BlockSpec(memory_space=pltpu.HBM)
@@ -591,7 +609,7 @@
             (pltpu.HBM((tokens, lanes), BF16), shape((8, 128))) if before else out,
             in_specs=[in_vmem] * len(operands) + [anywhere] * len(after),
             out_specs=(in_hbm, in_vmem) if before else in_vmem,
-            scratch_shapes=[out, pltpu.SemaphoreType.DMA((chunks,))] if before else [],
+            scratch_shapes=[out, pltpu.SemaphoreType.DMA((chunks + groups,))] if before else [],
         )(*operands, *after)
 
     def read_part(ops, final, *after):
@@ -623,12 +641,12 @@
             keep, fresh, held = fresh_part(inner[-1])
             after = [keep]
         if hop == count - 2 and k > 1:
-            after = [token(got[hop + 1, k - 2], tie, flops=5 * TOKEN_COST)]
+            after = [token(got[hop + 1, k - 2], tie, flops=GAP_COSTS[k - 2])]
         tie, carry, *following = call(
             functools.partial(pass_kernel, hop, bounds[k], more),
             (sent_shape(hop + 1, k), shape((N, lanes), BF16))
             + ((sent_shape(1, k + 2),) if more else ()),
-            flops=PASS_COST if k % 2 == 0 else 1,
+            flops=PASS_COSTS.get((hop, k), 1),
             in_specs=[in_vmem] * len(operands) + [anywhere] * len(after),
             input_output_aliases={} if carry is None else {3: 1},
         )(*operands, *after)

time: 36.8 us -> 35.6 us (0.967)
  starting transfers between devices: 18.3 us -> 16.6 us
    ppermute x18, starting transfers between devices: 18.3 us -> 16.6 us  [swap(): return lax.ppermute(value, ('seq', 'tp'), pairs)]
  transfers between devices with their start and end apart: 18 -> 18, of which waited for: 6 -> 5; matrix products, arithmetic and copies ran while one was open for 0% -> 0% of each run, Pallas kernels for 21% -> 22%
where the time goes in v15:
time: 35.6 us; the launch traced here: 35.4 us
  starting transfers between devices  16.6 us (47%)
  Pallas kernels  10.5 us (29%)
  waiting for transfers between devices  7.42 us (21%)
  between operations  0.87 us (2%)
    ppermute x18, starting transfers between devices, swap(): return lax.ppermute(value, ('seq', 'tp'), pairs)  16.6 us
    ppermute x18, waiting for transfers between devices, swap(): return lax.ppermute(value, ('seq', 'tp'), pairs)  7.42 us
    pallas_call x2, Pallas kernels, inner_part(): call(functools.partial(inner_kernel, g), shape((tokens, group_lanes)), in...  2.17 us
    pallas_call x2, Pallas kernels, outer_part(): call(functools.partial(outer_kernel, parts, bounds, count), (pltpu.HBM((t...  2.11 us
    pallas_call x1, Pallas kernels, shards(): call(functools.partial(first_kernel, len(inputs)), tuple((shape(value.sha...  1.88 us
    pallas_call x1, Pallas kernels, state_part(): call(functools.partial(state_kernel, bounds), decay_shapes + total_shapes...  1.31 us
    pallas_call x1, Pallas kernels, ask_part(): call(functools.partial(ask_kernel, ride), (shape((rows, lanes)), shape((r...  0.92 us
    pallas_call x1, Pallas kernels, shards(): call(functools.partial(finish_kernel, ops), jax.ShapeDtypeStruct((count,...  0.73 us
  transfers between devices with their start and end apart: 18, of which 5 were waited for; matrix products, arithmetic and copies ran while one was open for 0% of the time, Pallas kernels for 22%

profile of v15, /device:TPU:0, one launch (start us, length us, event | category | flops | bytes accessed | tf_op | source)
XLA Modules:
  0.0 35.4 jit_solution(8171571703945192006)
XLA Ops:
  0.6 1.9 %first_kernel.1 = (bf16[256,2048]{1,0:T(8,128)(2,1)S(1)}, bf16[256,256]{1,0:T(8,128)(2,1)S(1)}, f32[1,32]{1,0:T(1,128)S(1)}, bf16[4,4,256]{2,1,0:T(4,128)(2,1)S(...) custom-call(bf16[256,2048]{1,0:T(8,128)(2,1)} %refs_0_.1, ...), custom_call_target="tpu_custom_call" | custom-call | flops 1 | bytes 1 | tf_op jit(solution)/shard_map/first_kernel/pallas_call | solution.py:528
  2.5 3.1 %collective-permute-start.1 = (bf16[144,384]{1,0:T(8,128)(2,1)S(1)}, bf16[144,384]{1,0:T(8,128)(2,1)S(1)}, u32[]{:S(2)}, u32[]{:S(2)}) collective-permute-start(bf16[144,384]{1,0:T(8,128)(2,1)S(1)} %get-tuple-element.71.rest_2_), channel_id=1, source_target_pairs={{0,4},{1,5},{2,6},{3,7},{4,0},{5,1},{6,2},{7,3},{8,12},{9,13},{10,... | collective-permute-start | bytes 331784 | tf_op jit(solution)/shard_map/hop1_chunk0/ppermute | solution.py:566
  5.6 1.1 %inner_kernel.2.rest_0_.rest_2_ = f32[256,1024]{1,0:T(8,128)S(1)} custom-call(bf16[256,2048]{1,0:T(8,128)(2,1)S(1)} %get-tuple-element.62.x_ref, bf16[256,256]{1,0:T(8,128)(2,1)S(1)} %get-tuple-element.63.b_ref, bf16[256,256]{1,0:T(8,128)(2,1)S(1)} %get-tuple-element.60.c_ref, f32[32,256]{1,0:T(8,128)S(1)} %get-tuple-element.61.cum_ref, ...), custom_call_target="tpu_custom_call" | custom-call | flops 1 | bytes 1 | tf_op jit(solution)/shard_map/inner_kernel/pallas_call | solution.py:577
  6.7 1.3 %state_kernel.1 = (f32[1,384]{1,0:T(1,128)S(1)}, f32[1,512]{1,0:T(1,128)S(1)}, f32[1,640]{1,0:T(1,128)S(1)}, f32[1,512]{1,0:T(1,128)S(1)}, f32[128,512]{1,0:T(8,...) custom-call(bf16[256,2048]{1,0:T(8,128)(2,1)S(1)} %get-tuple-element.62.x_ref, ...), custom_call_target="tpu_custom_call" | custom-call | flops 1 | bytes 1 | tf_op jit(solution)/shard_map/state_kernel/pallas_call | solution.py:551
  8.0 0.1 collective-permute-start
  8.1 0.6 %collective-permute-done.1.got_ref.rest_3_ = bf16[144,384]{1,0:T(8,128)(2,1)S(1)} collective-permute-done((bf16[144,384]{1,0:T(8,128)(2,1)S(1)}, bf16[144,384]{1,0:T(8,128)(2,1)S(1)}, u32[]{:S(2)}, u32[]{:S(2)}) %collective-permute-start.1) | collective-permute-done | bytes 110624 | tf_op jit(solution)/shard_map/hop1_chunk0/ppermute | solution.py:566
  8.7 0.1 pass_kernel.8
  8.7 1.8 %collective-permute-start.4 = (bf16[128,640]{1,0:T(8,128)(2,1)S(1)}, bf16[128,640]{1,0:T(8,128)(2,1)S(1)}, u32[]{:S(2)}, u32[]{:S(2)}) collective-permute-start(bf16[128,640]{1,0:T(8,128)(2,1)S(1)} %get-tuple-element.89), channel_id=1, source_target_pairs={{0,4},{1,5},{2,6},{3,7},{4,0},{5,1},{6,2},{7,3},{8,9},{9,8},{10,11... | collective-permute-start | bytes 491528 | tf_op jit(solution)/shard_map/hop1_chunk2/ppermute | solution.py:566
  10.6 0.0 collective-permute-start.5
  10.6 1.1 %inner_kernel.3.rest_0_.rest_3_ = f32[256,1024]{1,0:T(8,128)S(1)} custom-call(bf16[256,2048]{1,0:T(8,128)(2,1)S(1)} %get-tuple-element.62.x_ref, bf16[256,256]{1,0:T(8,128)(2,1)S(1)} %get-tuple-element.63.b_ref, bf16[256,256]{1,0:T(8,128)(2,1)S(1)} %get-tuple-element.60.c_ref, f32[32,256]{1,0:T(8,128)S(1)} %get-tuple-element.61.cum_ref, ...), custom_call_target="tpu_custom_call" | custom-call | flops 1 | bytes 1 | tf_op jit(solution)/shard_map/inner_kernel/pallas_call | solution.py:577
  11.6 0.4 %fresh_kernel.1 = (f32[4,4,2048]{2,1,0:T(4,128)S(1)}, f32[4,4,2048]{2,1,0:T(4,128)S(1)}, f32[4,4,128]{2,1,0:T(4,128)S(1)}) custom-call(bf16[4,4,2048]{2,1,0:T(4,128)(2,1)S(1)} %get-tuple-element.77.x_ref, bf16[4,4,256]{2,1,0:T(4,128)(2,1)S(1)} %get-tuple-element.78.b_ref, bf16[4,4,256]{2,1,0:T(4,128)(2,1)S(1)} %get-tuple-element.79.c_ref, ...), custom_call_target="tpu_custom_call" | custom-call | flops 1 | bytes 1 | tf_op jit(solution)/shard_map/fresh_kernel/pallas_call | solution.py:597
  12.1 2.4 %collective-permute-done.got_ref = bf16[128,512]{1,0:T(8,128)(2,1)S(1)} collective-permute-done((bf16[128,512]{1,0:T(8,128)(2,1)S(1)}, bf16[128,512]{1,0:T(8,128)(2,1)S(1)}, u32[]{:S(2)}, u32[]{:S(2)}) %collective-permute-start) | collective-permute-done | bytes 131104 | tf_op jit(solution)/shard_map/hop1_chunk1/ppermute | solution.py:566
  14.6 0.1 collective-permute-start.3
  14.6 0.1 collective-permute-start.2
  14.7 0.0 collective-permute-done.5.got_ref
  14.8 0.5 %collective-permute-start.8 = (bf16[128,384]{1,0:T(8,128)(2,1)S(1)}, bf16[128,384]{1,0:T(8,128)(2,1)S(1)}, u32[]{:S(2)}, u32[]{:S(2)}) collective-permute-start(bf16[128,384]{1,0:T(8,128)(2,1)S(1)} %get-tuple-element.98), channel_id=1, source_target_pairs={{0,1},{1,0},{2,3},{3,2},{4,5},{5,4},{6,7},{7,6},{8,12},{9,13},{10,... | collective-permute-start | bytes 294920 | tf_op jit(solution)/shard_map/hop3_chunk0/ppermute | solution.py:566
  15.2 1.3 %collective-permute-done.4.got_ref = bf16[128,640]{1,0:T(8,128)(2,1)S(1)} collective-permute-done((bf16[128,640]{1,0:T(8,128)(2,1)S(1)}, bf16[128,640]{1,0:T(8,128)(2,1)S(1)}, u32[]{:S(2)}, u32[]{:S(2)}) %collective-permute-start.4) | collective-permute-done | bytes 163872 | tf_op jit(solution)/shard_map/hop1_chunk2/ppermute | solution.py:566
  16.6 0.1 collective-permute-start.7
  16.7 0.0 collective-permute-done.3.got_ref.rest_1_
  16.7 3.2 %collective-permute-start.9 = (bf16[144,512]{1,0:T(8,128)(2,1)S(1)}, bf16[144,512]{1,0:T(8,128)(2,1)S(1)}, u32[]{:S(2)}, u32[]{:S(2)}) collective-permute-start(bf16[144,512]{1,0:T(8,128)(2,1)S(1)} %get-tuple-element.100), channel_id=1, source_target_pairs={{0,4},{1,5},{2,6},{3,7},{4,0},{5,1},{6,2},{7,3},{8,12},{9,13},{10,... | collective-permute-start | bytes 442376 | tf_op jit(solution)/shard_map/hop3_chunk1/ppermute | solution.py:566
  19.9 1.1 %collective-permute-done.2.got_ref = bf16[128,512]{1,0:T(8,128)(2,1)S(1)} collective-permute-done((bf16[128,512]{1,0:T(8,128)(2,1)S(1)}, bf16[128,512]{1,0:T(8,128)(2,1)S(1)}, u32[]{:S(2)}, u32[]{:S(2)}) %collective-permute-start.2) | collective-permute-done | bytes 131104 | tf_op jit(solution)/shard_map/hop1_chunk3/ppermute | solution.py:566
  21.0 0.1 collective-permute-start.6
  21.1 0.0 collective-permute-done.8.refs_0_.rest_0_
  21.1 0.0 collective-permute-done.7.got_ref
  21.2 0.1 pass_kernel.14
  21.2 0.5 %collective-permute-start.10 = (bf16[128,640]{1,0:T(8,128)(2,1)S(1)}, bf16[128,640]{1,0:T(8,128)(2,1)S(1)}, u32[]{:S(2)}, u32[]{:S(2)}) collective-permute-start(bf16[128,640]{1,0:T(8,128)(2,1)S(1)} %get-tuple-element.101.refs_1_), channel_id=1, source_target_pairs={{0,1},{1,0},{2,3},{3,2},{4,5},{5,4},{6,7},{7,6},{8,12},{9,13},{10,... | collective-permute-start | bytes 491528 | tf_op jit(solution)/shard_map/hop3_chunk2/ppermute | solution.py:566
  21.8 2.0 %collective-permute-done.9.refs_0_.rest_2_.rest_1_ = bf16[144,512]{1,0:T(8,128)(2,1)S(1)} collective-permute-done((bf16[144,512]{1,0:T(8,128)(2,1)S(1)}, bf16[144,512]{1,0:T(8,128)(2,1)S(1)}, u32[]{:S(2)}, u32[]{:S(2)}) %collective-permute-start.9) | collective-permute-done | bytes 147488 | tf_op jit(solution)/shard_map/hop3_chunk1/ppermute | solution.py:566
  23.7 0.0 collective-permute-done.6.got_ref
  23.8 0.1 collective-permute-start.11
  23.8 0.9 %ask_kernel.1 = (f32[16,2048]{1,0:T(8,128)S(1)}, f32[16,32]{1,0:T(8,128)S(1)}, bf16[16,256]{1,0:T(8,128)(2,1)S(1)}) custom-call(bf16[256,2048]{1,0:T(8,128)(2,1)S(1)} %get-tuple-element.62.x_ref, bf16[256,256]{1,0:T(8,128)(2,1)S(1)} %get-tuple-element.63.b_ref, f32[32,256]{1,0:T(8,128)S(1)} %get-tuple-element.61.cum_ref, ...), custom_call_target="tpu_custom_call" | custom-call | flops 1 | bytes 1 | tf_op jit(solution)/shard_map/ask_kernel/pallas_call | solution.py:585
  24.8 0.3 read_kernel.2
  25.0 2.6 %collective-permute-start.13 = (bf16[4,2048]{1,0:T(4,128)(2,1)S(1)}, bf16[4,2048]{1,0:T(4,128)(2,1)S(1)}, u32[]{:S(2)}, u32[]{:S(2)}) collective-permute-start(bf16[4,2048]{1,0:T(4,128)(2,1)S(1)} %get-tuple-element.112), channel_id=1, source_target_pairs={{0,8},{1,9},{2,10},{3,11},{4,5},{5,4},{6,7},{7,6},{8,0},{9,1},{10,... | collective-permute-start | bytes 49160 | tf_op jit(solution)/shard_map/ppermute | solution.py:566
  27.6 0.0 collective-permute-start.14
  27.6 0.9 %collective-permute-start.12 = (bf16[4,2048]{1,0:T(4,128)(2,1)S(1)}, bf16[4,2048]{1,0:T(4,128)(2,1)S(1)}, u32[]{:S(2)}, u32[]{:S(2)}) collective-permute-start(bf16[4,2048]{1,0:T(4,128)(2,1)S(1)} %get-tuple-element.107.refs_1_), channel_id=1, source_target_pairs={{0,4},{1,5},{2,6},{3,7},{4,0},{5,1},{6,2},{7,3},{8,9},{9,8},{10,11... | collective-permute-start | bytes 49160 | tf_op jit(solution)/shard_map/ppermute | solution.py:566
  28.6 0.0 collective-permute-done.10.refs_0_.rest_2_.rest_0_
  28.6 0.0 collective-permute-done.11.rest_3_.rest_1_
  28.6 0.3 read_kernel.3
  28.9 3.0 %collective-permute-start.15 = (bf16[4,2048]{1,0:T(4,128)(2,1)S(1)}, bf16[4,2048]{1,0:T(4,128)(2,1)S(1)}, u32[]{:S(2)}, u32[]{:S(2)}) collective-permute-start(bf16[4,2048]{1,0:T(4,128)(2,1)S(1)} %get-tuple-element.114), channel_id=1, source_target_pairs={{0,12},{1,13},{2,14},{3,15},{4,5},{5,4},{6,7},{7,6},{8,9},{9,8},{1... | collective-permute-start | bytes 49160 | tf_op jit(solution)/shard_map/ppermute | solution.py:566
  31.9 0.0 collective-permute-start.16
  31.9 0.0 collective-permute-done.13.refs_2_.rest_1_
  31.9 0.5 %collective-permute-start.17 = (bf16[4,2048]{1,0:T(4,128)(2,1)S(1)}, bf16[4,2048]{1,0:T(4,128)(2,1)S(1)}, u32[]{:S(2)}, u32[]{:S(2)}) collective-permute-start(bf16[4,2048]{1,0:T(4,128)(2,1)S(1)} %get-tuple-element.116), channel_id=1, source_target_pairs={{0,1},{1,0},{2,3},{3,2},{4,5},{5,4},{6,7},{7,6},{8,12},{9,13},{10,... | collective-permute-start | bytes 49160 | tf_op jit(solution)/shard_map/ppermute | solution.py:566
  32.4 0.6 %outer_kernel.2.rest_4_ = bf16[256,896]{1,0:T(8,128)(2,1)S(1)} custom-call(bf16[256,256]{1,0:T(8,128)(2,1)S(1)} %get-tuple-element.60.c_ref, f32[32,256]{1,0:T(8,128)S(1)} %get-tuple-element.61.cum_ref, bf16[128,2048]{1,0:T(8,128)(2,1)S(1)} %get-tuple-element.102.carry_ref, bf16[128,384]{1,0:T(8,128)(2,1)S(1)} %collective-permute-done.8.refs_0_.rest_0_, ...), custom_call_target="tpu_custom_call" | custom-call | flops 1 | bytes 1 | tf_op jit(solution)/shard_map/outer_kernel/pallas_call | solution.py:607
  33.1 1.5 %outer_kernel.3 = (bf16[256,2048]{1,0:T(8,128)(2,1)}, f32[8,128]{1,0:T(8,128)S(1)}) custom-call(bf16[256,256]{1,0:T(8,128)(2,1)S(1)} %get-tuple-element.60.c_ref, f32[32,256]{1,0:T(8,128)S(1)} %get-tuple-element.61.cum_ref, bf16[128,2048]{1,0:T(8,128)(2,1)S(1)} %get-tuple-element.102.carry_ref, ...), custom_call_target="tpu_custom_call" | custom-call | flops 1 | bytes 1 | tf_op jit(solution)/shard_map/outer_kernel/pallas_call | solution.py:607
  34.6 0.0 collective-permute-done.14.refs_3_.rest_2_
  34.6 0.0 collective-permute-done.12.refs_1_.rest_0_
  34.6 0.0 collective-permute-done.15.rest_3_
  34.6 0.0 collective-permute-done.16.rest_4_
  34.6 0.0 collective-permute-done.17.rest_5_
  34.6 0.7 %finish_kernel.1 = bf16[4,4,2048]{2,1,0:T(4,128)(2,1)} custom-call(f32[4,4,2048]{2,1,0:T(4,128)S(1)} %get-tuple-element.85.rest_4_.keep_ref, f32[4,4,2048]{2,1,0:T(4,128)S(1)} %get-tuple-element.110.fresh_ref, f32[4,4,128]{2,1,0:T(4,128)S(1)} %get-tuple-element.111.held_ref, bf16[4,2048]{1,0:T(4,128)(2,1)S(1)} %collective-permute-done.12.refs_1_.rest_0_, ...), custom_call_target="tpu_custom_call" | custom-call | flops 1 | bytes 1 | tf_op jit(solution)/shard_map/finish_kernel/pallas_call | solution.py:678
  (10 shorter events, 0.2 us)
Async XLA Ops:
  2.5 6.1 %collective-permute-start.1 = (bf16[144,384]{1,0:T(8,128)(2,1)S(1)}, bf16[144,384]{1,0:T(8,128)(2,1)S(1)}, u32[]{:S(2)}, u32[]{:S(2)}) collective-permute-start(bf16[144,384]{1,0:T(8,128)(2,1)S(1)} %get-tuple-element.71.rest_2_), channel_id=1, source_target_pairs={{0,4},{1,5},{2,6},{3,7},{4,0},{5,1},{6,2},{7,3},{8,12},{9,13},{10,... | collective-permute-start | bytes 331784 | tf_op jit(solution)/shard_map/hop1_chunk0/ppermute | solution.py:566
  8.0 6.5 %collective-permute-start = (bf16[128,512]{1,0:T(8,128)(2,1)S(1)}, bf16[128,512]{1,0:T(8,128)(2,1)S(1)}, u32[]{:S(2)}, u32[]{:S(2)}) collective-permute-start(bf16[128,512]{1,0:T(8,128)(2,1)S(1)} %get-tuple-element.68), channel_id=1, source_target_pairs={{0,4},{1,5},{2,6},{3,7},{4,0},{5,1},{6,2},{7,3},{8,9},{9,8},{10,11... | collective-permute-start | bytes 393224 | tf_op jit(solution)/shard_map/hop1_chunk1/ppermute | solution.py:566
  8.7 7.8 %collective-permute-start.4 = (bf16[128,640]{1,0:T(8,128)(2,1)S(1)}, bf16[128,640]{1,0:T(8,128)(2,1)S(1)}, u32[]{:S(2)}, u32[]{:S(2)}) collective-permute-start(bf16[128,640]{1,0:T(8,128)(2,1)S(1)} %get-tuple-element.89), channel_id=1, source_target_pairs={{0,4},{1,5},{2,6},{3,7},{4,0},{5,1},{6,2},{7,3},{8,9},{9,8},{10,11... | collective-permute-start | bytes 491528 | tf_op jit(solution)/shard_map/hop1_chunk2/ppermute | solution.py:566
  10.6 4.2 %collective-permute-start.5 = (bf16[128,384]{1,0:T(8,128)(2,1)S(1)}, bf16[128,384]{1,0:T(8,128)(2,1)S(1)}, u32[]{:S(2)}, u32[]{:S(2)}) collective-permute-start(bf16[128,384]{1,0:T(8,128)(2,1)S(1)} %get-tuple-element.84.rest_0_), channel_id=1, source_target_pairs={{0,1},{1,0},{2,3},{3,2},{4,8},{5,9},{6,10},{7,11},{8,4},{9,5},{10,... | collective-permute-start | bytes 294920 | tf_op jit(solution)/shard_map/hop2_chunk0/ppermute | solution.py:566
  14.6 2.1 %collective-permute-start.3 = (bf16[144,512]{1,0:T(8,128)(2,1)S(1)}, bf16[144,512]{1,0:T(8,128)(2,1)S(1)}, u32[]{:S(2)}, u32[]{:S(2)}) collective-permute-start(bf16[144,512]{1,0:T(8,128)(2,1)S(1)} %get-tuple-element.88.rest_0_), channel_id=1, source_target_pairs={{0,1},{1,0},{2,3},{3,2},{4,8},{5,9},{6,10},{7,11},{8,4},{9,5},{10,... | collective-permute-start | bytes 442376 | tf_op jit(solution)/shard_map/hop2_chunk1/ppermute | solution.py:566
  14.6 6.4 %collective-permute-start.2 = (bf16[128,512]{1,0:T(8,128)(2,1)S(1)}, bf16[128,512]{1,0:T(8,128)(2,1)S(1)}, u32[]{:S(2)}, u32[]{:S(2)}) collective-permute-start(bf16[128,512]{1,0:T(8,128)(2,1)S(1)} %get-tuple-element.86), channel_id=1, source_target_pairs={{0,4},{1,5},{2,6},{3,7},{4,0},{5,1},{6,2},{7,3},{8,9},{9,8},{10,11... | collective-permute-start | bytes 393224 | tf_op jit(solution)/shard_map/hop1_chunk3/ppermute | solution.py:566
  14.8 6.4 %collective-permute-start.8 = (bf16[128,384]{1,0:T(8,128)(2,1)S(1)}, bf16[128,384]{1,0:T(8,128)(2,1)S(1)}, u32[]{:S(2)}, u32[]{:S(2)}) collective-permute-start(bf16[128,384]{1,0:T(8,128)(2,1)S(1)} %get-tuple-element.98), channel_id=1, source_target_pairs={{0,1},{1,0},{2,3},{3,2},{4,5},{5,4},{6,7},{7,6},{8,12},{9,13},{10,... | collective-permute-start | bytes 294920 | tf_op jit(solution)/shard_map/hop3_chunk0/ppermute | solution.py:566
  16.6 4.5 %collective-permute-start.7 = (bf16[128,640]{1,0:T(8,128)(2,1)S(1)}, bf16[128,640]{1,0:T(8,128)(2,1)S(1)}, u32[]{:S(2)}, u32[]{:S(2)}) collective-permute-start(bf16[128,640]{1,0:T(8,128)(2,1)S(1)} %get-tuple-element.96), channel_id=1, source_target_pairs={{0,1},{1,0},{2,3},{3,2},{4,8},{5,9},{6,10},{7,11},{8,4},{9,5},{10,... | collective-permute-start | bytes 491528 | tf_op jit(solution)/shard_map/hop2_chunk2/ppermute | solution.py:566
  16.7 7.0 %collective-permute-start.9 = (bf16[144,512]{1,0:T(8,128)(2,1)S(1)}, bf16[144,512]{1,0:T(8,128)(2,1)S(1)}, u32[]{:S(2)}, u32[]{:S(2)}) collective-permute-start(bf16[144,512]{1,0:T(8,128)(2,1)S(1)} %get-tuple-element.100), channel_id=1, source_target_pairs={{0,4},{1,5},{2,6},{3,7},{4,0},{5,1},{6,2},{7,3},{8,12},{9,13},{10,... | collective-permute-start | bytes 442376 | tf_op jit(solution)/shard_map/hop3_chunk1/ppermute | solution.py:566
  21.0 2.7 %collective-permute-start.6 = (bf16[128,512]{1,0:T(8,128)(2,1)S(1)}, bf16[128,512]{1,0:T(8,128)(2,1)S(1)}, u32[]{:S(2)}, u32[]{:S(2)}) collective-permute-start(bf16[128,512]{1,0:T(8,128)(2,1)S(1)} %get-tuple-element.95.refs_1_), channel_id=1, source_target_pairs={{0,1},{1,0},{2,3},{3,2},{4,8},{5,9},{6,10},{7,11},{8,4},{9,5},{10,... | collective-permute-start | bytes 393224 | tf_op jit(solution)/shard_map/hop2_chunk3/ppermute | solution.py:566
  21.2 7.4 %collective-permute-start.10 = (bf16[128,640]{1,0:T(8,128)(2,1)S(1)}, bf16[128,640]{1,0:T(8,128)(2,1)S(1)}, u32[]{:S(2)}, u32[]{:S(2)}) collective-permute-start(bf16[128,640]{1,0:T(8,128)(2,1)S(1)} %get-tuple-element.101.refs_1_), channel_id=1, source_target_pairs={{0,1},{1,0},{2,3},{3,2},{4,5},{5,4},{6,7},{7,6},{8,12},{9,13},{10,... | collective-permute-start | bytes 491528 | tf_op jit(solution)/shard_map/hop3_chunk2/ppermute | solution.py:566
  23.8 4.8 %collective-permute-start.11 = (bf16[128,512]{1,0:T(8,128)(2,1)S(1)}, bf16[128,512]{1,0:T(8,128)(2,1)S(1)}, u32[]{:S(2)}, u32[]{:S(2)}) collective-permute-start(bf16[128,512]{1,0:T(8,128)(2,1)S(1)} %get-tuple-element.103.rest_3_), channel_id=1, source_target_pairs={{0,1},{1,0},{2,3},{3,2},{4,5},{5,4},{6,7},{7,6},{8,12},{9,13},{10,... | collective-permute-start | bytes 393224 | tf_op jit(solution)/shard_map/hop3_chunk3/ppermute | solution.py:566
  25.0 6.9 %collective-permute-start.13 = (bf16[4,2048]{1,0:T(4,128)(2,1)S(1)}, bf16[4,2048]{1,0:T(4,128)(2,1)S(1)}, u32[]{:S(2)}, u32[]{:S(2)}) collective-permute-start(bf16[4,2048]{1,0:T(4,128)(2,1)S(1)} %get-tuple-element.112), channel_id=1, source_target_pairs={{0,8},{1,9},{2,10},{3,11},{4,5},{5,4},{6,7},{7,6},{8,0},{9,1},{10,... | collective-permute-start | bytes 49160 | tf_op jit(solution)/shard_map/ppermute | solution.py:566
  27.6 6.9 %collective-permute-start.14 = (bf16[4,2048]{1,0:T(4,128)(2,1)S(1)}, bf16[4,2048]{1,0:T(4,128)(2,1)S(1)}, u32[]{:S(2)}, u32[]{:S(2)}) collective-permute-start(bf16[4,2048]{1,0:T(4,128)(2,1)S(1)} %get-tuple-element.113), channel_id=1, source_target_pairs={{0,1},{1,0},{2,3},{3,2},{4,8},{5,9},{6,10},{7,11},{8,4},{9,5},{10,... | collective-permute-start | bytes 49160 | tf_op jit(solution)/shard_map/ppermute | solution.py:566
  27.6 6.9 %collective-permute-start.12 = (bf16[4,2048]{1,0:T(4,128)(2,1)S(1)}, bf16[4,2048]{1,0:T(4,128)(2,1)S(1)}, u32[]{:S(2)}, u32[]{:S(2)}) collective-permute-start(bf16[4,2048]{1,0:T(4,128)(2,1)S(1)} %get-tuple-element.107.refs_1_), channel_id=1, source_target_pairs={{0,4},{1,5},{2,6},{3,7},{4,0},{5,1},{6,2},{7,3},{8,9},{9,8},{10,11... | collective-permute-start | bytes 49160 | tf_op jit(solution)/shard_map/ppermute | solution.py:566
  28.9 5.7 %collective-permute-start.15 = (bf16[4,2048]{1,0:T(4,128)(2,1)S(1)}, bf16[4,2048]{1,0:T(4,128)(2,1)S(1)}, u32[]{:S(2)}, u32[]{:S(2)}) collective-permute-start(bf16[4,2048]{1,0:T(4,128)(2,1)S(1)} %get-tuple-element.114), channel_id=1, source_target_pairs={{0,12},{1,13},{2,14},{3,15},{4,5},{5,4},{6,7},{7,6},{8,9},{9,8},{1... | collective-permute-start | bytes 49160 | tf_op jit(solution)/shard_map/ppermute | solution.py:566
  31.9 2.7 %collective-permute-start.16 = (bf16[4,2048]{1,0:T(4,128)(2,1)S(1)}, bf16[4,2048]{1,0:T(4,128)(2,1)S(1)}, u32[]{:S(2)}, u32[]{:S(2)}) collective-permute-start(bf16[4,2048]{1,0:T(4,128)(2,1)S(1)} %get-tuple-element.115), channel_id=1, source_target_pairs={{0,1},{1,0},{2,3},{3,2},{4,12},{5,13},{6,14},{7,15},{8,9},{9,8},{1... | collective-permute-start | bytes 49160 | tf_op jit(solution)/shard_map/ppermute | solution.py:566
  31.9 2.7 %collective-permute-start.17 = (bf16[4,2048]{1,0:T(4,128)(2,1)S(1)}, bf16[4,2048]{1,0:T(4,128)(2,1)S(1)}, u32[]{:S(2)}, u32[]{:S(2)}) collective-permute-start(bf16[4,2048]{1,0:T(4,128)(2,1)S(1)} %get-tuple-element.116), channel_id=1, source_target_pairs={{0,1},{1,0},{2,3},{3,2},{4,5},{5,4},{6,7},{7,6},{8,12},{9,13},{10,... | collective-permute-start | bytes 49160 | tf_op jit(solution)/shard_map/ppermute | solution.py:566

commit v16 on v15

--- a/solution.py
+++ b/solution.py
@@ -66,7 +66,9 @@
 
 
 def exact_dot_right(value, ones, pieces):
-    return sum(dot(piece, ones) for piece in split(value, pieces))
+    parts = [piece.astype(F32) for piece in split(value, pieces)]
+    stacked = jnp.concatenate(parts, axis=1).astype(BF16)
+    return dot(stacked, jnp.concatenate([ones] * pieces, axis=0))
 
 
 def shape(dims, dtype=F32):

time: 35.6 us -> 35.8 us (level)
  starting transfers between devices: 16.6 us -> 17.4 us
  waiting for transfers between devices: 7.42 us -> 6.93 us
    ppermute x18, starting transfers between devices: 16.6 us -> 17.4 us  [swap(): return lax.ppermute(value, ('seq', 'tp'), pairs)]
    ppermute x18, waiting for transfers between devices: 7.42 us -> 6.93 us  [swap(): return lax.ppermute(value, ('seq', 'tp'), pairs)]
where the time goes in v16:
time: 35.8 us; the launch traced here: 35.5 us
  starting transfers between devices  17.4 us (49%)
  Pallas kernels  10.4 us (29%)
  waiting for transfers between devices  6.93 us (19%)
  between operations  0.85 us (2%)
    ppermute x18, starting transfers between devices, swap(): return lax.ppermute(value, ('seq', 'tp'), pairs)  17.4 us
    ppermute x18, waiting for transfers between devices, swap(): return lax.ppermute(value, ('seq', 'tp'), pairs)  6.93 us
    pallas_call x2, Pallas kernels, inner_part(): call(functools.partial(inner_kernel, g), shape((tokens, group_lanes)), in...  2.17 us
    pallas_call x2, Pallas kernels, outer_part(): call(functools.partial(outer_kernel, parts, bounds, count), (pltpu.HBM((t...  2.14 us
    pallas_call x1, Pallas kernels, shards(): call(functools.partial(first_kernel, len(inputs)), tuple((shape(value.sha...  1.88 us
    pallas_call x1, Pallas kernels, state_part(): call(functools.partial(state_kernel, bounds), decay_shapes + total_shapes...  1.09 us
    pallas_call x1, Pallas kernels, ask_part(): call(functools.partial(ask_kernel, ride), (shape((rows, lanes)), shape((r...  0.92 us
    pallas_call x1, Pallas kernels, shards(): call(functools.partial(finish_kernel, ops), jax.ShapeDtypeStruct((count,...  0.73 us
  transfers between devices with their start and end apart: 18, of which 5 were waited for; matrix products, arithmetic and copies ran while one was open for 0% of the time, Pallas kernels for 22%

profile of v16, /device:TPU:0, one launch (start us, length us, event | category | flops | bytes accessed | tf_op | source)
XLA Modules:
  0.0 35.5 jit_solution(11236321414726220384)
XLA Ops:
  0.6 1.9 %first_kernel.1 = (bf16[256,2048]{1,0:T(8,128)(2,1)S(1)}, bf16[256,256]{1,0:T(8,128)(2,1)S(1)}, f32[1,32]{1,0:T(1,128)S(1)}, bf16[4,4,256]{2,1,0:T(4,128)(2,1)S(...) custom-call(bf16[256,2048]{1,0:T(8,128)(2,1)} %refs_0_.1, ...), custom_call_target="tpu_custom_call" | custom-call | flops 1 | bytes 1 | tf_op jit(solution)/shard_map/first_kernel/pallas_call | solution.py:530
  2.5 3.1 %collective-permute-start.1 = (bf16[144,384]{1,0:T(8,128)(2,1)S(1)}, bf16[144,384]{1,0:T(8,128)(2,1)S(1)}, u32[]{:S(2)}, u32[]{:S(2)}) collective-permute-start(bf16[144,384]{1,0:T(8,128)(2,1)S(1)} %get-tuple-element.71.rest_2_), channel_id=1, source_target_pairs={{0,4},{1,5},{2,6},{3,7},{4,0},{5,1},{6,2},{7,3},{8,12},{9,13},{10,... | collective-permute-start | bytes 331784 | tf_op jit(solution)/shard_map/hop1_chunk0/ppermute | solution.py:568
  5.6 1.1 %inner_kernel.2.rest_0_.rest_2_ = f32[256,1024]{1,0:T(8,128)S(1)} custom-call(bf16[256,2048]{1,0:T(8,128)(2,1)S(1)} %get-tuple-element.62.x_ref, bf16[256,256]{1,0:T(8,128)(2,1)S(1)} %get-tuple-element.63.b_ref, bf16[256,256]{1,0:T(8,128)(2,1)S(1)} %get-tuple-element.60.c_ref, f32[32,256]{1,0:T(8,128)S(1)} %get-tuple-element.61.cum_ref, ...), custom_call_target="tpu_custom_call" | custom-call | flops 1 | bytes 1 | tf_op jit(solution)/shard_map/inner_kernel/pallas_call | solution.py:579
  6.7 1.1 %state_kernel.1 = (f32[1,384]{1,0:T(1,128)S(1)}, f32[1,512]{1,0:T(1,128)S(1)}, f32[1,640]{1,0:T(1,128)S(1)}, f32[1,512]{1,0:T(1,128)S(1)}, f32[128,512]{1,0:T(8,...) custom-call(bf16[256,2048]{1,0:T(8,128)(2,1)S(1)} %get-tuple-element.62.x_ref, ...), custom_call_target="tpu_custom_call" | custom-call | flops 1 | bytes 1 | tf_op jit(solution)/shard_map/state_kernel/pallas_call | solution.py:553
  7.8 0.1 collective-permute-start
  7.9 0.8 %collective-permute-done.1.got_ref.rest_3_ = bf16[144,384]{1,0:T(8,128)(2,1)S(1)} collective-permute-done((bf16[144,384]{1,0:T(8,128)(2,1)S(1)}, bf16[144,384]{1,0:T(8,128)(2,1)S(1)}, u32[]{:S(2)}, u32[]{:S(2)}) %collective-permute-start.1) | collective-permute-done | bytes 110624 | tf_op jit(solution)/shard_map/hop1_chunk0/ppermute | solution.py:568
  8.7 0.1 pass_kernel.8
  8.7 1.9 %collective-permute-start.4 = (bf16[128,640]{1,0:T(8,128)(2,1)S(1)}, bf16[128,640]{1,0:T(8,128)(2,1)S(1)}, u32[]{:S(2)}, u32[]{:S(2)}) collective-permute-start(bf16[128,640]{1,0:T(8,128)(2,1)S(1)} %get-tuple-element.89), channel_id=1, source_target_pairs={{0,4},{1,5},{2,6},{3,7},{4,0},{5,1},{6,2},{7,3},{8,9},{9,8},{10,11... | collective-permute-start | bytes 491528 | tf_op jit(solution)/shard_map/hop1_chunk2/ppermute | solution.py:568
  10.6 0.0 collective-permute-start.5
  10.6 1.1 %inner_kernel.3.rest_0_.rest_3_ = f32[256,1024]{1,0:T(8,128)S(1)} custom-call(bf16[256,2048]{1,0:T(8,128)(2,1)S(1)} %get-tuple-element.62.x_ref, bf16[256,256]{1,0:T(8,128)(2,1)S(1)} %get-tuple-element.63.b_ref, bf16[256,256]{1,0:T(8,128)(2,1)S(1)} %get-tuple-element.60.c_ref, f32[32,256]{1,0:T(8,128)S(1)} %get-tuple-element.61.cum_ref, ...), custom_call_target="tpu_custom_call" | custom-call | flops 1 | bytes 1 | tf_op jit(solution)/shard_map/inner_kernel/pallas_call | solution.py:579
  11.7 0.5 %fresh_kernel.1 = (f32[4,4,2048]{2,1,0:T(4,128)S(1)}, f32[4,4,2048]{2,1,0:T(4,128)S(1)}, f32[4,4,128]{2,1,0:T(4,128)S(1)}) custom-call(bf16[4,4,2048]{2,1,0:T(4,128)(2,1)S(1)} %get-tuple-element.77.x_ref, bf16[4,4,256]{2,1,0:T(4,128)(2,1)S(1)} %get-tuple-element.78.b_ref, bf16[4,4,256]{2,1,0:T(4,128)(2,1)S(1)} %get-tuple-element.79.c_ref, ...), custom_call_target="tpu_custom_call" | custom-call | flops 1 | bytes 1 | tf_op jit(solution)/shard_map/fresh_kernel/pallas_call | solution.py:599
  12.3 2.0 %collective-permute-done.got_ref = bf16[128,512]{1,0:T(8,128)(2,1)S(1)} collective-permute-done((bf16[128,512]{1,0:T(8,128)(2,1)S(1)}, bf16[128,512]{1,0:T(8,128)(2,1)S(1)}, u32[]{:S(2)}, u32[]{:S(2)}) %collective-permute-start) | collective-permute-done | bytes 131104 | tf_op jit(solution)/shard_map/hop1_chunk1/ppermute | solution.py:568
  14.3 0.1 collective-permute-start.3
  14.4 0.2 collective-permute-start.2
  14.6 0.0 collective-permute-done.5.got_ref
  14.6 0.4 %collective-permute-start.8 = (bf16[128,384]{1,0:T(8,128)(2,1)S(1)}, bf16[128,384]{1,0:T(8,128)(2,1)S(1)}, u32[]{:S(2)}, u32[]{:S(2)}) collective-permute-start(bf16[128,384]{1,0:T(8,128)(2,1)S(1)} %get-tuple-element.98), channel_id=1, source_target_pairs={{0,1},{1,0},{2,3},{3,2},{4,5},{5,4},{6,7},{7,6},{8,12},{9,13},{10,... | collective-permute-start | bytes 294920 | tf_op jit(solution)/shard_map/hop3_chunk0/ppermute | solution.py:568
  15.0 1.3 %collective-permute-done.4.got_ref = bf16[128,640]{1,0:T(8,128)(2,1)S(1)} collective-permute-done((bf16[128,640]{1,0:T(8,128)(2,1)S(1)}, bf16[128,640]{1,0:T(8,128)(2,1)S(1)}, u32[]{:S(2)}, u32[]{:S(2)}) %collective-permute-start.4) | collective-permute-done | bytes 163872 | tf_op jit(solution)/shard_map/hop1_chunk2/ppermute | solution.py:568
  16.4 0.1 collective-permute-start.7
  16.5 0.0 collective-permute-done.3.got_ref.rest_1_
  16.5 3.5 %collective-permute-start.9 = (bf16[144,512]{1,0:T(8,128)(2,1)S(1)}, bf16[144,512]{1,0:T(8,128)(2,1)S(1)}, u32[]{:S(2)}, u32[]{:S(2)}) collective-permute-start(bf16[144,512]{1,0:T(8,128)(2,1)S(1)} %get-tuple-element.100), channel_id=1, source_target_pairs={{0,4},{1,5},{2,6},{3,7},{4,0},{5,1},{6,2},{7,3},{8,12},{9,13},{10,... | collective-permute-start | bytes 442376 | tf_op jit(solution)/shard_map/hop3_chunk1/ppermute | solution.py:568
  20.0 0.8 %collective-permute-done.2.got_ref = bf16[128,512]{1,0:T(8,128)(2,1)S(1)} collective-permute-done((bf16[128,512]{1,0:T(8,128)(2,1)S(1)}, bf16[128,512]{1,0:T(8,128)(2,1)S(1)}, u32[]{:S(2)}, u32[]{:S(2)}) %collective-permute-start.2) | collective-permute-done | bytes 131104 | tf_op jit(solution)/shard_map/hop1_chunk3/ppermute | solution.py:568
  20.8 0.1 collective-permute-start.6
  20.9 0.0 collective-permute-done.8.refs_0_.rest_0_
  20.9 0.0 collective-permute-done.7.got_ref
  20.9 0.1 pass_kernel.14
  21.0 0.5 %collective-permute-start.10 = (bf16[128,640]{1,0:T(8,128)(2,1)S(1)}, bf16[128,640]{1,0:T(8,128)(2,1)S(1)}, u32[]{:S(2)}, u32[]{:S(2)}) collective-permute-start(bf16[128,640]{1,0:T(8,128)(2,1)S(1)} %get-tuple-element.101.refs_1_), channel_id=1, source_target_pairs={{0,1},{1,0},{2,3},{3,2},{4,5},{5,4},{6,7},{7,6},{8,12},{9,13},{10,... | collective-permute-start | bytes 491528 | tf_op jit(solution)/shard_map/hop3_chunk2/ppermute | solution.py:568
  21.5 2.0 %collective-permute-done.9.refs_0_.rest_2_.rest_1_ = bf16[144,512]{1,0:T(8,128)(2,1)S(1)} collective-permute-done((bf16[144,512]{1,0:T(8,128)(2,1)S(1)}, bf16[144,512]{1,0:T(8,128)(2,1)S(1)}, u32[]{:S(2)}, u32[]{:S(2)}) %collective-permute-start.9) | collective-permute-done | bytes 147488 | tf_op jit(solution)/shard_map/hop3_chunk1/ppermute | solution.py:568
  23.5 0.0 collective-permute-done.6.got_ref
  23.5 0.1 collective-permute-start.11
  23.6 0.9 %ask_kernel.1 = (f32[16,2048]{1,0:T(8,128)S(1)}, f32[16,32]{1,0:T(8,128)S(1)}, bf16[16,256]{1,0:T(8,128)(2,1)S(1)}) custom-call(bf16[256,2048]{1,0:T(8,128)(2,1)S(1)} %get-tuple-element.62.x_ref, bf16[256,256]{1,0:T(8,128)(2,1)S(1)} %get-tuple-element.63.b_ref, f32[32,256]{1,0:T(8,128)S(1)} %get-tuple-element.61.cum_ref, ...), custom_call_target="tpu_custom_call" | custom-call | flops 1 | bytes 1 | tf_op jit(solution)/shard_map/ask_kernel/pallas_call | solution.py:587
  24.5 0.3 read_kernel.2
  24.8 2.8 %collective-permute-start.13 = (bf16[4,2048]{1,0:T(4,128)(2,1)S(1)}, bf16[4,2048]{1,0:T(4,128)(2,1)S(1)}, u32[]{:S(2)}, u32[]{:S(2)}) collective-permute-start(bf16[4,2048]{1,0:T(4,128)(2,1)S(1)} %get-tuple-element.112), channel_id=1, source_target_pairs={{0,8},{1,9},{2,10},{3,11},{4,5},{5,4},{6,7},{7,6},{8,0},{9,1},{10,... | collective-permute-start | bytes 49160 | tf_op jit(solution)/shard_map/ppermute | solution.py:568
  27.7 0.0 collective-permute-start.14
  27.7 0.7 %collective-permute-start.12 = (bf16[4,2048]{1,0:T(4,128)(2,1)S(1)}, bf16[4,2048]{1,0:T(4,128)(2,1)S(1)}, u32[]{:S(2)}, u32[]{:S(2)}) collective-permute-start(bf16[4,2048]{1,0:T(4,128)(2,1)S(1)} %get-tuple-element.107.refs_1_), channel_id=1, source_target_pairs={{0,4},{1,5},{2,6},{3,7},{4,0},{5,1},{6,2},{7,3},{8,9},{9,8},{10,11... | collective-permute-start | bytes 49160 | tf_op jit(solution)/shard_map/ppermute | solution.py:568
  28.4 0.0 collective-permute-done.10.refs_0_.rest_2_.rest_0_
  28.4 0.0 collective-permute-done.11.rest_3_.rest_1_
  28.4 0.3 read_kernel.3
  28.7 3.4 %collective-permute-start.15 = (bf16[4,2048]{1,0:T(4,128)(2,1)S(1)}, bf16[4,2048]{1,0:T(4,128)(2,1)S(1)}, u32[]{:S(2)}, u32[]{:S(2)}) collective-permute-start(bf16[4,2048]{1,0:T(4,128)(2,1)S(1)} %get-tuple-element.114), channel_id=1, source_target_pairs={{0,12},{1,13},{2,14},{3,15},{4,5},{5,4},{6,7},{7,6},{8,9},{9,8},{1... | collective-permute-start | bytes 49160 | tf_op jit(solution)/shard_map/ppermute | solution.py:568
  32.1 0.0 collective-permute-start.16
  32.1 0.0 collective-permute-done.13.refs_2_.rest_1_
  32.1 0.5 %collective-permute-start.17 = (bf16[4,2048]{1,0:T(4,128)(2,1)S(1)}, bf16[4,2048]{1,0:T(4,128)(2,1)S(1)}, u32[]{:S(2)}, u32[]{:S(2)}) collective-permute-start(bf16[4,2048]{1,0:T(4,128)(2,1)S(1)} %get-tuple-element.116), channel_id=1, source_target_pairs={{0,1},{1,0},{2,3},{3,2},{4,5},{5,4},{6,7},{7,6},{8,12},{9,13},{10,... | collective-permute-start | bytes 49160 | tf_op jit(solution)/shard_map/ppermute | solution.py:568
  32.6 0.6 %outer_kernel.2.rest_4_ = bf16[256,896]{1,0:T(8,128)(2,1)S(1)} custom-call(bf16[256,256]{1,0:T(8,128)(2,1)S(1)} %get-tuple-element.60.c_ref, f32[32,256]{1,0:T(8,128)S(1)} %get-tuple-element.61.cum_ref, bf16[128,2048]{1,0:T(8,128)(2,1)S(1)} %get-tuple-element.102.carry_ref, bf16[128,384]{1,0:T(8,128)(2,1)S(1)} %collective-permute-done.8.refs_0_.rest_0_, ...), custom_call_target="tpu_custom_call" | custom-call | flops 1 | bytes 1 | tf_op jit(solution)/shard_map/outer_kernel/pallas_call | solution.py:609
  33.2 1.5 %outer_kernel.3 = (bf16[256,2048]{1,0:T(8,128)(2,1)}, f32[8,128]{1,0:T(8,128)S(1)}) custom-call(bf16[256,256]{1,0:T(8,128)(2,1)S(1)} %get-tuple-element.60.c_ref, f32[32,256]{1,0:T(8,128)S(1)} %get-tuple-element.61.cum_ref, bf16[128,2048]{1,0:T(8,128)(2,1)S(1)} %get-tuple-element.102.carry_ref, ...), custom_call_target="tpu_custom_call" | custom-call | flops 1 | bytes 1 | tf_op jit(solution)/shard_map/outer_kernel/pallas_call | solution.py:609
  34.7 0.0 collective-permute-done.14.refs_3_.rest_2_
  34.8 0.0 collective-permute-done.12.refs_1_.rest_0_
  34.8 0.0 collective-permute-done.15.rest_3_
  34.8 0.0 collective-permute-done.16.rest_4_
  34.8 0.0 collective-permute-done.17.rest_5_
  34.8 0.7 %finish_kernel.1 = bf16[4,4,2048]{2,1,0:T(4,128)(2,1)} custom-call(f32[4,4,2048]{2,1,0:T(4,128)S(1)} %get-tuple-element.85.rest_4_.keep_ref, f32[4,4,2048]{2,1,0:T(4,128)S(1)} %get-tuple-element.110.fresh_ref, f32[4,4,128]{2,1,0:T(4,128)S(1)} %get-tuple-element.111.held_ref, bf16[4,2048]{1,0:T(4,128)(2,1)S(1)} %collective-permute-done.12.refs_1_.rest_0_, ...), custom_call_target="tpu_custom_call" | custom-call | flops 1 | bytes 1 | tf_op jit(solution)/shard_map/finish_kernel/pallas_call | solution.py:680
  (10 shorter events, 0.2 us)
Async XLA Ops:
  2.5 6.2 %collective-permute-start.1 = (bf16[144,384]{1,0:T(8,128)(2,1)S(1)}, bf16[144,384]{1,0:T(8,128)(2,1)S(1)}, u32[]{:S(2)}, u32[]{:S(2)}) collective-permute-start(bf16[144,384]{1,0:T(8,128)(2,1)S(1)} %get-tuple-element.71.rest_2_), channel_id=1, source_target_pairs={{0,4},{1,5},{2,6},{3,7},{4,0},{5,1},{6,2},{7,3},{8,12},{9,13},{10,... | collective-permute-start | bytes 331784 | tf_op jit(solution)/shard_map/hop1_chunk0/ppermute | solution.py:568
  7.8 6.5 %collective-permute-start = (bf16[128,512]{1,0:T(8,128)(2,1)S(1)}, bf16[128,512]{1,0:T(8,128)(2,1)S(1)}, u32[]{:S(2)}, u32[]{:S(2)}) collective-permute-start(bf16[128,512]{1,0:T(8,128)(2,1)S(1)} %get-tuple-element.68), channel_id=1, source_target_pairs={{0,4},{1,5},{2,6},{3,7},{4,0},{5,1},{6,2},{7,3},{8,9},{9,8},{10,11... | collective-permute-start | bytes 393224 | tf_op jit(solution)/shard_map/hop1_chunk1/ppermute | solution.py:568
  8.7 7.6 %collective-permute-start.4 = (bf16[128,640]{1,0:T(8,128)(2,1)S(1)}, bf16[128,640]{1,0:T(8,128)(2,1)S(1)}, u32[]{:S(2)}, u32[]{:S(2)}) collective-permute-start(bf16[128,640]{1,0:T(8,128)(2,1)S(1)} %get-tuple-element.89), channel_id=1, source_target_pairs={{0,4},{1,5},{2,6},{3,7},{4,0},{5,1},{6,2},{7,3},{8,9},{9,8},{10,11... | collective-permute-start | bytes 491528 | tf_op jit(solution)/shard_map/hop1_chunk2/ppermute | solution.py:568
  10.6 4.0 %collective-permute-start.5 = (bf16[128,384]{1,0:T(8,128)(2,1)S(1)}, bf16[128,384]{1,0:T(8,128)(2,1)S(1)}, u32[]{:S(2)}, u32[]{:S(2)}) collective-permute-start(bf16[128,384]{1,0:T(8,128)(2,1)S(1)} %get-tuple-element.84.rest_0_), channel_id=1, source_target_pairs={{0,1},{1,0},{2,3},{3,2},{4,8},{5,9},{6,10},{7,11},{8,4},{9,5},{10,... | collective-permute-start | bytes 294920 | tf_op jit(solution)/shard_map/hop2_chunk0/ppermute | solution.py:568
  14.3 2.1 %collective-permute-start.3 = (bf16[144,512]{1,0:T(8,128)(2,1)S(1)}, bf16[144,512]{1,0:T(8,128)(2,1)S(1)}, u32[]{:S(2)}, u32[]{:S(2)}) collective-permute-start(bf16[144,512]{1,0:T(8,128)(2,1)S(1)} %get-tuple-element.88.rest_0_), channel_id=1, source_target_pairs={{0,1},{1,0},{2,3},{3,2},{4,8},{5,9},{6,10},{7,11},{8,4},{9,5},{10,... | collective-permute-start | bytes 442376 | tf_op jit(solution)/shard_map/hop2_chunk1/ppermute | solution.py:568
  14.4 6.4 %collective-permute-start.2 = (bf16[128,512]{1,0:T(8,128)(2,1)S(1)}, bf16[128,512]{1,0:T(8,128)(2,1)S(1)}, u32[]{:S(2)}, u32[]{:S(2)}) collective-permute-start(bf16[128,512]{1,0:T(8,128)(2,1)S(1)} %get-tuple-element.86), channel_id=1, source_target_pairs={{0,4},{1,5},{2,6},{3,7},{4,0},{5,1},{6,2},{7,3},{8,9},{9,8},{10,11... | collective-permute-start | bytes 393224 | tf_op jit(solution)/shard_map/hop1_chunk3/ppermute | solution.py:568
  14.6 6.3 %collective-permute-start.8 = (bf16[128,384]{1,0:T(8,128)(2,1)S(1)}, bf16[128,384]{1,0:T(8,128)(2,1)S(1)}, u32[]{:S(2)}, u32[]{:S(2)}) collective-permute-start(bf16[128,384]{1,0:T(8,128)(2,1)S(1)} %get-tuple-element.98), channel_id=1, source_target_pairs={{0,1},{1,0},{2,3},{3,2},{4,5},{5,4},{6,7},{7,6},{8,12},{9,13},{10,... | collective-permute-start | bytes 294920 | tf_op jit(solution)/shard_map/hop3_chunk0/ppermute | solution.py:568
  16.4 4.5 %collective-permute-start.7 = (bf16[128,640]{1,0:T(8,128)(2,1)S(1)}, bf16[128,640]{1,0:T(8,128)(2,1)S(1)}, u32[]{:S(2)}, u32[]{:S(2)}) collective-permute-start(bf16[128,640]{1,0:T(8,128)(2,1)S(1)} %get-tuple-element.96), channel_id=1, source_target_pairs={{0,1},{1,0},{2,3},{3,2},{4,8},{5,9},{6,10},{7,11},{8,4},{9,5},{10,... | collective-permute-start | bytes 491528 | tf_op jit(solution)/shard_map/hop2_chunk2/ppermute | solution.py:568
  16.5 7.0 %collective-permute-start.9 = (bf16[144,512]{1,0:T(8,128)(2,1)S(1)}, bf16[144,512]{1,0:T(8,128)(2,1)S(1)}, u32[]{:S(2)}, u32[]{:S(2)}) collective-permute-start(bf16[144,512]{1,0:T(8,128)(2,1)S(1)} %get-tuple-element.100), channel_id=1, source_target_pairs={{0,4},{1,5},{2,6},{3,7},{4,0},{5,1},{6,2},{7,3},{8,12},{9,13},{10,... | collective-permute-start | bytes 442376 | tf_op jit(solution)/shard_map/hop3_chunk1/ppermute | solution.py:568
  20.8 2.7 %collective-permute-start.6 = (bf16[128,512]{1,0:T(8,128)(2,1)S(1)}, bf16[128,512]{1,0:T(8,128)(2,1)S(1)}, u32[]{:S(2)}, u32[]{:S(2)}) collective-permute-start(bf16[128,512]{1,0:T(8,128)(2,1)S(1)} %get-tuple-element.95.refs_1_), channel_id=1, source_target_pairs={{0,1},{1,0},{2,3},{3,2},{4,8},{5,9},{6,10},{7,11},{8,4},{9,5},{10,... | collective-permute-start | bytes 393224 | tf_op jit(solution)/shard_map/hop2_chunk3/ppermute | solution.py:568
  21.0 7.4 %collective-permute-start.10 = (bf16[128,640]{1,0:T(8,128)(2,1)S(1)}, bf16[128,640]{1,0:T(8,128)(2,1)S(1)}, u32[]{:S(2)}, u32[]{:S(2)}) collective-permute-start(bf16[128,640]{1,0:T(8,128)(2,1)S(1)} %get-tuple-element.101.refs_1_), channel_id=1, source_target_pairs={{0,1},{1,0},{2,3},{3,2},{4,5},{5,4},{6,7},{7,6},{8,12},{9,13},{10,... | collective-permute-start | bytes 491528 | tf_op jit(solution)/shard_map/hop3_chunk2/ppermute | solution.py:568
  23.5 4.9 %collective-permute-start.11 = (bf16[128,512]{1,0:T(8,128)(2,1)S(1)}, bf16[128,512]{1,0:T(8,128)(2,1)S(1)}, u32[]{:S(2)}, u32[]{:S(2)}) collective-permute-start(bf16[128,512]{1,0:T(8,128)(2,1)S(1)} %get-tuple-element.103.rest_3_), channel_id=1, source_target_pairs={{0,1},{1,0},{2,3},{3,2},{4,5},{5,4},{6,7},{7,6},{8,12},{9,13},{10,... | collective-permute-start | bytes 393224 | tf_op jit(solution)/shard_map/hop3_chunk3/ppermute | solution.py:568
  24.8 7.2 %collective-permute-start.13 = (bf16[4,2048]{1,0:T(4,128)(2,1)S(1)}, bf16[4,2048]{1,0:T(4,128)(2,1)S(1)}, u32[]{:S(2)}, u32[]{:S(2)}) collective-permute-start(bf16[4,2048]{1,0:T(4,128)(2,1)S(1)} %get-tuple-element.112), channel_id=1, source_target_pairs={{0,8},{1,9},{2,10},{3,11},{4,5},{5,4},{6,7},{7,6},{8,0},{9,1},{10,... | collective-permute-start | bytes 49160 | tf_op jit(solution)/shard_map/ppermute | solution.py:568
  27.7 7.1 %collective-permute-start.14 = (bf16[4,2048]{1,0:T(4,128)(2,1)S(1)}, bf16[4,2048]{1,0:T(4,128)(2,1)S(1)}, u32[]{:S(2)}, u32[]{:S(2)}) collective-permute-start(bf16[4,2048]{1,0:T(4,128)(2,1)S(1)} %get-tuple-element.113), channel_id=1, source_target_pairs={{0,1},{1,0},{2,3},{3,2},{4,8},{5,9},{6,10},{7,11},{8,4},{9,5},{10,... | collective-permute-start | bytes 49160 | tf_op jit(solution)/shard_map/ppermute | solution.py:568
  27.7 7.1 %collective-permute-start.12 = (bf16[4,2048]{1,0:T(4,128)(2,1)S(1)}, bf16[4,2048]{1,0:T(4,128)(2,1)S(1)}, u32[]{:S(2)}, u32[]{:S(2)}) collective-permute-start(bf16[4,2048]{1,0:T(4,128)(2,1)S(1)} %get-tuple-element.107.refs_1_), channel_id=1, source_target_pairs={{0,4},{1,5},{2,6},{3,7},{4,0},{5,1},{6,2},{7,3},{8,9},{9,8},{10,11... | collective-permute-start | bytes 49160 | tf_op jit(solution)/shard_map/ppermute | solution.py:568
  28.7 6.1 %collective-permute-start.15 = (bf16[4,2048]{1,0:T(4,128)(2,1)S(1)}, bf16[4,2048]{1,0:T(4,128)(2,1)S(1)}, u32[]{:S(2)}, u32[]{:S(2)}) collective-permute-start(bf16[4,2048]{1,0:T(4,128)(2,1)S(1)} %get-tuple-element.114), channel_id=1, source_target_pairs={{0,12},{1,13},{2,14},{3,15},{4,5},{5,4},{6,7},{7,6},{8,9},{9,8},{1... | collective-permute-start | bytes 49160 | tf_op jit(solution)/shard_map/ppermute | solution.py:568
  32.1 2.7 %collective-permute-start.16 = (bf16[4,2048]{1,0:T(4,128)(2,1)S(1)}, bf16[4,2048]{1,0:T(4,128)(2,1)S(1)}, u32[]{:S(2)}, u32[]{:S(2)}) collective-permute-start(bf16[4,2048]{1,0:T(4,128)(2,1)S(1)} %get-tuple-element.115), channel_id=1, source_target_pairs={{0,1},{1,0},{2,3},{3,2},{4,12},{5,13},{6,14},{7,15},{8,9},{9,8},{1... | collective-permute-start | bytes 49160 | tf_op jit(solution)/shard_map/ppermute | solution.py:568
  32.1 2.7 %collective-permute-start.17 = (bf16[4,2048]{1,0:T(4,128)(2,1)S(1)}, bf16[4,2048]{1,0:T(4,128)(2,1)S(1)}, u32[]{:S(2)}, u32[]{:S(2)}) collective-permute-start(bf16[4,2048]{1,0:T(4,128)(2,1)S(1)} %get-tuple-element.116), channel_id=1, source_target_pairs={{0,1},{1,0},{2,3},{3,2},{4,5},{5,4},{6,7},{7,6},{8,12},{9,13},{10,... | collective-permute-start | bytes 49160 | tf_op jit(solution)/shard_map/ppermute | solution.py:568

commit v17 on v15

--- a/solution.py
+++ b/solution.py
@@ -372,15 +372,12 @@
 
 
 def outer_kernel(parts, bounds, count, c_ref, cum_ref, carry_ref, *rest):
-    final = len(parts) > 1
     part = parts[-1]
+    final = True
     got_refs = rest[: len(part)]
     inner_refs = rest[len(part) : len(part) + cum_ref.shape[0] // (H // G)]
-    if final:
-        early_ref, out_hbm, token_ref, out_ref, sems = rest[-5:]
-        token_ref[...] = jnp.zeros_like(token_ref)
-    else:
-        out_ref = rest[-1]
+    out_hbm, token_ref, out_ref, sems = rest[-4:]
+    token_ref[...] = jnp.zeros_like(token_ref)
     heads, tokens = cum_ref.shape
     spans = tokens // SPAN
     group_lanes = H // G * P_SIZE
@@ -391,8 +388,6 @@
         copies.append(pltpu.make_async_copy(source, out_hbm.at[:, lanes], sems.at[len(copies)]))
         copies[-1].start()
 
-    if final:
-        send(early_ref, 0, early_ref.shape[1])
     last = lax.axis_index("seq") == count - 1
     start = jnp.zeros((heads, 1), F32)
     gains = []
@@ -606,10 +601,10 @@
         operands = [c, cum, carry, *[got[count - 1, k] for k in part], *inner, *before]
         return call(
             functools.partial(outer_kernel, parts, bounds, count),
-            (pltpu.HBM((tokens, lanes), BF16), shape((8, 128))) if before else out,
+            (pltpu.HBM((tokens, lanes), BF16), shape((8, 128))),
             in_specs=[in_vmem] * len(operands) + [anywhere] * len(after),
-            out_specs=(in_hbm, in_vmem) if before else in_vmem,
-            scratch_shapes=[out, pltpu.SemaphoreType.DMA((chunks + groups,))] if before else [],
+            out_specs=(in_hbm, in_vmem),
+            scratch_shapes=[out, pltpu.SemaphoreType.DMA((chunks + groups,))],
         )(*operands, *after)
 
     def read_part(ops, final, *after):
@@ -670,8 +665,7 @@
     last_back = [
         swap(value, op) if four else shift(value, -op) for op, value in zip(ends, reading)
     ]
-    outer = outer_part((early,), carry, [], mine)
-    prefill, end_token = outer_part((early, late), carry, [outer])
+    prefill, end_token = outer_part((early + late,), carry, [], mine)
     end_token = token(end_token, *back, flops=TOKEN_COST)
     ops, back = ops + ends, back + last_back
 

time: 35.6 us -> 35.5 us (level)
    pallas_call x2 -> x1, Pallas kernels: 2.11 us -> 1.88 us  [outer_part(): call(functools.partial(outer_kernel, parts, bounds, count), (pltpu.HBM((t...]
  transfers between devices with their start and end apart: 18 -> 18, of which waited for: 5 -> 6; matrix products, arithmetic and copies ran while one was open for 0% -> 0% of each run, Pallas kernels for 22% -> 22%
where the time goes in v17:
time: 35.5 us; the launch traced here: 35.2 us
  starting transfers between devices  16.6 us (47%)
  Pallas kernels  10.2 us (29%)
  waiting for transfers between devices  7.54 us (21%)
  between operations  0.84 us (2%)
    ppermute x18, starting transfers between devices, swap(): return lax.ppermute(value, ('seq', 'tp'), pairs)  16.6 us
    ppermute x18, waiting for transfers between devices, swap(): return lax.ppermute(value, ('seq', 'tp'), pairs)  7.54 us
    pallas_call x2, Pallas kernels, inner_part(): call(functools.partial(inner_kernel, g), shape((tokens, group_lanes)), in...  2.16 us
    pallas_call x1, Pallas kernels, outer_part(): call(functools.partial(outer_kernel, parts, bounds, count), (pltpu.HBM((t...  1.88 us
    pallas_call x1, Pallas kernels, shards(): call(functools.partial(first_kernel, len(inputs)), tuple((shape(value.sha...  1.88 us
    pallas_call x1, Pallas kernels, state_part(): call(functools.partial(state_kernel, bounds), decay_shapes + total_shapes...  1.31 us
    pallas_call x1, Pallas kernels, ask_part(): call(functools.partial(ask_kernel, ride), (shape((rows, lanes)), shape((r...  0.92 us
    pallas_call x1, Pallas kernels, shards(): call(functools.partial(finish_kernel, ops), jax.ShapeDtypeStruct((count,...  0.72 us
  transfers between devices with their start and end apart: 18, of which 6 were waited for; matrix products, arithmetic and copies ran while one was open for 0% of the time, Pallas kernels for 22%

profile of v17, /device:TPU:0, one launch (start us, length us, event | category | flops | bytes accessed | tf_op | source)
XLA Modules:
  0.0 35.2 jit_solution(954028598358055632)
XLA Ops:
  0.6 1.9 %first_kernel.1 = (bf16[256,2048]{1,0:T(8,128)(2,1)S(1)}, bf16[256,256]{1,0:T(8,128)(2,1)S(1)}, f32[1,32]{1,0:T(1,128)S(1)}, bf16[4,4,256]{2,1,0:T(4,128)(2,1)S(...) custom-call(bf16[256,2048]{1,0:T(8,128)(2,1)} %refs_0_.1, ...), custom_call_target="tpu_custom_call" | custom-call | flops 1 | bytes 1 | tf_op jit(solution)/shard_map/first_kernel/pallas_call | solution.py:523
  2.5 3.1 %collective-permute-start.1 = (bf16[144,384]{1,0:T(8,128)(2,1)S(1)}, bf16[144,384]{1,0:T(8,128)(2,1)S(1)}, u32[]{:S(2)}, u32[]{:S(2)}) collective-permute-start(bf16[144,384]{1,0:T(8,128)(2,1)S(1)} %get-tuple-element.71.rest_2_), channel_id=1, source_target_pairs={{0,4},{1,5},{2,6},{3,7},{4,0},{5,1},{6,2},{7,3},{8,12},{9,13},{10,... | collective-permute-start | bytes 331784 | tf_op jit(solution)/shard_map/hop1_chunk0/ppermute | solution.py:561
  5.6 1.1 %inner_kernel.2.rest_0_.rest_4_ = f32[256,1024]{1,0:T(8,128)S(1)} custom-call(bf16[256,2048]{1,0:T(8,128)(2,1)S(1)} %get-tuple-element.62.x_ref, bf16[256,256]{1,0:T(8,128)(2,1)S(1)} %get-tuple-element.63.b_ref, bf16[256,256]{1,0:T(8,128)(2,1)S(1)} %get-tuple-element.60.c_ref, f32[32,256]{1,0:T(8,128)S(1)} %get-tuple-element.61.cum_ref, ...), custom_call_target="tpu_custom_call" | custom-call | flops 1 | bytes 1 | tf_op jit(solution)/shard_map/inner_kernel/pallas_call | solution.py:572
  6.7 1.3 %state_kernel.1 = (f32[1,384]{1,0:T(1,128)S(1)}, f32[1,512]{1,0:T(1,128)S(1)}, f32[1,640]{1,0:T(1,128)S(1)}, f32[1,512]{1,0:T(1,128)S(1)}, f32[128,512]{1,0:T(8,...) custom-call(bf16[256,2048]{1,0:T(8,128)(2,1)S(1)} %get-tuple-element.62.x_ref, ...), custom_call_target="tpu_custom_call" | custom-call | flops 1 | bytes 1 | tf_op jit(solution)/shard_map/state_kernel/pallas_call | solution.py:546
  8.0 0.1 collective-permute-start
  8.1 0.6 %collective-permute-done.1.got_ref.rest_3_ = bf16[144,384]{1,0:T(8,128)(2,1)S(1)} collective-permute-done((bf16[144,384]{1,0:T(8,128)(2,1)S(1)}, bf16[144,384]{1,0:T(8,128)(2,1)S(1)}, u32[]{:S(2)}, u32[]{:S(2)}) %collective-permute-start.1) | collective-permute-done | bytes 110624 | tf_op jit(solution)/shard_map/hop1_chunk0/ppermute | solution.py:561
  8.7 0.1 pass_kernel.8
  8.7 1.8 %collective-permute-start.4 = (bf16[128,640]{1,0:T(8,128)(2,1)S(1)}, bf16[128,640]{1,0:T(8,128)(2,1)S(1)}, u32[]{:S(2)}, u32[]{:S(2)}) collective-permute-start(bf16[128,640]{1,0:T(8,128)(2,1)S(1)} %get-tuple-element.89), channel_id=1, source_target_pairs={{0,4},{1,5},{2,6},{3,7},{4,0},{5,1},{6,2},{7,3},{8,9},{9,8},{10,11... | collective-permute-start | bytes 491528 | tf_op jit(solution)/shard_map/hop1_chunk2/ppermute | solution.py:561
  10.6 0.0 collective-permute-start.5
  10.6 1.1 %inner_kernel.3.rest_0_.rest_5_ = f32[256,1024]{1,0:T(8,128)S(1)} custom-call(bf16[256,2048]{1,0:T(8,128)(2,1)S(1)} %get-tuple-element.62.x_ref, bf16[256,256]{1,0:T(8,128)(2,1)S(1)} %get-tuple-element.63.b_ref, bf16[256,256]{1,0:T(8,128)(2,1)S(1)} %get-tuple-element.60.c_ref, f32[32,256]{1,0:T(8,128)S(1)} %get-tuple-element.61.cum_ref, ...), custom_call_target="tpu_custom_call" | custom-call | flops 1 | bytes 1 | tf_op jit(solution)/shard_map/inner_kernel/pallas_call | solution.py:572
  11.6 0.4 %fresh_kernel.1 = (f32[4,4,2048]{2,1,0:T(4,128)S(1)}, f32[4,4,2048]{2,1,0:T(4,128)S(1)}, f32[4,4,128]{2,1,0:T(4,128)S(1)}) custom-call(bf16[4,4,2048]{2,1,0:T(4,128)(2,1)S(1)} %get-tuple-element.77.x_ref, bf16[4,4,256]{2,1,0:T(4,128)(2,1)S(1)} %get-tuple-element.78.b_ref, bf16[4,4,256]{2,1,0:T(4,128)(2,1)S(1)} %get-tuple-element.79.c_ref, ...), custom_call_target="tpu_custom_call" | custom-call | flops 1 | bytes 1 | tf_op jit(solution)/shard_map/fresh_kernel/pallas_call | solution.py:592
  12.1 2.4 %collective-permute-done.got_ref = bf16[128,512]{1,0:T(8,128)(2,1)S(1)} collective-permute-done((bf16[128,512]{1,0:T(8,128)(2,1)S(1)}, bf16[128,512]{1,0:T(8,128)(2,1)S(1)}, u32[]{:S(2)}, u32[]{:S(2)}) %collective-permute-start) | collective-permute-done | bytes 131104 | tf_op jit(solution)/shard_map/hop1_chunk1/ppermute | solution.py:561
  14.5 0.1 pass_kernel.9
  14.6 0.1 collective-permute-start.3
  14.6 0.1 collective-permute-start.2
  14.7 0.0 collective-permute-done.5.got_ref
  14.8 0.5 %collective-permute-start.8 = (bf16[128,384]{1,0:T(8,128)(2,1)S(1)}, bf16[128,384]{1,0:T(8,128)(2,1)S(1)}, u32[]{:S(2)}, u32[]{:S(2)}) collective-permute-start(bf16[128,384]{1,0:T(8,128)(2,1)S(1)} %get-tuple-element.98), channel_id=1, source_target_pairs={{0,1},{1,0},{2,3},{3,2},{4,5},{5,4},{6,7},{7,6},{8,12},{9,13},{10,... | collective-permute-start | bytes 294920 | tf_op jit(solution)/shard_map/hop3_chunk0/ppermute | solution.py:561
  15.2 1.3 %collective-permute-done.4.got_ref = bf16[128,640]{1,0:T(8,128)(2,1)S(1)} collective-permute-done((bf16[128,640]{1,0:T(8,128)(2,1)S(1)}, bf16[128,640]{1,0:T(8,128)(2,1)S(1)}, u32[]{:S(2)}, u32[]{:S(2)}) %collective-permute-start.4) | collective-permute-done | bytes 163872 | tf_op jit(solution)/shard_map/hop1_chunk2/ppermute | solution.py:561
  16.5 0.1 pass_kernel.11
  16.6 0.1 collective-permute-start.7
  16.7 0.0 collective-permute-done.3.got_ref.rest_1_
  16.7 3.1 %collective-permute-start.9 = (bf16[144,512]{1,0:T(8,128)(2,1)S(1)}, bf16[144,512]{1,0:T(8,128)(2,1)S(1)}, u32[]{:S(2)}, u32[]{:S(2)}) collective-permute-start(bf16[144,512]{1,0:T(8,128)(2,1)S(1)} %get-tuple-element.100), channel_id=1, source_target_pairs={{0,4},{1,5},{2,6},{3,7},{4,0},{5,1},{6,2},{7,3},{8,12},{9,13},{10,... | collective-permute-start | bytes 442376 | tf_op jit(solution)/shard_map/hop3_chunk1/ppermute | solution.py:561
  19.9 1.1 %collective-permute-done.2.got_ref = bf16[128,512]{1,0:T(8,128)(2,1)S(1)} collective-permute-done((bf16[128,512]{1,0:T(8,128)(2,1)S(1)}, bf16[128,512]{1,0:T(8,128)(2,1)S(1)}, u32[]{:S(2)}, u32[]{:S(2)}) %collective-permute-start.2) | collective-permute-done | bytes 131104 | tf_op jit(solution)/shard_map/hop1_chunk3/ppermute | solution.py:561
  21.0 0.1 collective-permute-start.6
  21.1 0.0 collective-permute-done.8.refs_0_.rest_0_
  21.1 0.0 collective-permute-done.7.got_ref
  21.2 0.1 pass_kernel.14
  21.2 0.5 %collective-permute-start.10 = (bf16[128,640]{1,0:T(8,128)(2,1)S(1)}, bf16[128,640]{1,0:T(8,128)(2,1)S(1)}, u32[]{:S(2)}, u32[]{:S(2)}) collective-permute-start(bf16[128,640]{1,0:T(8,128)(2,1)S(1)} %get-tuple-element.101.refs_1_), channel_id=1, source_target_pairs={{0,1},{1,0},{2,3},{3,2},{4,5},{5,4},{6,7},{7,6},{8,12},{9,13},{10,... | collective-permute-start | bytes 491528 | tf_op jit(solution)/shard_map/hop3_chunk2/ppermute | solution.py:561
  21.8 2.0 %collective-permute-done.9.refs_0_.rest_2_.rest_1_ = bf16[144,512]{1,0:T(8,128)(2,1)S(1)} collective-permute-done((bf16[144,512]{1,0:T(8,128)(2,1)S(1)}, bf16[144,512]{1,0:T(8,128)(2,1)S(1)}, u32[]{:S(2)}, u32[]{:S(2)}) %collective-permute-start.9) | collective-permute-done | bytes 147488 | tf_op jit(solution)/shard_map/hop3_chunk1/ppermute | solution.py:561
  23.7 0.0 collective-permute-done.6.got_ref
  23.8 0.1 collective-permute-start.11
  23.8 0.9 %ask_kernel.1 = (f32[16,2048]{1,0:T(8,128)S(1)}, f32[16,32]{1,0:T(8,128)S(1)}, bf16[16,256]{1,0:T(8,128)(2,1)S(1)}) custom-call(bf16[256,2048]{1,0:T(8,128)(2,1)S(1)} %get-tuple-element.62.x_ref, bf16[256,256]{1,0:T(8,128)(2,1)S(1)} %get-tuple-element.63.b_ref, f32[32,256]{1,0:T(8,128)S(1)} %get-tuple-element.61.cum_ref, ...), custom_call_target="tpu_custom_call" | custom-call | flops 1 | bytes 1 | tf_op jit(solution)/shard_map/ask_kernel/pallas_call | solution.py:580
  24.8 0.3 read_kernel.2
  25.0 2.6 %collective-permute-start.13 = (bf16[4,2048]{1,0:T(4,128)(2,1)S(1)}, bf16[4,2048]{1,0:T(4,128)(2,1)S(1)}, u32[]{:S(2)}, u32[]{:S(2)}) collective-permute-start(bf16[4,2048]{1,0:T(4,128)(2,1)S(1)} %get-tuple-element.112), channel_id=1, source_target_pairs={{0,8},{1,9},{2,10},{3,11},{4,5},{5,4},{6,7},{7,6},{8,0},{9,1},{10,... | collective-permute-start | bytes 49160 | tf_op jit(solution)/shard_map/ppermute | solution.py:561
  27.6 0.0 collective-permute-start.14
  27.7 0.9 %collective-permute-start.12 = (bf16[4,2048]{1,0:T(4,128)(2,1)S(1)}, bf16[4,2048]{1,0:T(4,128)(2,1)S(1)}, u32[]{:S(2)}, u32[]{:S(2)}) collective-permute-start(bf16[4,2048]{1,0:T(4,128)(2,1)S(1)} %get-tuple-element.107.refs_1_), channel_id=1, source_target_pairs={{0,4},{1,5},{2,6},{3,7},{4,0},{5,1},{6,2},{7,3},{8,9},{9,8},{10,11... | collective-permute-start | bytes 49160 | tf_op jit(solution)/shard_map/ppermute | solution.py:561
  28.6 0.0 collective-permute-done.10.refs_0_.rest_2_
  28.6 0.0 collective-permute-done.11.rest_3_
  28.6 0.3 read_kernel.3
  28.9 3.1 %collective-permute-start.15 = (bf16[4,2048]{1,0:T(4,128)(2,1)S(1)}, bf16[4,2048]{1,0:T(4,128)(2,1)S(1)}, u32[]{:S(2)}, u32[]{:S(2)}) collective-permute-start(bf16[4,2048]{1,0:T(4,128)(2,1)S(1)} %get-tuple-element.114), channel_id=1, source_target_pairs={{0,12},{1,13},{2,14},{3,15},{4,5},{5,4},{6,7},{7,6},{8,9},{9,8},{1... | collective-permute-start | bytes 49160 | tf_op jit(solution)/shard_map/ppermute | solution.py:561
  31.9 0.0 collective-permute-start.16
  32.0 0.0 collective-permute-done.13.refs_2_.rest_1_
  32.0 0.5 %collective-permute-start.17 = (bf16[4,2048]{1,0:T(4,128)(2,1)S(1)}, bf16[4,2048]{1,0:T(4,128)(2,1)S(1)}, u32[]{:S(2)}, u32[]{:S(2)}) collective-permute-start(bf16[4,2048]{1,0:T(4,128)(2,1)S(1)} %get-tuple-element.116), channel_id=1, source_target_pairs={{0,1},{1,0},{2,3},{3,2},{4,5},{5,4},{6,7},{7,6},{8,12},{9,13},{10,... | collective-permute-start | bytes 49160 | tf_op jit(solution)/shard_map/ppermute | solution.py:561
  32.5 1.9 %outer_kernel.1 = (bf16[256,2048]{1,0:T(8,128)(2,1)}, f32[8,128]{1,0:T(8,128)S(1)}) custom-call(bf16[256,256]{1,0:T(8,128)(2,1)S(1)} %get-tuple-element.60.c_ref, f32[32,256]{1,0:T(8,128)S(1)} %get-tuple-element.61.cum_ref, bf16[128,2048]{1,0:T(8,128)(2,1)S(1)} %get-tuple-element.102.carry_ref, bf16[128,384]{1,0:T(8,128)(2,1)S(1)} %collective-permute-done.8.refs_0_.rest_0_, ...), custom_call_target="tpu_custom_call" | custom-call | flops 1 | bytes 1 | tf_op jit(solution)/shard_map/outer_kernel/pallas_call | solution.py:602
  34.4 0.0 collective-permute-done.14.refs_3_.rest_2_
  34.4 0.0 collective-permute-done.12.refs_1_.rest_0_
  34.4 0.1 collective-permute-done.15.rest_3_
  34.5 0.0 collective-permute-done.16.rest_4_
  34.5 0.0 collective-permute-done.17.rest_5_
  34.5 0.7 %finish_kernel.1 = bf16[4,4,2048]{2,1,0:T(4,128)(2,1)} custom-call(f32[4,4,2048]{2,1,0:T(4,128)S(1)} %get-tuple-element.85.rest_4_.keep_ref, f32[4,4,2048]{2,1,0:T(4,128)S(1)} %get-tuple-element.110.fresh_ref, f32[4,4,128]{2,1,0:T(4,128)S(1)} %get-tuple-element.111.held_ref, bf16[4,2048]{1,0:T(4,128)(2,1)S(1)} %collective-permute-done.12.refs_1_.rest_0_, ...), custom_call_target="tpu_custom_call" | custom-call | flops 1 | bytes 1 | tf_op jit(solution)/shard_map/finish_kernel/pallas_call | solution.py:672
  (8 shorter events, 0.1 us)
Async XLA Ops:
  2.5 6.1 %collective-permute-start.1 = (bf16[144,384]{1,0:T(8,128)(2,1)S(1)}, bf16[144,384]{1,0:T(8,128)(2,1)S(1)}, u32[]{:S(2)}, u32[]{:S(2)}) collective-permute-start(bf16[144,384]{1,0:T(8,128)(2,1)S(1)} %get-tuple-element.71.rest_2_), channel_id=1, source_target_pairs={{0,4},{1,5},{2,6},{3,7},{4,0},{5,1},{6,2},{7,3},{8,12},{9,13},{10,... | collective-permute-start | bytes 331784 | tf_op jit(solution)/shard_map/hop1_chunk0/ppermute | solution.py:561
  8.0 6.5 %collective-permute-start = (bf16[128,512]{1,0:T(8,128)(2,1)S(1)}, bf16[128,512]{1,0:T(8,128)(2,1)S(1)}, u32[]{:S(2)}, u32[]{:S(2)}) collective-permute-start(bf16[128,512]{1,0:T(8,128)(2,1)S(1)} %get-tuple-element.68), channel_id=1, source_target_pairs={{0,4},{1,5},{2,6},{3,7},{4,0},{5,1},{6,2},{7,3},{8,9},{9,8},{10,11... | collective-permute-start | bytes 393224 | tf_op jit(solution)/shard_map/hop1_chunk1/ppermute | solution.py:561
  8.7 7.8 %collective-permute-start.4 = (bf16[128,640]{1,0:T(8,128)(2,1)S(1)}, bf16[128,640]{1,0:T(8,128)(2,1)S(1)}, u32[]{:S(2)}, u32[]{:S(2)}) collective-permute-start(bf16[128,640]{1,0:T(8,128)(2,1)S(1)} %get-tuple-element.89), channel_id=1, source_target_pairs={{0,4},{1,5},{2,6},{3,7},{4,0},{5,1},{6,2},{7,3},{8,9},{9,8},{10,11... | collective-permute-start | bytes 491528 | tf_op jit(solution)/shard_map/hop1_chunk2/ppermute | solution.py:561
  10.6 4.2 %collective-permute-start.5 = (bf16[128,384]{1,0:T(8,128)(2,1)S(1)}, bf16[128,384]{1,0:T(8,128)(2,1)S(1)}, u32[]{:S(2)}, u32[]{:S(2)}) collective-permute-start(bf16[128,384]{1,0:T(8,128)(2,1)S(1)} %get-tuple-element.84.rest_0_), channel_id=1, source_target_pairs={{0,1},{1,0},{2,3},{3,2},{4,8},{5,9},{6,10},{7,11},{8,4},{9,5},{10,... | collective-permute-start | bytes 294920 | tf_op jit(solution)/shard_map/hop2_chunk0/ppermute | solution.py:561
  14.6 2.1 %collective-permute-start.3 = (bf16[144,512]{1,0:T(8,128)(2,1)S(1)}, bf16[144,512]{1,0:T(8,128)(2,1)S(1)}, u32[]{:S(2)}, u32[]{:S(2)}) collective-permute-start(bf16[144,512]{1,0:T(8,128)(2,1)S(1)} %get-tuple-element.88.rest_0_), channel_id=1, source_target_pairs={{0,1},{1,0},{2,3},{3,2},{4,8},{5,9},{6,10},{7,11},{8,4},{9,5},{10,... | collective-permute-start | bytes 442376 | tf_op jit(solution)/shard_map/hop2_chunk1/ppermute | solution.py:561
  14.6 6.4 %collective-permute-start.2 = (bf16[128,512]{1,0:T(8,128)(2,1)S(1)}, bf16[128,512]{1,0:T(8,128)(2,1)S(1)}, u32[]{:S(2)}, u32[]{:S(2)}) collective-permute-start(bf16[128,512]{1,0:T(8,128)(2,1)S(1)} %get-tuple-element.86), channel_id=1, source_target_pairs={{0,4},{1,5},{2,6},{3,7},{4,0},{5,1},{6,2},{7,3},{8,9},{9,8},{10,11... | collective-permute-start | bytes 393224 | tf_op jit(solution)/shard_map/hop1_chunk3/ppermute | solution.py:561
  14.8 6.4 %collective-permute-start.8 = (bf16[128,384]{1,0:T(8,128)(2,1)S(1)}, bf16[128,384]{1,0:T(8,128)(2,1)S(1)}, u32[]{:S(2)}, u32[]{:S(2)}) collective-permute-start(bf16[128,384]{1,0:T(8,128)(2,1)S(1)} %get-tuple-element.98), channel_id=1, source_target_pairs={{0,1},{1,0},{2,3},{3,2},{4,5},{5,4},{6,7},{7,6},{8,12},{9,13},{10,... | collective-permute-start | bytes 294920 | tf_op jit(solution)/shard_map/hop3_chunk0/ppermute | solution.py:561
  16.6 4.5 %collective-permute-start.7 = (bf16[128,640]{1,0:T(8,128)(2,1)S(1)}, bf16[128,640]{1,0:T(8,128)(2,1)S(1)}, u32[]{:S(2)}, u32[]{:S(2)}) collective-permute-start(bf16[128,640]{1,0:T(8,128)(2,1)S(1)} %get-tuple-element.96), channel_id=1, source_target_pairs={{0,1},{1,0},{2,3},{3,2},{4,8},{5,9},{6,10},{7,11},{8,4},{9,5},{10,... | collective-permute-start | bytes 491528 | tf_op jit(solution)/shard_map/hop2_chunk2/ppermute | solution.py:561
  16.7 7.0 %collective-permute-start.9 = (bf16[144,512]{1,0:T(8,128)(2,1)S(1)}, bf16[144,512]{1,0:T(8,128)(2,1)S(1)}, u32[]{:S(2)}, u32[]{:S(2)}) collective-permute-start(bf16[144,512]{1,0:T(8,128)(2,1)S(1)} %get-tuple-element.100), channel_id=1, source_target_pairs={{0,4},{1,5},{2,6},{3,7},{4,0},{5,1},{6,2},{7,3},{8,12},{9,13},{10,... | collective-permute-start | bytes 442376 | tf_op jit(solution)/shard_map/hop3_chunk1/ppermute | solution.py:561
  21.0 2.7 %collective-permute-start.6 = (bf16[128,512]{1,0:T(8,128)(2,1)S(1)}, bf16[128,512]{1,0:T(8,128)(2,1)S(1)}, u32[]{:S(2)}, u32[]{:S(2)}) collective-permute-start(bf16[128,512]{1,0:T(8,128)(2,1)S(1)} %get-tuple-element.95.refs_1_), channel_id=1, source_target_pairs={{0,1},{1,0},{2,3},{3,2},{4,8},{5,9},{6,10},{7,11},{8,4},{9,5},{10,... | collective-permute-start | bytes 393224 | tf_op jit(solution)/shard_map/hop2_chunk3/ppermute | solution.py:561
  21.2 7.4 %collective-permute-start.10 = (bf16[128,640]{1,0:T(8,128)(2,1)S(1)}, bf16[128,640]{1,0:T(8,128)(2,1)S(1)}, u32[]{:S(2)}, u32[]{:S(2)}) collective-permute-start(bf16[128,640]{1,0:T(8,128)(2,1)S(1)} %get-tuple-element.101.refs_1_), channel_id=1, source_target_pairs={{0,1},{1,0},{2,3},{3,2},{4,5},{5,4},{6,7},{7,6},{8,12},{9,13},{10,... | collective-permute-start | bytes 491528 | tf_op jit(solution)/shard_map/hop3_chunk2/ppermute | solution.py:561
  23.8 4.8 %collective-permute-start.11 = (bf16[128,512]{1,0:T(8,128)(2,1)S(1)}, bf16[128,512]{1,0:T(8,128)(2,1)S(1)}, u32[]{:S(2)}, u32[]{:S(2)}) collective-permute-start(bf16[128,512]{1,0:T(8,128)(2,1)S(1)} %get-tuple-element.103.rest_3_), channel_id=1, source_target_pairs={{0,1},{1,0},{2,3},{3,2},{4,5},{5,4},{6,7},{7,6},{8,12},{9,13},{10,... | collective-permute-start | bytes 393224 | tf_op jit(solution)/shard_map/hop3_chunk3/ppermute | solution.py:561
  25.0 6.9 %collective-permute-start.13 = (bf16[4,2048]{1,0:T(4,128)(2,1)S(1)}, bf16[4,2048]{1,0:T(4,128)(2,1)S(1)}, u32[]{:S(2)}, u32[]{:S(2)}) collective-permute-start(bf16[4,2048]{1,0:T(4,128)(2,1)S(1)} %get-tuple-element.112), channel_id=1, source_target_pairs={{0,8},{1,9},{2,10},{3,11},{4,5},{5,4},{6,7},{7,6},{8,0},{9,1},{10,... | collective-permute-start | bytes 49160 | tf_op jit(solution)/shard_map/ppermute | solution.py:561
  27.6 6.7 %collective-permute-start.14 = (bf16[4,2048]{1,0:T(4,128)(2,1)S(1)}, bf16[4,2048]{1,0:T(4,128)(2,1)S(1)}, u32[]{:S(2)}, u32[]{:S(2)}) collective-permute-start(bf16[4,2048]{1,0:T(4,128)(2,1)S(1)} %get-tuple-element.113), channel_id=1, source_target_pairs={{0,1},{1,0},{2,3},{3,2},{4,8},{5,9},{6,10},{7,11},{8,4},{9,5},{10,... | collective-permute-start | bytes 49160 | tf_op jit(solution)/shard_map/ppermute | solution.py:561
  27.7 6.7 %collective-permute-start.12 = (bf16[4,2048]{1,0:T(4,128)(2,1)S(1)}, bf16[4,2048]{1,0:T(4,128)(2,1)S(1)}, u32[]{:S(2)}, u32[]{:S(2)}) collective-permute-start(bf16[4,2048]{1,0:T(4,128)(2,1)S(1)} %get-tuple-element.107.refs_1_), channel_id=1, source_target_pairs={{0,4},{1,5},{2,6},{3,7},{4,0},{5,1},{6,2},{7,3},{8,9},{9,8},{10,11... | collective-permute-start | bytes 49160 | tf_op jit(solution)/shard_map/ppermute | solution.py:561
  28.9 5.6 %collective-permute-start.15 = (bf16[4,2048]{1,0:T(4,128)(2,1)S(1)}, bf16[4,2048]{1,0:T(4,128)(2,1)S(1)}, u32[]{:S(2)}, u32[]{:S(2)}) collective-permute-start(bf16[4,2048]{1,0:T(4,128)(2,1)S(1)} %get-tuple-element.114), channel_id=1, source_target_pairs={{0,12},{1,13},{2,14},{3,15},{4,5},{5,4},{6,7},{7,6},{8,9},{9,8},{1... | collective-permute-start | bytes 49160 | tf_op jit(solution)/shard_map/ppermute | solution.py:561
  31.9 2.5 %collective-permute-start.16 = (bf16[4,2048]{1,0:T(4,128)(2,1)S(1)}, bf16[4,2048]{1,0:T(4,128)(2,1)S(1)}, u32[]{:S(2)}, u32[]{:S(2)}) collective-permute-start(bf16[4,2048]{1,0:T(4,128)(2,1)S(1)} %get-tuple-element.115), channel_id=1, source_target_pairs={{0,1},{1,0},{2,3},{3,2},{4,12},{5,13},{6,14},{7,15},{8,9},{9,8},{1... | collective-permute-start | bytes 49160 | tf_op jit(solution)/shard_map/ppermute | solution.py:561
  32.0 2.5 %collective-permute-start.17 = (bf16[4,2048]{1,0:T(4,128)(2,1)S(1)}, bf16[4,2048]{1,0:T(4,128)(2,1)S(1)}, u32[]{:S(2)}, u32[]{:S(2)}) collective-permute-start(bf16[4,2048]{1,0:T(4,128)(2,1)S(1)} %get-tuple-element.116), channel_id=1, source_target_pairs={{0,1},{1,0},{2,3},{3,2},{4,5},{5,4},{6,7},{7,6},{8,12},{9,13},{10,... | collective-permute-start | bytes 49160 | tf_op jit(solution)/shard_map/ppermute | solution.py:561
